TPU v7x, 32 devices: a whole 2x2x4 slice. The times are simulated.
32 devices in a mesh: parts: 2 (over y), row: 4 (over x, core), col: 4 (over z).
Axes of the slice: x: 2, y: 2, z: 4, core: 2. Of those that a mesh axis runs over, the one named last changes fastest.
Arguments:
- activations: bfloat16 [64, 512, 192], P(('parts', 'row'), 'col'), parts along dimension 0, may hold values from -6 to 6
- cotangent: bfloat16 [64, 512, 192], P(('parts', 'row'), 'col'), parts along dimension 0, may hold values from -6 to 6
- norm_gain: float32 [192], replicated, may hold values from 0.5 to 1.5
- w_qkv: bfloat16 [192, 576], replicated, may hold values from -5 to 5
- w_proj: bfloat16 [192, 192], replicated, may hold values from -0.4375 to 0.4375
Outputs:
- grad_input: bfloat16 [64, 512, 192], P(('parts', 'row'), 'col'), parts along dimension 0
- grad_wqkv: float32 [384, 576], P('parts'), parts along dimension 0
- grad_wproj: float32 [384, 192], P('parts'), parts along dimension 0
- grad_gain: float32 [384], P('parts'), parts along dimension 0
There are 2 independent parts, one for each index of `parts`. A program takes and returns all parts, laid end to end along the dimension named above; an argument that names none is the same for every part. Nothing has to cross between parts.
All inputs are finite; a program needn't handle non-finite values.
Results may differ from a plain program's by a relative error of at most 0.006.
The roundings to bfloat16 on the way count: a program that leaves them out, or rounds other values in their place, can miss the bound.
Values may be sent and summed in bfloat16 or wider, within the bound.
No kernel may reach another device: no remote copies, remote signals or barrier semaphores. Data moves between devices by JAX's collectives and lax.ppermute only.
A program may use at most 64 MiB of HBM per device.

v0:
```python
import math

import jax
import jax.numpy as jnp
from jax import lax
from jax.sharding import PartitionSpec as P

HEADS = 6
HEAD_DIM = 32
WINDOW = 8
SHIFT = 4


EPSILON = 1e-05
MASKED = -100.0


def shifted(block, axis, distance):
    devices = range(lax.axis_size(axis))
    route = [((i - distance) % len(devices), i) for i in devices]
    return lax.ppermute(block, axis, route)


def normalize(tokens):
    centred = tokens.astype(jnp.float32)
    centred = centred - jnp.mean(centred, axis=-1, keepdims=True)
    inv_std = lax.rsqrt(jnp.mean(centred * centred, axis=-1, keepdims=True) + EPSILON)
    return (centred * inv_std, inv_std)


def to_windows(grid):
    extent_r, extent_c = (grid.shape[0], grid.shape[1])
    others = grid.shape[2:]
    blocked = grid.reshape((extent_r // WINDOW, WINDOW, extent_c // WINDOW, WINDOW) + others)
    blocked = jnp.swapaxes(blocked, 1, 2)
    return blocked.reshape((extent_r // WINDOW * (extent_c // WINDOW), WINDOW * WINDOW) + others)


def from_windows(blocks, extent_r, extent_c):
    others = blocks.shape[2:]
    blocked = blocks.reshape((extent_r // WINDOW, extent_c // WINDOW, WINDOW, WINDOW) + others)
    blocked = jnp.swapaxes(blocked, 1, 2)
    return blocked.reshape((extent_r, extent_c) + others)


def region(position, extent):
    return (position >= extent - WINDOW).astype(jnp.int32) + (position >= extent - SHIFT).astype(
        jnp.int32
    )


def split_heads(flat, window_count):
    return flat.reshape(window_count, WINDOW * WINDOW, HEADS, HEAD_DIM)


def contract_rows(left, right):
    return lax.dot_general(
        left, right, (((0,), (0,)), ((), ())), preferred_element_type=jnp.float32
    )


def attend(queries, key_vecs, values, masking):
    score_scale = HEAD_DIM ** (-0.5)
    scores = jnp.einsum("wqhd,wkhd->whqk", queries, key_vecs, preferred_element_type=jnp.float32)
    scores = scores * score_scale + masking[:, None]
    attn_probs = jax.nn.softmax(scores, axis=-1)
    rounded = attn_probs.astype(jnp.bfloat16)
    attended = jnp.einsum("whqk,wkhd->wqhd", rounded, values, preferred_element_type=jnp.float32)
    return (attended.astype(jnp.bfloat16), attn_probs, rounded)


def attend_back(queries, key_vecs, values, grad_out, attn_probs, rounded):
    score_scale = HEAD_DIM ** (-0.5)
    grad_probs = jnp.einsum("wqhd,wkhd->whqk", grad_out, values, preferred_element_type=jnp.float32)
    grad_value = jnp.einsum(
        "whqk,wqhd->wkhd", rounded, grad_out, preferred_element_type=jnp.float32
    )
    inner = jnp.sum(grad_probs * attn_probs, axis=-1, keepdims=True)
    grad_scores = (attn_probs * (grad_probs - inner) * score_scale).astype(jnp.bfloat16)
    grad_query = jnp.einsum(
        "whqk,wkhd->wqhd", grad_scores, key_vecs, preferred_element_type=jnp.float32
    )
    grad_key = jnp.einsum(
        "whqk,wqhd->wkhd", grad_scores, queries, preferred_element_type=jnp.float32
    )
    return (
        grad_query.astype(jnp.bfloat16),
        grad_key.astype(jnp.bfloat16),
        grad_value.astype(jnp.bfloat16),
    )


def on_device(activations, cotangent, norm_gain, w_qkv, w_proj):
    tile_rows, tile_cols, channels = activations.shape
    stacked = jnp.concatenate((activations, cotangent), axis=2)
    arrived = shifted(stacked[:SHIFT], "row", -1)
    stacked = jnp.concatenate((stacked[SHIFT:], arrived), axis=0)
    arrived = shifted(stacked[:, :SHIFT], "col", -1)
    stacked = jnp.concatenate((stacked[:, SHIFT:], arrived), axis=1)
    frame_rows = tile_rows * lax.axis_size("row")
    frame_cols = tile_cols * lax.axis_size("col")
    row_pos = lax.axis_index("row") * tile_rows + jnp.arange(tile_rows, dtype=jnp.int32)
    col_pos = lax.axis_index("col") * tile_cols + jnp.arange(tile_cols, dtype=jnp.int32)
    labels = 3 * region(row_pos, frame_rows)[:, None] + region(col_pos, frame_cols)[None, :]
    window_labels = to_windows(labels)
    window_count = window_labels.shape[0]
    masking = jnp.where(window_labels[:, :, None] == window_labels[:, None, :], 0.0, MASKED).astype(
        jnp.float32
    )
    windowed = to_windows(stacked).reshape(-1, 2 * channels)
    tokens = windowed[:, :channels]
    upstream = windowed[:, channels:]
    x_hat, inv_std = normalize(tokens)
    normed = (x_hat * norm_gain).astype(jnp.bfloat16)
    projected = jnp.dot(normed, w_qkv, preferred_element_type=jnp.float32).astype(jnp.bfloat16)
    grad_out = jnp.dot(upstream, w_proj.T, preferred_element_type=jnp.float32).astype(jnp.bfloat16)
    queries = split_heads(projected[:, :channels], window_count)
    key_vecs = split_heads(projected[:, channels : 2 * channels], window_count)
    values = split_heads(projected[:, 2 * channels :], window_count)
    attended, attn_probs, rounded = attend(queries, key_vecs, values, masking)
    grad_proj = contract_rows(attended.reshape(-1, channels), upstream)
    grad_query, grad_key, grad_value = attend_back(
        queries, key_vecs, values, split_heads(grad_out, window_count), attn_probs, rounded
    )
    grad_qkv = jnp.concatenate(
        (
            grad_query.reshape(-1, channels),
            grad_key.reshape(-1, channels),
            grad_value.reshape(-1, channels),
        ),
        axis=1,
    )
    grad_wqkv = contract_rows(normed, grad_qkv)
    grad_normed = jnp.dot(grad_qkv, w_qkv.T, preferred_element_type=jnp.float32)
    grad_gain = jnp.sum(grad_normed * x_hat, axis=0)
    grad_hat = grad_normed * norm_gain
    branch = inv_std * (
        grad_hat
        - jnp.mean(grad_hat, axis=-1, keepdims=True)
        - x_hat * jnp.mean(grad_hat * x_hat, axis=-1, keepdims=True)
    )
    branch = from_windows(
        branch.reshape(window_count, WINDOW * WINDOW, channels), tile_rows, tile_cols
    )
    arrived = shifted(branch[:, -SHIFT:], "col", 1)
    branch = jnp.concatenate((arrived, branch[:, :-SHIFT]), axis=1)
    arrived = shifted(branch[-SHIFT:].astype(jnp.bfloat16), "row", 1).astype(jnp.float32)
    branch = jnp.concatenate((arrived, branch[:-SHIFT]), axis=0)
    grad_input = (cotangent.astype(jnp.float32) + branch).astype(jnp.bfloat16)
    grad_wqkv, grad_proj, grad_gain = lax.psum((grad_wqkv, grad_proj, grad_gain), ("row", "col"))
    factor = 1.0 / math.sqrt(frame_rows * frame_cols)
    return (grad_input, grad_wqkv * factor, grad_proj * factor, grad_gain * factor)


def solution(mesh):
    in_specs = (P(("parts", "row"), "col", None), P(("parts", "row"), "col", None), P(), P(), P())
    out_specs = (P(("parts", "row"), "col", None), P("parts", None), P("parts", None), P("parts"))
    return jax.shard_map(
        on_device, mesh=mesh, in_specs=in_specs, out_specs=out_specs, check_vma=False
    )
```

profile of v0, /device:TPU:0, one launch (start us, length us, event | category | flops | bytes accessed | tf_op | source)
XLA Modules:
  0.0 177.2 jit_solution(14391996073897955282)
XLA Ops:
  7.2 1.3 copy.23
  8.5 1.2 copy.24
  9.7 0.3 fusion.62
  10.0 2.4 %collective-permute-start = (bf16[4,128,384]{2,1,0:T(8,128)(2,1)S(1)}, bf16[4,128,384]{2,1,0:T(8,128)(2,1)S(1)}, u32[]{:S(2)}, u32[]{:S(2)}) collective-permute-start(bf16[4,128,384]{2,1,0:T(8,128)(2,1)S(1)} %get-tuple-element.17), channel_id=1, source_target_pairs={{4,0},{8,4},{12,8},{0,12},{5,1},{9,5},{13,9},{1,13},{6,2},{10,6},{... | collective-permute-start | bytes 1179656 | tf_op jit(solution)/shard_map/ppermute | solution.py:21
  12.6 1.0 compare_select_fusion
  13.6 4.1 %collective-permute-done = bf16[4,128,384]{2,1,0:T(8,128)(2,1)S(1)} collective-permute-done((bf16[4,128,384]{2,1,0:T(8,128)(2,1)S(1)}, bf16[4,128,384]{2,1,0:T(8,128)(2,1)S(1)}, u32[]{:S(2)}, u32[]{:S(2)}) %collective-permute-start) | collective-permute-done | bytes 393248 | tf_op jit(solution)/shard_map/ppermute | solution.py:21
  17.7 3.7 %collective-permute-start.1 = (bf16[8,4,384]{2,1,0:T(4,128)(2,1)S(1)}, bf16[8,4,384]{2,1,0:T(4,128)(2,1)S(1)}, u32[]{:S(2)}, u32[]{:S(2)}) collective-permute-start(bf16[8,4,384]{2,1,0:T(4,128)(2,1)S(1)} %pad_maximum_fusion.2), channel_id=1, source_target_pairs={{1,0},{2,1},{3,2},{0,3},{5,4},{6,5},{7,6},{4,7},{9,8},{10,9},{11,1... | collective-permute-start | bytes 73736 | tf_op jit(solution)/shard_map/ppermute | solution.py:21
  21.4 0.2 slice_maximum_fusion
  21.7 1.3 collective-permute-done.1
  23.6 0.6 convolution_convert_fusion
  24.2 1.0 fusion.75
  25.2 0.5 reshape.104
  25.7 1.6 reshape.105
  27.3 2.4 %reshape.107 = bf16[16,64,6,32]{1,0,3,2:T(8,128)(2,1)} reshape(bf16[1024,192]{0,1:T(8,128)(2,1)} %get-tuple-element.14) | data formatting | bytes 786432 | tf_op jit(solution)/shard_map/reshape | solution.py:53
  29.7 2.0 %convolution_convert_fusion.3 = bf16[1024,192]{0,1:T(8,128)(2,1)} fusion(bf16[192,192]{1,0:T(8,128)(2,1)} %param.9, bf16[1024,384]{1,0:T(8,128)(2,1)S(1)} %bitcast.58), kind=kOutput, calls=%fused_computation.24 | convolution fusion | flops 75694080 | bytes 991232 | tf_op jit(solution)/shard_map/dot_general | solution.py:116
  31.7 2.4 %reshape.106 = bf16[16,64,6,32]{1,0,3,2:T(8,128)(2,1)} reshape(bf16[1024,192]{0,1:T(8,128)(2,1)} %convolution_convert_fusion.3) | data formatting | bytes 786432 | tf_op jit(solution)/shard_map/reshape | solution.py:53
  34.1 0.7 fusion.47
  34.8 0.4 copy-done.4
  35.2 1.6 fusion.76
  36.8 1.4 fusion.29
  38.3 0.4 copy-done.3
  38.7 1.8 %fusion.28 = bf16[16,64,6,32]{1,3,2,0:T(8,128)(2,1)} fusion(bf16[16,64,6,32]{1,0,3,2:T(8,128)(2,1)S(1)} %copy-done.2, f32[16,6,64,64]{2,3,1,0:T(8,128)S(1)} %get-tuple-element.19, f32[16,6,64]{2,1,0:T(8,128)S(1)} %get-tuple-element.18), kind=kOutput, calls=%fused_computation.22 | convolution fusion | flops 26148864 | bytes 2383872 | tf_op jit(solution)/shard_map/whqk,wqhd->wkhd/dot_general | solution.py:75
  40.5 2.4 %fusion.51 = f32[16,6,64,64]{2,3,1,0:T(8,128)} fusion(bf16[16,64,6,32]{1,0,3,2:T(8,128)(2,1)S(1)} %copy-done.1, bf16[16,64,6,32]{1,0,3,2:T(8,128)(2,1)S(1)} %copy-done.2), kind=kOutput, calls=%fused_computation.56 | convolution fusion | flops 25165824 | bytes 2359296 | tf_op jit(solution)/shard_map/wqhd,wkhd->whqk/dot_general | solution.py:74
  42.9 6.9 %fusion.22 = bf16[16,64,6,32]{1,3,2,0:T(8,128)(2,1)} fusion(f32[16,6,64,64]{2,3,1,0:T(8,128)} %fusion.51, bf16[16,64,6,32]{1,0,3,2:T(8,128)(2,1)S(1)} %reshape.105, f32[16,6,64,64]{2,3,1,0:T(8,128)} %copy-done.3, f32[16,6,64]{2,1,0:T(8,128)} %copy-done.7), kind=kOutput, calls=%fused_computation.20 | convolution fusion | flops 28121152 | bytes 3956736 | tf_op jit(solution)/shard_map/whqk,wqhd->wkhd/dot_general | solution.py:83
  49.8 6.9 %fusion.25 = bf16[16,64,6,32]{1,3,2,0:T(8,128)(2,1)} fusion(f32[16,6,64,64]{2,3,1,0:T(8,128)} %fusion.51, bf16[16,64,6,32]{1,0,3,2:T(8,128)(2,1)S(1)} %reshape.104, f32[16,6,64,64]{2,3,1,0:T(8,128)} %copy-done.3, f32[16,6,64]{2,1,0:T(8,128)} %copy-done.7), kind=kOutput, calls=%fused_computation.21 | convolution fusion | flops 28121152 | bytes 3956736 | tf_op jit(solution)/shard_map/whqk,wkhd->wqhd/dot_general | solution.py:80
  56.7 0.5 copy.42
  57.2 0.5 reshape.110
  57.8 1.6 copy.39
  59.4 0.5 reshape.109
  60.0 1.6 copy.36
  61.6 1.3 reshape.108
  62.9 1.0 constant_dynamic-update-slice_fusion.2
  64.0 1.4 fusion.63
  65.4 1.4 fusion.43
  66.8 0.5 copy.47
  67.3 0.5 reshape.112
  67.9 1.4 fusion.42
  69.3 1.3 copy.43
  70.6 1.3 copy.71
  71.9 0.5 collective-permute-start.2
  72.4 1.1 fusion.59
  73.5 33.6 %psum.23 = f32[192]{0:T(256)S(1)} all-reduce(f32[192]{0:T(256)S(1)} %get-tuple-element.8), channel_id=1, replica_groups=mesh['parts'=2,'row'=4,'col'=4] {'row','col'}, use_global_device_ids=true, to_apply=%region_10.11 | all-reduce | flops 192 | bytes 1536 | tf_op jit(solution)/shard_map/psum | solution.py:150
  107.2 0.6 broadcast_multiply_fusion.5
  107.8 5.2 %collective-permute-done.3 = bf16[4,128,192]{2,1,0:T(8,128)(2,1)S(1)} collective-permute-done((bf16[4,128,192]{2,1,0:T(8,128)(2,1)S(1)}, bf16[4,128,192]{2,1,0:T(8,128)(2,1)S(1)}, u32[]{:S(2)}, u32[]{:S(2)}) %collective-permute-start.3) | collective-permute-done | bytes 196640 | tf_op jit(solution)/shard_map/ppermute | solution.py:21
  113.2 1.0 copy.48
  114.2 52.7 %all-reduce.3.cloned.1.call-done = (f32[192,576]{1,0:T(8,128)}, f32[192,192]{1,0:T(8,128)}) async-done(((f32[192,576]{1,0:T(8,128)}, f32[192,192]{1,0:T(8,128)}), (f32[192,576]{1,0:T(8,128)}, f32[192,192]{1,0:T(8,128)})) %all-reduce.3.cloned.1.call-update) | async-done | bytes 589840 | tf_op jit(solution)/shard_map/psum | solution.py:150
  166.9 1.8 %broadcast_multiply_fusion = f32[192,576]{1,0:T(8,128)} fusion(f32[192,576]{1,0:T(8,128)} %get-tuple-element.11), kind=kLoop, calls=%fused_computation.71 | loop fusion | flops 110592 | bytes 884736 | tf_op jit(solution)/shard_map/mul | solution.py:152
  168.7 1.6 broadcast_multiply_fusion.1
  (40 shorter events, 1.3 us)
Async XLA Ops:
  7.2 16.4 %copy-start = (bf16[192,576]{1,0:T(8,128)(2,1)S(1)}, bf16[192,576]{1,0:T(8,128)(2,1)}, u32[]{:S(2)}) copy-start(bf16[192,576]{1,0:T(8,128)(2,1)} %param.8) | copy-start | bytes 663556
  7.2 159.7 %all-reduce.3.cloned.1.call-start = ((), (), s32[]{:S(2)}) async-start(), calls=%async_computation | async-start | bytes 1376256 | tf_op jit(solution)/shard_map/psum | solution.py:150
  10.0 7.7 %collective-permute-start = (bf16[4,128,384]{2,1,0:T(8,128)(2,1)S(1)}, bf16[4,128,384]{2,1,0:T(8,128)(2,1)S(1)}, u32[]{:S(2)}, u32[]{:S(2)}) collective-permute-start(bf16[4,128,384]{2,1,0:T(8,128)(2,1)S(1)} %get-tuple-element.17), channel_id=1, source_target_pairs={{4,0},{8,4},{12,8},{0,12},{5,1},{9,5},{13,9},{1,13},{6,2},{10,6},{... | collective-permute-start | bytes 1179656 | tf_op jit(solution)/shard_map/ppermute | solution.py:21
  17.7 5.2 %collective-permute-start.1 = (bf16[8,4,384]{2,1,0:T(4,128)(2,1)S(1)}, bf16[8,4,384]{2,1,0:T(4,128)(2,1)S(1)}, u32[]{:S(2)}, u32[]{:S(2)}) collective-permute-start(bf16[8,4,384]{2,1,0:T(4,128)(2,1)S(1)} %pad_maximum_fusion.2), channel_id=1, source_target_pairs={{1,0},{2,1},{3,2},{0,3},{5,4},{6,5},{7,6},{4,7},{9,8},{10,9},{11,1... | collective-permute-start | bytes 73736 | tf_op jit(solution)/shard_map/ppermute | solution.py:21
  21.6 2.0 %copy-start.8 = (f32[192]{0:T(256)S(1)}, f32[192]{0:T(256)}, u32[]{:S(2)}) copy-start(f32[192]{0:T(256)} %param.7) | copy-start | bytes 2308
  34.1 1.0 copy-start.4
  35.2 1.7 copy-start.1
  36.8 1.9 %copy-start.3 = (f32[16,6,64,64]{2,3,1,0:T(8,128)}, f32[16,6,64,64]{2,3,1,0:T(8,128)S(1)}, u32[]{:S(2)}) copy-start(f32[16,6,64,64]{2,3,1,0:T(8,128)S(1)} %get-tuple-element.19) | copy-start | bytes 4718596
  36.8 1.9 %copy-start.7 = (f32[16,6,64]{2,1,0:T(8,128)}, f32[16,6,64]{2,1,0:T(8,128)S(1)}, u32[]{:S(2)}) copy-start(f32[16,6,64]{2,1,0:T(8,128)S(1)} %get-tuple-element.18) | copy-start | bytes 73732
  36.8 1.9 %copy-start.2 = (bf16[16,64,6,32]{1,0,3,2:T(8,128)(2,1)S(1)}, bf16[16,64,6,32]{1,0,3,2:T(8,128)(2,1)}, u32[]{:S(2)}) copy-start(bf16[16,64,6,32]{1,0,3,2:T(8,128)(2,1)} %reshape.106) | copy-start | bytes 1179652
  49.8 6.9 %copy-start.6 = (bf16[16,64,6,32]{1,3,2,0:T(8,128)(2,1)S(1)}, bf16[16,64,6,32]{1,3,2,0:T(8,128)(2,1)}, u32[]{:S(2)}) copy-start(bf16[16,64,6,32]{1,3,2,0:T(8,128)(2,1)} %fusion.28) | copy-start | bytes 1179652
  64.0 2.9 %copy-start.5 = (bf16[16,64,6,32]{1,3,2,0:T(8,128)(2,1)S(1)}, bf16[16,64,6,32]{1,3,2,0:T(8,128)(2,1)}, u32[]{:S(2)}) copy-start(bf16[16,64,6,32]{1,3,2,0:T(8,128)(2,1)} %fusion.29) | copy-start | bytes 1179652
  71.9 35.2 %collective-permute-start.2 = (f32[8,4,192]{2,1,0:T(4,128)S(1)}, f32[8,4,192]{2,1,0:T(4,128)S(1)}, u32[]{:S(2)}, u32[]{:S(2)}) collective-permute-start(f32[8,4,192]{2,1,0:T(4,128)S(1)} %slice.62), channel_id=1, source_target_pairs={{3,0},{0,1},{1,2},{2,3},{7,4},{4,5},{5,6},{6,7},{11,8},{8,9},{9,10... | collective-permute-start | bytes 73736 | tf_op jit(solution)/shard_map/ppermute | solution.py:21
  107.2 5.8 %collective-permute-start.3 = (bf16[4,128,192]{2,1,0:T(8,128)(2,1)S(1)}, bf16[4,128,192]{2,1,0:T(8,128)(2,1)S(1)}, u32[]{:S(2)}, u32[]{:S(2)}) collective-permute-start(bf16[4,128,192]{2,1,0:T(8,128)(2,1)S(1)} %fusion.58), channel_id=1, source_target_pairs={{12,0},{0,4},{4,8},{8,12},{13,1},{1,5},{5,9},{9,13},{14,2},{2,6},{... | collective-permute-start | bytes 589832 | tf_op jit(solution)/shard_map/ppermute | solution.py:21
Sparse Core Ops, SparseCore 0:
  73.6 93.2 all-reduce.2
where the time goes:
time: 178 us; the launch traced here: 177 us
  waiting for transfers between devices  63.3 us (36%)
  blocking collectives  33.6 us (19%)
  matrix products  26.6 us (15%)
  local copies, waits for them, and re-layouts  23.5 us (13%)
  between operations  14.3 us (8%)
  other arithmetic  9.25 us (5%)
  starting transfers between devices  6.64 us (4%)
    psum x1, waiting for transfers between devices, on_device(): lax.psum((grad_wqkv, grad_proj, grad_gain), ('row', 'col'))  52.7 us
    psum x1, blocking collectives, on_device(): lax.psum((grad_wqkv, grad_proj, grad_gain), ('row', 'col'))  33.6 us
    ppermute x4, waiting for transfers between devices, shifted(): return lax.ppermute(block, axis, route)  10.6 us
    dot_general x1, matrix products, attend_back(): jnp.einsum('whqk,wkhd->wqhd', grad_scores, key_vecs, preferred_element_ty...  6.94 us
    reshape x4, local copies, waits for them, and re-layouts, split_heads(): return flat.reshape(window_count, WINDOW * WINDOW, HEADS, HEAD_DIM)  6.88 us
    dot_general x1, matrix products, attend_back(): jnp.einsum('whqk,wqhd->wkhd', grad_scores, queries, preferred_element_typ...  6.87 us
    ppermute x4, starting transfers between devices, shifted(): return lax.ppermute(block, axis, route)  6.61 us
    unnamed x24, local copies, waits for them, and re-layouts  5.5 us
  transfers between devices with their start and end apart: 5, of which 4 were waited for; matrix products, arithmetic and copies ran while one was open for 2% of the time, Pallas kernels for 0%

commit v1 on v0

v1 whole, which is shorter than its diff:
```python
import functools
import math

import jax
import jax.numpy as jnp
from jax import lax
from jax.experimental import pallas as pl
from jax.experimental.pallas import tpu as pltpu
from jax.sharding import PartitionSpec as P

HEADS = 6
HEAD_DIM = 32
WINDOW = 8
SHIFT = 4
PAIR = 2 * WINDOW * WINDOW
EPSILON = 1e-05
MASKED = -100.0
SCALE = HEAD_DIM ** (-0.5)
F32 = jnp.float32
BF16 = jnp.bfloat16


def dot_nn(a, b):
    return lax.dot_general(a, b, (((1,), (0,)), ((), ())), preferred_element_type=F32)


def dot_nt(a, b):
    return lax.dot_general(a, b, (((1,), (1,)), ((), ())), preferred_element_type=F32)


def body(
    flags, x, dy, row_halo, col_halo, corner, gain, w_qkv, w_qkv_t, w_proj,
    out, grads, gain_out,
    xs, dys, x_hat, inv_std, normed, upstream, q_t, k_t, v_t, do_t, k_n, v_n, packed, mask,
):
    rows, cols, channels = x.shape
    windows = cols // WINDOW
    tokens = rows * cols
    pairs = tokens // PAIR
    for i in range(rows):
        for tile, arrived, dest in ((x, 0, xs), (dy, SHIFT, dys)):
            if i < rows - SHIFT:
                line = tile[i + SHIFT].astype(F32)
                tail = col_halo[arrived + i].astype(F32)
            else:
                j = i - (rows - SHIFT)
                line = row_halo[arrived + j].astype(F32)
                tail = corner[arrived + j].astype(F32)
            dest[i] = pltpu.roll(line, cols - SHIFT, 0)
            dest[i, cols - SHIFT :, :] = tail
    k_pos = lax.broadcasted_iota(jnp.int32, (PAIR // 2, PAIR), 0)
    lane = lax.broadcasted_iota(jnp.int32, (PAIR // 2, PAIR), 1)
    q_pos = lane % (PAIR // 2)
    second = lane >= PAIR // 2
    row_cut = (k_pos // WINDOW >= SHIFT) != (q_pos // WINDOW >= SHIFT)
    col_cut = (k_pos % WINDOW >= SHIFT) != (q_pos % WINDOW >= SHIFT)
    row_mask = jnp.where(row_cut, 1.0, 0.0) * flags[0].astype(F32)
    col_mask = jnp.where(col_cut & second, 1.0, 0.0) * flags[1].astype(F32)
    mask[0] = row_mask * MASKED
    mask[1] = jnp.maximum(row_mask, col_mask) * MASKED

    gain_row = gain[...]

    def normalize(p, carry):
        for half in range(2):
            w = 2 * p + half
            at = pl.ds(pl.multiple_of(w * WINDOW, WINDOW), WINDOW)
            to = pl.ds(pl.multiple_of(w * (PAIR // 2), PAIR // 2), PAIR // 2)
            token = xs[:, at, :].reshape(PAIR // 2, channels)
            centred = token - jnp.mean(token, axis=-1, keepdims=True)
            inv = lax.rsqrt(jnp.mean(centred * centred, axis=-1, keepdims=True) + EPSILON)
            hat = centred * inv
            x_hat[to, :] = hat
            inv_std[to, :] = jnp.broadcast_to(inv, (PAIR // 2, 128))
            normed[to, :] = (hat * gain_row).astype(BF16)
            upstream[to, :] = dys[:, at, :].reshape(PAIR // 2, channels).astype(BF16)
        return carry

    lax.fori_loop(0, pairs, normalize, 0)

    n_all = normed[...]
    q_t[...] = dot_nt(w_qkv_t[0:channels], n_all).astype(BF16)
    k_t[...] = dot_nt(w_qkv_t[channels : 2 * channels], n_all).astype(BF16)
    v_t[...] = dot_nt(w_qkv_t[2 * channels :], n_all).astype(BF16)
    k_n[...] = dot_nn(n_all, w_qkv[:, channels : 2 * channels]).astype(BF16)
    v_n[...] = dot_nn(n_all, w_qkv[:, 2 * channels :]).astype(BF16)
    do_t[...] = dot_nt(w_proj[...], upstream[...]).astype(BF16)

    half_n = PAIR // 2
    first_lanes = lax.broadcasted_iota(jnp.int32, (half_n, PAIR), 1) < half_n

    def fold(full):
        return jnp.where(first_lanes, full[:half_n], full[half_n:])

    def spread(v):
        zero = jnp.zeros_like(v)
        return jnp.concatenate(
            (jnp.where(first_lanes, v, zero), jnp.where(first_lanes, zero, v)), axis=0
        ).astype(BF16)

    def attend(p, carry):
        at = pl.ds(pl.multiple_of(p * PAIR, PAIR), PAIR)
        masking = mask[jnp.where(p == pairs - 1, 1, 0)]
        for h in range(HEADS):
            lo = (h // 4) * 128
            hi = min(lo + 128, channels)
            me = slice(h * HEAD_DIM, (h + 1) * HEAD_DIM)
            before, after = h * HEAD_DIM - lo, hi - (h + 1) * HEAD_DIM

            def place(v):
                parts = [v]
                if before:
                    parts = [jnp.zeros((before, PAIR), BF16)] + parts
                if after:
                    parts = parts + [jnp.zeros((after, PAIR), BF16)]
                return jnp.concatenate(parts, axis=0) if len(parts) > 1 else v

            qh, doh = q_t[me, at], do_t[me, at]
            scores = fold(dot_nn(k_n[at, lo:hi], place(qh))) * SCALE + masking
            grown = jnp.exp(scores - jnp.max(scores, axis=0, keepdims=True))
            probs = grown * (1.0 / jnp.sum(grown, axis=0, keepdims=True))
            grad_probs = fold(dot_nn(v_n[at, lo:hi], place(doh)))
            inner = jnp.sum(grad_probs * probs, axis=0, keepdims=True)
            grad_scores = probs * (grad_probs - inner) * SCALE
            p_bd = spread(probs)
            s_bd = spread(grad_scores)
            packed[h * HEAD_DIM : (h + 1) * HEAD_DIM, at] = dot_nn(k_t[me, at], s_bd).astype(BF16)
            r = channels + h * HEAD_DIM
            packed[r : r + HEAD_DIM, at] = dot_nt(qh, s_bd).astype(BF16)
            r = 2 * channels + h * HEAD_DIM
            packed[r : r + HEAD_DIM, at] = dot_nt(doh, p_bd).astype(BF16)
            r = 3 * channels + h * HEAD_DIM
            packed[r : r + HEAD_DIM, at] = dot_nn(v_t[me, at], p_bd).astype(BF16)
        return carry

    lax.fori_loop(0, pairs, attend, 0)

    grads[0 : 3 * channels, :] = dot_nn(packed[0 : 3 * channels, :], n_all).astype(grads.dtype)
    grads[3 * channels :, :] = dot_nn(packed[3 * channels :, :], upstream[...]).astype(grads.dtype)

    def finish(p, total):
        at = pl.ds(pl.multiple_of(p * PAIR, PAIR), PAIR)
        g_t = dot_nn(w_qkv[...], packed[0 : 3 * channels, at])
        g = jnp.transpose(g_t)
        hat = x_hat[at, :]
        gx = g * hat
        total = total + jnp.sum(gx, axis=0, keepdims=True)
        gh = g * gain_row
        ghx = gx * gain_row
        mean_a = jnp.mean(gh, axis=-1, keepdims=True)
        mean_b = jnp.mean(ghx, axis=-1, keepdims=True)
        branch = inv_std[at, 0:1] * (gh - mean_a - hat * mean_b)
        for half in range(2):
            w = 2 * p + half
            to = pl.ds(pl.multiple_of(w * WINDOW, WINDOW), WINDOW)
            piece = branch[half * half_n : (half + 1) * half_n].reshape(WINDOW, WINDOW, channels)
            xs[:, to, :] = dys[:, to, :] + piece
        return total

    gain_out[...] = lax.fori_loop(0, pairs, finish, jnp.zeros((1, channels), F32))
    for i in range(rows):
        out[i] = pltpu.roll(xs[i], SHIFT, 0).astype(BF16)


def half_block(flags, x, dy, row_halo, col_halo, corner, gain, w_qkv, w_qkv_t, w_proj):
    rows, cols, channels = x.shape
    tokens = rows * cols
    vm = pl.BlockSpec(memory_space=pltpu.VMEM)
    flat = lambda dtype: pltpu.VMEM((tokens, channels), dtype)
    turned = pltpu.VMEM((channels, tokens), BF16)
    return pl.pallas_call(
        body,
        out_shape=(
            jax.ShapeDtypeStruct((rows, cols, channels), BF16),
            jax.ShapeDtypeStruct((4 * channels, channels), BF16),
            jax.ShapeDtypeStruct((1, channels), F32),
        ),
        in_specs=[pl.BlockSpec(memory_space=pltpu.SMEM)] + [vm] * 9,
        out_specs=(vm, vm, vm),
        scratch_shapes=[
            pltpu.VMEM((rows, cols, channels), F32),
            pltpu.VMEM((rows, cols, channels), F32),
            flat(F32),
            pltpu.VMEM((tokens, 128), F32),
            flat(BF16),
            flat(BF16),
            turned, turned, turned, turned,
            flat(BF16),
            flat(BF16),
            pltpu.VMEM((4 * channels, tokens), BF16),
            pltpu.VMEM((2, PAIR // 2, PAIR), F32),
        ],
        compiler_params=pltpu.CompilerParams(vmem_limit_bytes=40 * 2**20),
        name="half_block",
    )(flags, x, dy, row_halo, col_halo, corner, gain, w_qkv, w_qkv_t, w_proj)


def flip(extent, bit):
    return [(i, i ^ bit) for i in range(extent)]


def all_sum(block, row_index, row_extent, col_extent):
    n = block.shape[0] // 2
    upper = row_index % 2 == 1
    keep = jnp.where(upper, block[n:], block[:n])
    send = jnp.where(upper, block[:n], block[n:])
    total = keep + lax.ppermute(send, "row", flip(row_extent, 1))
    bit = 2
    while bit < row_extent:
        total = total + lax.ppermute(total, "row", flip(row_extent, bit))
        bit *= 2
    bit = 1
    while bit < col_extent:
        total = total + lax.ppermute(total, "col", flip(col_extent, bit))
        bit *= 2
    other = lax.ppermute(total, "row", flip(row_extent, 1))
    return jnp.concatenate((jnp.where(upper, other, total), jnp.where(upper, total, other)), axis=0)


def on_device(activations, cotangent, norm_gain, w_qkv, w_proj):
    rows, cols, channels = activations.shape
    row_extent, col_extent = lax.axis_size("row"), lax.axis_size("col")
    row_index, col_index = lax.axis_index("row"), lax.axis_index("col")
    up = [(i, (i - 1) % row_extent) for i in range(row_extent)]
    left = [(i, (i - 1) % col_extent) for i in range(col_extent)]
    both = [
        (r * col_extent + c, (r - 1) % row_extent * col_extent + (c - 1) % col_extent)
        for r in range(row_extent)
        for c in range(col_extent)
    ]
    turn = lambda route: [(b, a) for a, b in route]
    row_halo = lax.ppermute(
        jnp.concatenate((activations[:SHIFT], cotangent[:SHIFT]), axis=0), "row", up
    )
    col_halo = lax.ppermute(
        jnp.concatenate((activations[SHIFT:, :SHIFT], cotangent[SHIFT:, :SHIFT]), axis=0),
        "col",
        left,
    )
    corner = lax.ppermute(
        jnp.concatenate((activations[:SHIFT, :SHIFT], cotangent[:SHIFT, :SHIFT]), axis=0),
        ("row", "col"),
        both,
    )
    flags = jnp.stack((row_index == row_extent - 1, col_index == col_extent - 1)).astype(jnp.int32)
    shifted_out, grads, gain_sum = half_block(
        flags, activations, cotangent, row_halo, col_halo, corner,
        norm_gain.reshape(1, channels), w_qkv, w_qkv.T, w_proj,
    )
    rows_back = lax.ppermute(shifted_out[rows - SHIFT :], "row", turn(up))
    cols_back = lax.ppermute(shifted_out[: rows - SHIFT, :SHIFT], "col", turn(left))
    corner_back = lax.ppermute(
        shifted_out[rows - SHIFT :, :SHIFT], ("row", "col"), turn(both)
    )
    lower = shifted_out[: rows - SHIFT].at[:, :SHIFT].set(cols_back)
    higher = rows_back.at[:, :SHIFT].set(corner_back)
    grad_input = jnp.concatenate((higher, lower), axis=0)

    gain_rows = jnp.pad(gain_sum.astype(BF16), ((0, 31), (0, 0)))
    flat = jnp.concatenate((grads, gain_rows), axis=0)
    total = all_sum(flat, row_index, row_extent, col_extent).astype(F32)
    frame = rows * row_extent * cols * col_extent
    factor = 1.0 / math.sqrt(frame)
    total = total * factor
    grad_wqkv = total[: 3 * channels].T
    grad_wproj = total[3 * channels : 4 * channels]
    return grad_input, grad_wqkv, grad_wproj, total[4 * channels]


def solution(mesh):
    tile = P(("parts", "row"), "col", None)
    return jax.shard_map(
        on_device,
        mesh=mesh,
        in_specs=(tile, tile, P(), P(), P()),
        out_specs=(tile, P("parts", None), P("parts", None), P("parts")),
        check_vma=False,
    )
```

time: 178 us -> 66.8 us (0.38)
  waiting for transfers between devices: 63.3 us -> 21.6 us
  blocking collectives: 33.6 us -> 0 us
  matrix products: 26.6 us -> 0 us
  Pallas kernels: 0 us -> 20.6 us
  local copies, waits for them, and re-layouts: 23.5 us -> 7.7 us
  between operations: 14.3 us -> 0.82 us
  other arithmetic: 9.25 us -> 0.7 us
  starting transfers between devices: 6.64 us -> 15.1 us
    psum x1 -> x0, waiting for transfers between devices: 52.7 us -> none  [on_device(): lax.psum((grad_wqkv, grad_proj, grad_gain), ('row', 'col'))]
    psum x1 -> x0, blocking collectives: 33.6 us -> none  [on_device(): lax.psum((grad_wqkv, grad_proj, grad_gain), ('row', 'col'))]
    dot_general x11 -> x0, matrix products: 26.6 us -> none  [the longest x1 6.94 us: attend_back(): jnp.einsum('whqk,wkhd->wqhd', grad_scores, key_vecs, preferred_element_ty...]
    pallas_call x0 -> x1, Pallas kernels: none -> 20.6 us  [half_block(): pl.pallas_call(body, out_shape=(jax.ShapeDtypeStruct((rows, cols, channel...]
    ppermute x4 -> x11, waiting for transfers between devices: 10.6 us -> 21.6 us  [the longest x2 8 us: all_sum(): total = total + lax.ppermute(total, 'col', flip(col_extent, bit))]
    reshape x8 -> x0, local copies, waits for them, and re-layouts: 9.77 us -> none  [the longest x4 6.88 us: split_heads(): return flat.reshape(window_count, WINDOW * WINDOW, HEADS, HEAD_DIM)]
    ppermute x4 -> x11, starting transfers between devices: 6.61 us -> 15.1 us  [the longest x2 4.3 us: all_sum(): total = total + lax.ppermute(total, 'col', flip(col_extent, bit))]
    mul x5 -> x1, other arithmetic: 5.39 us -> 0.07 us  [on_device(): total = total * factor]
  transfers between devices with their start and end apart: 5 -> 11, of which waited for: 4 -> 8; matrix products, arithmetic and copies ran while one was open for 2% -> 2% of each run, Pallas kernels for 0% -> 0%
where the time goes in v1:
time: 66.8 us; the launch traced here: 66.5 us
  waiting for transfers between devices  21.6 us (32%)
  Pallas kernels  20.6 us (31%)
  starting transfers between devices  15.1 us (23%)
  local copies, waits for them, and re-layouts  7.7 us (12%)
  between operations  0.82 us (1%)
  other arithmetic  0.7 us (1%)
    pallas_call x1, Pallas kernels, half_block(): pl.pallas_call(body, out_shape=(jax.ShapeDtypeStruct((rows, cols, channel...  20.6 us
    ppermute x2, waiting for transfers between devices, all_sum(): total = total + lax.ppermute(total, 'col', flip(col_extent, bit))  8 us
    ppermute x1, waiting for transfers between devices, all_sum(): total = total + lax.ppermute(total, 'row', flip(row_extent, bit))  5.88 us
    unnamed x17, local copies, waits for them, and re-layouts  5.39 us
    ppermute x2, starting transfers between devices, all_sum(): total = total + lax.ppermute(total, 'col', flip(col_extent, bit))  4.3 us
    ppermute x1, waiting for transfers between devices, on_device(): lax.ppermute(shifted_out[:rows - SHIFT, :SHIFT], 'col', turn(left))  3.88 us
    ppermute x1, starting transfers between devices, on_device(): lax.ppermute(jnp.concatenate((activations[SHIFT:, :SHIFT], cotangent[SHIF...  3.66 us
    ppermute x1, starting transfers between devices, on_device(): lax.ppermute(jnp.concatenate((activations[:SHIFT], cotangent[:SHIFT]), ax...  2.43 us
  transfers between devices with their start and end apart: 11, of which 8 were waited for; matrix products, arithmetic and copies ran while one was open for 2% of the time, Pallas kernels for 0%

profile of v1, /device:TPU:0, one launch (start us, length us, event | category | flops | bytes accessed | tf_op | source)
XLA Modules:
  0.0 66.5 jit_solution(15136416685448290704)
XLA Ops:
  0.6 1.2 %copy.16.x = bf16[8,128,192]{2,1,0:T(8,128)(2,1)S(1)} copy(bf16[8,128,192]{1,2,0:T(8,128)(2,1)} %param.9) | data formatting | bytes 786432 | tf_op args[0]
  1.8 0.0 copy-start
  1.8 0.0 copy-start.5
  1.9 0.8 %copy-done = bf16[8,128,192]{2,1,0:T(8,128)(2,1)} copy-done((bf16[8,128,192]{2,1,0:T(8,128)(2,1)}, bf16[8,128,192]{2,1,0:T(8,128)(2,1)S(1)}, u32[]{:S(2)}) %copy-start) | copy-done | bytes 393240
  2.6 0.4 copy-done.5
  3.0 0.2 copy.17.dy
  3.3 0.0 slice-start
  3.3 0.9 %slice-done = bf16[4,128,192]{2,1,0:T(8,128)(2,1)S(1)} async-done(((bf16[8,128,192]{2,1,0:T(8,128)(2,1)}), bf16[4,128,192]{2,1,0:T(8,128)(2,1)S(1)}, s32[]{:S(2)}) %slice-start) | async-done | bytes 196632 | tf_op jit(solution)/shard_map/slice | solution.py:233
  4.2 0.1 pad_maximum_fusion
  4.3 2.4 %collective-permute-start = (bf16[8,128,192]{2,1,0:T(8,128)(2,1)S(1)}, bf16[8,128,192]{2,1,0:T(8,128)(2,1)S(1)}, u32[]{:S(2)}, u32[]{:S(2)}) collective-permute-start(bf16[8,128,192]{2,1,0:T(8,128)(2,1)S(1)} %pad_maximum_fusion), channel_id=1, source_target_pairs={{0,12},{4,0},{8,4},{12,8},{1,13},{5,1},{9,5},{13,9},{2,14},{6,2},{... | collective-permute-start | bytes 1179656 | tf_op jit(solution)/shard_map/ppermute | solution.py:232
  6.7 0.0 copy-done.1
  6.8 3.7 %collective-permute-start.1 = (bf16[8,4,192]{2,1,0:T(4,128)(2,1)S(1)}, bf16[8,4,192]{2,1,0:T(4,128)(2,1)S(1)}, u32[]{:S(2)}, u32[]{:S(2)}) collective-permute-start(bf16[8,4,192]{2,1,0:T(4,128)(2,1)S(1)} %pad_maximum_fusion.2), channel_id=1, source_target_pairs={{0,3},{1,0},{2,1},{3,2},{4,7},{5,4},{6,5},{7,6},{8,11},{9,8},{10,9... | collective-permute-start | bytes 36872 | tf_op jit(solution)/shard_map/ppermute | solution.py:235
  10.5 0.5 collective-permute-start.2
  11.0 0.1 add_convert_fusion.flags
  11.1 0.0 copy-done.2
  11.1 0.2 copy.15
  11.2 0.6 collective-permute-done.1.col_halo
  11.9 1.8 %collective-permute-done.2.corner = bf16[8,4,192]{2,1,0:T(4,128)(2,1)S(1)} collective-permute-done((bf16[8,4,192]{2,1,0:T(4,128)(2,1)S(1)}, bf16[8,4,192]{2,1,0:T(4,128)(2,1)S(1)}, u32[]{:S(2)}, u32[]{:S(2)}) %collective-permute-start.2) | collective-permute-done | bytes 12320 | tf_op jit(solution)/shard_map/ppermute | solution.py:240
  13.7 0.0 collective-permute-done.row_halo
  13.7 0.7 %copy-done.4 = f32[192]{0:T(256)S(1)} copy-done((f32[192]{0:T(256)S(1)}, f32[192]{0:T(256)}, u32[]{:S(2)}) %copy-start.4) | copy-done | bytes 792
  14.4 20.6 %half_block.1 = (bf16[8,128,192]{2,1,0:T(8,128)(2,1)S(1)}, bf16[768,192]{1,0:T(8,128)(2,1)S(1)}, f32[1,192]{1,0:T(1,128)S(1)}) custom-call(s32[2]{0:T(128)S(1)} %add_convert_fusion.flags, bf16[8,128,192]{2,1,0:T(8,128)(2,1)S(1)} %copy-done.1, bf16[8,128,192]{2,1,0:T(8,128)(2,1)S(1)} %copy.17.dy, bf16[8,128,192]{2,1,0:T(8,128)(2,1)S(1)} %collective-permute-done.row_halo, ...), custom_call_target="tpu_custom_call" | custom-call | tf_op jit(solution)/shard_map/half_block/pallas_call | solution.py:171
  35.0 0.1 broadcast_select_fusion.2
  35.1 0.8 %collective-permute-start.6 = (bf16[400,192]{1,0:T(8,128)(2,1)S(1)}, bf16[400,192]{1,0:T(8,128)(2,1)S(1)}, u32[]{:S(2)}, u32[]{:S(2)}) collective-permute-start(bf16[400,192]{1,0:T(8,128)(2,1)S(1)} %broadcast_select_fusion.2), channel_id=1, source_target_pairs={{0,4},{4,0},{8,12},{12,8},{1,5},{5,1},{9,13},{13,9},{2,6},{6,2},{1... | collective-permute-start | bytes 460808 | tf_op jit(solution)/shard_map/ppermute | solution.py:207
  35.9 1.1 %collective-permute-done.6 = bf16[400,192]{1,0:T(8,128)(2,1)S(1)} collective-permute-done((bf16[400,192]{1,0:T(8,128)(2,1)S(1)}, bf16[400,192]{1,0:T(8,128)(2,1)S(1)}, u32[]{:S(2)}, u32[]{:S(2)}) %collective-permute-start.6) | collective-permute-done | bytes 153632 | tf_op jit(solution)/shard_map/ppermute | solution.py:207
  37.0 0.1 select_add_fusion
  37.1 1.5 %collective-permute-start.7 = (bf16[400,192]{1,0:T(8,128)(2,1)S(1)}, bf16[400,192]{1,0:T(8,128)(2,1)S(1)}, u32[]{:S(2)}, u32[]{:S(2)}) collective-permute-start(bf16[400,192]{1,0:T(8,128)(2,1)S(1)} %select_add_fusion), channel_id=1, source_target_pairs={{0,8},{4,12},{8,0},{12,4},{1,9},{5,13},{9,1},{13,5},{2,10},{6,14},... | collective-permute-start | bytes 460808 | tf_op jit(solution)/shard_map/ppermute | solution.py:210
  38.6 5.9 %collective-permute-done.7 = bf16[400,192]{1,0:T(8,128)(2,1)S(1)} collective-permute-done((bf16[400,192]{1,0:T(8,128)(2,1)S(1)}, bf16[400,192]{1,0:T(8,128)(2,1)S(1)}, u32[]{:S(2)}, u32[]{:S(2)}) %collective-permute-start.7) | collective-permute-done | bytes 153632 | tf_op jit(solution)/shard_map/ppermute | solution.py:210
  44.5 0.1 add.24
  44.5 1.6 %collective-permute-start.8 = (bf16[400,192]{1,0:T(8,128)(2,1)S(1)}, bf16[400,192]{1,0:T(8,128)(2,1)S(1)}, u32[]{:S(2)}, u32[]{:S(2)}) collective-permute-start(bf16[400,192]{1,0:T(8,128)(2,1)S(1)} %add.24), channel_id=1, source_target_pairs={{0,1},{1,0},{2,3},{3,2},{4,5},{5,4},{6,7},{7,6},{8,9},{9,8},{10,11... | collective-permute-start | bytes 460808 | tf_op jit(solution)/shard_map/ppermute | solution.py:214
  46.2 0.1 collective-permute-start.3
  46.3 4.9 %collective-permute-done.8 = bf16[400,192]{1,0:T(8,128)(2,1)S(1)} collective-permute-done((bf16[400,192]{1,0:T(8,128)(2,1)S(1)}, bf16[400,192]{1,0:T(8,128)(2,1)S(1)}, u32[]{:S(2)}, u32[]{:S(2)}) %collective-permute-start.8) | collective-permute-done | bytes 153632 | tf_op jit(solution)/shard_map/ppermute | solution.py:214
  51.1 0.1 add.25
  51.2 2.7 %collective-permute-start.9 = (bf16[400,192]{1,0:T(8,128)(2,1)S(1)}, bf16[400,192]{1,0:T(8,128)(2,1)S(1)}, u32[]{:S(2)}, u32[]{:S(2)}) collective-permute-start(bf16[400,192]{1,0:T(8,128)(2,1)S(1)} %add.25), channel_id=1, source_target_pairs={{0,2},{1,3},{2,0},{3,1},{4,6},{5,7},{6,4},{7,5},{8,10},{9,11},{10,... | collective-permute-start | bytes 460808 | tf_op jit(solution)/shard_map/ppermute | solution.py:214
  53.9 1.6 %collective-permute-start.5 = (bf16[4,4,192]{2,1,0:T(4,128)(2,1)S(1)}, bf16[4,4,192]{2,1,0:T(4,128)(2,1)S(1)}, u32[]{:S(2)}, u32[]{:S(2)}) collective-permute-start(bf16[4,4,192]{2,1,0:T(4,128)(2,1)S(1)} %get-tuple-element.39), channel_id=1, source_target_pairs={{3,0},{0,1},{1,2},{2,3},{7,4},{4,5},{5,6},{6,7},{11,8},{8,9},{9,10... | collective-permute-start | bytes 18440 | tf_op jit(solution)/shard_map/ppermute | solution.py:251
  55.5 0.0 collective-permute-start.4
  55.5 3.9 %collective-permute-done.5 = bf16[4,4,192]{2,1,0:T(4,128)(2,1)S(1)} collective-permute-done((bf16[4,4,192]{2,1,0:T(4,128)(2,1)S(1)}, bf16[4,4,192]{2,1,0:T(4,128)(2,1)S(1)}, u32[]{:S(2)}, u32[]{:S(2)}) %collective-permute-start.5) | collective-permute-done | bytes 6176 | tf_op jit(solution)/shard_map/ppermute | solution.py:251
  59.4 3.1 %collective-permute-done.9 = bf16[400,192]{1,0:T(8,128)(2,1)S(1)} collective-permute-done((bf16[400,192]{1,0:T(8,128)(2,1)S(1)}, bf16[400,192]{1,0:T(8,128)(2,1)S(1)}, u32[]{:S(2)}, u32[]{:S(2)}) %collective-permute-start.9) | collective-permute-done | bytes 153632 | tf_op jit(solution)/shard_map/ppermute | solution.py:214
  62.5 0.1 add.26
  62.6 0.1 collective-permute-start.10
  62.7 0.0 collective-permute-done.4
  62.7 0.0 collective-permute-done.3
  62.7 0.1 pad_maximum_fusion.1
  62.8 1.0 %copy.18 = bf16[8,128,192]{1,2,0:T(8,128)(2,1)} copy(bf16[8,128,192]{2,1,0:T(8,128)(2,1)S(1)} %pad_maximum_fusion.1) | data formatting | bytes 786432
  63.8 0.3 collective-permute-done.10
  64.2 0.1 convert_multiply_fusion
  64.2 0.6 slice.114
  64.8 0.7 %slice.113 = f32[192,192]{1,0:T(8,128)} slice(f32[800,192]{1,0:T(8,128)S(1)} %convert_multiply_fusion), slice={[576:768], [0:192]} | slice | bytes 294912 | tf_op jit(solution)/shard_map/slice | solution.py:266
  65.5 1.0 %copy.19 = f32[192,576]{1,0:T(8,128)} copy(f32[192,576]{0,1:T(8,128)S(1)} %slice_bitcast_fusion) | data formatting | bytes 884736
  (16 shorter events, 0.2 us)
Async XLA Ops:
  1.8 0.8 %copy-start = (bf16[8,128,192]{2,1,0:T(8,128)(2,1)}, bf16[8,128,192]{2,1,0:T(8,128)(2,1)S(1)}, u32[]{:S(2)}) copy-start(bf16[8,128,192]{2,1,0:T(8,128)(2,1)S(1)} %copy.16.x) | copy-start | bytes 1179652
  1.8 1.2 %copy-start.5 = (bf16[8,128,192]{1,2,0:T(8,128)(2,1)S(1)}, bf16[8,128,192]{1,2,0:T(8,128)(2,1)}, u32[]{:S(2)}) copy-start(bf16[8,128,192]{1,2,0:T(8,128)(2,1)} %param.10) | copy-start | bytes 1179652
  3.3 1.0 %slice-start = ((bf16[8,128,192]{2,1,0:T(8,128)(2,1)}), bf16[4,128,192]{2,1,0:T(8,128)(2,1)S(1)}, s32[]{:S(2)}) async-start(bf16[8,128,192]{2,1,0:T(8,128)(2,1)} %copy-done), calls=%async_computation | async-start | bytes 524288 | tf_op jit(solution)/shard_map/slice | solution.py:233
  4.2 2.5 %copy-start.1 = (bf16[8,128,192]{2,1,0:T(8,128)(2,1)S(1)}, bf16[8,128,192]{2,1,0:T(8,128)(2,1)}, u32[]{:S(2)}) copy-start(bf16[8,128,192]{2,1,0:T(8,128)(2,1)} %copy-done) | copy-start | bytes 1179652
  4.2 6.9 %copy-start.2 = (bf16[192,576]{1,0:T(8,128)(2,1)S(1)}, bf16[192,576]{1,0:T(8,128)(2,1)}, u32[]{:S(2)}) copy-start(bf16[192,576]{1,0:T(8,128)(2,1)} %w_qkv.1) | copy-start | bytes 663556
  4.3 9.4 %collective-permute-start = (bf16[8,128,192]{2,1,0:T(8,128)(2,1)S(1)}, bf16[8,128,192]{2,1,0:T(8,128)(2,1)S(1)}, u32[]{:S(2)}, u32[]{:S(2)}) collective-permute-start(bf16[8,128,192]{2,1,0:T(8,128)(2,1)S(1)} %pad_maximum_fusion), channel_id=1, source_target_pairs={{0,12},{4,0},{8,4},{12,8},{1,13},{5,1},{9,5},{13,9},{2,14},{6,2},{... | collective-permute-start | bytes 1179656 | tf_op jit(solution)/shard_map/ppermute | solution.py:232
  6.8 5.1 %collective-permute-start.1 = (bf16[8,4,192]{2,1,0:T(4,128)(2,1)S(1)}, bf16[8,4,192]{2,1,0:T(4,128)(2,1)S(1)}, u32[]{:S(2)}, u32[]{:S(2)}) collective-permute-start(bf16[8,4,192]{2,1,0:T(4,128)(2,1)S(1)} %pad_maximum_fusion.2), channel_id=1, source_target_pairs={{0,3},{1,0},{2,1},{3,2},{4,7},{5,4},{6,5},{7,6},{8,11},{9,8},{10,9... | collective-permute-start | bytes 36872 | tf_op jit(solution)/shard_map/ppermute | solution.py:235
  10.5 3.2 %collective-permute-start.2 = (bf16[8,4,192]{2,1,0:T(4,128)(2,1)S(1)}, bf16[8,4,192]{2,1,0:T(4,128)(2,1)S(1)}, u32[]{:S(2)}, u32[]{:S(2)}) collective-permute-start(bf16[8,4,192]{2,1,0:T(4,128)(2,1)S(1)} %pad_maximum_fusion.3), channel_id=1, source_target_pairs={{0,15},{1,12},{2,13},{3,14},{4,3},{5,0},{6,1},{7,2},{8,7},{9,4},{1... | collective-permute-start | bytes 36872 | tf_op jit(solution)/shard_map/ppermute | solution.py:240
  11.1 2.6 %copy-start.3 = (bf16[192,192]{1,0:T(8,128)(2,1)S(1)}, bf16[192,192]{1,0:T(8,128)(2,1)}, u32[]{:S(2)}) copy-start(bf16[192,192]{1,0:T(8,128)(2,1)} %w_proj.1) | copy-start | bytes 221188
  13.7 0.7 %copy-start.4 = (f32[192]{0:T(256)S(1)}, f32[192]{0:T(256)}, u32[]{:S(2)}) copy-start(f32[192]{0:T(256)} %param.11) | copy-start | bytes 2308
  35.1 1.9 %collective-permute-start.6 = (bf16[400,192]{1,0:T(8,128)(2,1)S(1)}, bf16[400,192]{1,0:T(8,128)(2,1)S(1)}, u32[]{:S(2)}, u32[]{:S(2)}) collective-permute-start(bf16[400,192]{1,0:T(8,128)(2,1)S(1)} %broadcast_select_fusion.2), channel_id=1, source_target_pairs={{0,4},{4,0},{8,12},{12,8},{1,5},{5,1},{9,13},{13,9},{2,6},{6,2},{1... | collective-permute-start | bytes 460808 | tf_op jit(solution)/shard_map/ppermute | solution.py:207
  37.1 7.4 %collective-permute-start.7 = (bf16[400,192]{1,0:T(8,128)(2,1)S(1)}, bf16[400,192]{1,0:T(8,128)(2,1)S(1)}, u32[]{:S(2)}, u32[]{:S(2)}) collective-permute-start(bf16[400,192]{1,0:T(8,128)(2,1)S(1)} %select_add_fusion), channel_id=1, source_target_pairs={{0,8},{4,12},{8,0},{12,4},{1,9},{5,13},{9,1},{13,5},{2,10},{6,14},... | collective-permute-start | bytes 460808 | tf_op jit(solution)/shard_map/ppermute | solution.py:210
  44.5 6.6 %collective-permute-start.8 = (bf16[400,192]{1,0:T(8,128)(2,1)S(1)}, bf16[400,192]{1,0:T(8,128)(2,1)S(1)}, u32[]{:S(2)}, u32[]{:S(2)}) collective-permute-start(bf16[400,192]{1,0:T(8,128)(2,1)S(1)} %add.24), channel_id=1, source_target_pairs={{0,1},{1,0},{2,3},{3,2},{4,5},{5,4},{6,7},{7,6},{8,9},{9,8},{10,11... | collective-permute-start | bytes 460808 | tf_op jit(solution)/shard_map/ppermute | solution.py:214
  46.2 16.5 %collective-permute-start.3 = (bf16[4,128,192]{2,1,0:T(8,128)(2,1)S(1)}, bf16[4,128,192]{2,1,0:T(8,128)(2,1)S(1)}, u32[]{:S(2)}, u32[]{:S(2)}) collective-permute-start(bf16[4,128,192]{2,1,0:T(8,128)(2,1)S(1)} %get-tuple-element.40), channel_id=1, source_target_pairs={{12,0},{0,4},{4,8},{8,12},{13,1},{1,5},{5,9},{9,13},{14,2},{2,6},{... | collective-permute-start | bytes 589832 | tf_op jit(solution)/shard_map/ppermute | solution.py:250
  51.2 11.3 %collective-permute-start.9 = (bf16[400,192]{1,0:T(8,128)(2,1)S(1)}, bf16[400,192]{1,0:T(8,128)(2,1)S(1)}, u32[]{:S(2)}, u32[]{:S(2)}) collective-permute-start(bf16[400,192]{1,0:T(8,128)(2,1)S(1)} %add.25), channel_id=1, source_target_pairs={{0,2},{1,3},{2,0},{3,1},{4,6},{5,7},{6,4},{7,5},{8,10},{9,11},{10,... | collective-permute-start | bytes 460808 | tf_op jit(solution)/shard_map/ppermute | solution.py:214
  53.9 5.5 %collective-permute-start.5 = (bf16[4,4,192]{2,1,0:T(4,128)(2,1)S(1)}, bf16[4,4,192]{2,1,0:T(4,128)(2,1)S(1)}, u32[]{:S(2)}, u32[]{:S(2)}) collective-permute-start(bf16[4,4,192]{2,1,0:T(4,128)(2,1)S(1)} %get-tuple-element.39), channel_id=1, source_target_pairs={{3,0},{0,1},{1,2},{2,3},{7,4},{4,5},{5,6},{6,7},{11,8},{8,9},{9,10... | collective-permute-start | bytes 18440 | tf_op jit(solution)/shard_map/ppermute | solution.py:251
  55.5 7.2 %collective-permute-start.4 = (bf16[4,4,192]{2,1,0:T(4,128)(2,1)S(1)}, bf16[4,4,192]{2,1,0:T(4,128)(2,1)S(1)}, u32[]{:S(2)}, u32[]{:S(2)}) collective-permute-start(bf16[4,4,192]{2,1,0:T(4,128)(2,1)S(1)} %get-tuple-element.38), channel_id=1, source_target_pairs={{15,0},{12,1},{13,2},{14,3},{3,4},{0,5},{1,6},{2,7},{7,8},{4,9},{5... | collective-permute-start | bytes 18440 | tf_op jit(solution)/shard_map/ppermute | solution.py:252
  62.6 1.5 %collective-permute-start.10 = (bf16[400,192]{1,0:T(8,128)(2,1)S(1)}, bf16[400,192]{1,0:T(8,128)(2,1)S(1)}, u32[]{:S(2)}, u32[]{:S(2)}) collective-permute-start(bf16[400,192]{1,0:T(8,128)(2,1)S(1)} %add.26), channel_id=1, source_target_pairs={{0,4},{4,0},{8,12},{12,8},{1,5},{5,1},{9,13},{13,9},{2,6},{6,2},{1... | collective-permute-start | bytes 460808 | tf_op jit(solution)/shard_map/ppermute | solution.py:216

commit v2 on v1

--- a/solution.py
+++ b/solution.py
@@ -30,17 +30,18 @@
 
 def body(
     flags, x, dy, row_halo, col_halo, corner, gain, w_qkv, w_qkv_t, w_proj,
-    out, grads, gain_out,
-    xs, dys, x_hat, inv_std, normed, upstream, q_t, k_t, v_t, do_t, k_n, v_n, packed, mask,
+    low, high, low_tail, high_tail, keep, send,
+    xs, dys, x_hat, inv_std, normed, upstream, q_t, k_t, v_t, do_t, k_n, v_n, packed, mask, halves,
 ):
-    rows, cols, channels = x.shape
+    cols, channels = x.shape[1:]
+    rows = 2 * SHIFT
     windows = cols // WINDOW
     tokens = rows * cols
     pairs = tokens // PAIR
     for i in range(rows):
         for tile, arrived, dest in ((x, 0, xs), (dy, SHIFT, dys)):
             if i < rows - SHIFT:
-                line = tile[i + SHIFT].astype(F32)
+                line = tile[i].astype(F32)
                 tail = col_halo[arrived + i].astype(F32)
             else:
                 j = i - (rows - SHIFT)
@@ -76,7 +77,7 @@
             upstream[to, :] = dys[:, at, :].reshape(PAIR // 2, channels).astype(BF16)
         return carry
 
-    lax.fori_loop(0, pairs, normalize, 0)
+    lax.fori_loop(0, pairs, normalize, 0, unroll=True)
 
     n_all = normed[...]
     q_t[...] = dot_nt(w_qkv_t[0:channels], n_all).astype(BF16)
@@ -101,42 +102,63 @@
     def attend(p, carry):
         at = pl.ds(pl.multiple_of(p * PAIR, PAIR), PAIR)
         masking = mask[jnp.where(p == pairs - 1, 1, 0)]
+        q, do = q_t[:, at], do_t[:, at]
+        heads = [slice(h * HEAD_DIM, (h + 1) * HEAD_DIM) for h in range(HEADS)]
+
+        def place(v, h, lo, hi):
+            before, after = h * HEAD_DIM - lo, hi - (h + 1) * HEAD_DIM
+            parts = [v[heads[h]]]
+            if before:
+                parts = [jnp.zeros((before, PAIR), BF16)] + parts
+            if after:
+                parts = parts + [jnp.zeros((after, PAIR), BF16)]
+            return jnp.concatenate(parts, axis=0) if len(parts) > 1 else parts[0]
+
+        def by_head(tall, v):
+            found = []
+            for lo in range(0, channels, 128):
+                hi = min(lo + 128, channels)
+                here = range(lo // HEAD_DIM, hi // HEAD_DIM)
+                wide = jnp.concatenate([place(v, h, lo, hi) for h in here], axis=1)
+                full = dot_nn(tall[at, lo:hi], wide)
+                found += [fold(full[:, n * PAIR : (n + 1) * PAIR]) for n in range(len(here))]
+            return found
+
+        scores = by_head(k_n, q)
+        grad_probs = by_head(v_n, do)
+        p_bd, s_bd = [], []
         for h in range(HEADS):
-            lo = (h // 4) * 128
-            hi = min(lo + 128, channels)
-            me = slice(h * HEAD_DIM, (h + 1) * HEAD_DIM)
-            before, after = h * HEAD_DIM - lo, hi - (h + 1) * HEAD_DIM
-
-            def place(v):
-                parts = [v]
-                if before:
-                    parts = [jnp.zeros((before, PAIR), BF16)] + parts
-                if after:
-                    parts = parts + [jnp.zeros((after, PAIR), BF16)]
-                return jnp.concatenate(parts, axis=0) if len(parts) > 1 else v
-
-            qh, doh = q_t[me, at], do_t[me, at]
-            scores = fold(dot_nn(k_n[at, lo:hi], place(qh))) * SCALE + masking
-            grown = jnp.exp(scores - jnp.max(scores, axis=0, keepdims=True))
+            s = scores[h] * SCALE + masking
+            grown = jnp.exp(s - jnp.max(s, axis=0, keepdims=True))
             probs = grown * (1.0 / jnp.sum(grown, axis=0, keepdims=True))
-            grad_probs = fold(dot_nn(v_n[at, lo:hi], place(doh)))
-            inner = jnp.sum(grad_probs * probs, axis=0, keepdims=True)
-            grad_scores = probs * (grad_probs - inner) * SCALE
-            p_bd = spread(probs)
-            s_bd = spread(grad_scores)
-            packed[h * HEAD_DIM : (h + 1) * HEAD_DIM, at] = dot_nn(k_t[me, at], s_bd).astype(BF16)
-            r = channels + h * HEAD_DIM
-            packed[r : r + HEAD_DIM, at] = dot_nt(qh, s_bd).astype(BF16)
-            r = 2 * channels + h * HEAD_DIM
-            packed[r : r + HEAD_DIM, at] = dot_nt(doh, p_bd).astype(BF16)
-            r = 3 * channels + h * HEAD_DIM
-            packed[r : r + HEAD_DIM, at] = dot_nn(v_t[me, at], p_bd).astype(BF16)
+            inner = jnp.sum(grad_probs[h] * probs, axis=0, keepdims=True)
+            grad_scores = probs * (grad_probs[h] - inner) * SCALE
+            p_bd.append(spread(probs))
+            s_bd.append(spread(grad_scores))
+        results = []
+        for h in range(HEADS):
+            results.append((
+                dot_nn(k_t[heads[h], at], s_bd[h]),
+                dot_nt(q[heads[h]], s_bd[h]),
+                dot_nt(do[heads[h]], p_bd[h]),
+                dot_nn(v_t[heads[h], at], p_bd[h]),
+            ))
+        for h in range(HEADS):
+            for n in range(4):
+                r = n * channels + h * HEAD_DIM
+                packed[r : r + HEAD_DIM, at] = results[h][n].astype(BF16)
         return carry
 
-    lax.fori_loop(0, pairs, attend, 0)
-
-    grads[0 : 3 * channels, :] = dot_nn(packed[0 : 3 * channels, :], n_all).astype(grads.dtype)
-    grads[3 * channels :, :] = dot_nn(packed[3 * channels :, :], upstream[...]).astype(grads.dtype)
+    lax.fori_loop(0, pairs, attend, 0, unroll=True)
+
+    wide = jnp.transpose(dot_nn(packed[0 : 3 * channels, :], n_all))
+    proj = dot_nn(packed[3 * channels :, :], upstream[...])
+    both = jnp.concatenate((wide, proj), axis=1)
+    core = flags[2]
+    for n in range(2):
+        for j in range(3):
+            lane = (3 * n + j) * 128
+            halves[n, j * channels : (j + 1) * channels, :] = both[:, lane : lane + 128].astype(BF16)
 
     def finish(p, total):
         at = pl.ds(pl.multiple_of(p * PAIR, PAIR), PAIR)
@@ -157,26 +179,44 @@
             xs[:, to, :] = dys[:, to, :] + piece
         return total
 
-    gain_out[...] = lax.fori_loop(0, pairs, finish, jnp.zeros((1, channels), F32))
+    gain_sum = lax.fori_loop(0, pairs, finish, jnp.zeros((1, channels), F32), unroll=True)
+    gain_block = jnp.broadcast_to(
+        jnp.concatenate((gain_sum, jnp.zeros((1, 256 - channels), F32)), axis=1), (16, 256)
+    )
+    for n in range(2):
+        halves[n, 3 * channels :, :] = gain_block[:, n * 128 : (n + 1) * 128].astype(BF16)
+    keep[...] = halves[core]
+    send[...] = halves[1 - core]
     for i in range(rows):
-        out[i] = pltpu.roll(xs[i], SHIFT, 0).astype(BF16)
+        line = pltpu.roll(xs[i], SHIFT, 0)
+        if i < rows - SHIFT:
+            low[i] = jnp.transpose(line.astype(BF16))
+            low_tail[i] = line[:SHIFT].astype(BF16)
+        else:
+            high[i - (rows - SHIFT)] = jnp.transpose(line.astype(BF16))
+            high_tail[i - (rows - SHIFT)] = line[:SHIFT].astype(BF16)
 
 
 def half_block(flags, x, dy, row_halo, col_halo, corner, gain, w_qkv, w_qkv_t, w_proj):
-    rows, cols, channels = x.shape
+    half_rows, cols, channels = x.shape
+    rows = 2 * half_rows
     tokens = rows * cols
     vm = pl.BlockSpec(memory_space=pltpu.VMEM)
     flat = lambda dtype: pltpu.VMEM((tokens, channels), dtype)
     turned = pltpu.VMEM((channels, tokens), BF16)
+    shape = lambda *dims: jax.ShapeDtypeStruct(dims, BF16)
     return pl.pallas_call(
         body,
         out_shape=(
-            jax.ShapeDtypeStruct((rows, cols, channels), BF16),
-            jax.ShapeDtypeStruct((4 * channels, channels), BF16),
-            jax.ShapeDtypeStruct((1, channels), F32),
+            shape(half_rows, channels, cols),
+            shape(half_rows, channels, cols),
+            shape(half_rows, SHIFT, channels),
+            shape(half_rows, SHIFT, channels),
+            shape(3 * channels + 16, 128),
+            shape(3 * channels + 16, 128),
         ),
         in_specs=[pl.BlockSpec(memory_space=pltpu.SMEM)] + [vm] * 9,
-        out_specs=(vm, vm, vm),
+        out_specs=(vm,) * 6,
         scratch_shapes=[
             pltpu.VMEM((rows, cols, channels), F32),
             pltpu.VMEM((rows, cols, channels), F32),
@@ -189,21 +229,78 @@
             flat(BF16),
             pltpu.VMEM((4 * channels, tokens), BF16),
             pltpu.VMEM((2, PAIR // 2, PAIR), F32),
+            pltpu.VMEM((2, 3 * channels + 16, 128), BF16),
         ],
         compiler_params=pltpu.CompilerParams(vmem_limit_bytes=40 * 2**20),
         name="half_block",
     )(flags, x, dy, row_halo, col_halo, corner, gain, w_qkv, w_qkv_t, w_proj)
 
 
+def place_body(low, high, low_tail, high_tail, out):
+    lanes = lax.broadcasted_iota(jnp.int32, low.shape[1:], 1)
+    for source, tails, base in ((high, high_tail, 0), (low, low_tail, SHIFT)):
+        for i in range(SHIFT):
+            tail = jnp.transpose(jnp.concatenate([tails[i]] * (low.shape[2] // SHIFT), axis=0))
+            out[base + i] = jnp.where(lanes < SHIFT, tail, source[i])
+
+
+def place(low, high, low_tail, high_tail):
+    half_rows, channels, cols = low.shape
+    vm = pl.BlockSpec(memory_space=pltpu.VMEM)
+    return pl.pallas_call(
+        place_body,
+        out_shape=jax.ShapeDtypeStruct((2 * half_rows, channels, cols), BF16),
+        in_specs=[vm] * 4,
+        out_specs=vm,
+        compiler_params=pltpu.CompilerParams(vmem_limit_bytes=16 * 2**20),
+        name="place",
+    )(low, high, low_tail, high_tail)
+
+
+def scale_body(flags, mine, other, wqkv, wproj, gain, *, factor):
+    channels = wproj.shape[0]
+    core = flags[2]
+
+    def emit(first, second):
+        wide = jnp.concatenate(
+            [h[j * channels : (j + 1) * channels, :] for h in (first, second) for j in range(3)],
+            axis=1,
+        ).astype(F32) * factor
+        wqkv[...] = wide[:, : 3 * channels]
+        wproj[...] = wide[:, 3 * channels :]
+        row = jnp.concatenate((first[3 * channels :, :], second[3 * channels :, :]), axis=1)
+        gain[...] = row[0:1, :channels].astype(F32) * factor
+
+    @pl.when(core == 0)
+    def _():
+        emit(mine, other)
+
+    @pl.when(core != 0)
+    def _():
+        emit(other, mine)
+
+
+def scale(flags, mine, other, channels, factor):
+    vm = pl.BlockSpec(memory_space=pltpu.VMEM)
+    return pl.pallas_call(
+        functools.partial(scale_body, factor=factor),
+        out_shape=(
+            jax.ShapeDtypeStruct((channels, 3 * channels), F32),
+            jax.ShapeDtypeStruct((channels, channels), F32),
+            jax.ShapeDtypeStruct((1, channels), F32),
+        ),
+        in_specs=[pl.BlockSpec(memory_space=pltpu.SMEM), vm, vm],
+        out_specs=(vm, vm, vm),
+        compiler_params=pltpu.CompilerParams(vmem_limit_bytes=16 * 2**20),
+        name="scale",
+    )(flags, mine, other)
+
+
 def flip(extent, bit):
     return [(i, i ^ bit) for i in range(extent)]
 
 
-def all_sum(block, row_index, row_extent, col_extent):
-    n = block.shape[0] // 2
-    upper = row_index % 2 == 1
-    keep = jnp.where(upper, block[n:], block[:n])
-    send = jnp.where(upper, block[:n], block[n:])
+def sum_half(keep, send, row_extent, col_extent):
     total = keep + lax.ppermute(send, "row", flip(row_extent, 1))
     bit = 2
     while bit < row_extent:
@@ -213,8 +310,7 @@
     while bit < col_extent:
         total = total + lax.ppermute(total, "col", flip(col_extent, bit))
         bit *= 2
-    other = lax.ppermute(total, "row", flip(row_extent, 1))
-    return jnp.concatenate((jnp.where(upper, other, total), jnp.where(upper, total, other)), axis=0)
+    return total
 
 
 def on_device(activations, cotangent, norm_gain, w_qkv, w_proj):
@@ -229,9 +325,9 @@
         for c in range(col_extent)
     ]
     turn = lambda route: [(b, a) for a, b in route]
-    row_halo = lax.ppermute(
-        jnp.concatenate((activations[:SHIFT], cotangent[:SHIFT]), axis=0), "row", up
-    )
+    swap = lambda v: jnp.transpose(v, (0, 2, 1))
+    x_t, dy_t = swap(activations), swap(cotangent)
+    row_halo = lax.ppermute(jnp.concatenate((x_t[:SHIFT], dy_t[:SHIFT]), axis=0), "row", up)
     col_halo = lax.ppermute(
         jnp.concatenate((activations[SHIFT:, :SHIFT], cotangent[SHIFT:, :SHIFT]), axis=0),
         "col",
@@ -242,29 +338,23 @@
         ("row", "col"),
         both,
     )
-    flags = jnp.stack((row_index == row_extent - 1, col_index == col_extent - 1)).astype(jnp.int32)
-    shifted_out, grads, gain_sum = half_block(
-        flags, activations, cotangent, row_halo, col_halo, corner,
+    flags = jnp.stack(
+        (row_index == row_extent - 1, col_index == col_extent - 1, row_index % 2 == 1)
+    ).astype(jnp.int32)
+    low, high, low_tail, high_tail, keep, send = half_block(
+        flags, activations[SHIFT:], cotangent[SHIFT:], swap(row_halo), col_halo, corner,
         norm_gain.reshape(1, channels), w_qkv, w_qkv.T, w_proj,
     )
-    rows_back = lax.ppermute(shifted_out[rows - SHIFT :], "row", turn(up))
-    cols_back = lax.ppermute(shifted_out[: rows - SHIFT, :SHIFT], "col", turn(left))
-    corner_back = lax.ppermute(
-        shifted_out[rows - SHIFT :, :SHIFT], ("row", "col"), turn(both)
-    )
-    lower = shifted_out[: rows - SHIFT].at[:, :SHIFT].set(cols_back)
-    higher = rows_back.at[:, :SHIFT].set(corner_back)
-    grad_input = jnp.concatenate((higher, lower), axis=0)
-
-    gain_rows = jnp.pad(gain_sum.astype(BF16), ((0, 31), (0, 0)))
-    flat = jnp.concatenate((grads, gain_rows), axis=0)
-    total = all_sum(flat, row_index, row_extent, col_extent).astype(F32)
-    frame = rows * row_extent * cols * col_extent
-    factor = 1.0 / math.sqrt(frame)
-    total = total * factor
-    grad_wqkv = total[: 3 * channels].T
-    grad_wproj = total[3 * channels : 4 * channels]
-    return grad_input, grad_wqkv, grad_wproj, total[4 * channels]
+    total = sum_half(keep, send, row_extent, col_extent)
+    other = lax.ppermute(total, "row", flip(row_extent, 1))
+    factor = 1.0 / math.sqrt(rows * row_extent * cols * col_extent)
+    grad_wqkv, grad_wproj, grad_gain = scale(flags, total, other, channels, factor)
+
+    high = lax.ppermute(high, "row", turn(up))
+    low_tail = lax.ppermute(low_tail, "col", turn(left))
+    high_tail = lax.ppermute(high_tail, ("row", "col"), turn(both))
+    grad_input = swap(place(low, high, low_tail, high_tail))
+    return grad_input, grad_wqkv, grad_wproj, grad_gain.reshape(channels)
 
 
 def solution(mesh):

time: 66.8 us -> 52.4 us (0.78)
  Pallas kernels: 20.6 us -> 10.8 us
  local copies, waits for them, and re-layouts: 7.7 us -> 3.3 us
  waiting for transfers between devices: 21.6 us -> 23 us
  starting transfers between devices: 15.1 us -> 14 us
    pallas_call x1 -> x3, Pallas kernels: 20.6 us -> 10.8 us  [the longest x1 8.35 us: half_block(): pl.pallas_call(body, out_shape=(shape(half_rows, channels, cols), shape(h...]
    unnamed x17 -> x11, local copies, waits for them, and re-layouts: 5.39 us -> 3.22 us
    slice x7 -> x4, local copies, waits for them, and re-layouts: 2.23 us -> 0.07 us  [the longest x1 0.02 us: on_device(): cotangent[SHIFT:]]
    ppermute x9, waiting for transfers between devices: 19.2 us -> 21.3 us  [the longest x2 9.85 us: sum_half(): total = total + lax.ppermute(total, 'col', flip(col_extent, bit))]
    ppermute x9, starting transfers between devices: 10.9 us -> 9.99 us  [the longest x2 4.3 us: sum_half(): total = total + lax.ppermute(total, 'col', flip(col_extent, bit))]
  transfers between devices with their start and end apart: 11 -> 11, of which waited for: 8 -> 7; matrix products, arithmetic and copies ran while one was open for 2% -> 1% of each run, Pallas kernels for 0% -> 2%
where the time goes in v2:
time: 52.4 us; the launch traced here: 52.2 us
  waiting for transfers between devices  23 us (44%)
  starting transfers between devices  14 us (27%)
  Pallas kernels  10.8 us (21%)
  local copies, waits for them, and re-layouts  3.3 us (6%)
  between operations  0.78 us (1%)
    ppermute x2, waiting for transfers between devices, sum_half(): total = total + lax.ppermute(total, 'col', flip(col_extent, bit))  9.85 us
    pallas_call x1, Pallas kernels, half_block(): pl.pallas_call(body, out_shape=(shape(half_rows, channels, cols), shape(h...  8.35 us
    ppermute x1, waiting for transfers between devices, sum_half(): total = total + lax.ppermute(total, 'row', flip(row_extent, bit))  4.74 us
    ppermute x1, waiting for transfers between devices, on_device(): low_tail = lax.ppermute(low_tail, 'col', turn(left))  4.69 us
    ppermute x2, starting transfers between devices, sum_half(): total = total + lax.ppermute(total, 'col', flip(col_extent, bit))  4.3 us
    ppermute x1, starting transfers between devices, on_device(): lax.ppermute(jnp.concatenate((activations[SHIFT:, :SHIFT], cotangent[SHIF...  3.66 us
    unnamed x11, local copies, waits for them, and re-layouts  3.22 us
    ppermute x1, starting transfers between devices, on_device(): lax.ppermute(jnp.concatenate((x_t[:SHIFT], dy_t[:SHIFT]), axis=0), 'row',...  2.43 us
  transfers between devices with their start and end apart: 11, of which 7 were waited for; matrix products, arithmetic and copies ran while one was open for 1% of the time, Pallas kernels for 2%

profile of v2, /device:TPU:0, one launch (start us, length us, event | category | flops | bytes accessed | tf_op | source)
XLA Modules:
  0.0 52.2 jit_solution(12477631456604369369)
XLA Ops:
  0.6 0.0 copy-start.3
  0.6 1.2 %copy.10 = bf16[8,128,192]{2,1,0:T(8,128)(2,1)S(1)} copy(bf16[8,128,192]{1,2,0:T(8,128)(2,1)} %param.6) | data formatting | bytes 786432 | tf_op args[1]
  1.9 0.0 copy-done.3
  1.9 0.2 copy.9
  2.2 0.1 pad_maximum_fusion
  2.3 2.4 %collective-permute-start = (bf16[8,192,128]{1,2,0:T(8,128)(2,1)S(1)}, bf16[8,192,128]{1,2,0:T(8,128)(2,1)S(1)}, u32[]{:S(2)}, u32[]{:S(2)}) collective-permute-start(bf16[8,192,128]{1,2,0:T(8,128)(2,1)S(1)} %pad_maximum_fusion), channel_id=1, source_target_pairs={{0,12},{4,0},{8,4},{12,8},{1,13},{5,1},{9,5},{13,9},{2,14},{6,2},{... | collective-permute-start | bytes 1179656 | tf_op jit(solution)/shard_map/ppermute | solution.py:330
  4.7 3.7 %collective-permute-start.1 = (bf16[8,4,192]{2,1,0:T(4,128)(2,1)S(1)}, bf16[8,4,192]{2,1,0:T(4,128)(2,1)S(1)}, u32[]{:S(2)}, u32[]{:S(2)}) collective-permute-start(bf16[8,4,192]{2,1,0:T(4,128)(2,1)S(1)} %pad_maximum_fusion.1), channel_id=1, source_target_pairs={{0,3},{1,0},{2,1},{3,2},{4,7},{5,4},{6,5},{7,6},{8,11},{9,8},{10,9... | collective-permute-start | bytes 36872 | tf_op jit(solution)/shard_map/ppermute | solution.py:331
  8.4 0.3 collective-permute-start.2
  8.8 0.1 add_convert_fusion.flags
  8.9 0.0 copy-start
  8.9 0.9 %copy-done = bf16[192,576]{1,0:T(8,128)(2,1)S(1)} copy-done((bf16[192,576]{1,0:T(8,128)(2,1)S(1)}, bf16[192,576]{1,0:T(8,128)(2,1)}, u32[]{:S(2)}) %copy-start) | copy-done | bytes 221208
  9.8 0.0 copy-start.1
  9.8 0.2 copy.17
  10.0 0.0 collective-permute-done.1.col_halo
  10.0 1.7 %collective-permute-done.2.corner = bf16[8,4,192]{2,1,0:T(4,128)(2,1)S(1)} collective-permute-done((bf16[8,4,192]{2,1,0:T(4,128)(2,1)S(1)}, bf16[8,4,192]{2,1,0:T(4,128)(2,1)S(1)}, u32[]{:S(2)}, u32[]{:S(2)}) %collective-permute-start.2) | collective-permute-done | bytes 12320 | tf_op jit(solution)/shard_map/ppermute | solution.py:336
  11.6 0.0 collective-permute-done
  11.6 0.0 copy-start.2
  11.6 0.0 copy-done.1
  11.7 0.7 %copy-done.2 = f32[192]{0:T(256)S(1)} copy-done((f32[192]{0:T(256)S(1)}, f32[192]{0:T(256)}, u32[]{:S(2)}) %copy-start.2) | copy-done | bytes 792
  12.3 8.3 %half_block.1 = (bf16[4,192,128]{2,1,0:T(8,128)(2,1)S(1)}, bf16[4,192,128]{2,1,0:T(8,128)(2,1)S(1)}, bf16[4,4,192]{2,1,0:T(4,128)(2,1)S(1)}, bf16[4,4,192]{2,1,0...) custom-call(s32[3]{0:T(128)S(1)} %add_convert_fusion.flags, ...), custom_call_target="tpu_custom_call" | custom-call | tf_op jit(solution)/shard_map/half_block/pallas_call | solution.py:208
  20.7 0.8 %collective-permute-start.6 = (bf16[592,128]{1,0:T(8,128)(2,1)S(1)}, bf16[592,128]{1,0:T(8,128)(2,1)S(1)}, u32[]{:S(2)}, u32[]{:S(2)}) collective-permute-start(bf16[592,128]{1,0:T(8,128)(2,1)S(1)} %get-tuple-element.18), channel_id=1, source_target_pairs={{0,4},{4,0},{8,12},{12,8},{1,5},{5,1},{9,13},{13,9},{2,6},{6,2},{1... | collective-permute-start | bytes 454664 | tf_op jit(solution)/shard_map/ppermute | solution.py:304
  21.5 1.0 %collective-permute-done.6 = bf16[592,128]{1,0:T(8,128)(2,1)S(1)} collective-permute-done((bf16[592,128]{1,0:T(8,128)(2,1)S(1)}, bf16[592,128]{1,0:T(8,128)(2,1)S(1)}, u32[]{:S(2)}, u32[]{:S(2)}) %collective-permute-start.6) | collective-permute-done | bytes 151584 | tf_op jit(solution)/shard_map/ppermute | solution.py:304
  22.6 1.5 %collective-permute-start.7 = (bf16[592,128]{1,0:T(8,128)(2,1)S(1)}, bf16[592,128]{1,0:T(8,128)(2,1)S(1)}, u32[]{:S(2)}, u32[]{:S(2)}) collective-permute-start(bf16[592,128]{1,0:T(8,128)(2,1)S(1)} %add.17), channel_id=1, source_target_pairs={{0,8},{4,12},{8,0},{12,4},{1,9},{5,13},{9,1},{13,5},{2,10},{6,14},... | collective-permute-start | bytes 454664 | tf_op jit(solution)/shard_map/ppermute | solution.py:307
  24.1 4.7 %collective-permute-done.7 = bf16[592,128]{1,0:T(8,128)(2,1)S(1)} collective-permute-done((bf16[592,128]{1,0:T(8,128)(2,1)S(1)}, bf16[592,128]{1,0:T(8,128)(2,1)S(1)}, u32[]{:S(2)}, u32[]{:S(2)}) %collective-permute-start.7) | collective-permute-done | bytes 151584 | tf_op jit(solution)/shard_map/ppermute | solution.py:307
  28.9 1.6 %collective-permute-start.8 = (bf16[592,128]{1,0:T(8,128)(2,1)S(1)}, bf16[592,128]{1,0:T(8,128)(2,1)S(1)}, u32[]{:S(2)}, u32[]{:S(2)}) collective-permute-start(bf16[592,128]{1,0:T(8,128)(2,1)S(1)} %add.18), channel_id=1, source_target_pairs={{0,1},{1,0},{2,3},{3,2},{4,5},{5,4},{6,7},{7,6},{8,9},{9,8},{10,11... | collective-permute-start | bytes 454664 | tf_op jit(solution)/shard_map/ppermute | solution.py:311
  30.5 3.8 %collective-permute-done.8 = bf16[592,128]{1,0:T(8,128)(2,1)S(1)} collective-permute-done((bf16[592,128]{1,0:T(8,128)(2,1)S(1)}, bf16[592,128]{1,0:T(8,128)(2,1)S(1)}, u32[]{:S(2)}, u32[]{:S(2)}) %collective-permute-start.8) | collective-permute-done | bytes 151584 | tf_op jit(solution)/shard_map/ppermute | solution.py:311
  34.4 2.7 %collective-permute-start.9 = (bf16[592,128]{1,0:T(8,128)(2,1)S(1)}, bf16[592,128]{1,0:T(8,128)(2,1)S(1)}, u32[]{:S(2)}, u32[]{:S(2)}) collective-permute-start(bf16[592,128]{1,0:T(8,128)(2,1)S(1)} %add.19), channel_id=1, source_target_pairs={{0,2},{1,3},{2,0},{3,1},{4,6},{5,7},{6,4},{7,5},{8,10},{9,11},{10,... | collective-permute-start | bytes 454664 | tf_op jit(solution)/shard_map/ppermute | solution.py:311
  37.1 0.0 collective-permute-start.3
  37.1 6.0 %collective-permute-done.9 = bf16[592,128]{1,0:T(8,128)(2,1)S(1)} collective-permute-done((bf16[592,128]{1,0:T(8,128)(2,1)S(1)}, bf16[592,128]{1,0:T(8,128)(2,1)S(1)}, u32[]{:S(2)}, u32[]{:S(2)}) %collective-permute-start.9) | collective-permute-done | bytes 151584 | tf_op jit(solution)/shard_map/ppermute | solution.py:311
  43.1 0.1 collective-permute-start.10
  43.2 0.7 %collective-permute-start.4 = (bf16[4,4,192]{2,1,0:T(4,128)(2,1)S(1)}, bf16[4,4,192]{2,1,0:T(4,128)(2,1)S(1)}, u32[]{:S(2)}, u32[]{:S(2)}) collective-permute-start(bf16[4,4,192]{2,1,0:T(4,128)(2,1)S(1)} %get-tuple-element.15), channel_id=1, source_target_pairs={{3,0},{0,1},{1,2},{2,3},{7,4},{4,5},{5,6},{6,7},{11,8},{8,9},{9,10... | collective-permute-start | bytes 18440 | tf_op jit(solution)/shard_map/ppermute | solution.py:354
  44.0 0.1 collective-permute-start.5
  44.0 4.7 %collective-permute-done.4.low_tail = bf16[4,4,192]{2,1,0:T(4,128)(2,1)S(1)} collective-permute-done((bf16[4,4,192]{2,1,0:T(4,128)(2,1)S(1)}, bf16[4,4,192]{2,1,0:T(4,128)(2,1)S(1)}, u32[]{:S(2)}, u32[]{:S(2)}) %collective-permute-start.4) | collective-permute-done | bytes 6176 | tf_op jit(solution)/shard_map/ppermute | solution.py:354
  48.7 1.0 %collective-permute-done.5.high_tail = bf16[4,4,192]{2,1,0:T(4,128)(2,1)S(1)} collective-permute-done((bf16[4,4,192]{2,1,0:T(4,128)(2,1)S(1)}, bf16[4,4,192]{2,1,0:T(4,128)(2,1)S(1)}, u32[]{:S(2)}, u32[]{:S(2)}) %collective-permute-start.5) | collective-permute-done | bytes 6176 | tf_op jit(solution)/shard_map/ppermute | solution.py:355
  49.7 0.0 collective-permute-done.3.high
  49.7 0.9 %place.1 = bf16[8,192,128]{2,1,0:T(8,128)(2,1)} custom-call(bf16[4,192,128]{2,1,0:T(8,128)(2,1)S(1)} %get-tuple-element.13.low, bf16[4,192,128]{2,1,0:T(8,128)(2,1)S(1)} %collective-permute-done.3.high, bf16[4,4,192]{2,1,0:T(4,128)(2,1)S(1)} %collective-permute-done.4.low_tail, bf16[4,4,192]{2,1,0:T(4,128)(2,1)S(1)} %collective-permute-done.5.high_tail), custom_call_target="tpu_custom_call" | custom-call | tf_op jit(solution)/shard_map/place/pallas_call | solution.py:250
  50.7 0.0 collective-permute-done.10.other
  50.7 1.5 %scale.1 = (f32[192,576]{1,0:T(8,128)}, f32[192,192]{1,0:T(8,128)}, f32[1,192]{1,0:T(1,128)}) custom-call(s32[3]{0:T(128)S(1)} %add_convert_fusion.flags, bf16[592,128]{1,0:T(8,128)(2,1)S(1)} %add.20.mine, bf16[592,128]{1,0:T(8,128)(2,1)S(1)} %collective-permute-done.10.other), custom_call_target="tpu_custom_call" | custom-call | tf_op jit(solution)/shard_map/scale/pallas_call | solution.py:285
  (11 shorter events, 0.3 us)
Async XLA Ops:
  0.6 1.3 %copy-start.3 = (bf16[8,128,192]{1,2,0:T(8,128)(2,1)S(1)}, bf16[8,128,192]{1,2,0:T(8,128)(2,1)}, u32[]{:S(2)}) copy-start(bf16[8,128,192]{1,2,0:T(8,128)(2,1)} %param.5) | copy-start | bytes 1179652
  2.3 9.4 %collective-permute-start = (bf16[8,192,128]{1,2,0:T(8,128)(2,1)S(1)}, bf16[8,192,128]{1,2,0:T(8,128)(2,1)S(1)}, u32[]{:S(2)}, u32[]{:S(2)}) collective-permute-start(bf16[8,192,128]{1,2,0:T(8,128)(2,1)S(1)} %pad_maximum_fusion), channel_id=1, source_target_pairs={{0,12},{4,0},{8,4},{12,8},{1,13},{5,1},{9,5},{13,9},{2,14},{6,2},{... | collective-permute-start | bytes 1179656 | tf_op jit(solution)/shard_map/ppermute | solution.py:330
  4.7 5.2 %collective-permute-start.1 = (bf16[8,4,192]{2,1,0:T(4,128)(2,1)S(1)}, bf16[8,4,192]{2,1,0:T(4,128)(2,1)S(1)}, u32[]{:S(2)}, u32[]{:S(2)}) collective-permute-start(bf16[8,4,192]{2,1,0:T(4,128)(2,1)S(1)} %pad_maximum_fusion.1), channel_id=1, source_target_pairs={{0,3},{1,0},{2,1},{3,2},{4,7},{5,4},{6,5},{7,6},{8,11},{9,8},{10,9... | collective-permute-start | bytes 36872 | tf_op jit(solution)/shard_map/ppermute | solution.py:331
  8.4 3.2 %collective-permute-start.2 = (bf16[8,4,192]{2,1,0:T(4,128)(2,1)S(1)}, bf16[8,4,192]{2,1,0:T(4,128)(2,1)S(1)}, u32[]{:S(2)}, u32[]{:S(2)}) collective-permute-start(bf16[8,4,192]{2,1,0:T(4,128)(2,1)S(1)} %pad_maximum_fusion.2), channel_id=1, source_target_pairs={{0,15},{1,12},{2,13},{3,14},{4,3},{5,0},{6,1},{7,2},{8,7},{9,4},{1... | collective-permute-start | bytes 36872 | tf_op jit(solution)/shard_map/ppermute | solution.py:336
  8.9 0.9 %copy-start = (bf16[192,576]{1,0:T(8,128)(2,1)S(1)}, bf16[192,576]{1,0:T(8,128)(2,1)}, u32[]{:S(2)}) copy-start(bf16[192,576]{1,0:T(8,128)(2,1)} %w_qkv.1) | copy-start | bytes 663556
  9.8 1.8 %copy-start.1 = (bf16[192,192]{1,0:T(8,128)(2,1)S(1)}, bf16[192,192]{1,0:T(8,128)(2,1)}, u32[]{:S(2)}) copy-start(bf16[192,192]{1,0:T(8,128)(2,1)} %w_proj.1) | copy-start | bytes 221188
  11.6 0.7 %copy-start.2 = (f32[192]{0:T(256)S(1)}, f32[192]{0:T(256)}, u32[]{:S(2)}) copy-start(f32[192]{0:T(256)} %param.7) | copy-start | bytes 2308
  20.7 1.9 %collective-permute-start.6 = (bf16[592,128]{1,0:T(8,128)(2,1)S(1)}, bf16[592,128]{1,0:T(8,128)(2,1)S(1)}, u32[]{:S(2)}, u32[]{:S(2)}) collective-permute-start(bf16[592,128]{1,0:T(8,128)(2,1)S(1)} %get-tuple-element.18), channel_id=1, source_target_pairs={{0,4},{4,0},{8,12},{12,8},{1,5},{5,1},{9,13},{13,9},{2,6},{6,2},{1... | collective-permute-start | bytes 454664 | tf_op jit(solution)/shard_map/ppermute | solution.py:304
  22.6 6.3 %collective-permute-start.7 = (bf16[592,128]{1,0:T(8,128)(2,1)S(1)}, bf16[592,128]{1,0:T(8,128)(2,1)S(1)}, u32[]{:S(2)}, u32[]{:S(2)}) collective-permute-start(bf16[592,128]{1,0:T(8,128)(2,1)S(1)} %add.17), channel_id=1, source_target_pairs={{0,8},{4,12},{8,0},{12,4},{1,9},{5,13},{9,1},{13,5},{2,10},{6,14},... | collective-permute-start | bytes 454664 | tf_op jit(solution)/shard_map/ppermute | solution.py:307
  28.9 5.5 %collective-permute-start.8 = (bf16[592,128]{1,0:T(8,128)(2,1)S(1)}, bf16[592,128]{1,0:T(8,128)(2,1)S(1)}, u32[]{:S(2)}, u32[]{:S(2)}) collective-permute-start(bf16[592,128]{1,0:T(8,128)(2,1)S(1)} %add.18), channel_id=1, source_target_pairs={{0,1},{1,0},{2,3},{3,2},{4,5},{5,4},{6,7},{7,6},{8,9},{9,8},{10,11... | collective-permute-start | bytes 454664 | tf_op jit(solution)/shard_map/ppermute | solution.py:311
  34.4 8.7 %collective-permute-start.9 = (bf16[592,128]{1,0:T(8,128)(2,1)S(1)}, bf16[592,128]{1,0:T(8,128)(2,1)S(1)}, u32[]{:S(2)}, u32[]{:S(2)}) collective-permute-start(bf16[592,128]{1,0:T(8,128)(2,1)S(1)} %add.19), channel_id=1, source_target_pairs={{0,2},{1,3},{2,0},{3,1},{4,6},{5,7},{6,4},{7,5},{8,10},{9,11},{10,... | collective-permute-start | bytes 454664 | tf_op jit(solution)/shard_map/ppermute | solution.py:311
  37.1 12.7 %collective-permute-start.3 = (bf16[4,192,128]{2,1,0:T(8,128)(2,1)S(1)}, bf16[4,192,128]{2,1,0:T(8,128)(2,1)S(1)}, u32[]{:S(2)}, u32[]{:S(2)}) collective-permute-start(bf16[4,192,128]{2,1,0:T(8,128)(2,1)S(1)} %get-tuple-element.14), channel_id=1, source_target_pairs={{12,0},{0,4},{4,8},{8,12},{13,1},{1,5},{5,9},{9,13},{14,2},{2,6},{... | collective-permute-start | bytes 589832 | tf_op jit(solution)/shard_map/ppermute | solution.py:353
  43.1 7.5 %collective-permute-start.10 = (bf16[592,128]{1,0:T(8,128)(2,1)S(1)}, bf16[592,128]{1,0:T(8,128)(2,1)S(1)}, u32[]{:S(2)}, u32[]{:S(2)}) collective-permute-start(bf16[592,128]{1,0:T(8,128)(2,1)S(1)} %add.20.mine), channel_id=1, source_target_pairs={{0,4},{4,0},{8,12},{12,8},{1,5},{5,1},{9,13},{13,9},{2,6},{6,2},{1... | collective-permute-start | bytes 454664 | tf_op jit(solution)/shard_map/ppermute | solution.py:349
  43.2 5.5 %collective-permute-start.4 = (bf16[4,4,192]{2,1,0:T(4,128)(2,1)S(1)}, bf16[4,4,192]{2,1,0:T(4,128)(2,1)S(1)}, u32[]{:S(2)}, u32[]{:S(2)}) collective-permute-start(bf16[4,4,192]{2,1,0:T(4,128)(2,1)S(1)} %get-tuple-element.15), channel_id=1, source_target_pairs={{3,0},{0,1},{1,2},{2,3},{7,4},{4,5},{5,6},{6,7},{11,8},{8,9},{9,10... | collective-permute-start | bytes 18440 | tf_op jit(solution)/shard_map/ppermute | solution.py:354
  44.0 5.8 %collective-permute-start.5 = (bf16[4,4,192]{2,1,0:T(4,128)(2,1)S(1)}, bf16[4,4,192]{2,1,0:T(4,128)(2,1)S(1)}, u32[]{:S(2)}, u32[]{:S(2)}) collective-permute-start(bf16[4,4,192]{2,1,0:T(4,128)(2,1)S(1)} %get-tuple-element.16), channel_id=1, source_target_pairs={{15,0},{12,1},{13,2},{14,3},{3,4},{0,5},{1,6},{2,7},{7,8},{4,9},{5... | collective-permute-start | bytes 18440 | tf_op jit(solution)/shard_map/ppermute | solution.py:355

commit v3 on v2

--- a/solution.py
+++ b/solution.py
@@ -28,27 +28,111 @@
     return lax.dot_general(a, b, (((1,), (1,)), ((), ())), preferred_element_type=F32)
 
 
-def body(
-    flags, x, dy, row_halo, col_halo, corner, gain, w_qkv, w_qkv_t, w_proj,
-    low, high, low_tail, high_tail, keep, send,
-    xs, dys, x_hat, inv_std, normed, upstream, q_t, k_t, v_t, do_t, k_n, v_n, packed, mask, halves,
+VMEM = pl.BlockSpec(memory_space=pltpu.VMEM)
+SMEM = pl.BlockSpec(memory_space=pltpu.SMEM)
+ANY = pl.BlockSpec(memory_space=pl.ANY)
+HBM = pl.BlockSpec(memory_space=pltpu.HBM)
+
+
+def params(mib):
+    return pltpu.CompilerParams(vmem_limit_bytes=mib * 2**20)
+
+
+def shape(dtype, *dims):
+    return jax.ShapeDtypeStruct(dims, dtype)
+
+
+def gather_body(
+    x, dy, w_qkv, w_proj, gain,
+    message, rest, strip, corner, w_qkv_out, w_proj_out, gain_out, sems,
 ):
-    cols, channels = x.shape[1:]
-    rows = 2 * SHIFT
-    windows = cols // WINDOW
+    sources = (x, dy)
+    copies = [
+        pltpu.make_async_copy(
+            source.at[pl.ds(k * SHIFT, SHIFT)], dest.at[pl.ds(n * SHIFT, SHIFT)], sems.at[2 * k + n]
+        )
+        for k, dest in enumerate((message, rest))
+        for n, source in enumerate(sources)
+    ]
+    pairs = ((w_qkv, w_qkv_out), (w_proj, w_proj_out), (gain, gain_out))
+    copies += [pltpu.make_async_copy(a, b, sems.at[4 + n]) for n, (a, b) in enumerate(pairs)]
+    for copy in copies:
+        copy.start()
+    for copy in copies[:4]:
+        copy.wait()
+    for i in range(2 * SHIFT):
+        strip[i] = jnp.transpose(rest[i])[:SHIFT]
+        corner[i] = jnp.transpose(message[i])[:SHIFT]
+    for copy in copies[4:]:
+        copy.wait()
+
+
+def gather(x, dy, w_qkv, w_proj, gain):
+    rows, channels, cols = x.shape
+    operands = [pltpu.with_memory_space_constraint(v, pltpu.HBM) for v in (x, dy, w_qkv, w_proj, gain)]
+    return pl.pallas_call(
+        gather_body,
+        out_shape=(
+            shape(BF16, 2 * SHIFT, channels, cols),
+            shape(BF16, 2 * SHIFT, channels, cols),
+            shape(BF16, 2 * SHIFT, SHIFT, channels),
+            shape(BF16, 2 * SHIFT, SHIFT, channels),
+            shape(BF16, *w_qkv.shape),
+            shape(BF16, *w_proj.shape),
+            shape(F32, *gain.shape),
+        ),
+        in_specs=[HBM] * 5,
+        out_specs=(VMEM,) * 7,
+        scratch_shapes=[pltpu.SemaphoreType.DMA((7,))],
+        compiler_params=params(8),
+        name="gather",
+    )(*operands)
+
+
+def prep_body(rest, w_qkv, xs, dys, w_qkv_t):
+    cols = rest.shape[2]
+    for n, dest in enumerate((xs, dys)):
+        for i in range(SHIFT):
+            line = jnp.transpose(rest[n * SHIFT + i])
+            dest[i] = pltpu.roll(line.astype(F32), cols - SHIFT, 0)
+    w_qkv_t[...] = jnp.transpose(w_qkv[...])
+
+
+def prep(rest, w_qkv):
+    _, channels, cols = rest.shape
+    return pl.pallas_call(
+        prep_body,
+        out_shape=(
+            shape(F32, SHIFT, cols, channels),
+            shape(F32, SHIFT, cols, channels),
+            shape(BF16, w_qkv.shape[1], channels),
+        ),
+        in_specs=[VMEM] * 2,
+        out_specs=(VMEM,) * 3,
+        compiler_params=params(8),
+        name="prep",
+    )(rest, w_qkv)
+
+
+def main_body(
+    flags, x_low, dy_low, row_halo, strip, corner, gain, w_qkv, w_qkv_t, w_proj,
+    keep, send, packed, x_hat, inv_std, dys,
+    xs, normed, upstream, q_t, k_t, v_t, do_t, k_n, v_n, mask, halves,
+):
+    half_rows, cols, channels = x_low.shape
+    rows = 2 * half_rows
     tokens = rows * cols
     pairs = tokens // PAIR
-    for i in range(rows):
-        for tile, arrived, dest in ((x, 0, xs), (dy, SHIFT, dys)):
-            if i < rows - SHIFT:
-                line = tile[i].astype(F32)
-                tail = col_halo[arrived + i].astype(F32)
+    for n, (tile, dest) in enumerate(((x_low, xs), (dy_low, dys))):
+        for i in range(rows):
+            j = n * SHIFT + i % SHIFT
+            if i < half_rows:
+                dest[i] = tile[i]
+                dest[i, cols - SHIFT :, :] = strip[j].astype(F32)
             else:
-                j = i - (rows - SHIFT)
-                line = row_halo[arrived + j].astype(F32)
-                tail = corner[arrived + j].astype(F32)
-            dest[i] = pltpu.roll(line, cols - SHIFT, 0)
-            dest[i, cols - SHIFT :, :] = tail
+                line = jnp.transpose(row_halo[j]).astype(F32)
+                dest[i] = pltpu.roll(line, cols - SHIFT, 0)
+                dest[i, cols - SHIFT :, :] = corner[j].astype(F32)
     k_pos = lax.broadcasted_iota(jnp.int32, (PAIR // 2, PAIR), 0)
     lane = lax.broadcasted_iota(jnp.int32, (PAIR // 2, PAIR), 1)
     q_pos = lane % (PAIR // 2)
@@ -151,110 +235,160 @@
 
     lax.fori_loop(0, pairs, attend, 0, unroll=True)
 
-    wide = jnp.transpose(dot_nn(packed[0 : 3 * channels, :], n_all))
+    wide_t = dot_nn(packed[0 : 3 * channels, :], n_all)
+    gain_sum = jnp.sum(wide_t * w_qkv_t[...].astype(F32), axis=0, keepdims=True) / gain_row
+    wide = jnp.transpose(wide_t)
     proj = dot_nn(packed[3 * channels :, :], upstream[...])
     both = jnp.concatenate((wide, proj), axis=1)
+    gain_block = jnp.broadcast_to(
+        jnp.concatenate((gain_sum, jnp.zeros((1, 256 - channels), F32)), axis=1), (16, 256)
+    )
     core = flags[2]
     for n in range(2):
         for j in range(3):
             lane = (3 * n + j) * 128
             halves[n, j * channels : (j + 1) * channels, :] = both[:, lane : lane + 128].astype(BF16)
-
-    def finish(p, total):
-        at = pl.ds(pl.multiple_of(p * PAIR, PAIR), PAIR)
-        g_t = dot_nn(w_qkv[...], packed[0 : 3 * channels, at])
-        g = jnp.transpose(g_t)
-        hat = x_hat[at, :]
-        gx = g * hat
-        total = total + jnp.sum(gx, axis=0, keepdims=True)
-        gh = g * gain_row
-        ghx = gx * gain_row
-        mean_a = jnp.mean(gh, axis=-1, keepdims=True)
-        mean_b = jnp.mean(ghx, axis=-1, keepdims=True)
-        branch = inv_std[at, 0:1] * (gh - mean_a - hat * mean_b)
-        for half in range(2):
-            w = 2 * p + half
-            to = pl.ds(pl.multiple_of(w * WINDOW, WINDOW), WINDOW)
-            piece = branch[half * half_n : (half + 1) * half_n].reshape(WINDOW, WINDOW, channels)
-            xs[:, to, :] = dys[:, to, :] + piece
-        return total
-
-    gain_sum = lax.fori_loop(0, pairs, finish, jnp.zeros((1, channels), F32), unroll=True)
-    gain_block = jnp.broadcast_to(
-        jnp.concatenate((gain_sum, jnp.zeros((1, 256 - channels), F32)), axis=1), (16, 256)
-    )
-    for n in range(2):
         halves[n, 3 * channels :, :] = gain_block[:, n * 128 : (n + 1) * 128].astype(BF16)
     keep[...] = halves[core]
     send[...] = halves[1 - core]
-    for i in range(rows):
-        line = pltpu.roll(xs[i], SHIFT, 0)
-        if i < rows - SHIFT:
-            low[i] = jnp.transpose(line.astype(BF16))
-            low_tail[i] = line[:SHIFT].astype(BF16)
-        else:
-            high[i - (rows - SHIFT)] = jnp.transpose(line.astype(BF16))
-            high_tail[i - (rows - SHIFT)] = line[:SHIFT].astype(BF16)
-
-
-def half_block(flags, x, dy, row_halo, col_halo, corner, gain, w_qkv, w_qkv_t, w_proj):
-    half_rows, cols, channels = x.shape
+
+
+def main(flags, x_low, dy_low, row_halo, strip, corner, gain, w_qkv, w_qkv_t, w_proj):
+    half_rows, cols, channels = x_low.shape
     rows = 2 * half_rows
     tokens = rows * cols
-    vm = pl.BlockSpec(memory_space=pltpu.VMEM)
-    flat = lambda dtype: pltpu.VMEM((tokens, channels), dtype)
+    flat = pltpu.VMEM((tokens, channels), BF16)
     turned = pltpu.VMEM((channels, tokens), BF16)
-    shape = lambda *dims: jax.ShapeDtypeStruct(dims, BF16)
-    return pl.pallas_call(
-        body,
+    return pl.pallas_call(
+        main_body,
         out_shape=(
-            shape(half_rows, channels, cols),
-            shape(half_rows, channels, cols),
-            shape(half_rows, SHIFT, channels),
-            shape(half_rows, SHIFT, channels),
-            shape(3 * channels + 16, 128),
-            shape(3 * channels + 16, 128),
-        ),
-        in_specs=[pl.BlockSpec(memory_space=pltpu.SMEM)] + [vm] * 9,
-        out_specs=(vm,) * 6,
+            shape(BF16, 3 * channels + 16, 128),
+            shape(BF16, 3 * channels + 16, 128),
+            shape(BF16, 4 * channels, tokens),
+            shape(F32, tokens, channels),
+            shape(F32, tokens, 128),
+            shape(F32, rows, cols, channels),
+        ),
+        in_specs=[SMEM] + [VMEM] * 9,
+        out_specs=(VMEM,) * 6,
         scratch_shapes=[
             pltpu.VMEM((rows, cols, channels), F32),
-            pltpu.VMEM((rows, cols, channels), F32),
-            flat(F32),
-            pltpu.VMEM((tokens, 128), F32),
-            flat(BF16),
-            flat(BF16),
+            flat, flat,
             turned, turned, turned, turned,
-            flat(BF16),
-            flat(BF16),
-            pltpu.VMEM((4 * channels, tokens), BF16),
+            flat, flat,
             pltpu.VMEM((2, PAIR // 2, PAIR), F32),
             pltpu.VMEM((2, 3 * channels + 16, 128), BF16),
         ],
-        compiler_params=pltpu.CompilerParams(vmem_limit_bytes=40 * 2**20),
-        name="half_block",
-    )(flags, x, dy, row_halo, col_halo, corner, gain, w_qkv, w_qkv_t, w_proj)
-
-
-def place_body(low, high, low_tail, high_tail, out):
-    lanes = lax.broadcasted_iota(jnp.int32, low.shape[1:], 1)
-    for source, tails, base in ((high, high_tail, 0), (low, low_tail, SHIFT)):
-        for i in range(SHIFT):
-            tail = jnp.transpose(jnp.concatenate([tails[i]] * (low.shape[2] // SHIFT), axis=0))
-            out[base + i] = jnp.where(lanes < SHIFT, tail, source[i])
-
-
-def place(low, high, low_tail, high_tail):
-    half_rows, channels, cols = low.shape
-    vm = pl.BlockSpec(memory_space=pltpu.VMEM)
-    return pl.pallas_call(
-        place_body,
-        out_shape=jax.ShapeDtypeStruct((2 * half_rows, channels, cols), BF16),
-        in_specs=[vm] * 4,
-        out_specs=vm,
-        compiler_params=pltpu.CompilerParams(vmem_limit_bytes=16 * 2**20),
-        name="place",
-    )(low, high, low_tail, high_tail)
+        compiler_params=params(40),
+        name="main",
+    )(flags, x_low, dy_low, row_halo, strip, corner, gain, w_qkv, w_qkv_t, w_proj)
+
+
+def back_body(packed, x_hat, inv_std, dys, gain, w_qkv, low, high, strip, out):
+    rows, cols, channels = dys.shape
+    tokens = rows * cols
+    half_n = PAIR // 2
+    gain_row = gain[...]
+    for p in range(tokens // PAIR):
+        at = pl.ds(p * PAIR, PAIR)
+        g = jnp.transpose(dot_nn(w_qkv[...], packed[0 : 3 * channels, at]))
+        hat = x_hat[at, :]
+        gh = g * gain_row
+        mean_a = jnp.mean(gh, axis=-1, keepdims=True)
+        mean_b = jnp.mean(gh * hat, axis=-1, keepdims=True)
+        branch = inv_std[at, 0:1] * (gh - mean_a - hat * mean_b)
+        for half in range(2):
+            to = pl.ds((2 * p + half) * WINDOW, WINDOW)
+            piece = branch[half * half_n : (half + 1) * half_n].reshape(WINDOW, WINDOW, channels)
+            out[:, to, :] = dys[:, to, :] + piece
+    for i in range(rows):
+        line = pltpu.roll(out[i], SHIFT, 0)
+        strip[i] = line[:SHIFT].astype(BF16)
+        dest = low if i < rows // 2 else high
+        dest[i % SHIFT] = jnp.transpose(line.astype(BF16))
+
+
+def back(packed, x_hat, inv_std, dys, gain, w_qkv):
+    rows, cols, channels = dys.shape
+    return pl.pallas_call(
+        back_body,
+        out_shape=(
+            shape(BF16, rows // 2, channels, cols),
+            shape(BF16, rows // 2, channels, cols),
+            shape(BF16, rows, SHIFT, channels),
+        ),
+        in_specs=[VMEM] * 6,
+        out_specs=(VMEM,) * 3,
+        scratch_shapes=[pltpu.VMEM((rows, cols, channels), F32)],
+        compiler_params=params(32),
+        cost_estimate=pl.CostEstimate(
+            flops=2 * rows * cols * channels * 3 * channels, bytes_accessed=8 * 2**20, transcendentals=0
+        ),
+        name="back",
+    )(packed, x_hat, inv_std, dys, gain, w_qkv)
+
+
+def insert(source, tail, n):
+    lanes = lax.broadcasted_iota(jnp.int32, source.shape[1:], 1)
+    wide = jnp.transpose(jnp.concatenate([tail] * (source.shape[2] // SHIFT), axis=0))
+    return jnp.where(lanes < SHIFT, wide, source[n])
+
+
+def fill_body(low, high, strip, low_out, high_out):
+    for n in range(SHIFT):
+        low_out[n] = insert(low, strip[n], n)
+        high_out[n] = insert(high, strip[SHIFT + n], n)
+
+
+def fill(low, high, strip):
+    return pl.pallas_call(
+        fill_body,
+        out_shape=(shape(BF16, *low.shape), shape(BF16, *high.shape)),
+        in_specs=[VMEM] * 3,
+        out_specs=(VMEM,) * 2,
+        compiler_params=params(8),
+        name="fill",
+    )(low, high, strip)
+
+
+def add_body(after, a, b, out):
+    out[...] = a[...] + b[...]
+
+
+def add(after, a, b):
+    return pl.pallas_call(
+        add_body,
+        out_shape=shape(a.dtype, *a.shape),
+        in_specs=[ANY] + [VMEM] * 2,
+        out_specs=VMEM,
+        compiler_params=params(4),
+        name="add",
+    )(after, a, b)
+
+
+def join_body(after, high, low, out, sems):
+    half = high.shape[0]
+    copies = [
+        pltpu.make_async_copy(source, out.at[pl.ds(n * half, half)], sems.at[n])
+        for n, source in enumerate((high, low))
+    ]
+    for copy in copies:
+        copy.start()
+    for copy in copies:
+        copy.wait()
+
+
+def join(after, high, low):
+    half_rows, channels, cols = high.shape
+    return pl.pallas_call(
+        join_body,
+        out_shape=shape(BF16, 2 * half_rows, channels, cols),
+        in_specs=[ANY] + [VMEM] * 2,
+        out_specs=HBM,
+        scratch_shapes=[pltpu.SemaphoreType.DMA((2,))],
+        compiler_params=params(4),
+        name="join",
+    )(after, high, low)
 
 
 def scale_body(flags, mine, other, wqkv, wproj, gain, *, factor):
@@ -300,16 +434,18 @@
     return [(i, i ^ bit) for i in range(extent)]
 
 
-def sum_half(keep, send, row_extent, col_extent):
+def sum_half(keep, send, after, row_extent, col_extent):
+    bits = [b * col_extent for b in (2**n for n in range(1, 16)) if b < row_extent]
+    bits += [b for b in (2**n for n in range(16)) if b < col_extent]
+    turn = len(bits) // 2
+    orders = (bits, bits[-turn:] + bits[:-turn])
     total = keep + lax.ppermute(send, "row", flip(row_extent, 1))
-    bit = 2
-    while bit < row_extent:
-        total = total + lax.ppermute(total, "row", flip(row_extent, bit))
-        bit *= 2
-    bit = 1
-    while bit < col_extent:
-        total = total + lax.ppermute(total, "col", flip(col_extent, bit))
-        bit *= 2
+    for step in range(len(bits)):
+        route = [
+            (i, i ^ orders[i // col_extent % 2][step]) for i in range(row_extent * col_extent)
+        ]
+        arrived = lax.ppermute(total, ("row", "col"), route)
+        total = total + arrived if step not in after else add(after[step], total, arrived)
     return total
 
 
@@ -327,33 +463,28 @@
     turn = lambda route: [(b, a) for a, b in route]
     swap = lambda v: jnp.transpose(v, (0, 2, 1))
     x_t, dy_t = swap(activations), swap(cotangent)
-    row_halo = lax.ppermute(jnp.concatenate((x_t[:SHIFT], dy_t[:SHIFT]), axis=0), "row", up)
-    col_halo = lax.ppermute(
-        jnp.concatenate((activations[SHIFT:, :SHIFT], cotangent[SHIFT:, :SHIFT]), axis=0),
-        "col",
-        left,
+    message, rest, strip, corner, w_qkv, w_proj, gain = gather(
+        x_t, dy_t, w_qkv, w_proj, norm_gain.reshape(1, channels)
     )
-    corner = lax.ppermute(
-        jnp.concatenate((activations[:SHIFT, :SHIFT], cotangent[:SHIFT, :SHIFT]), axis=0),
-        ("row", "col"),
-        both,
-    )
+    row_halo = lax.ppermute(message, "row", up)
+    strip = lax.ppermute(strip, "col", left)
+    corner = lax.ppermute(corner, ("row", "col"), both)
+    x_low, dy_low, w_qkv_t = prep(rest, w_qkv)
     flags = jnp.stack(
         (row_index == row_extent - 1, col_index == col_extent - 1, row_index % 2 == 1)
     ).astype(jnp.int32)
-    low, high, low_tail, high_tail, keep, send = half_block(
-        flags, activations[SHIFT:], cotangent[SHIFT:], swap(row_halo), col_halo, corner,
-        norm_gain.reshape(1, channels), w_qkv, w_qkv.T, w_proj,
+    keep, send, packed, x_hat, inv_std, dys = main(
+        flags, x_low, dy_low, row_halo, strip, corner, gain, w_qkv, w_qkv_t, w_proj
     )
-    total = sum_half(keep, send, row_extent, col_extent)
+    low, high, strip = back(packed, x_hat, inv_std, dys, gain, w_qkv)
+    strip = lax.ppermute(strip, "col", turn(left))
+    own, lower = fill(low, high, strip)
+    total = sum_half(keep, send, {0: low, 1: own}, row_extent, col_extent)
+    lower = lax.ppermute(lower, "row", turn(up))
+    grad_input = swap(join(total, lower, own))
     other = lax.ppermute(total, "row", flip(row_extent, 1))
     factor = 1.0 / math.sqrt(rows * row_extent * cols * col_extent)
     grad_wqkv, grad_wproj, grad_gain = scale(flags, total, other, channels, factor)
-
-    high = lax.ppermute(high, "row", turn(up))
-    low_tail = lax.ppermute(low_tail, "col", turn(left))
-    high_tail = lax.ppermute(high_tail, ("row", "col"), turn(both))
-    grad_input = swap(place(low, high, low_tail, high_tail))
     return grad_input, grad_wqkv, grad_wproj, grad_gain.reshape(channels)
 
 

time: 52.4 us -> 43.1 us (0.82)
  waiting for transfers between devices: 23 us -> 17.7 us
  local copies, waits for them, and re-layouts: 3.3 us -> 0 us
  starting transfers between devices: 14 us -> 10.9 us
  Pallas kernels: 10.8 us -> 13.4 us
    ppermute x9 -> x8, waiting for transfers between devices: 21.9 us -> 16 us  [the longest x3 8.92 us: sum_half(): arrived = lax.ppermute(total, ('row', 'col'), route)]
    unnamed x11 -> x0, local copies, waits for them, and re-layouts: 3.22 us -> none
    pallas_call x2 -> x8, Pallas kernels: 9.28 us -> 11.9 us  [the longest x1 7.51 us: main(): pl.pallas_call(main_body, out_shape=(shape(BF16, 3 * channels + 16, 128),...]
    ppermute x9 -> x8, starting transfers between devices: 13.1 us -> 10.5 us  [the longest x1 3.6 us: on_device(): strip = lax.ppermute(strip, 'col', left)]
    ppermute x1, waiting for transfers between devices: 0.01 us -> 0.58 us  [on_device(): other = lax.ppermute(total, 'row', flip(row_extent, 1))]
    ppermute x1, starting transfers between devices: 0.84 us -> 0.26 us  [sum_half(): total = keep + lax.ppermute(send, 'row', flip(row_extent, 1))]
  transfers between devices with their start and end apart: 11 -> 10, of which waited for: 7 -> 7; matrix products, arithmetic and copies ran while one was open for 1% -> 0% of each run, Pallas kernels for 2% -> 7%
where the time goes in v3:
time: 43.1 us; the launch traced here: 42.9 us
  waiting for transfers between devices  17.7 us (41%)
  Pallas kernels  13.4 us (31%)
  starting transfers between devices  10.9 us (25%)
  between operations  0.72 us (2%)
    ppermute x3, waiting for transfers between devices, sum_half(): arrived = lax.ppermute(total, ('row', 'col'), route)  8.92 us
    pallas_call x1, Pallas kernels, main(): pl.pallas_call(main_body, out_shape=(shape(BF16, 3 * channels + 16, 128),...  7.51 us
    ppermute x1, waiting for transfers between devices, on_device(): strip = lax.ppermute(strip, 'col', turn(left))  4.54 us
    ppermute x1, starting transfers between devices, on_device(): strip = lax.ppermute(strip, 'col', left)  3.6 us
    ppermute x3, starting transfers between devices, sum_half(): arrived = lax.ppermute(total, ('row', 'col'), route)  2.8 us
    ppermute x1, starting transfers between devices, on_device(): row_halo = lax.ppermute(message, 'row', up)  2.43 us
    ppermute x1, waiting for transfers between devices, on_device(): corner = lax.ppermute(corner, ('row', 'col'), both)  1.72 us
    pallas_call x1, Pallas kernels, back(): pl.pallas_call(back_body, out_shape=(shape(BF16, rows // 2, channels, col...  1.56 us
  transfers between devices with their start and end apart: 10, of which 7 were waited for; matrix products, arithmetic and copies ran while one was open for 0% of the time, Pallas kernels for 7%

profile of v3, /device:TPU:0, one launch (start us, length us, event | category | flops | bytes accessed | tf_op | source)
XLA Modules:
  0.0 42.9 jit_solution(12961256253212269272)
XLA Ops:
  0.6 1.5 %gather.1 = (bf16[8,192,128]{2,1,0:T(8,128)(2,1)S(1)}, bf16[8,192,128]{2,1,0:T(8,128)(2,1)S(1)}, bf16[8,4,192]{2,1,0:T(4,128)(2,1)S(1)}, bf16[8,4,192]{2,1,0:T(4...) custom-call(bf16[8,192,128]{2,1,0:T(8,128)(2,1)} %bitcast.8, ...), custom_call_target="tpu_custom_call" | custom-call | tf_op jit(solution)/shard_map/gather/pallas_call | solution.py:73
  2.2 2.4 %collective-permute-start = (bf16[8,192,128]{2,1,0:T(8,128)(2,1)S(1)}, bf16[8,192,128]{2,1,0:T(8,128)(2,1)S(1)}, u32[]{:S(2)}, u32[]{:S(2)}) collective-permute-start(bf16[8,192,128]{2,1,0:T(8,128)(2,1)S(1)} %get-tuple-element.32), channel_id=1, source_target_pairs={{0,12},{4,0},{8,4},{12,8},{1,13},{5,1},{9,5},{13,9},{2,14},{6,2},{... | collective-permute-start | bytes 1179656 | tf_op jit(solution)/shard_map/ppermute | solution.py:469
  4.6 3.6 %collective-permute-start.1 = (bf16[8,4,192]{2,1,0:T(4,128)(2,1)S(1)}, bf16[8,4,192]{2,1,0:T(4,128)(2,1)S(1)}, u32[]{:S(2)}, u32[]{:S(2)}) collective-permute-start(bf16[8,4,192]{2,1,0:T(4,128)(2,1)S(1)} %get-tuple-element.33), channel_id=1, source_target_pairs={{0,3},{1,0},{2,1},{3,2},{4,7},{5,4},{6,5},{7,6},{8,11},{9,8},{10,9... | collective-permute-start | bytes 36872 | tf_op jit(solution)/shard_map/ppermute | solution.py:470
  8.2 0.3 collective-permute-start.2
  8.5 0.1 add_convert_fusion.flags
  8.6 0.3 prep.1
  8.9 0.8 %collective-permute-done.1.strip = bf16[8,4,192]{2,1,0:T(4,128)(2,1)S(1)} collective-permute-done((bf16[8,4,192]{2,1,0:T(4,128)(2,1)S(1)}, bf16[8,4,192]{2,1,0:T(4,128)(2,1)S(1)}, u32[]{:S(2)}, u32[]{:S(2)}) %collective-permute-start.1) | collective-permute-done | bytes 12320 | tf_op jit(solution)/shard_map/ppermute | solution.py:470
  9.7 1.7 %collective-permute-done.2.corner = bf16[8,4,192]{2,1,0:T(4,128)(2,1)S(1)} collective-permute-done((bf16[8,4,192]{2,1,0:T(4,128)(2,1)S(1)}, bf16[8,4,192]{2,1,0:T(4,128)(2,1)S(1)}, u32[]{:S(2)}, u32[]{:S(2)}) %collective-permute-start.2) | collective-permute-done | bytes 12320 | tf_op jit(solution)/shard_map/ppermute | solution.py:471
  11.4 0.0 collective-permute-done.row_halo
  11.4 7.5 %main.1 = (bf16[592,128]{1,0:T(8,128)(2,1)S(1)}, bf16[592,128]{1,0:T(8,128)(2,1)S(1)}, bf16[768,1024]{1,0:T(8,128)(2,1)S(1)}, f32[1024,192]{1,0:T(8,128)S(1)}, f...) custom-call(s32[3]{0:T(128)S(1)} %add_convert_fusion.flags, f32[4,128,192]{2,1,0:T(8,128)S(1)} %get-tuple-element.30.x_low, ...), custom_call_target="tpu_custom_call" | custom-call | tf_op jit(solution)/shard_map/main/pallas_call | solution.py:262
  18.9 0.3 collective-permute-start.4
  19.2 1.2 %collective-permute-done.4 = bf16[592,128]{1,0:T(8,128)(2,1)S(1)} collective-permute-done((bf16[592,128]{1,0:T(8,128)(2,1)S(1)}, bf16[592,128]{1,0:T(8,128)(2,1)S(1)}, u32[]{:S(2)}, u32[]{:S(2)}) %collective-permute-start.4) | collective-permute-done | bytes 151584 | tf_op jit(solution)/shard_map/ppermute | solution.py:442
  20.4 1.4 %collective-permute-start.5 = (bf16[592,128]{1,0:T(8,128)(2,1)S(1)}, bf16[592,128]{1,0:T(8,128)(2,1)S(1)}, u32[]{:S(2)}, u32[]{:S(2)}) collective-permute-start(bf16[592,128]{1,0:T(8,128)(2,1)S(1)} %add.13.a), channel_id=1, source_target_pairs={{0,8},{1,9},{2,10},{3,11},{4,6},{5,7},{6,4},{7,5},{8,0},{9,1},{10,... | collective-permute-start | bytes 454664 | tf_op jit(solution)/shard_map/ppermute | solution.py:447
  21.8 1.6 %back.1 = (bf16[4,192,128]{2,1,0:T(8,128)(2,1)S(1)}, bf16[4,192,128]{2,1,0:T(8,128)(2,1)S(1)}, bf16[8,4,192]{2,1,0:T(4,128)(2,1)S(1)}) custom-call(bf16[768,1024]{1,0:T(8,128)(2,1)S(1)} %get-tuple-element.38.packed, f32[1024,192]{1,0:T(8,128)S(1)} %get-tuple-element.39.x_hat, f32[1024,128]{1,0:T(8,128)S(1)} %get-tuple-element.40.inv_std, ...), custom_call_target="tpu_custom_call" | custom-call | flops 226492416 | bytes 8388608 | tf_op jit(solution)/shard_map/back/pallas_call | solution.py:313
  23.4 2.3 %collective-permute-done.5.b = bf16[592,128]{1,0:T(8,128)(2,1)S(1)} collective-permute-done((bf16[592,128]{1,0:T(8,128)(2,1)S(1)}, bf16[592,128]{1,0:T(8,128)(2,1)S(1)}, u32[]{:S(2)}, u32[]{:S(2)}) %collective-permute-start.5) | collective-permute-done | bytes 151584 | tf_op jit(solution)/shard_map/ppermute | solution.py:447
  25.6 0.1 add.19.a
  25.7 0.8 %collective-permute-start.6 = (bf16[592,128]{1,0:T(8,128)(2,1)S(1)}, bf16[592,128]{1,0:T(8,128)(2,1)S(1)}, u32[]{:S(2)}, u32[]{:S(2)}) collective-permute-start(bf16[592,128]{1,0:T(8,128)(2,1)S(1)} %add.19.a), channel_id=1, source_target_pairs={{0,1},{1,0},{2,3},{3,2},{4,12},{5,13},{6,14},{7,15},{8,9},{9,8},{1... | collective-permute-start | bytes 454664 | tf_op jit(solution)/shard_map/ppermute | solution.py:447
  26.5 1.3 %collective-permute-start.3 = (bf16[8,4,192]{2,1,0:T(4,128)(2,1)S(1)}, bf16[8,4,192]{2,1,0:T(4,128)(2,1)S(1)}, u32[]{:S(2)}, u32[]{:S(2)}) collective-permute-start(bf16[8,4,192]{2,1,0:T(4,128)(2,1)S(1)} %get-tuple-element.44), channel_id=1, source_target_pairs={{3,0},{0,1},{1,2},{2,3},{7,4},{4,5},{5,6},{6,7},{11,8},{8,9},{9,10... | collective-permute-start | bytes 36872 | tf_op jit(solution)/shard_map/ppermute | solution.py:480
  27.8 4.5 %collective-permute-done.3.strip = bf16[8,4,192]{2,1,0:T(4,128)(2,1)S(1)} collective-permute-done((bf16[8,4,192]{2,1,0:T(4,128)(2,1)S(1)}, bf16[8,4,192]{2,1,0:T(4,128)(2,1)S(1)}, u32[]{:S(2)}, u32[]{:S(2)}) %collective-permute-start.3) | collective-permute-done | bytes 12320 | tf_op jit(solution)/shard_map/ppermute | solution.py:480
  32.3 0.2 fill.1
  32.5 0.0 collective-permute-done.6.b
  32.6 0.6 %collective-permute-start.7 = (bf16[592,128]{1,0:T(8,128)(2,1)S(1)}, bf16[592,128]{1,0:T(8,128)(2,1)S(1)}, u32[]{:S(2)}, u32[]{:S(2)}) collective-permute-start(bf16[592,128]{1,0:T(8,128)(2,1)S(1)} %add.20), channel_id=1, source_target_pairs={{0,2},{1,3},{2,0},{3,1},{4,5},{5,4},{6,7},{7,6},{8,10},{9,11},{10,... | collective-permute-start | bytes 454664 | tf_op jit(solution)/shard_map/ppermute | solution.py:447
  33.2 0.2 collective-permute-start.8
  33.3 6.6 %collective-permute-done.7 = bf16[592,128]{1,0:T(8,128)(2,1)S(1)} collective-permute-done((bf16[592,128]{1,0:T(8,128)(2,1)S(1)}, bf16[592,128]{1,0:T(8,128)(2,1)S(1)}, u32[]{:S(2)}, u32[]{:S(2)}) %collective-permute-start.7) | collective-permute-done | bytes 151584 | tf_op jit(solution)/shard_map/ppermute | solution.py:447
  40.0 0.1 collective-permute-start.9
  40.1 0.0 collective-permute-done.8.high
  40.1 0.8 %join.1 = bf16[8,192,128]{2,1,0:T(8,128)(2,1)} custom-call(bf16[592,128]{1,0:T(8,128)(2,1)S(1)} %add.14.after.mine, bf16[4,192,128]{2,1,0:T(8,128)(2,1)S(1)} %collective-permute-done.8.high, bf16[4,192,128]{2,1,0:T(8,128)(2,1)S(1)} %get-tuple-element.45.after.low), custom_call_target="tpu_custom_call" | custom-call | tf_op jit(solution)/shard_map/join/pallas_call | solution.py:383
  40.8 0.6 %collective-permute-done.9.other = bf16[592,128]{1,0:T(8,128)(2,1)S(1)} collective-permute-done((bf16[592,128]{1,0:T(8,128)(2,1)S(1)}, bf16[592,128]{1,0:T(8,128)(2,1)S(1)}, u32[]{:S(2)}, u32[]{:S(2)}) %collective-permute-start.9) | collective-permute-done | bytes 151584 | tf_op jit(solution)/shard_map/ppermute | solution.py:485
  41.4 1.5 %scale.1 = (f32[192,576]{1,0:T(8,128)}, f32[192,192]{1,0:T(8,128)}, f32[1,192]{1,0:T(1,128)}) custom-call(s32[3]{0:T(128)S(1)} %add_convert_fusion.flags, bf16[592,128]{1,0:T(8,128)(2,1)S(1)} %add.14.after.mine, bf16[592,128]{1,0:T(8,128)(2,1)S(1)} %collective-permute-done.9.other), custom_call_target="tpu_custom_call" | custom-call | tf_op jit(solution)/shard_map/scale/pallas_call | solution.py:419
  (3 shorter events, 0.1 us)
Async XLA Ops:
  2.2 9.2 %collective-permute-start = (bf16[8,192,128]{2,1,0:T(8,128)(2,1)S(1)}, bf16[8,192,128]{2,1,0:T(8,128)(2,1)S(1)}, u32[]{:S(2)}, u32[]{:S(2)}) collective-permute-start(bf16[8,192,128]{2,1,0:T(8,128)(2,1)S(1)} %get-tuple-element.32), channel_id=1, source_target_pairs={{0,12},{4,0},{8,4},{12,8},{1,13},{5,1},{9,5},{13,9},{2,14},{6,2},{... | collective-permute-start | bytes 1179656 | tf_op jit(solution)/shard_map/ppermute | solution.py:469
  4.6 5.0 %collective-permute-start.1 = (bf16[8,4,192]{2,1,0:T(4,128)(2,1)S(1)}, bf16[8,4,192]{2,1,0:T(4,128)(2,1)S(1)}, u32[]{:S(2)}, u32[]{:S(2)}) collective-permute-start(bf16[8,4,192]{2,1,0:T(4,128)(2,1)S(1)} %get-tuple-element.33), channel_id=1, source_target_pairs={{0,3},{1,0},{2,1},{3,2},{4,7},{5,4},{6,5},{7,6},{8,11},{9,8},{10,9... | collective-permute-start | bytes 36872 | tf_op jit(solution)/shard_map/ppermute | solution.py:470
  8.2 3.2 %collective-permute-start.2 = (bf16[8,4,192]{2,1,0:T(4,128)(2,1)S(1)}, bf16[8,4,192]{2,1,0:T(4,128)(2,1)S(1)}, u32[]{:S(2)}, u32[]{:S(2)}) collective-permute-start(bf16[8,4,192]{2,1,0:T(4,128)(2,1)S(1)} %get-tuple-element.34), channel_id=1, source_target_pairs={{0,15},{1,12},{2,13},{3,14},{4,3},{5,0},{6,1},{7,2},{8,7},{9,4},{1... | collective-permute-start | bytes 36872 | tf_op jit(solution)/shard_map/ppermute | solution.py:471
  18.9 1.4 %collective-permute-start.4 = (bf16[592,128]{1,0:T(8,128)(2,1)S(1)}, bf16[592,128]{1,0:T(8,128)(2,1)S(1)}, u32[]{:S(2)}, u32[]{:S(2)}) collective-permute-start(bf16[592,128]{1,0:T(8,128)(2,1)S(1)} %get-tuple-element.47), channel_id=1, source_target_pairs={{0,4},{4,0},{8,12},{12,8},{1,5},{5,1},{9,13},{13,9},{2,6},{6,2},{1... | collective-permute-start | bytes 454664 | tf_op jit(solution)/shard_map/ppermute | solution.py:442
  20.4 5.3 %collective-permute-start.5 = (bf16[592,128]{1,0:T(8,128)(2,1)S(1)}, bf16[592,128]{1,0:T(8,128)(2,1)S(1)}, u32[]{:S(2)}, u32[]{:S(2)}) collective-permute-start(bf16[592,128]{1,0:T(8,128)(2,1)S(1)} %add.13.a), channel_id=1, source_target_pairs={{0,8},{1,9},{2,10},{3,11},{4,6},{5,7},{6,4},{7,5},{8,0},{9,1},{10,... | collective-permute-start | bytes 454664 | tf_op jit(solution)/shard_map/ppermute | solution.py:447
  25.7 6.8 %collective-permute-start.6 = (bf16[592,128]{1,0:T(8,128)(2,1)S(1)}, bf16[592,128]{1,0:T(8,128)(2,1)S(1)}, u32[]{:S(2)}, u32[]{:S(2)}) collective-permute-start(bf16[592,128]{1,0:T(8,128)(2,1)S(1)} %add.19.a), channel_id=1, source_target_pairs={{0,1},{1,0},{2,3},{3,2},{4,12},{5,13},{6,14},{7,15},{8,9},{9,8},{1... | collective-permute-start | bytes 454664 | tf_op jit(solution)/shard_map/ppermute | solution.py:447
  26.5 5.8 %collective-permute-start.3 = (bf16[8,4,192]{2,1,0:T(4,128)(2,1)S(1)}, bf16[8,4,192]{2,1,0:T(4,128)(2,1)S(1)}, u32[]{:S(2)}, u32[]{:S(2)}) collective-permute-start(bf16[8,4,192]{2,1,0:T(4,128)(2,1)S(1)} %get-tuple-element.44), channel_id=1, source_target_pairs={{3,0},{0,1},{1,2},{2,3},{7,4},{4,5},{5,6},{6,7},{11,8},{8,9},{9,10... | collective-permute-start | bytes 36872 | tf_op jit(solution)/shard_map/ppermute | solution.py:480
  32.6 7.4 %collective-permute-start.7 = (bf16[592,128]{1,0:T(8,128)(2,1)S(1)}, bf16[592,128]{1,0:T(8,128)(2,1)S(1)}, u32[]{:S(2)}, u32[]{:S(2)}) collective-permute-start(bf16[592,128]{1,0:T(8,128)(2,1)S(1)} %add.20), channel_id=1, source_target_pairs={{0,2},{1,3},{2,0},{3,1},{4,5},{5,4},{6,7},{7,6},{8,10},{9,11},{10,... | collective-permute-start | bytes 454664 | tf_op jit(solution)/shard_map/ppermute | solution.py:447
  33.2 6.9 %collective-permute-start.8 = (bf16[4,192,128]{2,1,0:T(8,128)(2,1)S(1)}, bf16[4,192,128]{2,1,0:T(8,128)(2,1)S(1)}, u32[]{:S(2)}, u32[]{:S(2)}) collective-permute-start(bf16[4,192,128]{2,1,0:T(8,128)(2,1)S(1)} %get-tuple-element.48), channel_id=1, source_target_pairs={{12,0},{0,4},{4,8},{8,12},{13,1},{1,5},{5,9},{9,13},{14,2},{2,6},{... | collective-permute-start | bytes 589832 | tf_op jit(solution)/shard_map/ppermute | solution.py:483
  40.0 1.4 %collective-permute-start.9 = (bf16[592,128]{1,0:T(8,128)(2,1)S(1)}, bf16[592,128]{1,0:T(8,128)(2,1)S(1)}, u32[]{:S(2)}, u32[]{:S(2)}) collective-permute-start(bf16[592,128]{1,0:T(8,128)(2,1)S(1)} %add.14.after.mine), channel_id=1, source_target_pairs={{0,4},{4,0},{8,12},{12,8},{1,5},{5,1},{9,13},{13,9},{2,6},{6,2},{1... | collective-permute-start | bytes 454664 | tf_op jit(solution)/shard_map/ppermute | solution.py:485

commit v4 on v3

v4 whole, which is shorter than its diff:
```python
import functools
import math

import jax
import jax.numpy as jnp
from jax import lax
from jax.experimental import pallas as pl
from jax.experimental.pallas import tpu as pltpu
from jax.sharding import PartitionSpec as P

HEADS = 6
HEAD_DIM = 32
WINDOW = 8
SHIFT = 4
PAIR = 2 * WINDOW * WINDOW
EPSILON = 1e-05
MASKED = -100.0
SCALE = HEAD_DIM ** (-0.5)
F32 = jnp.float32
BF16 = jnp.bfloat16


def dot_nn(a, b):
    return lax.dot_general(a, b, (((1,), (0,)), ((), ())), preferred_element_type=F32)


def dot_nt(a, b):
    return lax.dot_general(a, b, (((1,), (1,)), ((), ())), preferred_element_type=F32)


VMEM = pl.BlockSpec(memory_space=pltpu.VMEM)
ANY = pl.BlockSpec(memory_space=pl.ANY)
HBM = pl.BlockSpec(memory_space=pltpu.HBM)


def params(mib):
    return pltpu.CompilerParams(vmem_limit_bytes=mib * 2**20)


def shape(dtype, *dims):
    return jax.ShapeDtypeStruct(dims, dtype)


def gather_body(
    x, dy, w_qkv, w_proj, gain,
    message, rest, strip, corner, w_qkv_out, w_proj_out, gain_out, sems,
):
    sources = (x, dy)
    copies = [
        pltpu.make_async_copy(
            source.at[pl.ds(k * SHIFT, SHIFT)], dest.at[pl.ds(n * SHIFT, SHIFT)], sems.at[2 * k + n]
        )
        for k, dest in enumerate((message, rest))
        for n, source in enumerate(sources)
    ]
    pairs = ((w_qkv, w_qkv_out), (w_proj, w_proj_out), (gain, gain_out))
    copies += [pltpu.make_async_copy(a, b, sems.at[4 + n]) for n, (a, b) in enumerate(pairs)]
    for copy in copies:
        copy.start()
    for copy in copies[:4]:
        copy.wait()
    for i in range(2 * SHIFT):
        strip[i] = jnp.transpose(rest[i])[:SHIFT]
        corner[i] = jnp.transpose(message[i])[:SHIFT]
    for copy in copies[4:]:
        copy.wait()


def gather(x, dy, w_qkv, w_proj, gain):
    rows, channels, cols = x.shape
    operands = [pltpu.with_memory_space_constraint(v, pltpu.HBM) for v in (x, dy, w_qkv, w_proj, gain)]
    return pl.pallas_call(
        gather_body,
        out_shape=(
            shape(BF16, 2 * SHIFT, channels, cols),
            shape(BF16, 2 * SHIFT, channels, cols),
            shape(BF16, 2 * SHIFT, SHIFT, channels),
            shape(BF16, 2 * SHIFT, SHIFT, channels),
            shape(BF16, *w_qkv.shape),
            shape(BF16, *w_proj.shape),
            shape(F32, *gain.shape),
        ),
        in_specs=[HBM] * 5,
        out_specs=(VMEM,) * 7,
        scratch_shapes=[pltpu.SemaphoreType.DMA((7,))],
        compiler_params=params(8),
        name="gather",
    )(*operands)


def prep_body(rest, w_qkv, xs, dys, w_qkv_t):
    cols = rest.shape[2]
    for n, dest in enumerate((xs, dys)):
        for i in range(SHIFT):
            line = jnp.transpose(rest[n * SHIFT + i])
            dest[i] = pltpu.roll(line.astype(F32), cols - SHIFT, 0)
    w_qkv_t[...] = jnp.transpose(w_qkv[...])


def prep(rest, w_qkv):
    _, channels, cols = rest.shape
    return pl.pallas_call(
        prep_body,
        out_shape=(
            shape(F32, SHIFT, cols, channels),
            shape(F32, SHIFT, cols, channels),
            shape(BF16, w_qkv.shape[1], channels),
        ),
        in_specs=[VMEM] * 2,
        out_specs=(VMEM,) * 3,
        compiler_params=params(8),
        name="prep",
    )(rest, w_qkv)


def is_last(axis):
    return (lax.axis_index(axis) == lax.axis_size(axis) - 1).astype(F32)


def core():
    return lax.rem(lax.axis_index("row"), 2)


def write_masks(mask):
    k_pos = lax.broadcasted_iota(jnp.int32, (PAIR // 2, PAIR), 0)
    lane = lax.broadcasted_iota(jnp.int32, (PAIR // 2, PAIR), 1)
    q_pos = lane % (PAIR // 2)
    second = lane >= PAIR // 2
    row_cut = (k_pos // WINDOW >= SHIFT) != (q_pos // WINDOW >= SHIFT)
    col_cut = (k_pos % WINDOW >= SHIFT) != (q_pos % WINDOW >= SHIFT)
    row_mask = jnp.where(row_cut, 1.0, 0.0) * is_last("row")
    col_mask = jnp.where(col_cut & second, 1.0, 0.0) * is_last("col")
    mask[0] = row_mask * MASKED
    mask[1] = jnp.maximum(row_mask, col_mask) * MASKED


def attention(
    last, xs, dys, gain, w_qkv, w_qkv_t, w_proj, mask,
    n_t, upstream, dq_t, dk_n, dv_n, att_t, x_hat, inv_std,
    normed, q_t, k_t, v_t, do_t, k_n, v_n, q_n, do_n,
):
    rows, cols, channels = xs.shape
    tokens = rows * cols
    pairs = tokens // PAIR
    gain_row = gain[...]
    for w in range(cols // WINDOW):
        at = slice(w * WINDOW, (w + 1) * WINDOW)
        to = slice(w * PAIR // 2, (w + 1) * PAIR // 2)
        token = xs[:, at, :].reshape(PAIR // 2, channels)
        centred = token - jnp.mean(token, axis=-1, keepdims=True)
        inv = lax.rsqrt(jnp.mean(centred * centred, axis=-1, keepdims=True) + EPSILON)
        hat = centred * inv
        x_hat[to, :] = hat
        inv_std[to, :] = jnp.broadcast_to(inv, (PAIR // 2, 128))
        normed[to, :] = (hat * gain_row).astype(BF16)
        upstream[to, :] = dys[:, at, :].reshape(PAIR // 2, channels).astype(BF16)

    n_all = normed[...]
    q_t[...] = dot_nt(w_qkv_t[0:channels], n_all).astype(BF16)
    k_t[...] = dot_nt(w_qkv_t[channels : 2 * channels], n_all).astype(BF16)
    v_t[...] = dot_nt(w_qkv_t[2 * channels :], n_all).astype(BF16)
    k_n[...] = dot_nn(n_all, w_qkv[:, channels : 2 * channels]).astype(BF16)
    v_n[...] = dot_nn(n_all, w_qkv[:, 2 * channels :]).astype(BF16)
    do_t[...] = dot_nt(w_proj[...], upstream[...]).astype(BF16)
    q_n[:, :channels] = dot_nn(n_all, w_qkv[:, :channels]).astype(BF16)
    do_n[:, :channels] = dot_nt(upstream[...], w_proj[...]).astype(BF16)
    for padded in (q_n, do_n):
        padded[:, channels:] = jnp.zeros((tokens, padded.shape[1] - channels), BF16)
    n_t[...] = jnp.transpose(n_all)

    half_n = PAIR // 2
    first_lanes = lax.broadcasted_iota(jnp.int32, (half_n, PAIR), 1) < half_n

    def fold(full):
        return jnp.where(first_lanes, full[:half_n], full[half_n:])

    def spread(v):
        zero = jnp.zeros_like(v)
        return jnp.concatenate(
            (jnp.where(first_lanes, v, zero), jnp.where(first_lanes, zero, v)), axis=0
        )

    head_lane = lax.broadcasted_iota(jnp.int32, (half_n, 128), 1) // HEAD_DIM

    def by_key(dense, other, at, dest):
        for lo in range(0, channels, 128):
            here = range(lo // HEAD_DIM, min(lo + 128, channels) // HEAD_DIM)
            tall = jnp.concatenate([dense[h] for h in here], axis=0)
            v = other[at, lo : lo + 128]
            zero = jnp.zeros((half_n, 128), BF16)
            wide = jnp.concatenate(
                (
                    jnp.concatenate((v[:half_n], zero), axis=1),
                    jnp.concatenate((zero, v[half_n:]), axis=1),
                ),
                axis=0,
            )
            full = dot_nn(tall, wide)
            for w in range(2):
                found = full[:half_n, w * 128 : (w + 1) * 128]
                for n in range(1, len(here)):
                    piece = full[n * half_n : (n + 1) * half_n, w * 128 : (w + 1) * 128]
                    found = jnp.where(head_lane >= n, piece, found)
                width = len(here) * HEAD_DIM
                dest[at.start + w * half_n : at.start + (w + 1) * half_n, lo : lo + width] = found[
                    :, :width
                ].astype(BF16)

    def front(p):
        at = slice(p * PAIR, (p + 1) * PAIR)
        masking = mask[1 if last and p == pairs - 1 else 0]
        q, do = q_t[:, at], do_t[:, at]
        heads = [slice(h * HEAD_DIM, (h + 1) * HEAD_DIM) for h in range(HEADS)]

        def place(v, h, lo, hi):
            before, after = h * HEAD_DIM - lo, hi - (h + 1) * HEAD_DIM
            parts = [v[heads[h]]]
            if before:
                parts = [jnp.zeros((before, PAIR), BF16)] + parts
            if after:
                parts = parts + [jnp.zeros((after, PAIR), BF16)]
            return jnp.concatenate(parts, axis=0) if len(parts) > 1 else parts[0]

        def by_head(tall, v):
            found = []
            for lo in range(0, channels, 128):
                hi = min(lo + 128, channels)
                here = range(lo // HEAD_DIM, hi // HEAD_DIM)
                wide = jnp.concatenate([place(v, h, lo, hi) for h in here], axis=1)
                full = dot_nn(tall[at, lo:hi], wide)
                found += [fold(full[:, n * PAIR : (n + 1) * PAIR]) for n in range(len(here))]
            return found

        scores = by_head(k_n, q)
        grad_probs = by_head(v_n, do)
        return at, masking, q, do, heads, scores, grad_probs

    def middle(state):
        at, masking, q, do, heads, scores, grad_probs = state
        p_bd, s_bd = [], []
        for h in range(HEADS):
            s = scores[h] * SCALE + masking
            grown = jnp.exp(s - jnp.max(s, axis=0, keepdims=True))
            probs = grown * (1.0 / jnp.sum(grown, axis=0, keepdims=True))
            inner = jnp.sum(grad_probs[h] * probs, axis=0, keepdims=True)
            grad_scores = probs * (grad_probs[h] - inner) * SCALE
            p_bd.append(probs.astype(BF16))
            s_bd.append(grad_scores.astype(BF16))
        return p_bd, s_bd

    def rear(state, p_bd, s_bd):
        at, masking, q, do, heads, scores, grad_probs = state
        results = []
        for h in range(HEADS):
            results.append((
                dot_nn(k_t[heads[h], at], spread(s_bd[h])),
                dot_nn(v_t[heads[h], at], spread(p_bd[h])),
            ))
        by_key(s_bd, q_n, at, dk_n)
        by_key(p_bd, do_n, at, dv_n)
        for h in range(HEADS):
            dq_t[heads[h], at] = results[h][0].astype(BF16)
            att_t[heads[h], at] = results[h][1].astype(BF16)

    state = front(0)
    done = None
    for p in range(pairs):
        later = front(p + 1) if p + 1 < pairs else None
        if done is not None:
            rear(*done)
        done = (state, *middle(state))
        state = later
    rear(*done)


def attention_outs(cols, rows, channels):
    tokens = rows * cols
    return (
        shape(BF16, channels, tokens),
        shape(BF16, tokens, channels),
        shape(BF16, channels, tokens),
        shape(BF16, tokens, channels),
        shape(BF16, tokens, channels),
        shape(BF16, channels, tokens),
        shape(F32, tokens, channels),
        shape(F32, tokens, 128),
    )


def attention_scratch(cols, rows, channels):
    tokens = rows * cols
    flat = pltpu.VMEM((tokens, channels), BF16)
    turned = pltpu.VMEM((channels, tokens), BF16)
    padded = pltpu.VMEM((tokens, 256), BF16)
    return [flat, turned, turned, turned, turned, flat, flat, padded, padded]


def first_body(x_low, dy_low, row_halo, gain, w_qkv, w_qkv_t, w_proj, *refs):
    xs_b, dys_b, dys, *refs = refs
    outs, (xs, mask), scratch = refs[:8], refs[8:10], refs[10:]
    half_rows, cols, channels = x_low.shape
    part = cols // 2
    for n, (tile, here, later) in enumerate(((x_low, xs, xs_b), (dy_low, dys, dys_b))):
        for i in range(2 * half_rows):
            if i < half_rows:
                line = tile[i]
            else:
                line = jnp.transpose(row_halo[n * half_rows + i - half_rows]).astype(F32)
                line = pltpu.roll(line, cols - SHIFT, 0)
            here[i] = line[:part]
            later[i] = line[part:]
    write_masks(mask)
    attention(False, xs, dys, gain, w_qkv, w_qkv_t, w_proj, mask, *outs, *scratch)


def first(x_low, dy_low, row_halo, gain, w_qkv, w_qkv_t, w_proj):
    half_rows, cols, channels = x_low.shape
    sizes = (cols // 2, 2 * half_rows, channels)
    block = shape(F32, 2 * half_rows, cols // 2, channels)
    return pl.pallas_call(
        first_body,
        out_shape=(block, block, block) + attention_outs(*sizes),
        in_specs=[VMEM] * 7,
        out_specs=(VMEM,) * 11,
        scratch_shapes=[
            pltpu.VMEM(block.shape, F32),
            pltpu.VMEM((2, PAIR // 2, PAIR), F32),
        ] + attention_scratch(*sizes),
        compiler_params=params(24),
        name="first",
    )(x_low, dy_low, row_halo, gain, w_qkv, w_qkv_t, w_proj)


def second_body(
    xs_in, dys_in, strip, corner, gain, w_qkv, w_qkv_t, w_proj,
    n_t_a, upstream_a, dq_t_a, dk_n_a, dv_n_a, att_t_a, *refs,
):
    keep, send, dys, dq_t, dk_n, dv_n, x_hat, inv_std, *refs = refs
    xs, mask, halves, n_t, upstream, att_t, *scratch = refs
    rows, cols, channels = dys.shape
    for n, (source, dest) in enumerate(((xs_in, xs), (dys_in, dys))):
        for i in range(rows):
            tail = (strip if i < SHIFT else corner)[n * SHIFT + i % SHIFT]
            dest[i, : cols - WINDOW, :] = source[i, : cols - WINDOW, :]
            dest[i, cols - WINDOW :, :] = jnp.concatenate(
                (source[i, cols - WINDOW : cols - SHIFT, :], tail.astype(F32)), axis=0
            )
    write_masks(mask)
    attention(
        True, xs, dys, gain, w_qkv, w_qkv_t, w_proj, mask,
        n_t, upstream, dq_t, dk_n, dv_n, att_t, x_hat, inv_std, *scratch,
    )
    wide = jnp.concatenate(
        (
            dot_nt(n_t_a[...], dq_t_a[...]) + dot_nt(n_t[...], dq_t[...]),
            dot_nn(n_t_a[...], dk_n_a[...]) + dot_nn(n_t[...], dk_n[...]),
            dot_nn(n_t_a[...], dv_n_a[...]) + dot_nn(n_t[...], dv_n[...]),
        ),
        axis=1,
    )
    gain_sum = jnp.sum(wide * w_qkv[...].astype(F32), axis=1, keepdims=True)
    gain_sum = jnp.transpose(jnp.broadcast_to(gain_sum, (channels, 128)))[0:1] / gain[...]
    proj = dot_nn(att_t_a[...], upstream_a[...]) + dot_nn(att_t[...], upstream[...])
    both = jnp.concatenate((wide, proj), axis=1)
    gain_block = jnp.broadcast_to(
        jnp.concatenate((gain_sum, jnp.zeros((1, 256 - channels), F32)), axis=1), (16, 256)
    )
    part = channels // 2
    for n in range(2):
        for j in range(6):
            piece = both[n * part : (n + 1) * part, j * 128 : (j + 1) * 128]
            halves[n, j * part : (j + 1) * part, :] = piece.astype(BF16)
        halves[n, 6 * part :, :] = gain_block[:, n * 128 : (n + 1) * 128].astype(BF16)
    keep[...] = halves[core()]
    send[...] = halves[1 - core()]


def second(xs, dys, strip, corner, gain, w_qkv, w_qkv_t, w_proj, *saved):
    rows, cols, channels = xs.shape
    sizes = (cols, rows, channels)
    n_t, upstream, dq_t, dk_n, dv_n, att_t, x_hat, inv_std = attention_outs(*sizes)
    half = shape(BF16, 3 * channels + 16, 128)
    return pl.pallas_call(
        second_body,
        out_shape=(half, half, shape(F32, *xs.shape), dq_t, dk_n, dv_n, x_hat, inv_std),
        in_specs=[VMEM] * 14,
        out_specs=(VMEM,) * 8,
        scratch_shapes=[
            pltpu.VMEM(xs.shape, F32),
            pltpu.VMEM((2, PAIR // 2, PAIR), F32),
            pltpu.VMEM((2, *half.shape), BF16),
            pltpu.VMEM(n_t.shape, BF16),
            pltpu.VMEM(upstream.shape, BF16),
            pltpu.VMEM(att_t.shape, BF16),
        ] + attention_scratch(*sizes),
        compiler_params=params(24),
        name="second",
    )(xs, dys, strip, corner, gain, w_qkv, w_qkv_t, w_proj, *saved)


def back_body(*refs):
    parts, (gain, w_qkv_t, low, high, strip, out) = (refs[:6], refs[6:12]), refs[12:]
    rows, cols, channels = out.shape
    half_n = PAIR // 2
    gain_row = gain[...]
    for n, (dq_t, dk_n, dv_n, x_hat, inv_std, dys) in enumerate(parts):
        part = dys.shape[1]
        for p in range(rows * part // PAIR):
            at = slice(p * PAIR, (p + 1) * PAIR)
            g = dot_nn(jnp.transpose(dq_t[:, at]), w_qkv_t[:channels])
            g = g + dot_nn(dk_n[at, :], w_qkv_t[channels : 2 * channels])
            g = g + dot_nn(dv_n[at, :], w_qkv_t[2 * channels :])
            hat = x_hat[at, :]
            gh = g * gain_row
            mean_a = jnp.mean(gh, axis=-1, keepdims=True)
            mean_b = jnp.mean(gh * hat, axis=-1, keepdims=True)
            branch = inv_std[at, 0:1] * (gh - mean_a - hat * mean_b)
            for half in range(2):
                w = (2 * p + half) * WINDOW
                piece = branch[half * half_n : (half + 1) * half_n]
                out[:, n * part + w : n * part + w + WINDOW, :] = dys[
                    :, w : w + WINDOW, :
                ] + piece.reshape(rows, WINDOW, channels)
    for i in range(rows):
        line = pltpu.roll(out[i], SHIFT, 0)
        if i < rows // 2:
            strip[i] = line[:SHIFT].astype(BF16)
        dest = low if i < rows // 2 else high
        dest[i % SHIFT] = jnp.transpose(line.astype(BF16))


def back(part_a, part_b, gain, w_qkv_t):
    rows, part, channels = part_a[-1].shape
    cols = 2 * part
    return pl.pallas_call(
        back_body,
        out_shape=(
            shape(BF16, rows // 2, channels, cols),
            shape(BF16, rows // 2, channels, cols),
            shape(BF16, rows // 2, SHIFT, channels),
        ),
        in_specs=[VMEM] * 14,
        out_specs=(VMEM,) * 3,
        scratch_shapes=[pltpu.VMEM((rows, cols, channels), F32)],
        compiler_params=params(24),
        cost_estimate=pl.CostEstimate(
            flops=2 * rows * cols * channels * 3 * channels, bytes_accessed=8 * 2**20, transcendentals=0
        ),
        name="back",
    )(*part_a, *part_b, gain, w_qkv_t)


def collect_body(rows_back, low_strip, out):
    half = low_strip.shape[0]
    for i in range(half):
        out[i] = jnp.transpose(rows_back[i])[:SHIFT]
    out[half:] = low_strip[...]


def collect(rows_back, low_strip):
    half_rows, columns, channels = low_strip.shape
    return pl.pallas_call(
        collect_body,
        out_shape=shape(BF16, 2 * half_rows, columns, channels),
        in_specs=[VMEM] * 2,
        out_specs=VMEM,
        compiler_params=params(4),
        name="collect",
    )(rows_back, low_strip)


def add_body(a, b, *refs):
    refs[-1][...] = a[...] + b[...]


def add(a, b, *after):
    return pl.pallas_call(
        add_body,
        out_shape=shape(a.dtype, *a.shape),
        in_specs=[VMEM] * 2 + [ANY] * len(after),
        out_specs=VMEM,
        compiler_params=params(4),
        name="add",
    )(a, b, *after)


def join_body(high, low, strip, out, token, filled, sems):
    half, channels, cols = high.shape
    lanes = lax.broadcasted_iota(jnp.int32, (channels, cols), 1)
    copies = []
    for n, source in enumerate((high, low)):
        for i in range(half):
            wide = jnp.transpose(jnp.concatenate([strip[n * half + i]] * (cols // SHIFT), axis=0))
            filled[n * half + i] = jnp.where(lanes < SHIFT, wide, source[i])
        rows = pl.ds(n * half, half)
        copies.append(pltpu.make_async_copy(filled.at[rows], out.at[rows], sems.at[n]))
        copies[n].start()
    token[...] = jnp.zeros(token.shape, token.dtype)
    for copy in copies:
        copy.wait()


def join(high, low, strip):
    half_rows, channels, cols = high.shape
    whole = (2 * half_rows, channels, cols)
    return pl.pallas_call(
        join_body,
        out_shape=(shape(BF16, *whole), shape(F32, 8, 128)),
        in_specs=[VMEM] * 3,
        out_specs=(HBM, VMEM),
        scratch_shapes=[pltpu.VMEM(whole, BF16), pltpu.SemaphoreType.DMA((2,))],
        compiler_params=params(4),
        cost_estimate=pl.CostEstimate(flops=4 * 10**9, bytes_accessed=0, transcendentals=0),
        name="join",
    )(high, low, strip)


def write_half(half, row, factor, wqkv, wproj, wide, tall, sems):
    part = wide.shape[0]
    whole = jnp.concatenate([half[j * part : (j + 1) * part, :] for j in range(6)], axis=1)
    whole = whole.astype(F32) * factor
    wide[...] = whole[:, : wide.shape[1]]
    tall[...] = whole[:, wide.shape[1] :]
    rows = pl.ds(pl.multiple_of(row, 8), part)
    copies = [
        pltpu.make_async_copy(wide, wqkv.at[rows], sems.at[0]),
        pltpu.make_async_copy(tall, wproj.at[rows], sems.at[1]),
    ]
    for copy in copies:
        copy.start()
    return copies


def own_body(mine, wqkv, wproj, wide, tall, line, sems, *, factor):
    for copy in write_half(mine, core() * wide.shape[0], factor, wqkv, wproj, wide, tall, sems):
        copy.wait()


def other_body(
    mine, other, wqkv_in, wproj_in, wqkv, wproj, gain, wide, tall, line, sems, *, factor
):
    part, channels = tall.shape
    copies = write_half(other, (1 - core()) * part, factor, wqkv, wproj, wide, tall, sems)
    a, b = mine[6 * part :, :], other[6 * part :, :]
    swapped = jnp.concatenate((b, a), axis=1).astype(F32)
    row = jnp.concatenate((a, b), axis=1).astype(F32)
    row = jnp.where(core() == 0, row, swapped)
    line[...] = row[0:1, :channels] * factor
    copies.append(pltpu.make_async_copy(line, gain, sems.at[2]))
    copies[2].start()
    for copy in copies:
        copy.wait()


def scale_scratch(channels):
    return [
        pltpu.VMEM((channels // 2, 3 * channels), F32),
        pltpu.VMEM((channels // 2, channels), F32),
        pltpu.VMEM((1, channels), F32),
        pltpu.SemaphoreType.DMA((3,)),
    ]


def scale_own(mine, channels, factor):
    return pl.pallas_call(
        functools.partial(own_body, factor=factor),
        out_shape=(shape(F32, channels, 3 * channels), shape(F32, channels, channels)),
        in_specs=[VMEM],
        out_specs=(HBM, HBM),
        scratch_shapes=scale_scratch(channels),
        compiler_params=params(4),
        cost_estimate=pl.CostEstimate(flops=10**9, bytes_accessed=0, transcendentals=0),
        name="scale_own",
    )(mine)


def scale_other(mine, other, wqkv, wproj, channels, factor):
    return pl.pallas_call(
        functools.partial(other_body, factor=factor),
        out_shape=(
            shape(F32, channels, 3 * channels),
            shape(F32, channels, channels),
            shape(F32, 1, channels),
        ),
        in_specs=[VMEM, VMEM, HBM, HBM],
        out_specs=(HBM, HBM, HBM),
        input_output_aliases={2: 0, 3: 1},
        scratch_shapes=scale_scratch(channels),
        compiler_params=params(4),
        name="scale_other",
    )(mine, other, wqkv, wproj)


def flip(extent, bit):
    return [(i, i ^ bit) for i in range(extent)]


def bit_orders(row_extent, col_extent):
    bits = [b * col_extent for b in (2**n for n in range(1, 16)) if b < row_extent]
    bits += [b for b in (2**n for n in range(16)) if b < col_extent]
    turn = len(bits) - len(bits) // 2
    return bits, bits[turn:] + bits[:turn]


def on_device(activations, cotangent, norm_gain, w_qkv, w_proj):
    rows, cols, channels = activations.shape
    row_extent, col_extent = lax.axis_size("row"), lax.axis_size("col")
    up = [(i, (i - 1) % row_extent) for i in range(row_extent)]
    left = [(i, (i - 1) % col_extent) for i in range(col_extent)]
    both = [
        (r * col_extent + c, (r - 1) % row_extent * col_extent + (c - 1) % col_extent)
        for r in range(row_extent)
        for c in range(col_extent)
    ]
    turn = lambda route: [(b, a) for a, b in route]
    swap = lambda v: jnp.transpose(v, (0, 2, 1))
    x_t, dy_t = swap(activations), swap(cotangent)
    message, rest, strip, corner, w_qkv, w_proj, gain = gather(
        x_t, dy_t, w_qkv, w_proj, norm_gain.reshape(1, channels)
    )
    row_halo = lax.ppermute(message, "row", up)
    strip = lax.ppermute(strip, "col", left)
    corner = lax.ppermute(corner, ("row", "col"), both)
    x_low, dy_low, w_qkv_t = prep(rest, w_qkv)
    weights = (gain, w_qkv, w_qkv_t, w_proj)
    xs_b, dys_b, dys_a, *out_a = first(x_low, dy_low, row_halo, *weights)
    keep, send, dys_b, *saved_b = second(
        xs_b, dys_b, strip, corner, *weights, *out_a[:6]
    )
    low, high, strip = back(
        (*out_a[2:5], *out_a[6:], dys_a), (*saved_b, dys_b), gain, w_qkv_t
    )
    rows_back = lax.ppermute(high, "row", turn(up))
    orders = bit_orders(row_extent, col_extent)
    total = keep + lax.ppermute(send, "row", flip(row_extent, 1))
    steps = len(orders[0])
    for step in range(steps):
        route = [
            (i, i ^ orders[i // col_extent % 2][step]) for i in range(row_extent * col_extent)
        ]
        arrived = lax.ppermute(total, ("row", "col"), route)
        if step == 0:
            beside = (low,)
        elif step == 1:
            strip = collect(rows_back, strip)
            beside = (strip,)
            strip = lax.ppermute(strip, "col", turn(left))
        elif step == steps - 1:
            grad_input, token = join(rows_back, low, strip)
            beside = (token,)
        else:
            beside = ()
        total = add(total, arrived, *beside)
    grad_input = swap(grad_input)
    other = lax.ppermute(total, "row", flip(row_extent, 1))
    factor = 1.0 / math.sqrt(rows * row_extent * cols * col_extent)
    grad_wqkv, grad_wproj = scale_own(total, channels, factor)
    grad_wqkv, grad_wproj, grad_gain = scale_other(
        total, other, grad_wqkv, grad_wproj, channels, factor
    )
    return grad_input, grad_wqkv, grad_wproj, grad_gain.reshape(channels)


def solution(mesh):
    tile = P(("parts", "row"), "col", None)
    return jax.shard_map(
        on_device,
        mesh=mesh,
        in_specs=(tile, tile, P(), P(), P()),
        out_specs=(tile, P("parts", None), P("parts", None), P("parts")),
        check_vma=False,
    )
```

time: 43.1 us -> 37.5 us (0.87)
  waiting for transfers between devices: 17.7 us -> 8.29 us
  starting transfers between devices: 10.9 us -> 16.6 us
  Pallas kernels: 13.4 us -> 11.2 us
    ppermute x5, starting transfers between devices: 3.22 us -> 8.53 us  [the longest x3 6.17 us: on_device(): arrived = lax.ppermute(total, ('row', 'col'), route)]
    ppermute x5, waiting for transfers between devices: 10.1 us -> 5.68 us  [the longest x3 3.11 us: on_device(): arrived = lax.ppermute(total, ('row', 'col'), route)]
    ppermute x1, waiting for transfers between devices: 4.54 us -> 1.01 us  [on_device(): strip = lax.ppermute(strip, 'col', turn(left))]
    pallas_call x6 -> x9, Pallas kernels: 10.1 us -> 8.14 us  [the longest x1 2.99 us: second(): pl.pallas_call(second_body, out_shape=(half, half, shape(F32, *xs.shape),...]
    ppermute x1, waiting for transfers between devices: 1.72 us -> 0.01 us  [on_device(): corner = lax.ppermute(corner, ('row', 'col'), both)]
    ppermute x1, waiting for transfers between devices: 0.01 us -> 1.12 us  [on_device(): row_halo = lax.ppermute(message, 'row', up)]
    ppermute x1, waiting for transfers between devices: 0.8 us -> 0.01 us  [on_device(): strip = lax.ppermute(strip, 'col', left)]
  transfers between devices with their start and end apart: 10 -> 10, of which waited for: 7 -> 8; matrix products, arithmetic and copies ran while one was open for 0% -> 0% of each run, Pallas kernels for 7% -> 16%
where the time goes in v4:
time: 37.5 us; the launch traced here: 36.9 us
  starting transfers between devices  16.6 us (44%)
  Pallas kernels  11.2 us (30%)
  waiting for transfers between devices  8.29 us (22%)
  between operations  0.71 us (2%)
    ppermute x3, starting transfers between devices, on_device(): arrived = lax.ppermute(total, ('row', 'col'), route)  6.17 us
    ppermute x1, starting transfers between devices, on_device(): strip = lax.ppermute(strip, 'col', left)  3.6 us
    ppermute x3, waiting for transfers between devices, on_device(): arrived = lax.ppermute(total, ('row', 'col'), route)  3.11 us
    pallas_call x1, Pallas kernels, second(): pl.pallas_call(second_body, out_shape=(half, half, shape(F32, *xs.shape),...  2.99 us
    pallas_call x1, Pallas kernels, first(): pl.pallas_call(first_body, out_shape=(block, block, block) + attention_ou...  2.52 us
    ppermute x1, starting transfers between devices, on_device(): row_halo = lax.ppermute(message, 'row', up)  2.43 us
    ppermute x1, starting transfers between devices, on_device(): strip = lax.ppermute(strip, 'col', turn(left))  1.62 us
    ppermute x1, waiting for transfers between devices, on_device(): rows_back = lax.ppermute(high, 'row', turn(up))  1.55 us
  transfers between devices with their start and end apart: 10, of which 8 were waited for; matrix products, arithmetic and copies ran while one was open for 0% of the time, Pallas kernels for 16%

profile of v4, /device:TPU:0, one launch (start us, length us, event | category | flops | bytes accessed | tf_op | source)
XLA Modules:
  0.0 36.9 jit_solution(7583213625978224583)
XLA Ops:
  0.6 1.5 %gather.1 = (bf16[8,192,128]{2,1,0:T(8,128)(2,1)S(1)}, bf16[8,192,128]{2,1,0:T(8,128)(2,1)S(1)}, bf16[8,4,192]{2,1,0:T(4,128)(2,1)S(1)}, bf16[8,4,192]{2,1,0:T(4...) custom-call(bf16[8,192,128]{2,1,0:T(8,128)(2,1)} %bitcast.5, ...), custom_call_target="tpu_custom_call" | custom-call | tf_op jit(solution)/shard_map/gather/pallas_call | solution.py:72
  2.2 2.4 %collective-permute-start = (bf16[8,192,128]{2,1,0:T(8,128)(2,1)S(1)}, bf16[8,192,128]{2,1,0:T(8,128)(2,1)S(1)}, u32[]{:S(2)}, u32[]{:S(2)}) collective-permute-start(bf16[8,192,128]{2,1,0:T(8,128)(2,1)S(1)} %get-tuple-element.47), channel_id=1, source_target_pairs={{0,12},{4,0},{8,4},{12,8},{1,13},{5,1},{9,5},{13,9},{2,14},{6,2},{... | collective-permute-start | bytes 1179656 | tf_op jit(solution)/shard_map/ppermute | solution.py:621
  4.6 3.6 %collective-permute-start.1 = (bf16[8,4,192]{2,1,0:T(4,128)(2,1)S(1)}, bf16[8,4,192]{2,1,0:T(4,128)(2,1)S(1)}, u32[]{:S(2)}, u32[]{:S(2)}) collective-permute-start(bf16[8,4,192]{2,1,0:T(4,128)(2,1)S(1)} %get-tuple-element.59), channel_id=1, source_target_pairs={{0,3},{1,0},{2,1},{3,2},{4,7},{5,4},{6,5},{7,6},{8,11},{9,8},{10,9... | collective-permute-start | bytes 36872 | tf_op jit(solution)/shard_map/ppermute | solution.py:622
  8.2 0.3 collective-permute-start.2
  8.5 0.3 prep.1
  8.8 1.1 %collective-permute-done.row_halo = bf16[8,192,128]{2,1,0:T(8,128)(2,1)S(1)} collective-permute-done((bf16[8,192,128]{2,1,0:T(8,128)(2,1)S(1)}, bf16[8,192,128]{2,1,0:T(8,128)(2,1)S(1)}, u32[]{:S(2)}, u32[]{:S(2)}) %collective-permute-start) | collective-permute-done | bytes 393248 | tf_op jit(solution)/shard_map/ppermute | solution.py:621
  9.9 2.5 %first.1 = (f32[8,64,192]{2,1,0:T(8,128)S(1)}, f32[8,64,192]{2,1,0:T(8,128)S(1)}, f32[8,64,192]{2,1,0:T(8,128)S(1)}, bf16[192,512]{1,0:T(8,128)(2,1)S(1)}, bf16[...) custom-call(f32[4,128,192]{2,1,0:T(8,128)S(1)} %get-tuple-element.45, ...), custom_call_target="tpu_custom_call" | custom-call | tf_op jit(solution)/shard_map/first/pallas_call | solution.py:320
  12.4 0.0 collective-permute-done.1.strip
  12.4 0.0 collective-permute-done.2.corner
  12.5 3.0 %second.1 = (bf16[592,128]{1,0:T(8,128)(2,1)S(1)}, bf16[592,128]{1,0:T(8,128)(2,1)S(1)}, f32[8,64,192]{2,1,0:T(8,128)S(1)}, bf16[192,512]{1,0:T(8,128)(2,1)S(1)}...) custom-call(f32[8,64,192]{2,1,0:T(8,128)S(1)} %get-tuple-element.57., ...), custom_call_target="tpu_custom_call" | custom-call | tf_op jit(solution)/shard_map/second/pallas_call | solution.py:383
  15.5 0.9 %collective-permute-start.5 = (bf16[592,128]{1,0:T(8,128)(2,1)S(1)}, bf16[592,128]{1,0:T(8,128)(2,1)S(1)}, u32[]{:S(2)}, u32[]{:S(2)}) collective-permute-start(bf16[592,128]{1,0:T(8,128)(2,1)S(1)} %get-tuple-element.75), channel_id=1, source_target_pairs={{0,4},{4,0},{8,12},{12,8},{1,5},{5,1},{9,13},{13,9},{2,6},{6,2},{1... | collective-permute-start | bytes 454664 | tf_op jit(solution)/shard_map/ppermute | solution.py:635
  16.4 1.0 %collective-permute-done.5 = bf16[592,128]{1,0:T(8,128)(2,1)S(1)} collective-permute-done((bf16[592,128]{1,0:T(8,128)(2,1)S(1)}, bf16[592,128]{1,0:T(8,128)(2,1)S(1)}, u32[]{:S(2)}, u32[]{:S(2)}) %collective-permute-start.5) | collective-permute-done | bytes 151584 | tf_op jit(solution)/shard_map/ppermute | solution.py:635
  17.4 1.5 %collective-permute-start.6 = (bf16[592,128]{1,0:T(8,128)(2,1)S(1)}, bf16[592,128]{1,0:T(8,128)(2,1)S(1)}, u32[]{:S(2)}, u32[]{:S(2)}) collective-permute-start(bf16[592,128]{1,0:T(8,128)(2,1)S(1)} %add.6.a), channel_id=1, source_target_pairs={{0,8},{1,9},{2,10},{3,11},{4,6},{5,7},{6,4},{7,5},{8,0},{9,1},{10,... | collective-permute-start | bytes 454664 | tf_op jit(solution)/shard_map/ppermute | solution.py:641
  19.0 1.3 %back.1 = (bf16[4,192,128]{2,1,0:T(8,128)(2,1)S(1)}, bf16[4,192,128]{2,1,0:T(8,128)(2,1)S(1)}, bf16[4,4,192]{2,1,0:T(4,128)(2,1)S(1)}) custom-call(bf16[192,512]{1,0:T(8,128)(2,1)S(1)} %get-tuple-element.51.dq_t_a.refs_0_, bf16[512,192]{1,0:T(8,128)(2,1)S(1)} %get-tuple-element.52.dk_n_a.refs_1_, bf16[512,192]{1,0:T(8,128)(2,1)S(1)} %get-tuple-element.53.dv_n_a.refs_2_, ...), custom_call_target="tpu_custom_call" | custom-call | flops 226492416 | bytes 8388608 | tf_op jit(solution)/shard_map/back/pallas_call | solution.py:435
  20.2 1.4 %collective-permute-start.3 = (bf16[4,192,128]{2,1,0:T(8,128)(2,1)S(1)}, bf16[4,192,128]{2,1,0:T(8,128)(2,1)S(1)}, u32[]{:S(2)}, u32[]{:S(2)}) collective-permute-start(bf16[4,192,128]{2,1,0:T(8,128)(2,1)S(1)} %get-tuple-element.70), channel_id=1, source_target_pairs={{12,0},{0,4},{4,8},{8,12},{13,1},{1,5},{5,9},{9,13},{14,2},{2,6},{... | collective-permute-start | bytes 589832 | tf_op jit(solution)/shard_map/ppermute | solution.py:633
  21.7 1.0 %collective-permute-done.6.b = bf16[592,128]{1,0:T(8,128)(2,1)S(1)} collective-permute-done((bf16[592,128]{1,0:T(8,128)(2,1)S(1)}, bf16[592,128]{1,0:T(8,128)(2,1)S(1)}, u32[]{:S(2)}, u32[]{:S(2)}) %collective-permute-start.6) | collective-permute-done | bytes 151584 | tf_op jit(solution)/shard_map/ppermute | solution.py:641
  22.7 1.8 %collective-permute-start.7 = (bf16[592,128]{1,0:T(8,128)(2,1)S(1)}, bf16[592,128]{1,0:T(8,128)(2,1)S(1)}, u32[]{:S(2)}, u32[]{:S(2)}) collective-permute-start(bf16[592,128]{1,0:T(8,128)(2,1)S(1)} %add.7.a), channel_id=1, source_target_pairs={{0,1},{1,0},{2,3},{3,2},{4,12},{5,13},{6,14},{7,15},{8,9},{9,8},{1... | collective-permute-start | bytes 454664 | tf_op jit(solution)/shard_map/ppermute | solution.py:641
  24.5 1.6 %collective-permute-done.3.rows_back.high = bf16[4,192,128]{2,1,0:T(8,128)(2,1)S(1)} collective-permute-done((bf16[4,192,128]{2,1,0:T(8,128)(2,1)S(1)}, bf16[4,192,128]{2,1,0:T(8,128)(2,1)S(1)}, u32[]{:S(2)}, u32[]{:S(2)}) %collective-permute-start.3) | collective-permute-done | bytes 196640 | tf_op jit(solution)/shard_map/ppermute | solution.py:633
  26.1 0.1 collect.1.refs_0_
  26.2 1.6 %collective-permute-start.4 = (bf16[8,4,192]{2,1,0:T(4,128)(2,1)S(1)}, bf16[8,4,192]{2,1,0:T(4,128)(2,1)S(1)}, u32[]{:S(2)}, u32[]{:S(2)}) collective-permute-start(bf16[8,4,192]{2,1,0:T(4,128)(2,1)S(1)} %collect.1.refs_0_), channel_id=1, source_target_pairs={{3,0},{0,1},{1,2},{2,3},{7,4},{4,5},{5,6},{6,7},{11,8},{8,9},{9,10... | collective-permute-start | bytes 36872 | tf_op jit(solution)/shard_map/ppermute | solution.py:647
  27.8 0.2 collective-permute-done.7.b
  28.0 2.8 %collective-permute-start.8 = (bf16[592,128]{1,0:T(8,128)(2,1)S(1)}, bf16[592,128]{1,0:T(8,128)(2,1)S(1)}, u32[]{:S(2)}, u32[]{:S(2)}) collective-permute-start(bf16[592,128]{1,0:T(8,128)(2,1)S(1)} %add.8.a), channel_id=1, source_target_pairs={{0,2},{1,3},{2,0},{3,1},{4,5},{5,4},{6,7},{7,6},{8,10},{9,11},{10,... | collective-permute-start | bytes 454664 | tf_op jit(solution)/shard_map/ppermute | solution.py:641
  30.8 1.0 %collective-permute-done.4.strip = bf16[8,4,192]{2,1,0:T(4,128)(2,1)S(1)} collective-permute-done((bf16[8,4,192]{2,1,0:T(4,128)(2,1)S(1)}, bf16[8,4,192]{2,1,0:T(4,128)(2,1)S(1)}, u32[]{:S(2)}, u32[]{:S(2)}) %collective-permute-start.4) | collective-permute-done | bytes 12320 | tf_op jit(solution)/shard_map/ppermute | solution.py:647
  31.9 0.9 %join.1 = (bf16[8,192,128]{2,1,0:T(8,128)(2,1)}, f32[8,128]{1,0:T(8,128)S(1)}) custom-call(bf16[4,192,128]{2,1,0:T(8,128)(2,1)S(1)} %collective-permute-done.3.rows_back.high, bf16[4,192,128]{2,1,0:T(8,128)(2,1)S(1)} %get-tuple-element.71.low.refs_0_, bf16[8,4,192]{2,1,0:T(4,128)(2,1)S(1)} %collective-permute-done.4.strip), custom_call_target="tpu_custom_call" | custom-call | flops 4000000000 | tf_op jit(solution)/shard_map/join/pallas_call | solution.py:506
  32.8 1.9 %collective-permute-done.8.b = bf16[592,128]{1,0:T(8,128)(2,1)S(1)} collective-permute-done((bf16[592,128]{1,0:T(8,128)(2,1)S(1)}, bf16[592,128]{1,0:T(8,128)(2,1)S(1)}, u32[]{:S(2)}, u32[]{:S(2)}) %collective-permute-start.8) | collective-permute-done | bytes 151584 | tf_op jit(solution)/shard_map/ppermute | solution.py:641
  34.7 0.2 collective-permute-start.9
  34.9 0.8 %scale_own.1 = (f32[192,576]{1,0:T(8,128)}, f32[192,192]{1,0:T(8,128)}) custom-call(bf16[592,128]{1,0:T(8,128)(2,1)S(1)} %add.9.mine), custom_call_target="tpu_custom_call" | custom-call | flops 1000000000 | tf_op jit(solution)/shard_map/scale_own/pallas_call | solution.py:565
  35.7 0.5 %collective-permute-done.9.other = bf16[592,128]{1,0:T(8,128)(2,1)S(1)} collective-permute-done((bf16[592,128]{1,0:T(8,128)(2,1)S(1)}, bf16[592,128]{1,0:T(8,128)(2,1)S(1)}, u32[]{:S(2)}, u32[]{:S(2)}) %collective-permute-start.9) | collective-permute-done | bytes 151584 | tf_op jit(solution)/shard_map/ppermute | solution.py:655
  36.1 0.8 %scale_other.1 = (f32[192,576]{1,0:T(8,128)}, f32[192,192]{1,0:T(8,128)}, f32[1,192]{1,0:T(1,128)}) custom-call(bf16[592,128]{1,0:T(8,128)(2,1)S(1)} %add.9.mine, bf16[592,128]{1,0:T(8,128)(2,1)S(1)} %collective-permute-done.9.other, f32[192,576]{1,0:T(8,128)} %get-tuple-element.77.wqkv_in, ...), custom_call_target="tpu_custom_call", output_to_operand_aliasing={{0}: (2, {}), {1}: (3, {})} | custom-call | tf_op jit(solution)/shard_map/scale_other/pallas_call | solution.py:578
  (4 shorter events, 0.1 us)
Async XLA Ops:
  2.2 7.7 %collective-permute-start = (bf16[8,192,128]{2,1,0:T(8,128)(2,1)S(1)}, bf16[8,192,128]{2,1,0:T(8,128)(2,1)S(1)}, u32[]{:S(2)}, u32[]{:S(2)}) collective-permute-start(bf16[8,192,128]{2,1,0:T(8,128)(2,1)S(1)} %get-tuple-element.47), channel_id=1, source_target_pairs={{0,12},{4,0},{8,4},{12,8},{1,13},{5,1},{9,5},{13,9},{2,14},{6,2},{... | collective-permute-start | bytes 1179656 | tf_op jit(solution)/shard_map/ppermute | solution.py:621
  4.6 7.8 %collective-permute-start.1 = (bf16[8,4,192]{2,1,0:T(4,128)(2,1)S(1)}, bf16[8,4,192]{2,1,0:T(4,128)(2,1)S(1)}, u32[]{:S(2)}, u32[]{:S(2)}) collective-permute-start(bf16[8,4,192]{2,1,0:T(4,128)(2,1)S(1)} %get-tuple-element.59), channel_id=1, source_target_pairs={{0,3},{1,0},{2,1},{3,2},{4,7},{5,4},{6,5},{7,6},{8,11},{9,8},{10,9... | collective-permute-start | bytes 36872 | tf_op jit(solution)/shard_map/ppermute | solution.py:622
  8.2 4.2 %collective-permute-start.2 = (bf16[8,4,192]{2,1,0:T(4,128)(2,1)S(1)}, bf16[8,4,192]{2,1,0:T(4,128)(2,1)S(1)}, u32[]{:S(2)}, u32[]{:S(2)}) collective-permute-start(bf16[8,4,192]{2,1,0:T(4,128)(2,1)S(1)} %get-tuple-element.60), channel_id=1, source_target_pairs={{0,15},{1,12},{2,13},{3,14},{4,3},{5,0},{6,1},{7,2},{8,7},{9,4},{1... | collective-permute-start | bytes 36872 | tf_op jit(solution)/shard_map/ppermute | solution.py:623
  15.5 1.9 %collective-permute-start.5 = (bf16[592,128]{1,0:T(8,128)(2,1)S(1)}, bf16[592,128]{1,0:T(8,128)(2,1)S(1)}, u32[]{:S(2)}, u32[]{:S(2)}) collective-permute-start(bf16[592,128]{1,0:T(8,128)(2,1)S(1)} %get-tuple-element.75), channel_id=1, source_target_pairs={{0,4},{4,0},{8,12},{12,8},{1,5},{5,1},{9,13},{13,9},{2,6},{6,2},{1... | collective-permute-start | bytes 454664 | tf_op jit(solution)/shard_map/ppermute | solution.py:635
  17.4 5.3 %collective-permute-start.6 = (bf16[592,128]{1,0:T(8,128)(2,1)S(1)}, bf16[592,128]{1,0:T(8,128)(2,1)S(1)}, u32[]{:S(2)}, u32[]{:S(2)}) collective-permute-start(bf16[592,128]{1,0:T(8,128)(2,1)S(1)} %add.6.a), channel_id=1, source_target_pairs={{0,8},{1,9},{2,10},{3,11},{4,6},{5,7},{6,4},{7,5},{8,0},{9,1},{10,... | collective-permute-start | bytes 454664 | tf_op jit(solution)/shard_map/ppermute | solution.py:641
  20.2 5.9 %collective-permute-start.3 = (bf16[4,192,128]{2,1,0:T(8,128)(2,1)S(1)}, bf16[4,192,128]{2,1,0:T(8,128)(2,1)S(1)}, u32[]{:S(2)}, u32[]{:S(2)}) collective-permute-start(bf16[4,192,128]{2,1,0:T(8,128)(2,1)S(1)} %get-tuple-element.70), channel_id=1, source_target_pairs={{12,0},{0,4},{4,8},{8,12},{13,1},{1,5},{5,9},{9,13},{14,2},{2,6},{... | collective-permute-start | bytes 589832 | tf_op jit(solution)/shard_map/ppermute | solution.py:633
  22.7 5.3 %collective-permute-start.7 = (bf16[592,128]{1,0:T(8,128)(2,1)S(1)}, bf16[592,128]{1,0:T(8,128)(2,1)S(1)}, u32[]{:S(2)}, u32[]{:S(2)}) collective-permute-start(bf16[592,128]{1,0:T(8,128)(2,1)S(1)} %add.7.a), channel_id=1, source_target_pairs={{0,1},{1,0},{2,3},{3,2},{4,12},{5,13},{6,14},{7,15},{8,9},{9,8},{1... | collective-permute-start | bytes 454664 | tf_op jit(solution)/shard_map/ppermute | solution.py:641
  26.2 5.7 %collective-permute-start.4 = (bf16[8,4,192]{2,1,0:T(4,128)(2,1)S(1)}, bf16[8,4,192]{2,1,0:T(4,128)(2,1)S(1)}, u32[]{:S(2)}, u32[]{:S(2)}) collective-permute-start(bf16[8,4,192]{2,1,0:T(4,128)(2,1)S(1)} %collect.1.refs_0_), channel_id=1, source_target_pairs={{3,0},{0,1},{1,2},{2,3},{7,4},{4,5},{5,6},{6,7},{11,8},{8,9},{9,10... | collective-permute-start | bytes 36872 | tf_op jit(solution)/shard_map/ppermute | solution.py:647
  28.0 6.6 %collective-permute-start.8 = (bf16[592,128]{1,0:T(8,128)(2,1)S(1)}, bf16[592,128]{1,0:T(8,128)(2,1)S(1)}, u32[]{:S(2)}, u32[]{:S(2)}) collective-permute-start(bf16[592,128]{1,0:T(8,128)(2,1)S(1)} %add.8.a), channel_id=1, source_target_pairs={{0,2},{1,3},{2,0},{3,1},{4,5},{5,4},{6,7},{7,6},{8,10},{9,11},{10,... | collective-permute-start | bytes 454664 | tf_op jit(solution)/shard_map/ppermute | solution.py:641
  34.7 1.4 %collective-permute-start.9 = (bf16[592,128]{1,0:T(8,128)(2,1)S(1)}, bf16[592,128]{1,0:T(8,128)(2,1)S(1)}, u32[]{:S(2)}, u32[]{:S(2)}) collective-permute-start(bf16[592,128]{1,0:T(8,128)(2,1)S(1)} %add.9.mine), channel_id=1, source_target_pairs={{0,4},{4,0},{8,12},{12,8},{1,5},{5,1},{9,13},{13,9},{2,6},{6,2},{1... | collective-permute-start | bytes 454664 | tf_op jit(solution)/shard_map/ppermute | solution.py:655

commit v5 on v4

--- a/solution.py
+++ b/solution.py
@@ -41,38 +41,65 @@
     return jax.ShapeDtypeStruct(dims, dtype)
 
 
-def gather_body(
-    x, dy, w_qkv, w_proj, gain,
-    message, rest, strip, corner, w_qkv_out, w_proj_out, gain_out, sems,
-):
-    sources = (x, dy)
+def in_hbm(*arrays):
+    return [pltpu.with_memory_space_constraint(v, pltpu.HBM) for v in arrays]
+
+
+def gather_body(x, dy, out, sems):
     copies = [
         pltpu.make_async_copy(
-            source.at[pl.ds(k * SHIFT, SHIFT)], dest.at[pl.ds(n * SHIFT, SHIFT)], sems.at[2 * k + n]
+            source.at[pl.ds(0, SHIFT)], out.at[pl.ds(n * SHIFT, SHIFT)], sems.at[n]
         )
-        for k, dest in enumerate((message, rest))
-        for n, source in enumerate(sources)
+        for n, source in enumerate((x, dy))
+    ]
+    for copy in copies:
+        copy.start()
+    for copy in copies:
+        copy.wait()
+
+
+def gather(x, dy):
+    _, channels, cols = x.shape
+    return pl.pallas_call(
+        gather_body,
+        out_shape=shape(BF16, 2 * SHIFT, channels, cols),
+        in_specs=[HBM] * 2,
+        out_specs=VMEM,
+        scratch_shapes=[pltpu.SemaphoreType.DMA((2,))],
+        compiler_params=params(8),
+        name="gather",
+    )(*in_hbm(x, dy))
+
+
+def fetch_body(
+    message, x, dy, w_qkv, w_proj, gain,
+    rest, strip, corner, w_qkv_out, w_proj_out, gain_out, sems,
+):
+    copies = [
+        pltpu.make_async_copy(
+            source.at[pl.ds(SHIFT, SHIFT)], rest.at[pl.ds(n * SHIFT, SHIFT)], sems.at[n]
+        )
+        for n, source in enumerate((x, dy))
     ]
     pairs = ((w_qkv, w_qkv_out), (w_proj, w_proj_out), (gain, gain_out))
-    copies += [pltpu.make_async_copy(a, b, sems.at[4 + n]) for n, (a, b) in enumerate(pairs)]
+    copies += [pltpu.make_async_copy(a, b, sems.at[2 + n]) for n, (a, b) in enumerate(pairs)]
     for copy in copies:
         copy.start()
-    for copy in copies[:4]:
+    for i in range(2 * SHIFT):
+        corner[i] = jnp.transpose(message[i])[:SHIFT]
+    for copy in copies[:2]:
         copy.wait()
     for i in range(2 * SHIFT):
         strip[i] = jnp.transpose(rest[i])[:SHIFT]
-        corner[i] = jnp.transpose(message[i])[:SHIFT]
-    for copy in copies[4:]:
+    for copy in copies[2:]:
         copy.wait()
 
 
-def gather(x, dy, w_qkv, w_proj, gain):
+def fetch(message, x, dy, w_qkv, w_proj, gain):
     rows, channels, cols = x.shape
-    operands = [pltpu.with_memory_space_constraint(v, pltpu.HBM) for v in (x, dy, w_qkv, w_proj, gain)]
-    return pl.pallas_call(
-        gather_body,
+    return pl.pallas_call(
+        fetch_body,
         out_shape=(
-            shape(BF16, 2 * SHIFT, channels, cols),
             shape(BF16, 2 * SHIFT, channels, cols),
             shape(BF16, 2 * SHIFT, SHIFT, channels),
             shape(BF16, 2 * SHIFT, SHIFT, channels),
@@ -80,12 +107,12 @@
             shape(BF16, *w_proj.shape),
             shape(F32, *gain.shape),
         ),
-        in_specs=[HBM] * 5,
-        out_specs=(VMEM,) * 7,
-        scratch_shapes=[pltpu.SemaphoreType.DMA((7,))],
+        in_specs=[VMEM] + [HBM] * 5,
+        out_specs=(VMEM,) * 6,
+        scratch_shapes=[pltpu.SemaphoreType.DMA((5,))],
         compiler_params=params(8),
-        name="gather",
-    )(*operands)
+        name="fetch",
+    )(message, *in_hbm(x, dy, w_qkv, w_proj, gain))
 
 
 def prep_body(rest, w_qkv, xs, dys, w_qkv_t):
@@ -123,13 +150,11 @@
 
 def write_masks(mask):
     k_pos = lax.broadcasted_iota(jnp.int32, (PAIR // 2, PAIR), 0)
-    lane = lax.broadcasted_iota(jnp.int32, (PAIR // 2, PAIR), 1)
-    q_pos = lane % (PAIR // 2)
-    second = lane >= PAIR // 2
+    q_pos = lax.broadcasted_iota(jnp.int32, (PAIR // 2, PAIR), 1) % (PAIR // 2)
     row_cut = (k_pos // WINDOW >= SHIFT) != (q_pos // WINDOW >= SHIFT)
     col_cut = (k_pos % WINDOW >= SHIFT) != (q_pos % WINDOW >= SHIFT)
     row_mask = jnp.where(row_cut, 1.0, 0.0) * is_last("row")
-    col_mask = jnp.where(col_cut & second, 1.0, 0.0) * is_last("col")
+    col_mask = jnp.where(col_cut, 1.0, 0.0) * is_last("col")
     mask[0] = row_mask * MASKED
     mask[1] = jnp.maximum(row_mask, col_mask) * MASKED
 
@@ -156,12 +181,22 @@
         upstream[to, :] = dys[:, at, :].reshape(PAIR // 2, channels).astype(BF16)
 
     n_all = normed[...]
-    q_t[...] = dot_nt(w_qkv_t[0:channels], n_all).astype(BF16)
+    for dest, left, right in (
+        (q_t, w_qkv_t[0:channels], n_all),
+        (do_t, w_proj[...], upstream[...]),
+    ):
+        full = dot_nt(left, right)
+        for h in range(HEADS):
+            me = slice(h * HEAD_DIM, (h + 1) * HEAD_DIM)
+            for p in range(pairs):
+                at = slice(p * PAIR, (p + 1) * PAIR)
+                piece = full[me, at]
+                piece = pltpu.roll(piece, PAIR // 2, 1) if h % 2 else piece
+                dest[me, at] = piece.astype(BF16)
     k_t[...] = dot_nt(w_qkv_t[channels : 2 * channels], n_all).astype(BF16)
     v_t[...] = dot_nt(w_qkv_t[2 * channels :], n_all).astype(BF16)
     k_n[...] = dot_nn(n_all, w_qkv[:, channels : 2 * channels]).astype(BF16)
     v_n[...] = dot_nn(n_all, w_qkv[:, 2 * channels :]).astype(BF16)
-    do_t[...] = dot_nt(w_proj[...], upstream[...]).astype(BF16)
     q_n[:, :channels] = dot_nn(n_all, w_qkv[:, :channels]).astype(BF16)
     do_n[:, :channels] = dot_nt(upstream[...], w_proj[...]).astype(BF16)
     for padded in (q_n, do_n):
@@ -169,98 +204,94 @@
     n_t[...] = jnp.transpose(n_all)
 
     half_n = PAIR // 2
-    first_lanes = lax.broadcasted_iota(jnp.int32, (half_n, PAIR), 1) < half_n
-
-    def fold(full):
-        return jnp.where(first_lanes, full[:half_n], full[half_n:])
-
-    def spread(v):
+    blocks = [range(lo // HEAD_DIM, min(lo + 128, channels) // HEAD_DIM) for lo in range(0, channels, 128)]
+
+    def left_lanes(rows):
+        return lax.broadcasted_iota(jnp.int32, (rows, PAIR), 1) < half_n
+
+    head_lane = lax.broadcasted_iota(jnp.int32, (half_n, 128), 1) // HEAD_DIM
+    no_row = jnp.zeros((HEAD_DIM, PAIR), BF16)
+
+    def by_query(tall, turned, at):
+        v = turned[:, at]
         zero = jnp.zeros_like(v)
-        return jnp.concatenate(
-            (jnp.where(first_lanes, v, zero), jnp.where(first_lanes, zero, v)), axis=0
-        )
-
-    head_lane = lax.broadcasted_iota(jnp.int32, (half_n, 128), 1) // HEAD_DIM
-
-    def by_key(dense, other, at, dest):
-        for lo in range(0, channels, 128):
-            here = range(lo // HEAD_DIM, min(lo + 128, channels) // HEAD_DIM)
-            tall = jnp.concatenate([dense[h] for h in here], axis=0)
-            v = other[at, lo : lo + 128]
-            zero = jnp.zeros((half_n, 128), BF16)
-            wide = jnp.concatenate(
-                (
-                    jnp.concatenate((v[:half_n], zero), axis=1),
-                    jnp.concatenate((zero, v[half_n:]), axis=1),
-                ),
-                axis=0,
-            )
-            full = dot_nn(tall, wide)
-            for w in range(2):
-                found = full[:half_n, w * 128 : (w + 1) * 128]
-                for n in range(1, len(here)):
-                    piece = full[n * half_n : (n + 1) * half_n, w * 128 : (w + 1) * 128]
-                    found = jnp.where(head_lane >= n, piece, found)
-                width = len(here) * HEAD_DIM
-                dest[at.start + w * half_n : at.start + (w + 1) * half_n, lo : lo + width] = found[
-                    :, :width
-                ].astype(BF16)
+        left = jnp.where(left_lanes(channels), v, zero)
+        right = jnp.where(left_lanes(channels), zero, v)
+        found = []
+        for w in range(2):
+            rows = slice(at.start + w * half_n, at.start + (w + 1) * half_n)
+            units = []
+            for heads in blocks:
+                wide = []
+                for j in range(len(heads) // 2):
+                    column = []
+                    for h in heads:
+                        me = slice(h * HEAD_DIM, (h + 1) * HEAD_DIM)
+                        source = left if h % 2 == w else right
+                        column.append(source[me] if (h - heads[0]) // 2 == j else no_row)
+                    wide.append(jnp.concatenate(column, axis=0))
+                lanes = slice(heads[0] * HEAD_DIM, (heads[-1] + 1) * HEAD_DIM)
+                full = dot_nn(tall[rows, lanes], jnp.concatenate(wide, axis=1))
+                units += [full[:, j * PAIR : (j + 1) * PAIR] for j in range(len(heads) // 2)]
+            found.append(units)
+        return found
+
+    def by_key(units, other, at, dest):
+        for w in range(2):
+            rows = slice(at.start + w * half_n, at.start + (w + 1) * half_n)
+            for n, heads in enumerate(blocks):
+                v = other[rows, n * 128 : (n + 1) * 128]
+                zero = jnp.zeros_like(v)
+                tall = []
+                for j in range(len(heads) // 2):
+                    for o in (w, 1 - w):
+                        tall.append(jnp.where(head_lane == 2 * j + o, v, zero))
+                first_unit = heads[0] // 2
+                wide = jnp.concatenate(units[w][first_unit : first_unit + len(heads) // 2], axis=1)
+                full = dot_nn(wide, jnp.concatenate(tall, axis=0))
+                width = len(heads) * HEAD_DIM
+                dest[rows, n * 128 : n * 128 + width] = full[:, :width].astype(BF16)
+
+    def by_channel(units, left, right, at, dest):
+        for j in range(HEADS // 2):
+            me = slice(2 * j * HEAD_DIM, 2 * (j + 1) * HEAD_DIM)
+            tall = jnp.concatenate((left[me], right[me]), axis=0)
+            full = dot_nn(tall, jnp.concatenate((units[0][j], units[1][j]), axis=0))
+            a, b, c, d = (full[n * HEAD_DIM : (n + 1) * HEAD_DIM] for n in range(4))
+            even = jnp.where(left_lanes(HEAD_DIM), a, c)
+            odd = pltpu.roll(jnp.where(left_lanes(HEAD_DIM), d, b), half_n, 1)
+            dest[me, at] = jnp.concatenate((even, odd), axis=0).astype(BF16)
 
     def front(p):
         at = slice(p * PAIR, (p + 1) * PAIR)
-        masking = mask[1 if last and p == pairs - 1 else 0]
-        q, do = q_t[:, at], do_t[:, at]
-        heads = [slice(h * HEAD_DIM, (h + 1) * HEAD_DIM) for h in range(HEADS)]
-
-        def place(v, h, lo, hi):
-            before, after = h * HEAD_DIM - lo, hi - (h + 1) * HEAD_DIM
-            parts = [v[heads[h]]]
-            if before:
-                parts = [jnp.zeros((before, PAIR), BF16)] + parts
-            if after:
-                parts = parts + [jnp.zeros((after, PAIR), BF16)]
-            return jnp.concatenate(parts, axis=0) if len(parts) > 1 else parts[0]
-
-        def by_head(tall, v):
-            found = []
-            for lo in range(0, channels, 128):
-                hi = min(lo + 128, channels)
-                here = range(lo // HEAD_DIM, hi // HEAD_DIM)
-                wide = jnp.concatenate([place(v, h, lo, hi) for h in here], axis=1)
-                full = dot_nn(tall[at, lo:hi], wide)
-                found += [fold(full[:, n * PAIR : (n + 1) * PAIR]) for n in range(len(here))]
-            return found
-
-        scores = by_head(k_n, q)
-        grad_probs = by_head(v_n, do)
-        return at, masking, q, do, heads, scores, grad_probs
-
-    def middle(state):
-        at, masking, q, do, heads, scores, grad_probs = state
-        p_bd, s_bd = [], []
-        for h in range(HEADS):
-            s = scores[h] * SCALE + masking
-            grown = jnp.exp(s - jnp.max(s, axis=0, keepdims=True))
-            probs = grown * (1.0 / jnp.sum(grown, axis=0, keepdims=True))
-            inner = jnp.sum(grad_probs[h] * probs, axis=0, keepdims=True)
-            grad_scores = probs * (grad_probs[h] - inner) * SCALE
-            p_bd.append(probs.astype(BF16))
-            s_bd.append(grad_scores.astype(BF16))
-        return p_bd, s_bd
-
-    def rear(state, p_bd, s_bd):
-        at, masking, q, do, heads, scores, grad_probs = state
-        results = []
-        for h in range(HEADS):
-            results.append((
-                dot_nn(k_t[heads[h], at], spread(s_bd[h])),
-                dot_nn(v_t[heads[h], at], spread(p_bd[h])),
-            ))
-        by_key(s_bd, q_n, at, dk_n)
-        by_key(p_bd, do_n, at, dv_n)
-        for h in range(HEADS):
-            dq_t[heads[h], at] = results[h][0].astype(BF16)
-            att_t[heads[h], at] = results[h][1].astype(BF16)
+        return at, by_query(k_n, q_t, at), by_query(v_n, do_t, at)
+
+    def middle(p, at, scores, grad_probs):
+        p_all, s_all = [], []
+        for w in range(2):
+            masking = mask[1 if last and p == pairs - 1 and w == 1 else 0]
+            p_units, s_units = [], []
+            for j in range(HEADS // 2):
+                s = scores[w][j] * SCALE + masking
+                grown = jnp.exp(s - jnp.max(s, axis=0, keepdims=True))
+                probs = grown * (1.0 / jnp.sum(grown, axis=0, keepdims=True))
+                inner = jnp.sum(grad_probs[w][j] * probs, axis=0, keepdims=True)
+                grad_scores = probs * (grad_probs[w][j] - inner) * SCALE
+                p_units.append(probs.astype(BF16))
+                s_units.append(grad_scores.astype(BF16))
+            p_all.append(p_units)
+            s_all.append(s_units)
+        return at, p_all, s_all
+
+    def rear(at, p_all, s_all):
+        for units, turned, dest in ((s_all, k_t, dq_t), (p_all, v_t, att_t)):
+            v = turned[:, at]
+            zero = jnp.zeros_like(v)
+            left = jnp.where(left_lanes(channels), v, zero)
+            right = jnp.where(left_lanes(channels), zero, v)
+            by_channel(units, left, right, at, dest)
+        by_key(s_all, q_n, at, dk_n)
+        by_key(p_all, do_n, at, dv_n)
 
     state = front(0)
     done = None
@@ -268,7 +299,7 @@
         later = front(p + 1) if p + 1 < pairs else None
         if done is not None:
             rear(*done)
-        done = (state, *middle(state))
+        done = middle(p, *state)
         state = later
     rear(*done)
 
@@ -596,10 +627,10 @@
 
 
 def bit_orders(row_extent, col_extent):
-    bits = [b * col_extent for b in (2**n for n in range(1, 16)) if b < row_extent]
-    bits += [b for b in (2**n for n in range(16)) if b < col_extent]
-    turn = len(bits) - len(bits) // 2
-    return bits, bits[turn:] + bits[:turn]
+    rows = [b * col_extent for b in (2**n for n in range(1, 16)) if b < row_extent]
+    cols = [b for b in (2**n for n in range(16)) if b < col_extent]
+    near, far = cols[:-1], cols[-1:]
+    return near + rows + far, rows + far + near
 
 
 def on_device(activations, cotangent, norm_gain, w_qkv, w_proj):
@@ -615,10 +646,11 @@
     turn = lambda route: [(b, a) for a, b in route]
     swap = lambda v: jnp.transpose(v, (0, 2, 1))
     x_t, dy_t = swap(activations), swap(cotangent)
-    message, rest, strip, corner, w_qkv, w_proj, gain = gather(
-        x_t, dy_t, w_qkv, w_proj, norm_gain.reshape(1, channels)
-    )
+    message = gather(x_t, dy_t)
     row_halo = lax.ppermute(message, "row", up)
+    rest, strip, corner, w_qkv, w_proj, gain = fetch(
+        message, x_t, dy_t, w_qkv, w_proj, norm_gain.reshape(1, channels)
+    )
     strip = lax.ppermute(strip, "col", left)
     corner = lax.ppermute(corner, ("row", "col"), both)
     x_low, dy_low, w_qkv_t = prep(rest, w_qkv)

time: 37.5 us -> 36.3 us (0.968)
  starting transfers between devices: 16.6 us -> 13.6 us
  waiting for transfers between devices: 8.29 us -> 10.1 us
  Pallas kernels: 11.2 us -> 11.7 us
    ppermute x3, waiting for transfers between devices: 3.11 us -> 6.42 us  [on_device(): arrived = lax.ppermute(total, ('row', 'col'), route)]
    ppermute x1, starting transfers between devices: 1.44 us -> 0.06 us  [on_device(): rows_back = lax.ppermute(high, 'row', turn(up))]
    ppermute x1, starting transfers between devices: 1.62 us -> 0.38 us  [on_device(): strip = lax.ppermute(strip, 'col', turn(left))]
    ppermute x1, waiting for transfers between devices: 1.12 us -> 0.01 us  [on_device(): row_halo = lax.ppermute(message, 'row', up)]
    pallas_call x1 -> x2, Pallas kernels: 1.54 us -> 2.29 us  [the longest x1 1.25 us: fetch(): pl.pallas_call(fetch_body, out_shape=(shape(BF16, 2 * SHIFT, channels, co...]
    ppermute x1, waiting for transfers between devices: 1.01 us -> 0.48 us  [on_device(): strip = lax.ppermute(strip, 'col', turn(left))]
    ppermute x1, starting transfers between devices: 0.92 us -> 0.45 us  [on_device(): total = keep + lax.ppermute(send, 'row', flip(row_extent, 1))]
  transfers between devices with their start and end apart: 10 -> 10, of which waited for: 8 -> 8; matrix products, arithmetic and copies ran while one was open for 0% -> 0% of each run, Pallas kernels for 16% -> 19%
where the time goes in v5:
time: 36.3 us; the launch traced here: 36.1 us
  starting transfers between devices  13.6 us (37%)
  Pallas kernels  11.7 us (32%)
  waiting for transfers between devices  10.1 us (28%)
  between operations  0.72 us (2%)
    ppermute x3, waiting for transfers between devices, on_device(): arrived = lax.ppermute(total, ('row', 'col'), route)  6.42 us
    ppermute x3, starting transfers between devices, on_device(): arrived = lax.ppermute(total, ('row', 'col'), route)  6.18 us
    ppermute x1, starting transfers between devices, on_device(): strip = lax.ppermute(strip, 'col', left)  3.66 us
    pallas_call x1, Pallas kernels, second(): pl.pallas_call(second_body, out_shape=(half, half, shape(F32, *xs.shape),...  2.88 us
    ppermute x1, starting transfers between devices, on_device(): row_halo = lax.ppermute(message, 'row', up)  2.43 us
    pallas_call x1, Pallas kernels, first(): pl.pallas_call(first_body, out_shape=(block, block, block) + attention_ou...  2.32 us
    ppermute x1, waiting for transfers between devices, on_device(): rows_back = lax.ppermute(high, 'row', turn(up))  1.42 us
    pallas_call x1, Pallas kernels, back(): pl.pallas_call(back_body, out_shape=(shape(BF16, rows // 2, channels, col...  1.26 us
  transfers between devices with their start and end apart: 10, of which 8 were waited for; matrix products, arithmetic and copies ran while one was open for 0% of the time, Pallas kernels for 19%

profile of v5, /device:TPU:0, one launch (start us, length us, event | category | flops | bytes accessed | tf_op | source)
XLA Modules:
  0.0 36.1 jit_solution(9085468009801062402)
XLA Ops:
  0.6 1.0 %gather.1.message = bf16[8,192,128]{2,1,0:T(8,128)(2,1)S(1)} custom-call(bf16[8,192,128]{2,1,0:T(8,128)(2,1)} %bitcast.5, bf16[8,192,128]{2,1,0:T(8,128)(2,1)} %bitcast.7), custom_call_target="tpu_custom_call" | custom-call | tf_op jit(solution)/shard_map/gather/pallas_call | solution.py:63
  1.7 2.4 %collective-permute-start = (bf16[8,192,128]{2,1,0:T(8,128)(2,1)S(1)}, bf16[8,192,128]{2,1,0:T(8,128)(2,1)S(1)}, u32[]{:S(2)}, u32[]{:S(2)}) collective-permute-start(bf16[8,192,128]{2,1,0:T(8,128)(2,1)S(1)} %gather.1.message), channel_id=1, source_target_pairs={{0,12},{4,0},{8,4},{12,8},{1,13},{5,1},{9,5},{13,9},{2,14},{6,2},{... | collective-permute-start | bytes 1179656 | tf_op jit(solution)/shard_map/ppermute | solution.py:650
  4.1 1.3 %fetch.1 = (bf16[8,192,128]{2,1,0:T(8,128)(2,1)S(1)}, bf16[8,4,192]{2,1,0:T(4,128)(2,1)S(1)}, bf16[8,4,192]{2,1,0:T(4,128)(2,1)S(1)}, bf16[192,576]{1,0:T(8,128)...) custom-call(bf16[8,192,128]{2,1,0:T(8,128)(2,1)S(1)} %gather.1.message, bf16[8,192,128]{2,1,0:T(8,128)(2,1)} %bitcast.6, ...), custom_call_target="tpu_custom_call" | custom-call | tf_op jit(solution)/shard_map/fetch/pallas_call | solution.py:100
  5.4 3.7 %collective-permute-start.1 = (bf16[8,4,192]{2,1,0:T(4,128)(2,1)S(1)}, bf16[8,4,192]{2,1,0:T(4,128)(2,1)S(1)}, u32[]{:S(2)}, u32[]{:S(2)}) collective-permute-start(bf16[8,4,192]{2,1,0:T(4,128)(2,1)S(1)} %get-tuple-element.57), channel_id=1, source_target_pairs={{0,3},{1,0},{2,1},{3,2},{4,7},{5,4},{6,5},{7,6},{8,11},{9,8},{10,9... | collective-permute-start | bytes 36872 | tf_op jit(solution)/shard_map/ppermute | solution.py:654
  9.0 0.3 collective-permute-start.2
  9.3 0.3 prep.1
  9.6 0.0 collective-permute-done.row_halo
  9.6 2.3 %first.1 = (f32[8,64,192]{2,1,0:T(8,128)S(1)}, f32[8,64,192]{2,1,0:T(8,128)S(1)}, f32[8,64,192]{2,1,0:T(8,128)S(1)}, bf16[192,512]{1,0:T(8,128)(2,1)S(1)}, bf16[...) custom-call(f32[4,128,192]{2,1,0:T(8,128)S(1)} %get-tuple-element.44, ...), custom_call_target="tpu_custom_call" | custom-call | tf_op jit(solution)/shard_map/first/pallas_call | solution.py:351
  11.9 0.0 collective-permute-done.1.strip
  11.9 0.2 collective-permute-done.2.corner
  12.2 2.9 %second.1 = (bf16[592,128]{1,0:T(8,128)(2,1)S(1)}, bf16[592,128]{1,0:T(8,128)(2,1)S(1)}, f32[8,64,192]{2,1,0:T(8,128)S(1)}, bf16[192,512]{1,0:T(8,128)(2,1)S(1)}...) custom-call(f32[8,64,192]{2,1,0:T(8,128)S(1)} %get-tuple-element.55., ...), custom_call_target="tpu_custom_call" | custom-call | tf_op jit(solution)/shard_map/second/pallas_call | solution.py:414
  15.1 0.4 %collective-permute-start.5 = (bf16[592,128]{1,0:T(8,128)(2,1)S(1)}, bf16[592,128]{1,0:T(8,128)(2,1)S(1)}, u32[]{:S(2)}, u32[]{:S(2)}) collective-permute-start(bf16[592,128]{1,0:T(8,128)(2,1)S(1)} %get-tuple-element.73), channel_id=1, source_target_pairs={{0,4},{4,0},{8,12},{12,8},{1,5},{5,1},{9,13},{13,9},{2,6},{6,2},{1... | collective-permute-start | bytes 454664 | tf_op jit(solution)/shard_map/ppermute | solution.py:667
  15.5 1.0 %collective-permute-done.5 = bf16[592,128]{1,0:T(8,128)(2,1)S(1)} collective-permute-done((bf16[592,128]{1,0:T(8,128)(2,1)S(1)}, bf16[592,128]{1,0:T(8,128)(2,1)S(1)}, u32[]{:S(2)}, u32[]{:S(2)}) %collective-permute-start.5) | collective-permute-done | bytes 151584 | tf_op jit(solution)/shard_map/ppermute | solution.py:667
  16.6 1.8 %collective-permute-start.6 = (bf16[592,128]{1,0:T(8,128)(2,1)S(1)}, bf16[592,128]{1,0:T(8,128)(2,1)S(1)}, u32[]{:S(2)}, u32[]{:S(2)}) collective-permute-start(bf16[592,128]{1,0:T(8,128)(2,1)S(1)} %add.6.a), channel_id=1, source_target_pairs={{0,1},{1,0},{2,3},{3,2},{4,12},{5,13},{6,14},{7,15},{8,9},{9,8},{1... | collective-permute-start | bytes 454664 | tf_op jit(solution)/shard_map/ppermute | solution.py:673
  18.4 1.3 %back.1 = (bf16[4,192,128]{2,1,0:T(8,128)(2,1)S(1)}, bf16[4,192,128]{2,1,0:T(8,128)(2,1)S(1)}, bf16[4,4,192]{2,1,0:T(4,128)(2,1)S(1)}) custom-call(bf16[192,512]{1,0:T(8,128)(2,1)S(1)} %get-tuple-element.49.dq_t_a.refs_0_, bf16[512,192]{1,0:T(8,128)(2,1)S(1)} %get-tuple-element.50.dk_n_a.refs_1_, bf16[512,192]{1,0:T(8,128)(2,1)S(1)} %get-tuple-element.51.dv_n_a.refs_2_, ...), custom_call_target="tpu_custom_call" | custom-call | flops 226492416 | bytes 8388608 | tf_op jit(solution)/shard_map/back/pallas_call | solution.py:466
  19.7 0.1 collective-permute-start.3
  19.7 2.1 %collective-permute-done.6.b = bf16[592,128]{1,0:T(8,128)(2,1)S(1)} collective-permute-done((bf16[592,128]{1,0:T(8,128)(2,1)S(1)}, bf16[592,128]{1,0:T(8,128)(2,1)S(1)}, u32[]{:S(2)}, u32[]{:S(2)}) %collective-permute-start.6) | collective-permute-done | bytes 151584 | tf_op jit(solution)/shard_map/ppermute | solution.py:673
  21.9 1.5 %collective-permute-start.7 = (bf16[592,128]{1,0:T(8,128)(2,1)S(1)}, bf16[592,128]{1,0:T(8,128)(2,1)S(1)}, u32[]{:S(2)}, u32[]{:S(2)}) collective-permute-start(bf16[592,128]{1,0:T(8,128)(2,1)S(1)} %add.7.a), channel_id=1, source_target_pairs={{0,8},{1,9},{2,10},{3,11},{4,6},{5,7},{6,4},{7,5},{8,0},{9,1},{10,... | collective-permute-start | bytes 454664 | tf_op jit(solution)/shard_map/ppermute | solution.py:673
  23.4 1.4 %collective-permute-done.3.rows_back.high = bf16[4,192,128]{2,1,0:T(8,128)(2,1)S(1)} collective-permute-done((bf16[4,192,128]{2,1,0:T(8,128)(2,1)S(1)}, bf16[4,192,128]{2,1,0:T(8,128)(2,1)S(1)}, u32[]{:S(2)}, u32[]{:S(2)}) %collective-permute-start.3) | collective-permute-done | bytes 196640 | tf_op jit(solution)/shard_map/ppermute | solution.py:665
  24.8 0.1 collect.1.refs_0_
  24.9 0.4 %collective-permute-start.4 = (bf16[8,4,192]{2,1,0:T(4,128)(2,1)S(1)}, bf16[8,4,192]{2,1,0:T(4,128)(2,1)S(1)}, u32[]{:S(2)}, u32[]{:S(2)}) collective-permute-start(bf16[8,4,192]{2,1,0:T(4,128)(2,1)S(1)} %collect.1.refs_0_), channel_id=1, source_target_pairs={{3,0},{0,1},{1,2},{2,3},{7,4},{4,5},{5,6},{6,7},{11,8},{8,9},{9,10... | collective-permute-start | bytes 36872 | tf_op jit(solution)/shard_map/ppermute | solution.py:679
  25.3 1.9 %collective-permute-done.7.b = bf16[592,128]{1,0:T(8,128)(2,1)S(1)} collective-permute-done((bf16[592,128]{1,0:T(8,128)(2,1)S(1)}, bf16[592,128]{1,0:T(8,128)(2,1)S(1)}, u32[]{:S(2)}, u32[]{:S(2)}) %collective-permute-start.7) | collective-permute-done | bytes 151584 | tf_op jit(solution)/shard_map/ppermute | solution.py:673
  27.2 2.8 %collective-permute-start.8 = (bf16[592,128]{1,0:T(8,128)(2,1)S(1)}, bf16[592,128]{1,0:T(8,128)(2,1)S(1)}, u32[]{:S(2)}, u32[]{:S(2)}) collective-permute-start(bf16[592,128]{1,0:T(8,128)(2,1)S(1)} %add.8.a), channel_id=1, source_target_pairs={{0,2},{1,3},{2,0},{3,1},{4,5},{5,4},{6,7},{7,6},{8,10},{9,11},{10,... | collective-permute-start | bytes 454664 | tf_op jit(solution)/shard_map/ppermute | solution.py:673
  30.0 0.5 %collective-permute-done.4.strip = bf16[8,4,192]{2,1,0:T(4,128)(2,1)S(1)} collective-permute-done((bf16[8,4,192]{2,1,0:T(4,128)(2,1)S(1)}, bf16[8,4,192]{2,1,0:T(4,128)(2,1)S(1)}, u32[]{:S(2)}, u32[]{:S(2)}) %collective-permute-start.4) | collective-permute-done | bytes 12320 | tf_op jit(solution)/shard_map/ppermute | solution.py:679
  30.5 0.9 %join.1 = (bf16[8,192,128]{2,1,0:T(8,128)(2,1)}, f32[8,128]{1,0:T(8,128)S(1)}) custom-call(bf16[4,192,128]{2,1,0:T(8,128)(2,1)S(1)} %collective-permute-done.3.rows_back.high, bf16[4,192,128]{2,1,0:T(8,128)(2,1)S(1)} %get-tuple-element.69.low.refs_0_, bf16[8,4,192]{2,1,0:T(4,128)(2,1)S(1)} %collective-permute-done.4.strip), custom_call_target="tpu_custom_call" | custom-call | flops 4000000000 | tf_op jit(solution)/shard_map/join/pallas_call | solution.py:537
  31.4 2.5 %collective-permute-done.8.b = bf16[592,128]{1,0:T(8,128)(2,1)S(1)} collective-permute-done((bf16[592,128]{1,0:T(8,128)(2,1)S(1)}, bf16[592,128]{1,0:T(8,128)(2,1)S(1)}, u32[]{:S(2)}, u32[]{:S(2)}) %collective-permute-start.8) | collective-permute-done | bytes 151584 | tf_op jit(solution)/shard_map/ppermute | solution.py:673
  33.9 0.2 collective-permute-start.9
  34.1 0.8 %scale_own.1 = (f32[192,576]{1,0:T(8,128)}, f32[192,192]{1,0:T(8,128)}) custom-call(bf16[592,128]{1,0:T(8,128)(2,1)S(1)} %add.9.mine), custom_call_target="tpu_custom_call" | custom-call | flops 1000000000 | tf_op jit(solution)/shard_map/scale_own/pallas_call | solution.py:596
  34.8 0.5 %collective-permute-done.9.other = bf16[592,128]{1,0:T(8,128)(2,1)S(1)} collective-permute-done((bf16[592,128]{1,0:T(8,128)(2,1)S(1)}, bf16[592,128]{1,0:T(8,128)(2,1)S(1)}, u32[]{:S(2)}, u32[]{:S(2)}) %collective-permute-start.9) | collective-permute-done | bytes 151584 | tf_op jit(solution)/shard_map/ppermute | solution.py:687
  35.3 0.8 %scale_other.1 = (f32[192,576]{1,0:T(8,128)}, f32[192,192]{1,0:T(8,128)}, f32[1,192]{1,0:T(1,128)}) custom-call(bf16[592,128]{1,0:T(8,128)(2,1)S(1)} %add.9.mine, bf16[592,128]{1,0:T(8,128)(2,1)S(1)} %collective-permute-done.9.other, f32[192,576]{1,0:T(8,128)} %get-tuple-element.75.wqkv_in, ...), custom_call_target="tpu_custom_call", output_to_operand_aliasing={{0}: (2, {}), {1}: (3, {})} | custom-call | tf_op jit(solution)/shard_map/scale_other/pallas_call | solution.py:609
  (4 shorter events, 0.1 us)
Async XLA Ops:
  1.7 7.9 %collective-permute-start = (bf16[8,192,128]{2,1,0:T(8,128)(2,1)S(1)}, bf16[8,192,128]{2,1,0:T(8,128)(2,1)S(1)}, u32[]{:S(2)}, u32[]{:S(2)}) collective-permute-start(bf16[8,192,128]{2,1,0:T(8,128)(2,1)S(1)} %gather.1.message), channel_id=1, source_target_pairs={{0,12},{4,0},{8,4},{12,8},{1,13},{5,1},{9,5},{13,9},{2,14},{6,2},{... | collective-permute-start | bytes 1179656 | tf_op jit(solution)/shard_map/ppermute | solution.py:650
  5.4 6.6 %collective-permute-start.1 = (bf16[8,4,192]{2,1,0:T(4,128)(2,1)S(1)}, bf16[8,4,192]{2,1,0:T(4,128)(2,1)S(1)}, u32[]{:S(2)}, u32[]{:S(2)}) collective-permute-start(bf16[8,4,192]{2,1,0:T(4,128)(2,1)S(1)} %get-tuple-element.57), channel_id=1, source_target_pairs={{0,3},{1,0},{2,1},{3,2},{4,7},{5,4},{6,5},{7,6},{8,11},{9,8},{10,9... | collective-permute-start | bytes 36872 | tf_op jit(solution)/shard_map/ppermute | solution.py:654
  9.0 3.2 %collective-permute-start.2 = (bf16[8,4,192]{2,1,0:T(4,128)(2,1)S(1)}, bf16[8,4,192]{2,1,0:T(4,128)(2,1)S(1)}, u32[]{:S(2)}, u32[]{:S(2)}) collective-permute-start(bf16[8,4,192]{2,1,0:T(4,128)(2,1)S(1)} %get-tuple-element.58), channel_id=1, source_target_pairs={{0,15},{1,12},{2,13},{3,14},{4,3},{5,0},{6,1},{7,2},{8,7},{9,4},{1... | collective-permute-start | bytes 36872 | tf_op jit(solution)/shard_map/ppermute | solution.py:655
  15.1 1.5 %collective-permute-start.5 = (bf16[592,128]{1,0:T(8,128)(2,1)S(1)}, bf16[592,128]{1,0:T(8,128)(2,1)S(1)}, u32[]{:S(2)}, u32[]{:S(2)}) collective-permute-start(bf16[592,128]{1,0:T(8,128)(2,1)S(1)} %get-tuple-element.73), channel_id=1, source_target_pairs={{0,4},{4,0},{8,12},{12,8},{1,5},{5,1},{9,13},{13,9},{2,6},{6,2},{1... | collective-permute-start | bytes 454664 | tf_op jit(solution)/shard_map/ppermute | solution.py:667
  16.6 5.3 %collective-permute-start.6 = (bf16[592,128]{1,0:T(8,128)(2,1)S(1)}, bf16[592,128]{1,0:T(8,128)(2,1)S(1)}, u32[]{:S(2)}, u32[]{:S(2)}) collective-permute-start(bf16[592,128]{1,0:T(8,128)(2,1)S(1)} %add.6.a), channel_id=1, source_target_pairs={{0,1},{1,0},{2,3},{3,2},{4,12},{5,13},{6,14},{7,15},{8,9},{9,8},{1... | collective-permute-start | bytes 454664 | tf_op jit(solution)/shard_map/ppermute | solution.py:673
  19.7 5.1 %collective-permute-start.3 = (bf16[4,192,128]{2,1,0:T(8,128)(2,1)S(1)}, bf16[4,192,128]{2,1,0:T(8,128)(2,1)S(1)}, u32[]{:S(2)}, u32[]{:S(2)}) collective-permute-start(bf16[4,192,128]{2,1,0:T(8,128)(2,1)S(1)} %get-tuple-element.68), channel_id=1, source_target_pairs={{12,0},{0,4},{4,8},{8,12},{13,1},{1,5},{5,9},{9,13},{14,2},{2,6},{... | collective-permute-start | bytes 589832 | tf_op jit(solution)/shard_map/ppermute | solution.py:665
  21.9 5.3 %collective-permute-start.7 = (bf16[592,128]{1,0:T(8,128)(2,1)S(1)}, bf16[592,128]{1,0:T(8,128)(2,1)S(1)}, u32[]{:S(2)}, u32[]{:S(2)}) collective-permute-start(bf16[592,128]{1,0:T(8,128)(2,1)S(1)} %add.7.a), channel_id=1, source_target_pairs={{0,8},{1,9},{2,10},{3,11},{4,6},{5,7},{6,4},{7,5},{8,0},{9,1},{10,... | collective-permute-start | bytes 454664 | tf_op jit(solution)/shard_map/ppermute | solution.py:673
  24.9 5.6 %collective-permute-start.4 = (bf16[8,4,192]{2,1,0:T(4,128)(2,1)S(1)}, bf16[8,4,192]{2,1,0:T(4,128)(2,1)S(1)}, u32[]{:S(2)}, u32[]{:S(2)}) collective-permute-start(bf16[8,4,192]{2,1,0:T(4,128)(2,1)S(1)} %collect.1.refs_0_), channel_id=1, source_target_pairs={{3,0},{0,1},{1,2},{2,3},{7,4},{4,5},{5,6},{6,7},{11,8},{8,9},{9,10... | collective-permute-start | bytes 36872 | tf_op jit(solution)/shard_map/ppermute | solution.py:679
  27.2 6.7 %collective-permute-start.8 = (bf16[592,128]{1,0:T(8,128)(2,1)S(1)}, bf16[592,128]{1,0:T(8,128)(2,1)S(1)}, u32[]{:S(2)}, u32[]{:S(2)}) collective-permute-start(bf16[592,128]{1,0:T(8,128)(2,1)S(1)} %add.8.a), channel_id=1, source_target_pairs={{0,2},{1,3},{2,0},{3,1},{4,5},{5,4},{6,7},{7,6},{8,10},{9,11},{10,... | collective-permute-start | bytes 454664 | tf_op jit(solution)/shard_map/ppermute | solution.py:673
  33.9 1.4 %collective-permute-start.9 = (bf16[592,128]{1,0:T(8,128)(2,1)S(1)}, bf16[592,128]{1,0:T(8,128)(2,1)S(1)}, u32[]{:S(2)}, u32[]{:S(2)}) collective-permute-start(bf16[592,128]{1,0:T(8,128)(2,1)S(1)} %add.9.mine), channel_id=1, source_target_pairs={{0,4},{4,0},{8,12},{12,8},{1,5},{5,1},{9,13},{13,9},{2,6},{6,2},{1... | collective-permute-start | bytes 454664 | tf_op jit(solution)/shard_map/ppermute | solution.py:687

commit v6 on v5

--- a/solution.py
+++ b/solution.py
@@ -45,74 +45,50 @@
     return [pltpu.with_memory_space_constraint(v, pltpu.HBM) for v in arrays]
 
 
-def gather_body(x, dy, out, sems):
+def gather_body(x, dy, gain, out, gain_out, sems):
     copies = [
         pltpu.make_async_copy(
             source.at[pl.ds(0, SHIFT)], out.at[pl.ds(n * SHIFT, SHIFT)], sems.at[n]
         )
         for n, source in enumerate((x, dy))
     ]
+    copies.append(pltpu.make_async_copy(gain, gain_out, sems.at[2]))
     for copy in copies:
         copy.start()
     for copy in copies:
         copy.wait()
 
 
-def gather(x, dy):
+def gather(x, dy, gain):
     _, channels, cols = x.shape
     return pl.pallas_call(
         gather_body,
-        out_shape=shape(BF16, 2 * SHIFT, channels, cols),
-        in_specs=[HBM] * 2,
-        out_specs=VMEM,
-        scratch_shapes=[pltpu.SemaphoreType.DMA((2,))],
+        out_shape=(shape(BF16, 2 * SHIFT, channels, cols), shape(F32, *gain.shape)),
+        in_specs=[HBM] * 3,
+        out_specs=(VMEM, VMEM),
+        scratch_shapes=[pltpu.SemaphoreType.DMA((3,))],
         compiler_params=params(8),
         name="gather",
-    )(*in_hbm(x, dy))
-
-
-def fetch_body(
-    message, x, dy, w_qkv, w_proj, gain,
-    rest, strip, corner, w_qkv_out, w_proj_out, gain_out, sems,
-):
-    copies = [
-        pltpu.make_async_copy(
-            source.at[pl.ds(SHIFT, SHIFT)], rest.at[pl.ds(n * SHIFT, SHIFT)], sems.at[n]
-        )
-        for n, source in enumerate((x, dy))
-    ]
-    pairs = ((w_qkv, w_qkv_out), (w_proj, w_proj_out), (gain, gain_out))
-    copies += [pltpu.make_async_copy(a, b, sems.at[2 + n]) for n, (a, b) in enumerate(pairs)]
-    for copy in copies:
-        copy.start()
+    )(*in_hbm(x, dy, gain))
+
+
+def strips_body(message, rest, strip, corner):
     for i in range(2 * SHIFT):
         corner[i] = jnp.transpose(message[i])[:SHIFT]
-    for copy in copies[:2]:
-        copy.wait()
-    for i in range(2 * SHIFT):
         strip[i] = jnp.transpose(rest[i])[:SHIFT]
-    for copy in copies[2:]:
-        copy.wait()
-
-
-def fetch(message, x, dy, w_qkv, w_proj, gain):
-    rows, channels, cols = x.shape
-    return pl.pallas_call(
-        fetch_body,
-        out_shape=(
-            shape(BF16, 2 * SHIFT, channels, cols),
-            shape(BF16, 2 * SHIFT, SHIFT, channels),
-            shape(BF16, 2 * SHIFT, SHIFT, channels),
-            shape(BF16, *w_qkv.shape),
-            shape(BF16, *w_proj.shape),
-            shape(F32, *gain.shape),
-        ),
-        in_specs=[VMEM] + [HBM] * 5,
-        out_specs=(VMEM,) * 6,
-        scratch_shapes=[pltpu.SemaphoreType.DMA((5,))],
+
+
+def strips(message, rest):
+    _, channels, cols = rest.shape
+    out = shape(BF16, 2 * SHIFT, SHIFT, channels)
+    return pl.pallas_call(
+        strips_body,
+        out_shape=(out, out),
+        in_specs=[VMEM] * 2,
+        out_specs=(VMEM,) * 2,
         compiler_params=params(8),
-        name="fetch",
-    )(message, *in_hbm(x, dy, w_qkv, w_proj, gain))
+        name="strips",
+    )(message, rest)
 
 
 def prep_body(rest, w_qkv, xs, dys, w_qkv_t):
@@ -181,11 +157,9 @@
         upstream[to, :] = dys[:, at, :].reshape(PAIR // 2, channels).astype(BF16)
 
     n_all = normed[...]
-    for dest, left, right in (
-        (q_t, w_qkv_t[0:channels], n_all),
-        (do_t, w_proj[...], upstream[...]),
-    ):
-        full = dot_nt(left, right)
+    n_t[...] = jnp.transpose(n_all)
+
+    def keep(dest, full):
         for h in range(HEADS):
             me = slice(h * HEAD_DIM, (h + 1) * HEAD_DIM)
             for p in range(pairs):
@@ -193,15 +167,20 @@
                 piece = full[me, at]
                 piece = pltpu.roll(piece, PAIR // 2, 1) if h % 2 else piece
                 dest[me, at] = piece.astype(BF16)
-    k_t[...] = dot_nt(w_qkv_t[channels : 2 * channels], n_all).astype(BF16)
-    v_t[...] = dot_nt(w_qkv_t[2 * channels :], n_all).astype(BF16)
+
+    turned = dot_nn(w_qkv_t[...], n_t[...])
+    k_t[...] = turned[channels : 2 * channels].astype(BF16)
+    v_t[...] = turned[2 * channels :].astype(BF16)
+    keep(q_t, turned[:channels])
+    up_t = jnp.transpose(upstream[...])
+    turned_do = dot_nn(w_proj[...], up_t)
+    keep(do_t, turned_do)
     k_n[...] = dot_nn(n_all, w_qkv[:, channels : 2 * channels]).astype(BF16)
     v_n[...] = dot_nn(n_all, w_qkv[:, 2 * channels :]).astype(BF16)
-    q_n[:, :channels] = dot_nn(n_all, w_qkv[:, :channels]).astype(BF16)
-    do_n[:, :channels] = dot_nt(upstream[...], w_proj[...]).astype(BF16)
+    q_n[:, :channels] = jnp.transpose(turned[:channels].astype(BF16))
+    do_n[:, :channels] = jnp.transpose(turned_do.astype(BF16))
     for padded in (q_n, do_n):
         padded[:, channels:] = jnp.zeros((tokens, padded.shape[1] - channels), BF16)
-    n_t[...] = jnp.transpose(n_all)
 
     half_n = PAIR // 2
     blocks = [range(lo // HEAD_DIM, min(lo + 128, channels) // HEAD_DIM) for lo in range(0, channels, 128)]
@@ -367,7 +346,7 @@
     n_t_a, upstream_a, dq_t_a, dk_n_a, dv_n_a, att_t_a, *refs,
 ):
     keep, send, dys, dq_t, dk_n, dv_n, x_hat, inv_std, *refs = refs
-    xs, mask, halves, n_t, upstream, att_t, *scratch = refs
+    xs, mask, partial, n_t, upstream, att_t, *scratch = refs
     rows, cols, channels = dys.shape
     for n, (source, dest) in enumerate(((xs_in, xs), (dys_in, dys))):
         for i in range(rows):
@@ -377,33 +356,52 @@
                 (source[i, cols - WINDOW : cols - SHIFT, :], tail.astype(F32)), axis=0
             )
     write_masks(mask)
+    for n, piece in enumerate(
+        (
+            dot_nt(n_t_a[...], dq_t_a[...]),
+            dot_nn(n_t_a[...], dk_n_a[...]),
+            dot_nn(n_t_a[...], dv_n_a[...]),
+            dot_nn(att_t_a[...], upstream_a[...]),
+        )
+    ):
+        partial[n] = piece
     attention(
         True, xs, dys, gain, w_qkv, w_qkv_t, w_proj, mask,
         n_t, upstream, dq_t, dk_n, dv_n, att_t, x_hat, inv_std, *scratch,
     )
     wide = jnp.concatenate(
         (
-            dot_nt(n_t_a[...], dq_t_a[...]) + dot_nt(n_t[...], dq_t[...]),
-            dot_nn(n_t_a[...], dk_n_a[...]) + dot_nn(n_t[...], dk_n[...]),
-            dot_nn(n_t_a[...], dv_n_a[...]) + dot_nn(n_t[...], dv_n[...]),
+            partial[0] + dot_nt(n_t[...], dq_t[...]),
+            partial[1] + dot_nn(n_t[...], dk_n[...]),
+            partial[2] + dot_nn(n_t[...], dv_n[...]),
         ),
         axis=1,
     )
-    gain_sum = jnp.sum(wide * w_qkv[...].astype(F32), axis=1, keepdims=True)
-    gain_sum = jnp.transpose(jnp.broadcast_to(gain_sum, (channels, 128)))[0:1] / gain[...]
-    proj = dot_nn(att_t_a[...], upstream_a[...]) + dot_nn(att_t[...], upstream[...])
+    terms = wide * w_qkv[...].astype(F32)
+    whole = terms.shape[1] // 128 * 128
+    folded = jnp.concatenate(
+        (terms[:, whole:], jnp.zeros((channels, 128 - terms.shape[1] + whole), F32)), axis=1
+    )
+    for lane in range(0, whole, 128):
+        folded = folded + terms[:, lane : lane + 128]
+    gain_sum = jnp.sum(jnp.transpose(folded), axis=0, keepdims=True) / gain[...]
+    proj = partial[3] + dot_nn(att_t[...], upstream[...])
     both = jnp.concatenate((wide, proj), axis=1)
     gain_block = jnp.broadcast_to(
         jnp.concatenate((gain_sum, jnp.zeros((1, 256 - channels), F32)), axis=1), (16, 256)
     )
     part = channels // 2
-    for n in range(2):
-        for j in range(6):
-            piece = both[n * part : (n + 1) * part, j * 128 : (j + 1) * 128]
-            halves[n, j * part : (j + 1) * part, :] = piece.astype(BF16)
-        halves[n, 6 * part :, :] = gain_block[:, n * 128 : (n + 1) * 128].astype(BF16)
-    keep[...] = halves[core()]
-    send[...] = halves[1 - core()]
+    even = core() == 0
+
+    def store(rows, one, two):
+        one, two = one.astype(BF16), two.astype(BF16)
+        keep[rows, :] = jnp.where(even, one, two)
+        send[rows, :] = jnp.where(even, two, one)
+
+    for j in range(6):
+        lanes = slice(j * 128, (j + 1) * 128)
+        store(slice(j * part, (j + 1) * part), both[:part, lanes], both[part:, lanes])
+    store(slice(6 * part, 6 * part + 16), gain_block[:, :128], gain_block[:, 128:])
 
 
 def second(xs, dys, strip, corner, gain, w_qkv, w_qkv_t, w_proj, *saved):
@@ -419,7 +417,7 @@
         scratch_shapes=[
             pltpu.VMEM(xs.shape, F32),
             pltpu.VMEM((2, PAIR // 2, PAIR), F32),
-            pltpu.VMEM((2, *half.shape), BF16),
+            pltpu.VMEM((4, channels, channels), F32),
             pltpu.VMEM(n_t.shape, BF16),
             pltpu.VMEM(upstream.shape, BF16),
             pltpu.VMEM(att_t.shape, BF16),
@@ -646,11 +644,10 @@
     turn = lambda route: [(b, a) for a, b in route]
     swap = lambda v: jnp.transpose(v, (0, 2, 1))
     x_t, dy_t = swap(activations), swap(cotangent)
-    message = gather(x_t, dy_t)
+    message, gain = gather(x_t, dy_t, norm_gain.reshape(1, channels))
     row_halo = lax.ppermute(message, "row", up)
-    rest, strip, corner, w_qkv, w_proj, gain = fetch(
-        message, x_t, dy_t, w_qkv, w_proj, norm_gain.reshape(1, channels)
-    )
+    rest = jnp.concatenate((x_t[SHIFT:], dy_t[SHIFT:]), axis=0)
+    strip, corner = strips(message, rest)
     strip = lax.ppermute(strip, "col", left)
     corner = lax.ppermute(corner, ("row", "col"), both)
     x_low, dy_low, w_qkv_t = prep(rest, w_qkv)

time: 36.3 us -> 35.8 us (0.986)
  Pallas kernels: 11.7 us -> 10.2 us
  starting transfers between devices: 13.6 us -> 14.3 us
    pallas_call x2, Pallas kernels: 2.29 us -> 1.33 us  [the longest x1 1.1 us: gather(): pl.pallas_call(gather_body, out_shape=(shape(BF16, 2 * SHIFT, channels, c...]
    ppermute x1, waiting for transfers between devices: 0.01 us -> 0.49 us  [on_device(): row_halo = lax.ppermute(message, 'row', up)]
    ppermute x1, starting transfers between devices: 0.45 us -> 0.91 us  [on_device(): total = keep + lax.ppermute(send, 'row', flip(row_extent, 1))]
  transfers between devices with their start and end apart: 10 -> 10, of which waited for: 8 -> 8; matrix products, arithmetic and copies ran while one was open for 0% -> 0% of each run, Pallas kernels for 19% -> 16%
where the time goes in v6:
time: 35.8 us; the launch traced here: 35.7 us
  starting transfers between devices  14.3 us (40%)
  waiting for transfers between devices  10.3 us (29%)
  Pallas kernels  10.2 us (28%)
  between operations  0.78 us (2%)
    ppermute x3, waiting for transfers between devices, on_device(): arrived = lax.ppermute(total, ('row', 'col'), route)  6.43 us
    ppermute x3, starting transfers between devices, on_device(): arrived = lax.ppermute(total, ('row', 'col'), route)  6.17 us
    ppermute x1, starting transfers between devices, on_device(): strip = lax.ppermute(strip, 'col', left)  3.65 us
    pallas_call x1, Pallas kernels, second(): pl.pallas_call(second_body, out_shape=(half, half, shape(F32, *xs.shape),...  2.55 us
    ppermute x1, starting transfers between devices, on_device(): row_halo = lax.ppermute(message, 'row', up)  2.43 us
    pallas_call x1, Pallas kernels, first(): pl.pallas_call(first_body, out_shape=(block, block, block) + attention_ou...  2.14 us
    ppermute x1, waiting for transfers between devices, on_device(): rows_back = lax.ppermute(high, 'row', turn(up))  1.42 us
    pallas_call x1, Pallas kernels, back(): pl.pallas_call(back_body, out_shape=(shape(BF16, rows // 2, channels, col...  1.26 us
  transfers between devices with their start and end apart: 10, of which 8 were waited for; matrix products, arithmetic and copies ran while one was open for 0% of the time, Pallas kernels for 16%

profile of v6, /device:TPU:0, one launch (start us, length us, event | category | flops | bytes accessed | tf_op | source)
XLA Modules:
  0.0 35.7 jit_solution(1747520924823038940)
XLA Ops:
  0.6 0.0 copy-start.2
  0.6 1.1 %gather.1 = (bf16[8,192,128]{2,1,0:T(8,128)(2,1)S(1)}, f32[1,192]{1,0:T(1,128)S(1)}) custom-call(bf16[8,192,128]{2,1,0:T(8,128)(2,1)} %bitcast.5, bf16[8,192,128]{2,1,0:T(8,128)(2,1)} %bitcast.7, f32[1,192]{1,0:T(1,128)} %bitcast.9), custom_call_target="tpu_custom_call" | custom-call | tf_op jit(solution)/shard_map/gather/pallas_call | solution.py:64
  1.7 0.0 copy-start.3
  1.8 2.4 %collective-permute-start = (bf16[8,192,128]{2,1,0:T(8,128)(2,1)S(1)}, bf16[8,192,128]{2,1,0:T(8,128)(2,1)S(1)}, u32[]{:S(2)}, u32[]{:S(2)}) collective-permute-start(bf16[8,192,128]{2,1,0:T(8,128)(2,1)S(1)} %get-tuple-element.42.message), channel_id=1, source_target_pairs={{0,12},{4,0},{8,4},{12,8},{1,13},{5,1},{9,5},{13,9},{2,14},{6,2},{... | collective-permute-start | bytes 1179656 | tf_op jit(solution)/shard_map/ppermute | solution.py:648
  4.2 0.0 copy-done.2
  4.2 0.0 copy-done.3
  4.3 0.0 copy-start
  4.3 0.2 strips.1
  4.5 3.6 %collective-permute-start.1 = (bf16[8,4,192]{2,1,0:T(4,128)(2,1)S(1)}, bf16[8,4,192]{2,1,0:T(4,128)(2,1)S(1)}, u32[]{:S(2)}, u32[]{:S(2)}) collective-permute-start(bf16[8,4,192]{2,1,0:T(4,128)(2,1)S(1)} %get-tuple-element.53), channel_id=1, source_target_pairs={{0,3},{1,0},{2,1},{3,2},{4,7},{5,4},{6,5},{7,6},{8,11},{9,8},{10,9... | collective-permute-start | bytes 36872 | tf_op jit(solution)/shard_map/ppermute | solution.py:651
  8.2 0.0 copy-start.1
  8.2 0.5 %collective-permute-start.2 = (bf16[8,4,192]{2,1,0:T(4,128)(2,1)S(1)}, bf16[8,4,192]{2,1,0:T(4,128)(2,1)S(1)}, u32[]{:S(2)}, u32[]{:S(2)}) collective-permute-start(bf16[8,4,192]{2,1,0:T(4,128)(2,1)S(1)} %get-tuple-element.54), channel_id=1, source_target_pairs={{0,15},{1,12},{2,13},{3,14},{4,3},{5,0},{6,1},{7,2},{8,7},{9,4},{1... | collective-permute-start | bytes 36872 | tf_op jit(solution)/shard_map/ppermute | solution.py:652
  8.7 0.0 copy-done
  8.7 0.3 prep.1
  9.0 0.5 %collective-permute-done.row_halo = bf16[8,192,128]{2,1,0:T(8,128)(2,1)S(1)} collective-permute-done((bf16[8,192,128]{2,1,0:T(8,128)(2,1)S(1)}, bf16[8,192,128]{2,1,0:T(8,128)(2,1)S(1)}, u32[]{:S(2)}, u32[]{:S(2)}) %collective-permute-start) | collective-permute-done | bytes 393248 | tf_op jit(solution)/shard_map/ppermute | solution.py:648
  9.5 0.0 copy-done.1
  9.5 2.1 %first.1 = (f32[8,64,192]{2,1,0:T(8,128)S(1)}, f32[8,64,192]{2,1,0:T(8,128)S(1)}, f32[8,64,192]{2,1,0:T(8,128)S(1)}, bf16[192,512]{1,0:T(8,128)(2,1)S(1)}, bf16[...) custom-call(f32[4,128,192]{2,1,0:T(8,128)S(1)} %get-tuple-element.40, ...), custom_call_target="tpu_custom_call" | custom-call | tf_op jit(solution)/shard_map/first/pallas_call | solution.py:330
  11.6 0.0 collective-permute-done.1.strip
  11.6 0.0 collective-permute-done.2.corner
  11.7 2.6 %second.1 = (bf16[592,128]{1,0:T(8,128)(2,1)S(1)}, bf16[592,128]{1,0:T(8,128)(2,1)S(1)}, f32[8,64,192]{2,1,0:T(8,128)S(1)}, bf16[192,512]{1,0:T(8,128)(2,1)S(1)}...) custom-call(f32[8,64,192]{2,1,0:T(8,128)S(1)} %get-tuple-element.51., ...), custom_call_target="tpu_custom_call" | custom-call | tf_op jit(solution)/shard_map/second/pallas_call | solution.py:412
  14.2 0.9 %collective-permute-start.5 = (bf16[592,128]{1,0:T(8,128)(2,1)S(1)}, bf16[592,128]{1,0:T(8,128)(2,1)S(1)}, u32[]{:S(2)}, u32[]{:S(2)}) collective-permute-start(bf16[592,128]{1,0:T(8,128)(2,1)S(1)} %get-tuple-element.69), channel_id=1, source_target_pairs={{0,4},{4,0},{8,12},{12,8},{1,5},{5,1},{9,13},{13,9},{2,6},{6,2},{1... | collective-permute-start | bytes 454664 | tf_op jit(solution)/shard_map/ppermute | solution.py:664
  15.1 1.0 %collective-permute-done.5 = bf16[592,128]{1,0:T(8,128)(2,1)S(1)} collective-permute-done((bf16[592,128]{1,0:T(8,128)(2,1)S(1)}, bf16[592,128]{1,0:T(8,128)(2,1)S(1)}, u32[]{:S(2)}, u32[]{:S(2)}) %collective-permute-start.5) | collective-permute-done | bytes 151584 | tf_op jit(solution)/shard_map/ppermute | solution.py:664
  16.2 1.8 %collective-permute-start.6 = (bf16[592,128]{1,0:T(8,128)(2,1)S(1)}, bf16[592,128]{1,0:T(8,128)(2,1)S(1)}, u32[]{:S(2)}, u32[]{:S(2)}) collective-permute-start(bf16[592,128]{1,0:T(8,128)(2,1)S(1)} %add.6.a), channel_id=1, source_target_pairs={{0,1},{1,0},{2,3},{3,2},{4,12},{5,13},{6,14},{7,15},{8,9},{9,8},{1... | collective-permute-start | bytes 454664 | tf_op jit(solution)/shard_map/ppermute | solution.py:670
  18.0 1.3 %back.1 = (bf16[4,192,128]{2,1,0:T(8,128)(2,1)S(1)}, bf16[4,192,128]{2,1,0:T(8,128)(2,1)S(1)}, bf16[4,4,192]{2,1,0:T(4,128)(2,1)S(1)}) custom-call(bf16[192,512]{1,0:T(8,128)(2,1)S(1)} %get-tuple-element.45.dq_t_a.refs_0_, bf16[512,192]{1,0:T(8,128)(2,1)S(1)} %get-tuple-element.46.dk_n_a.refs_1_, bf16[512,192]{1,0:T(8,128)(2,1)S(1)} %get-tuple-element.47.dv_n_a.refs_2_, ...), custom_call_target="tpu_custom_call" | custom-call | flops 226492416 | bytes 8388608 | tf_op jit(solution)/shard_map/back/pallas_call | solution.py:464
  19.3 0.1 collective-permute-start.3
  19.3 2.1 %collective-permute-done.6.b = bf16[592,128]{1,0:T(8,128)(2,1)S(1)} collective-permute-done((bf16[592,128]{1,0:T(8,128)(2,1)S(1)}, bf16[592,128]{1,0:T(8,128)(2,1)S(1)}, u32[]{:S(2)}, u32[]{:S(2)}) %collective-permute-start.6) | collective-permute-done | bytes 151584 | tf_op jit(solution)/shard_map/ppermute | solution.py:670
  21.5 1.5 %collective-permute-start.7 = (bf16[592,128]{1,0:T(8,128)(2,1)S(1)}, bf16[592,128]{1,0:T(8,128)(2,1)S(1)}, u32[]{:S(2)}, u32[]{:S(2)}) collective-permute-start(bf16[592,128]{1,0:T(8,128)(2,1)S(1)} %add.7.a), channel_id=1, source_target_pairs={{0,8},{1,9},{2,10},{3,11},{4,6},{5,7},{6,4},{7,5},{8,0},{9,1},{10,... | collective-permute-start | bytes 454664 | tf_op jit(solution)/shard_map/ppermute | solution.py:670
  23.0 1.4 %collective-permute-done.3.rows_back.high = bf16[4,192,128]{2,1,0:T(8,128)(2,1)S(1)} collective-permute-done((bf16[4,192,128]{2,1,0:T(8,128)(2,1)S(1)}, bf16[4,192,128]{2,1,0:T(8,128)(2,1)S(1)}, u32[]{:S(2)}, u32[]{:S(2)}) %collective-permute-start.3) | collective-permute-done | bytes 196640 | tf_op jit(solution)/shard_map/ppermute | solution.py:662
  24.4 0.1 collect.1.refs_0_
  24.5 0.4 %collective-permute-start.4 = (bf16[8,4,192]{2,1,0:T(4,128)(2,1)S(1)}, bf16[8,4,192]{2,1,0:T(4,128)(2,1)S(1)}, u32[]{:S(2)}, u32[]{:S(2)}) collective-permute-start(bf16[8,4,192]{2,1,0:T(4,128)(2,1)S(1)} %collect.1.refs_0_), channel_id=1, source_target_pairs={{3,0},{0,1},{1,2},{2,3},{7,4},{4,5},{5,6},{6,7},{11,8},{8,9},{9,10... | collective-permute-start | bytes 36872 | tf_op jit(solution)/shard_map/ppermute | solution.py:676
  24.9 1.9 %collective-permute-done.7.b = bf16[592,128]{1,0:T(8,128)(2,1)S(1)} collective-permute-done((bf16[592,128]{1,0:T(8,128)(2,1)S(1)}, bf16[592,128]{1,0:T(8,128)(2,1)S(1)}, u32[]{:S(2)}, u32[]{:S(2)}) %collective-permute-start.7) | collective-permute-done | bytes 151584 | tf_op jit(solution)/shard_map/ppermute | solution.py:670
  26.8 2.8 %collective-permute-start.8 = (bf16[592,128]{1,0:T(8,128)(2,1)S(1)}, bf16[592,128]{1,0:T(8,128)(2,1)S(1)}, u32[]{:S(2)}, u32[]{:S(2)}) collective-permute-start(bf16[592,128]{1,0:T(8,128)(2,1)S(1)} %add.8.a), channel_id=1, source_target_pairs={{0,2},{1,3},{2,0},{3,1},{4,5},{5,4},{6,7},{7,6},{8,10},{9,11},{10,... | collective-permute-start | bytes 454664 | tf_op jit(solution)/shard_map/ppermute | solution.py:670
  29.6 0.5 %collective-permute-done.4.strip = bf16[8,4,192]{2,1,0:T(4,128)(2,1)S(1)} collective-permute-done((bf16[8,4,192]{2,1,0:T(4,128)(2,1)S(1)}, bf16[8,4,192]{2,1,0:T(4,128)(2,1)S(1)}, u32[]{:S(2)}, u32[]{:S(2)}) %collective-permute-start.4) | collective-permute-done | bytes 12320 | tf_op jit(solution)/shard_map/ppermute | solution.py:676
  30.1 0.9 %join.1 = (bf16[8,192,128]{2,1,0:T(8,128)(2,1)}, f32[8,128]{1,0:T(8,128)S(1)}) custom-call(bf16[4,192,128]{2,1,0:T(8,128)(2,1)S(1)} %collective-permute-done.3.rows_back.high, bf16[4,192,128]{2,1,0:T(8,128)(2,1)S(1)} %get-tuple-element.65.low.refs_0_, bf16[8,4,192]{2,1,0:T(4,128)(2,1)S(1)} %collective-permute-done.4.strip), custom_call_target="tpu_custom_call" | custom-call | flops 4000000000 | tf_op jit(solution)/shard_map/join/pallas_call | solution.py:535
  31.0 2.5 %collective-permute-done.8.b = bf16[592,128]{1,0:T(8,128)(2,1)S(1)} collective-permute-done((bf16[592,128]{1,0:T(8,128)(2,1)S(1)}, bf16[592,128]{1,0:T(8,128)(2,1)S(1)}, u32[]{:S(2)}, u32[]{:S(2)}) %collective-permute-start.8) | collective-permute-done | bytes 151584 | tf_op jit(solution)/shard_map/ppermute | solution.py:670
  33.5 0.2 collective-permute-start.9
  33.7 0.8 %scale_own.1 = (f32[192,576]{1,0:T(8,128)}, f32[192,192]{1,0:T(8,128)}) custom-call(bf16[592,128]{1,0:T(8,128)(2,1)S(1)} %add.9.mine), custom_call_target="tpu_custom_call" | custom-call | flops 1000000000 | tf_op jit(solution)/shard_map/scale_own/pallas_call | solution.py:594
  34.4 0.5 %collective-permute-done.9.other = bf16[592,128]{1,0:T(8,128)(2,1)S(1)} collective-permute-done((bf16[592,128]{1,0:T(8,128)(2,1)S(1)}, bf16[592,128]{1,0:T(8,128)(2,1)S(1)}, u32[]{:S(2)}, u32[]{:S(2)}) %collective-permute-start.9) | collective-permute-done | bytes 151584 | tf_op jit(solution)/shard_map/ppermute | solution.py:684
  34.9 0.8 %scale_other.1 = (f32[192,576]{1,0:T(8,128)}, f32[192,192]{1,0:T(8,128)}, f32[1,192]{1,0:T(1,128)}) custom-call(bf16[592,128]{1,0:T(8,128)(2,1)S(1)} %add.9.mine, bf16[592,128]{1,0:T(8,128)(2,1)S(1)} %collective-permute-done.9.other, f32[192,576]{1,0:T(8,128)} %get-tuple-element.71.wqkv_in, ...), custom_call_target="tpu_custom_call", output_to_operand_aliasing={{0}: (2, {}), {1}: (3, {})} | custom-call | tf_op jit(solution)/shard_map/scale_other/pallas_call | solution.py:607
  (7 shorter events, 0.2 us)
Async XLA Ops:
  0.6 3.6 %copy-start.2 = (bf16[8,128,192]{1,2,0:T(8,128)(2,1)S(1)}, bf16[8,128,192]{1,2,0:T(8,128)(2,1)}, u32[]{:S(2)}) copy-start(bf16[8,128,192]{1,2,0:T(8,128)(2,1)} %param.5) | copy-start | bytes 1179652
  1.7 2.5 %copy-start.3 = (bf16[8,128,192]{1,2,0:T(8,128)(2,1)S(1)}, bf16[8,128,192]{1,2,0:T(8,128)(2,1)}, u32[]{:S(2)}) copy-start(bf16[8,128,192]{1,2,0:T(8,128)(2,1)} %param.6) | copy-start | bytes 1179652
  1.8 7.7 %collective-permute-start = (bf16[8,192,128]{2,1,0:T(8,128)(2,1)S(1)}, bf16[8,192,128]{2,1,0:T(8,128)(2,1)S(1)}, u32[]{:S(2)}, u32[]{:S(2)}) collective-permute-start(bf16[8,192,128]{2,1,0:T(8,128)(2,1)S(1)} %get-tuple-element.42.message), channel_id=1, source_target_pairs={{0,12},{4,0},{8,4},{12,8},{1,13},{5,1},{9,5},{13,9},{2,14},{6,2},{... | collective-permute-start | bytes 1179656 | tf_op jit(solution)/shard_map/ppermute | solution.py:648
  4.3 4.4 %copy-start = (bf16[192,576]{1,0:T(8,128)(2,1)S(1)}, bf16[192,576]{1,0:T(8,128)(2,1)}, u32[]{:S(2)}) copy-start(bf16[192,576]{1,0:T(8,128)(2,1)} %w_qkv.5) | copy-start | bytes 663556
  4.5 7.1 %collective-permute-start.1 = (bf16[8,4,192]{2,1,0:T(4,128)(2,1)S(1)}, bf16[8,4,192]{2,1,0:T(4,128)(2,1)S(1)}, u32[]{:S(2)}, u32[]{:S(2)}) collective-permute-start(bf16[8,4,192]{2,1,0:T(4,128)(2,1)S(1)} %get-tuple-element.53), channel_id=1, source_target_pairs={{0,3},{1,0},{2,1},{3,2},{4,7},{5,4},{6,5},{7,6},{8,11},{9,8},{10,9... | collective-permute-start | bytes 36872 | tf_op jit(solution)/shard_map/ppermute | solution.py:651
  8.2 1.3 %copy-start.1 = (bf16[192,192]{1,0:T(8,128)(2,1)S(1)}, bf16[192,192]{1,0:T(8,128)(2,1)}, u32[]{:S(2)}) copy-start(bf16[192,192]{1,0:T(8,128)(2,1)} %w_proj.3) | copy-start | bytes 221188
  8.2 3.5 %collective-permute-start.2 = (bf16[8,4,192]{2,1,0:T(4,128)(2,1)S(1)}, bf16[8,4,192]{2,1,0:T(4,128)(2,1)S(1)}, u32[]{:S(2)}, u32[]{:S(2)}) collective-permute-start(bf16[8,4,192]{2,1,0:T(4,128)(2,1)S(1)} %get-tuple-element.54), channel_id=1, source_target_pairs={{0,15},{1,12},{2,13},{3,14},{4,3},{5,0},{6,1},{7,2},{8,7},{9,4},{1... | collective-permute-start | bytes 36872 | tf_op jit(solution)/shard_map/ppermute | solution.py:652
  14.2 1.9 %collective-permute-start.5 = (bf16[592,128]{1,0:T(8,128)(2,1)S(1)}, bf16[592,128]{1,0:T(8,128)(2,1)S(1)}, u32[]{:S(2)}, u32[]{:S(2)}) collective-permute-start(bf16[592,128]{1,0:T(8,128)(2,1)S(1)} %get-tuple-element.69), channel_id=1, source_target_pairs={{0,4},{4,0},{8,12},{12,8},{1,5},{5,1},{9,13},{13,9},{2,6},{6,2},{1... | collective-permute-start | bytes 454664 | tf_op jit(solution)/shard_map/ppermute | solution.py:664
  16.2 5.3 %collective-permute-start.6 = (bf16[592,128]{1,0:T(8,128)(2,1)S(1)}, bf16[592,128]{1,0:T(8,128)(2,1)S(1)}, u32[]{:S(2)}, u32[]{:S(2)}) collective-permute-start(bf16[592,128]{1,0:T(8,128)(2,1)S(1)} %add.6.a), channel_id=1, source_target_pairs={{0,1},{1,0},{2,3},{3,2},{4,12},{5,13},{6,14},{7,15},{8,9},{9,8},{1... | collective-permute-start | bytes 454664 | tf_op jit(solution)/shard_map/ppermute | solution.py:670
  19.3 5.1 %collective-permute-start.3 = (bf16[4,192,128]{2,1,0:T(8,128)(2,1)S(1)}, bf16[4,192,128]{2,1,0:T(8,128)(2,1)S(1)}, u32[]{:S(2)}, u32[]{:S(2)}) collective-permute-start(bf16[4,192,128]{2,1,0:T(8,128)(2,1)S(1)} %get-tuple-element.64), channel_id=1, source_target_pairs={{12,0},{0,4},{4,8},{8,12},{13,1},{1,5},{5,9},{9,13},{14,2},{2,6},{... | collective-permute-start | bytes 589832 | tf_op jit(solution)/shard_map/ppermute | solution.py:662
  21.5 5.3 %collective-permute-start.7 = (bf16[592,128]{1,0:T(8,128)(2,1)S(1)}, bf16[592,128]{1,0:T(8,128)(2,1)S(1)}, u32[]{:S(2)}, u32[]{:S(2)}) collective-permute-start(bf16[592,128]{1,0:T(8,128)(2,1)S(1)} %add.7.a), channel_id=1, source_target_pairs={{0,8},{1,9},{2,10},{3,11},{4,6},{5,7},{6,4},{7,5},{8,0},{9,1},{10,... | collective-permute-start | bytes 454664 | tf_op jit(solution)/shard_map/ppermute | solution.py:670
  24.5 5.6 %collective-permute-start.4 = (bf16[8,4,192]{2,1,0:T(4,128)(2,1)S(1)}, bf16[8,4,192]{2,1,0:T(4,128)(2,1)S(1)}, u32[]{:S(2)}, u32[]{:S(2)}) collective-permute-start(bf16[8,4,192]{2,1,0:T(4,128)(2,1)S(1)} %collect.1.refs_0_), channel_id=1, source_target_pairs={{3,0},{0,1},{1,2},{2,3},{7,4},{4,5},{5,6},{6,7},{11,8},{8,9},{9,10... | collective-permute-start | bytes 36872 | tf_op jit(solution)/shard_map/ppermute | solution.py:676
  26.8 6.7 %collective-permute-start.8 = (bf16[592,128]{1,0:T(8,128)(2,1)S(1)}, bf16[592,128]{1,0:T(8,128)(2,1)S(1)}, u32[]{:S(2)}, u32[]{:S(2)}) collective-permute-start(bf16[592,128]{1,0:T(8,128)(2,1)S(1)} %add.8.a), channel_id=1, source_target_pairs={{0,2},{1,3},{2,0},{3,1},{4,5},{5,4},{6,7},{7,6},{8,10},{9,11},{10,... | collective-permute-start | bytes 454664 | tf_op jit(solution)/shard_map/ppermute | solution.py:670
  33.5 1.4 %collective-permute-start.9 = (bf16[592,128]{1,0:T(8,128)(2,1)S(1)}, bf16[592,128]{1,0:T(8,128)(2,1)S(1)}, u32[]{:S(2)}, u32[]{:S(2)}) collective-permute-start(bf16[592,128]{1,0:T(8,128)(2,1)S(1)} %add.9.mine), channel_id=1, source_target_pairs={{0,4},{4,0},{8,12},{12,8},{1,5},{5,1},{9,13},{13,9},{2,6},{6,2},{1... | collective-permute-start | bytes 454664 | tf_op jit(solution)/shard_map/ppermute | solution.py:684

commit v7 on v6

--- a/solution.py
+++ b/solution.py
@@ -91,12 +91,21 @@
     )(message, rest)
 
 
-def prep_body(rest, w_qkv, xs, dys, w_qkv_t):
+def standard(v, axis):
+    v = v.astype(F32)
+    centred = v - jnp.mean(v, axis=axis, keepdims=True)
+    inv = lax.rsqrt(jnp.mean(centred * centred, axis=axis, keepdims=True) + EPSILON)
+    return centred * inv, inv
+
+
+def prep_body(rest, w_qkv, hats, dys, inv, w_qkv_t):
     cols = rest.shape[2]
-    for n, dest in enumerate((xs, dys)):
-        for i in range(SHIFT):
-            line = jnp.transpose(rest[n * SHIFT + i])
-            dest[i] = pltpu.roll(line.astype(F32), cols - SHIFT, 0)
+    for i in range(SHIFT):
+        hat, inv_row = standard(rest[i], 0)
+        hats[i] = pltpu.roll(jnp.transpose(hat), cols - SHIFT, 0)
+        inv[i : i + 1, :] = inv_row
+        line = jnp.transpose(rest[SHIFT + i])
+        dys[i] = pltpu.roll(line.astype(F32), cols - SHIFT, 0)
     w_qkv_t[...] = jnp.transpose(w_qkv[...])
 
 
@@ -107,10 +116,11 @@
         out_shape=(
             shape(F32, SHIFT, cols, channels),
             shape(F32, SHIFT, cols, channels),
+            shape(F32, SHIFT, cols),
             shape(BF16, w_qkv.shape[1], channels),
         ),
         in_specs=[VMEM] * 2,
-        out_specs=(VMEM,) * 3,
+        out_specs=(VMEM,) * 4,
         compiler_params=params(8),
         name="prep",
     )(rest, w_qkv)
@@ -122,6 +132,20 @@
 
 def core():
     return lax.rem(lax.axis_index("row"), 2)
+
+
+def window(low, high, w, tails=None):
+    channels = low.shape[2]
+    at = slice(w * WINDOW, (w + 1) * WINDOW)
+    if tails is None:
+        rows = [low[:, at, :], high[:, at, :]]
+    else:
+        at = slice(w * WINDOW, w * WINDOW + SHIFT)
+        rows = [
+            jnp.concatenate((half[:, at, :], tail), axis=1)
+            for half, tail in zip((low, high), tails)
+        ]
+    return jnp.concatenate(rows, axis=0).reshape(WINDOW * WINDOW, channels)
 
 
 def write_masks(mask):
@@ -136,25 +160,18 @@
 
 
 def attention(
-    last, xs, dys, gain, w_qkv, w_qkv_t, w_proj, mask,
-    n_t, upstream, dq_t, dk_n, dv_n, att_t, x_hat, inv_std,
+    last, read, gain, w_qkv, w_qkv_t, w_proj, mask,
+    n_t, upstream, dq_t, dk_n, dv_n, att_t,
     normed, q_t, k_t, v_t, do_t, k_n, v_n, q_n, do_n,
 ):
-    rows, cols, channels = xs.shape
-    tokens = rows * cols
+    tokens, channels = upstream.shape
     pairs = tokens // PAIR
     gain_row = gain[...]
-    for w in range(cols // WINDOW):
-        at = slice(w * WINDOW, (w + 1) * WINDOW)
+    for w in range(2 * pairs):
         to = slice(w * PAIR // 2, (w + 1) * PAIR // 2)
-        token = xs[:, at, :].reshape(PAIR // 2, channels)
-        centred = token - jnp.mean(token, axis=-1, keepdims=True)
-        inv = lax.rsqrt(jnp.mean(centred * centred, axis=-1, keepdims=True) + EPSILON)
-        hat = centred * inv
-        x_hat[to, :] = hat
-        inv_std[to, :] = jnp.broadcast_to(inv, (PAIR // 2, 128))
+        hat, dy = read(w)
         normed[to, :] = (hat * gain_row).astype(BF16)
-        upstream[to, :] = dys[:, at, :].reshape(PAIR // 2, channels).astype(BF16)
+        upstream[to, :] = dy.astype(BF16)
 
     n_all = normed[...]
     n_t[...] = jnp.transpose(n_all)
@@ -292,8 +309,6 @@
         shape(BF16, tokens, channels),
         shape(BF16, tokens, channels),
         shape(BF16, channels, tokens),
-        shape(F32, tokens, channels),
-        shape(F32, tokens, 128),
     )
 
 
@@ -305,56 +320,61 @@
     return [flat, turned, turned, turned, turned, flat, flat, padded, padded]
 
 
-def first_body(x_low, dy_low, row_halo, gain, w_qkv, w_qkv_t, w_proj, *refs):
-    xs_b, dys_b, dys, *refs = refs
-    outs, (xs, mask), scratch = refs[:8], refs[8:10], refs[10:]
-    half_rows, cols, channels = x_low.shape
-    part = cols // 2
-    for n, (tile, here, later) in enumerate(((x_low, xs, xs_b), (dy_low, dys, dys_b))):
-        for i in range(2 * half_rows):
-            if i < half_rows:
-                line = tile[i]
-            else:
-                line = jnp.transpose(row_halo[n * half_rows + i - half_rows]).astype(F32)
-                line = pltpu.roll(line, cols - SHIFT, 0)
-            here[i] = line[:part]
-            later[i] = line[part:]
+def first_body(hat_low, dy_low, inv_low, row_halo, gain, w_qkv, w_qkv_t, w_proj, *refs):
+    hat_high, dy_high, inv, *refs = refs
+    outs, mask, scratch = refs[:6], refs[6], refs[7:]
+    half_rows, cols, channels = hat_low.shape
+    inv[:half_rows, :] = inv_low[...]
+    for i in range(half_rows):
+        hat, inv_row = standard(row_halo[i], 0)
+        inv[half_rows + i : half_rows + i + 1, :] = inv_row
+        hat_high[i] = pltpu.roll(jnp.transpose(hat), cols - SHIFT, 0)
+        dy = jnp.transpose(row_halo[half_rows + i]).astype(F32)
+        dy_high[i] = pltpu.roll(dy, cols - SHIFT, 0)
     write_masks(mask)
-    attention(False, xs, dys, gain, w_qkv, w_qkv_t, w_proj, mask, *outs, *scratch)
-
-
-def first(x_low, dy_low, row_halo, gain, w_qkv, w_qkv_t, w_proj):
-    half_rows, cols, channels = x_low.shape
+    read = lambda w: (window(hat_low, hat_high, w), window(dy_low, dy_high, w))
+    attention(False, read, gain, w_qkv, w_qkv_t, w_proj, mask, *outs, *scratch)
+
+
+def first(hat_low, dy_low, inv_low, row_halo, gain, w_qkv, w_qkv_t, w_proj):
+    half_rows, cols, channels = hat_low.shape
     sizes = (cols // 2, 2 * half_rows, channels)
-    block = shape(F32, 2 * half_rows, cols // 2, channels)
+    block = shape(F32, *hat_low.shape)
     return pl.pallas_call(
         first_body,
-        out_shape=(block, block, block) + attention_outs(*sizes),
-        in_specs=[VMEM] * 7,
-        out_specs=(VMEM,) * 11,
-        scratch_shapes=[
-            pltpu.VMEM(block.shape, F32),
-            pltpu.VMEM((2, PAIR // 2, PAIR), F32),
-        ] + attention_scratch(*sizes),
+        out_shape=(block, block, shape(F32, 2 * half_rows, cols)) + attention_outs(*sizes),
+        in_specs=[VMEM] * 8,
+        out_specs=(VMEM,) * 9,
+        scratch_shapes=[pltpu.VMEM((2, PAIR // 2, PAIR), F32)] + attention_scratch(*sizes),
         compiler_params=params(24),
         name="first",
-    )(x_low, dy_low, row_halo, gain, w_qkv, w_qkv_t, w_proj)
+    )(hat_low, dy_low, inv_low, row_halo, gain, w_qkv, w_qkv_t, w_proj)
 
 
 def second_body(
-    xs_in, dys_in, strip, corner, gain, w_qkv, w_qkv_t, w_proj,
+    hat_low, hat_high, dy_low, dy_high, strip, corner, gain, w_qkv, w_qkv_t, w_proj,
     n_t_a, upstream_a, dq_t_a, dk_n_a, dv_n_a, att_t_a, *refs,
 ):
-    keep, send, dys, dq_t, dk_n, dv_n, x_hat, inv_std, *refs = refs
-    xs, mask, partial, n_t, upstream, att_t, *scratch = refs
-    rows, cols, channels = dys.shape
-    for n, (source, dest) in enumerate(((xs_in, xs), (dys_in, dys))):
-        for i in range(rows):
-            tail = (strip if i < SHIFT else corner)[n * SHIFT + i % SHIFT]
-            dest[i, : cols - WINDOW, :] = source[i, : cols - WINDOW, :]
-            dest[i, cols - WINDOW :, :] = jnp.concatenate(
-                (source[i, cols - WINDOW : cols - SHIFT, :], tail.astype(F32)), axis=0
-            )
+    keep, send, hat_tail, inv_tail, dq_t, dk_n, dv_n, *refs = refs
+    mask, partial, n_t, upstream, att_t, *scratch = refs
+    half_rows, cols, channels = hat_low.shape
+    for n, arrived in enumerate((strip, corner)):
+        for i in range(SHIFT):
+            hat, inv = standard(arrived[i], 1)
+            hat_tail[n, i] = hat
+            inv_tail[n, i] = jnp.broadcast_to(inv, inv_tail.shape[2:])
+    skipped = cols // WINDOW // 2
+
+    def read(w):
+        w = w + skipped
+        if w < cols // WINDOW - 1:
+            return window(hat_low, hat_high, w), window(dy_low, dy_high, w)
+        tails = [v[SHIFT:].astype(F32) for v in (strip, corner)]
+        return (
+            window(hat_low, hat_high, w, (hat_tail[0], hat_tail[1])),
+            window(dy_low, dy_high, w, tails),
+        )
+
     write_masks(mask)
     for n, piece in enumerate(
         (
@@ -366,8 +386,8 @@
     ):
         partial[n] = piece
     attention(
-        True, xs, dys, gain, w_qkv, w_qkv_t, w_proj, mask,
-        n_t, upstream, dq_t, dk_n, dv_n, att_t, x_hat, inv_std, *scratch,
+        True, read, gain, w_qkv, w_qkv_t, w_proj, mask,
+        n_t, upstream, dq_t, dk_n, dv_n, att_t, *scratch,
     )
     wide = jnp.concatenate(
         (
@@ -404,18 +424,21 @@
     store(slice(6 * part, 6 * part + 16), gain_block[:, :128], gain_block[:, 128:])
 
 
-def second(xs, dys, strip, corner, gain, w_qkv, w_qkv_t, w_proj, *saved):
-    rows, cols, channels = xs.shape
-    sizes = (cols, rows, channels)
-    n_t, upstream, dq_t, dk_n, dv_n, att_t, x_hat, inv_std = attention_outs(*sizes)
+def second(hat_low, hat_high, dy_low, dy_high, strip, corner, gain, w_qkv, w_qkv_t, w_proj, *saved):
+    half_rows, cols, channels = hat_low.shape
+    sizes = (cols // 2, 2 * half_rows, channels)
+    n_t, upstream, dq_t, dk_n, dv_n, att_t = attention_outs(*sizes)
     half = shape(BF16, 3 * channels + 16, 128)
     return pl.pallas_call(
         second_body,
-        out_shape=(half, half, shape(F32, *xs.shape), dq_t, dk_n, dv_n, x_hat, inv_std),
-        in_specs=[VMEM] * 14,
-        out_specs=(VMEM,) * 8,
+        out_shape=(
+            half, half,
+            shape(F32, 2, half_rows, SHIFT, channels), shape(F32, 2, half_rows, SHIFT, 128),
+            dq_t, dk_n, dv_n,
+        ),
+        in_specs=[VMEM] * 16,
+        out_specs=(VMEM,) * 7,
         scratch_shapes=[
-            pltpu.VMEM(xs.shape, F32),
             pltpu.VMEM((2, PAIR // 2, PAIR), F32),
             pltpu.VMEM((4, channels, channels), F32),
             pltpu.VMEM(n_t.shape, BF16),
@@ -424,32 +447,51 @@
         ] + attention_scratch(*sizes),
         compiler_params=params(24),
         name="second",
-    )(xs, dys, strip, corner, gain, w_qkv, w_qkv_t, w_proj, *saved)
+    )(
+        hat_low, hat_high, dy_low, dy_high, strip, corner,
+        gain, w_qkv, w_qkv_t, w_proj, *saved,
+    )
 
 
 def back_body(*refs):
-    parts, (gain, w_qkv_t, low, high, strip, out) = (refs[:6], refs[6:12]), refs[12:]
+    parts = (refs[:3], refs[3:6])
+    hat_low, hat_high, dy_low, dy_high, hat_tail, inv_tail, inv, dy_strip, dy_corner = refs[6:15]
+    gain, w_qkv_t, low, high, strip, out, spread = refs[15:]
     rows, cols, channels = out.shape
+    half_rows = rows // 2
+    for i in range(rows):
+        column = jnp.transpose(jnp.broadcast_to(inv[i : i + 1, :], (128, cols)))
+        spread[i] = pltpu.roll(column, cols - SHIFT, 0)
+        spread[i, cols - SHIFT :, :] = inv_tail[i // half_rows, i % half_rows]
     half_n = PAIR // 2
     gain_row = gain[...]
-    for n, (dq_t, dk_n, dv_n, x_hat, inv_std, dys) in enumerate(parts):
-        part = dys.shape[1]
-        for p in range(rows * part // PAIR):
+
+    def read(w):
+        if w < cols // WINDOW - 1:
+            return window(hat_low, hat_high, w), window(dy_low, dy_high, w)
+        tails = [v[SHIFT:].astype(F32) for v in (dy_strip, dy_corner)]
+        return (
+            window(hat_low, hat_high, w, (hat_tail[0], hat_tail[1])),
+            window(dy_low, dy_high, w, tails),
+        )
+
+    for n, (dq_t, dk_n, dv_n) in enumerate(parts):
+        pairs = dk_n.shape[0] // PAIR
+        for p in range(pairs):
             at = slice(p * PAIR, (p + 1) * PAIR)
             g = dot_nn(jnp.transpose(dq_t[:, at]), w_qkv_t[:channels])
             g = g + dot_nn(dk_n[at, :], w_qkv_t[channels : 2 * channels])
             g = g + dot_nn(dv_n[at, :], w_qkv_t[2 * channels :])
-            hat = x_hat[at, :]
-            gh = g * gain_row
-            mean_a = jnp.mean(gh, axis=-1, keepdims=True)
-            mean_b = jnp.mean(gh * hat, axis=-1, keepdims=True)
-            branch = inv_std[at, 0:1] * (gh - mean_a - hat * mean_b)
             for half in range(2):
-                w = (2 * p + half) * WINDOW
-                piece = branch[half * half_n : (half + 1) * half_n]
-                out[:, n * part + w : n * part + w + WINDOW, :] = dys[
-                    :, w : w + WINDOW, :
-                ] + piece.reshape(rows, WINDOW, channels)
+                w = 2 * (n * pairs + p) + half
+                to = slice(w * WINDOW, (w + 1) * WINDOW)
+                hat, dy = read(w)
+                gh = g[half * half_n : (half + 1) * half_n] * gain_row
+                mean_a = jnp.mean(gh, axis=-1, keepdims=True)
+                mean_b = jnp.mean(gh * hat, axis=-1, keepdims=True)
+                inv_w = spread[:, to, :].reshape(half_n, 128)[:, 0:1]
+                branch = inv_w * (gh - mean_a - hat * mean_b)
+                out[:, to, :] = (dy + branch).reshape(rows, WINDOW, channels)
     for i in range(rows):
         line = pltpu.roll(out[i], SHIFT, 0)
         if i < rows // 2:
@@ -458,25 +500,28 @@
         dest[i % SHIFT] = jnp.transpose(line.astype(BF16))
 
 
-def back(part_a, part_b, gain, w_qkv_t):
-    rows, part, channels = part_a[-1].shape
-    cols = 2 * part
+def back(part_a, part_b, tokens, gain, w_qkv_t):
+    half_rows, cols, channels = tokens[0].shape
+    rows = 2 * half_rows
     return pl.pallas_call(
         back_body,
         out_shape=(
-            shape(BF16, rows // 2, channels, cols),
-            shape(BF16, rows // 2, channels, cols),
-            shape(BF16, rows // 2, SHIFT, channels),
+            shape(BF16, half_rows, channels, cols),
+            shape(BF16, half_rows, channels, cols),
+            shape(BF16, half_rows, SHIFT, channels),
         ),
-        in_specs=[VMEM] * 14,
+        in_specs=[VMEM] * 17,
         out_specs=(VMEM,) * 3,
-        scratch_shapes=[pltpu.VMEM((rows, cols, channels), F32)],
+        scratch_shapes=[
+            pltpu.VMEM((rows, cols, channels), F32),
+            pltpu.VMEM((rows, cols, 128), F32),
+        ],
         compiler_params=params(24),
         cost_estimate=pl.CostEstimate(
             flops=2 * rows * cols * channels * 3 * channels, bytes_accessed=8 * 2**20, transcendentals=0
         ),
         name="back",
-    )(*part_a, *part_b, gain, w_qkv_t)
+    )(*part_a, *part_b, *tokens, gain, w_qkv_t)
 
 
 def collect_body(rows_back, low_strip, out):
@@ -650,15 +695,13 @@
     strip, corner = strips(message, rest)
     strip = lax.ppermute(strip, "col", left)
     corner = lax.ppermute(corner, ("row", "col"), both)
-    x_low, dy_low, w_qkv_t = prep(rest, w_qkv)
+    hat_low, dy_low, inv_low, w_qkv_t = prep(rest, w_qkv)
     weights = (gain, w_qkv, w_qkv_t, w_proj)
-    xs_b, dys_b, dys_a, *out_a = first(x_low, dy_low, row_halo, *weights)
-    keep, send, dys_b, *saved_b = second(
-        xs_b, dys_b, strip, corner, *weights, *out_a[:6]
-    )
-    low, high, strip = back(
-        (*out_a[2:5], *out_a[6:], dys_a), (*saved_b, dys_b), gain, w_qkv_t
-    )
+    hat_high, dy_high, inv, *out_a = first(hat_low, dy_low, inv_low, row_halo, *weights)
+    tokens = (hat_low, hat_high, dy_low, dy_high)
+    keep, send, hat_tail, inv_tail, *out_b = second(*tokens, strip, corner, *weights, *out_a)
+    tokens += (hat_tail, inv_tail, inv, strip, corner)
+    low, high, strip = back(out_a[2:5], out_b, tokens, gain, w_qkv_t)
     rows_back = lax.ppermute(high, "row", turn(up))
     orders = bit_orders(row_extent, col_extent)
     total = keep + lax.ppermute(send, "row", flip(row_extent, 1))

time: 35.8 us -> 35.7 us (level)
    ppermute x3, waiting for transfers between devices: 6.43 us -> 6.05 us  [on_device(): arrived = lax.ppermute(total, ('row', 'col'), route)]
  transfers between devices with their start and end apart: 10 -> 10, of which waited for: 8 -> 8; matrix products, arithmetic and copies ran while one was open for 0% -> 0% of each run, Pallas kernels for 16% -> 17%
where the time goes in v7:
time: 35.7 us; the launch traced here: 35.6 us
  starting transfers between devices  14.2 us (40%)
  Pallas kernels  10.4 us (29%)
  waiting for transfers between devices  10 us (28%)
  between operations  0.78 us (2%)
    ppermute x3, starting transfers between devices, on_device(): arrived = lax.ppermute(total, ('row', 'col'), route)  6.16 us
    ppermute x3, waiting for transfers between devices, on_device(): arrived = lax.ppermute(total, ('row', 'col'), route)  6.05 us
    ppermute x1, starting transfers between devices, on_device(): strip = lax.ppermute(strip, 'col', left)  3.65 us
    pallas_call x1, Pallas kernels, second(): pl.pallas_call(second_body, out_shape=(half, half, shape(F32, 2, half_row...  2.45 us
    ppermute x1, starting transfers between devices, on_device(): row_halo = lax.ppermute(message, 'row', up)  2.43 us
    pallas_call x1, Pallas kernels, first(): pl.pallas_call(first_body, out_shape=(block, block, shape(F32, 2 * half_r...  2.09 us
    ppermute x1, waiting for transfers between devices, on_device(): rows_back = lax.ppermute(high, 'row', turn(up))  1.56 us
    pallas_call x1, Pallas kernels, back(): pl.pallas_call(back_body, out_shape=(shape(BF16, half_rows, channels, col...  1.41 us
  transfers between devices with their start and end apart: 10, of which 8 were waited for; matrix products, arithmetic and copies ran while one was open for 0% of the time, Pallas kernels for 17%

profile of v7, /device:TPU:0, one launch (start us, length us, event | category | flops | bytes accessed | tf_op | source)
XLA Modules:
  0.0 35.6 jit_solution(14407310961974648255)
XLA Ops:
  0.6 0.0 copy-start.2
  0.6 1.1 %gather.1 = (bf16[8,192,128]{2,1,0:T(8,128)(2,1)S(1)}, f32[1,192]{1,0:T(1,128)S(1)}) custom-call(bf16[8,192,128]{2,1,0:T(8,128)(2,1)} %bitcast.5, bf16[8,192,128]{2,1,0:T(8,128)(2,1)} %bitcast.7, f32[1,192]{1,0:T(1,128)} %bitcast.9), custom_call_target="tpu_custom_call" | custom-call | tf_op jit(solution)/shard_map/gather/pallas_call | solution.py:64
  1.7 0.0 copy-start.3
  1.8 2.4 %collective-permute-start = (bf16[8,192,128]{2,1,0:T(8,128)(2,1)S(1)}, bf16[8,192,128]{2,1,0:T(8,128)(2,1)S(1)}, u32[]{:S(2)}, u32[]{:S(2)}) collective-permute-start(bf16[8,192,128]{2,1,0:T(8,128)(2,1)S(1)} %get-tuple-element.41.message), channel_id=1, source_target_pairs={{0,12},{4,0},{8,4},{12,8},{1,13},{5,1},{9,5},{13,9},{2,14},{6,2},{... | collective-permute-start | bytes 1179656 | tf_op jit(solution)/shard_map/ppermute | solution.py:693
  4.2 0.0 copy-done.2
  4.2 0.0 copy-done.3
  4.3 0.0 copy-start
  4.3 0.2 strips.1
  4.5 3.6 %collective-permute-start.1 = (bf16[8,4,192]{2,1,0:T(4,128)(2,1)S(1)}, bf16[8,4,192]{2,1,0:T(4,128)(2,1)S(1)}, u32[]{:S(2)}, u32[]{:S(2)}) collective-permute-start(bf16[8,4,192]{2,1,0:T(4,128)(2,1)S(1)} %get-tuple-element.49), channel_id=1, source_target_pairs={{0,3},{1,0},{2,1},{3,2},{4,7},{5,4},{6,5},{7,6},{8,11},{9,8},{10,9... | collective-permute-start | bytes 36872 | tf_op jit(solution)/shard_map/ppermute | solution.py:696
  8.2 0.0 copy-start.1
  8.2 0.5 %collective-permute-start.2 = (bf16[8,4,192]{2,1,0:T(4,128)(2,1)S(1)}, bf16[8,4,192]{2,1,0:T(4,128)(2,1)S(1)}, u32[]{:S(2)}, u32[]{:S(2)}) collective-permute-start(bf16[8,4,192]{2,1,0:T(4,128)(2,1)S(1)} %get-tuple-element.50), channel_id=1, source_target_pairs={{0,15},{1,12},{2,13},{3,14},{4,3},{5,0},{6,1},{7,2},{8,7},{9,4},{1... | collective-permute-start | bytes 36872 | tf_op jit(solution)/shard_map/ppermute | solution.py:697
  8.7 0.0 copy-done
  8.7 0.5 %prep.1 = (f32[4,128,192]{2,1,0:T(8,128)S(1)}, f32[4,128,192]{2,1,0:T(8,128)S(1)}, f32[4,128]{1,0:T(4,128)S(1)}, bf16[576,192]{1,0:T(8,128)(2,1)S(1)}) custom-call(bf16[8,192,128]{2,1,0:T(8,128)(2,1)S(1)} %pad_maximum_fusion.rest, bf16[192,576]{1,0:T(8,128)(2,1)S(1)} %copy-done), custom_call_target="tpu_custom_call" | custom-call | tf_op jit(solution)/shard_map/prep/pallas_call | solution.py:114
  9.2 0.3 collective-permute-done.row_halo
  9.5 0.0 copy-done.1
  9.5 2.1 %first.1 = (f32[4,128,192]{2,1,0:T(8,128)S(1)}, f32[4,128,192]{2,1,0:T(8,128)S(1)}, f32[8,128]{1,0:T(8,128)S(1)}, bf16[192,512]{1,0:T(8,128)(2,1)S(1)}, bf16[512...) custom-call(f32[4,128,192]{2,1,0:T(8,128)S(1)} %get-tuple-element.38, ...), custom_call_target="tpu_custom_call" | custom-call | tf_op jit(solution)/shard_map/first/pallas_call | solution.py:343
  11.6 0.0 collective-permute-done.1.strip.refs_13_
  11.6 0.0 collective-permute-done.2.corner.refs_14_
  11.6 2.5 %second.1 = (bf16[592,128]{1,0:T(8,128)(2,1)S(1)}, bf16[592,128]{1,0:T(8,128)(2,1)S(1)}, f32[2,4,4,192]{3,2,1,0:T(4,128)S(1)}, f32[2,4,4,128]{3,2,1,0:T(4,128)S(...) custom-call(f32[4,128,192]{2,1,0:T(8,128)S(1)} %get-tuple-element.38.hat_low.refs_6_, ...), custom_call_target="tpu_custom_call" | custom-call | tf_op jit(solution)/shard_map/second/pallas_call | solution.py:432
  14.1 0.9 %collective-permute-start.5 = (bf16[592,128]{1,0:T(8,128)(2,1)S(1)}, bf16[592,128]{1,0:T(8,128)(2,1)S(1)}, u32[]{:S(2)}, u32[]{:S(2)}) collective-permute-start(bf16[592,128]{1,0:T(8,128)(2,1)S(1)} %get-tuple-element.65), channel_id=1, source_target_pairs={{0,4},{4,0},{8,12},{12,8},{1,5},{5,1},{9,13},{13,9},{2,6},{6,2},{1... | collective-permute-start | bytes 454664 | tf_op jit(solution)/shard_map/ppermute | solution.py:707
  15.0 1.0 %collective-permute-done.5 = bf16[592,128]{1,0:T(8,128)(2,1)S(1)} collective-permute-done((bf16[592,128]{1,0:T(8,128)(2,1)S(1)}, bf16[592,128]{1,0:T(8,128)(2,1)S(1)}, u32[]{:S(2)}, u32[]{:S(2)}) %collective-permute-start.5) | collective-permute-done | bytes 151584 | tf_op jit(solution)/shard_map/ppermute | solution.py:707
  16.0 1.8 %collective-permute-start.6 = (bf16[592,128]{1,0:T(8,128)(2,1)S(1)}, bf16[592,128]{1,0:T(8,128)(2,1)S(1)}, u32[]{:S(2)}, u32[]{:S(2)}) collective-permute-start(bf16[592,128]{1,0:T(8,128)(2,1)S(1)} %add.6.a), channel_id=1, source_target_pairs={{0,1},{1,0},{2,3},{3,2},{4,12},{5,13},{6,14},{7,15},{8,9},{9,8},{1... | collective-permute-start | bytes 454664 | tf_op jit(solution)/shard_map/ppermute | solution.py:713
  17.9 1.4 %back.1 = (bf16[4,192,128]{2,1,0:T(8,128)(2,1)S(1)}, bf16[4,192,128]{2,1,0:T(8,128)(2,1)S(1)}, bf16[4,4,192]{2,1,0:T(4,128)(2,1)S(1)}) custom-call(bf16[192,512]{1,0:T(8,128)(2,1)S(1)} %get-tuple-element.44.dq_t_a.refs_0_, bf16[512,192]{1,0:T(8,128)(2,1)S(1)} %get-tuple-element.45.dk_n_a.refs_1_, bf16[512,192]{1,0:T(8,128)(2,1)S(1)} %get-tuple-element.46.dv_n_a.refs_2_, ...), custom_call_target="tpu_custom_call" | custom-call | flops 226492416 | bytes 8388608 | tf_op jit(solution)/shard_map/back/pallas_call | solution.py:506
  19.3 0.1 collective-permute-start.3
  19.3 2.0 %collective-permute-done.6.b = bf16[592,128]{1,0:T(8,128)(2,1)S(1)} collective-permute-done((bf16[592,128]{1,0:T(8,128)(2,1)S(1)}, bf16[592,128]{1,0:T(8,128)(2,1)S(1)}, u32[]{:S(2)}, u32[]{:S(2)}) %collective-permute-start.6) | collective-permute-done | bytes 151584 | tf_op jit(solution)/shard_map/ppermute | solution.py:713
  21.3 1.5 %collective-permute-start.7 = (bf16[592,128]{1,0:T(8,128)(2,1)S(1)}, bf16[592,128]{1,0:T(8,128)(2,1)S(1)}, u32[]{:S(2)}, u32[]{:S(2)}) collective-permute-start(bf16[592,128]{1,0:T(8,128)(2,1)S(1)} %add.7.a), channel_id=1, source_target_pairs={{0,8},{1,9},{2,10},{3,11},{4,6},{5,7},{6,4},{7,5},{8,0},{9,1},{10,... | collective-permute-start | bytes 454664 | tf_op jit(solution)/shard_map/ppermute | solution.py:713
  22.9 1.6 %collective-permute-done.3.rows_back.high = bf16[4,192,128]{2,1,0:T(8,128)(2,1)S(1)} collective-permute-done((bf16[4,192,128]{2,1,0:T(8,128)(2,1)S(1)}, bf16[4,192,128]{2,1,0:T(8,128)(2,1)S(1)}, u32[]{:S(2)}, u32[]{:S(2)}) %collective-permute-start.3) | collective-permute-done | bytes 196640 | tf_op jit(solution)/shard_map/ppermute | solution.py:705
  24.4 0.1 collect.1.refs_0_
  24.5 0.3 collective-permute-start.4
  24.8 1.8 %collective-permute-done.7.b = bf16[592,128]{1,0:T(8,128)(2,1)S(1)} collective-permute-done((bf16[592,128]{1,0:T(8,128)(2,1)S(1)}, bf16[592,128]{1,0:T(8,128)(2,1)S(1)}, u32[]{:S(2)}, u32[]{:S(2)}) %collective-permute-start.7) | collective-permute-done | bytes 151584 | tf_op jit(solution)/shard_map/ppermute | solution.py:713
  26.6 2.8 %collective-permute-start.8 = (bf16[592,128]{1,0:T(8,128)(2,1)S(1)}, bf16[592,128]{1,0:T(8,128)(2,1)S(1)}, u32[]{:S(2)}, u32[]{:S(2)}) collective-permute-start(bf16[592,128]{1,0:T(8,128)(2,1)S(1)} %add.8.a), channel_id=1, source_target_pairs={{0,2},{1,3},{2,0},{3,1},{4,5},{5,4},{6,7},{7,6},{8,10},{9,11},{10,... | collective-permute-start | bytes 454664 | tf_op jit(solution)/shard_map/ppermute | solution.py:713
  29.5 0.6 %collective-permute-done.4.strip = bf16[8,4,192]{2,1,0:T(4,128)(2,1)S(1)} collective-permute-done((bf16[8,4,192]{2,1,0:T(4,128)(2,1)S(1)}, bf16[8,4,192]{2,1,0:T(4,128)(2,1)S(1)}, u32[]{:S(2)}, u32[]{:S(2)}) %collective-permute-start.4) | collective-permute-done | bytes 12320 | tf_op jit(solution)/shard_map/ppermute | solution.py:719
  30.1 0.9 %join.1 = (bf16[8,192,128]{2,1,0:T(8,128)(2,1)}, f32[8,128]{1,0:T(8,128)S(1)}) custom-call(bf16[4,192,128]{2,1,0:T(8,128)(2,1)S(1)} %collective-permute-done.3.rows_back.high, bf16[4,192,128]{2,1,0:T(8,128)(2,1)S(1)} %get-tuple-element.61.low.refs_0_, bf16[8,4,192]{2,1,0:T(4,128)(2,1)S(1)} %collective-permute-done.4.strip), custom_call_target="tpu_custom_call" | custom-call | flops 4000000000 | tf_op jit(solution)/shard_map/join/pallas_call | solution.py:580
  31.0 2.3 %collective-permute-done.8.b = bf16[592,128]{1,0:T(8,128)(2,1)S(1)} collective-permute-done((bf16[592,128]{1,0:T(8,128)(2,1)S(1)}, bf16[592,128]{1,0:T(8,128)(2,1)S(1)}, u32[]{:S(2)}, u32[]{:S(2)}) %collective-permute-start.8) | collective-permute-done | bytes 151584 | tf_op jit(solution)/shard_map/ppermute | solution.py:713
  33.3 0.2 collective-permute-start.9
  33.5 0.8 %scale_own.1 = (f32[192,576]{1,0:T(8,128)}, f32[192,192]{1,0:T(8,128)}) custom-call(bf16[592,128]{1,0:T(8,128)(2,1)S(1)} %add.9.mine), custom_call_target="tpu_custom_call" | custom-call | flops 1000000000 | tf_op jit(solution)/shard_map/scale_own/pallas_call | solution.py:639
  34.3 0.5 %collective-permute-done.9.other = bf16[592,128]{1,0:T(8,128)(2,1)S(1)} collective-permute-done((bf16[592,128]{1,0:T(8,128)(2,1)S(1)}, bf16[592,128]{1,0:T(8,128)(2,1)S(1)}, u32[]{:S(2)}, u32[]{:S(2)}) %collective-permute-start.9) | collective-permute-done | bytes 151584 | tf_op jit(solution)/shard_map/ppermute | solution.py:727
  34.8 0.8 %scale_other.1 = (f32[192,576]{1,0:T(8,128)}, f32[192,192]{1,0:T(8,128)}, f32[1,192]{1,0:T(1,128)}) custom-call(bf16[592,128]{1,0:T(8,128)(2,1)S(1)} %add.9.mine, bf16[592,128]{1,0:T(8,128)(2,1)S(1)} %collective-permute-done.9.other, f32[192,576]{1,0:T(8,128)} %get-tuple-element.67.wqkv_in, ...), custom_call_target="tpu_custom_call", output_to_operand_aliasing={{0}: (2, {}), {1}: (3, {})} | custom-call | tf_op jit(solution)/shard_map/scale_other/pallas_call | solution.py:652
  (7 shorter events, 0.2 us)
Async XLA Ops:
  0.6 3.6 %copy-start.2 = (bf16[8,128,192]{1,2,0:T(8,128)(2,1)S(1)}, bf16[8,128,192]{1,2,0:T(8,128)(2,1)}, u32[]{:S(2)}) copy-start(bf16[8,128,192]{1,2,0:T(8,128)(2,1)} %param.5) | copy-start | bytes 1179652
  1.7 2.5 %copy-start.3 = (bf16[8,128,192]{1,2,0:T(8,128)(2,1)S(1)}, bf16[8,128,192]{1,2,0:T(8,128)(2,1)}, u32[]{:S(2)}) copy-start(bf16[8,128,192]{1,2,0:T(8,128)(2,1)} %param.6) | copy-start | bytes 1179652
  1.8 7.7 %collective-permute-start = (bf16[8,192,128]{2,1,0:T(8,128)(2,1)S(1)}, bf16[8,192,128]{2,1,0:T(8,128)(2,1)S(1)}, u32[]{:S(2)}, u32[]{:S(2)}) collective-permute-start(bf16[8,192,128]{2,1,0:T(8,128)(2,1)S(1)} %get-tuple-element.41.message), channel_id=1, source_target_pairs={{0,12},{4,0},{8,4},{12,8},{1,13},{5,1},{9,5},{13,9},{2,14},{6,2},{... | collective-permute-start | bytes 1179656 | tf_op jit(solution)/shard_map/ppermute | solution.py:693
  4.3 4.4 %copy-start = (bf16[192,576]{1,0:T(8,128)(2,1)S(1)}, bf16[192,576]{1,0:T(8,128)(2,1)}, u32[]{:S(2)}) copy-start(bf16[192,576]{1,0:T(8,128)(2,1)} %w_qkv.5) | copy-start | bytes 663556
  4.5 7.1 %collective-permute-start.1 = (bf16[8,4,192]{2,1,0:T(4,128)(2,1)S(1)}, bf16[8,4,192]{2,1,0:T(4,128)(2,1)S(1)}, u32[]{:S(2)}, u32[]{:S(2)}) collective-permute-start(bf16[8,4,192]{2,1,0:T(4,128)(2,1)S(1)} %get-tuple-element.49), channel_id=1, source_target_pairs={{0,3},{1,0},{2,1},{3,2},{4,7},{5,4},{6,5},{7,6},{8,11},{9,8},{10,9... | collective-permute-start | bytes 36872 | tf_op jit(solution)/shard_map/ppermute | solution.py:696
  8.2 1.3 %copy-start.1 = (bf16[192,192]{1,0:T(8,128)(2,1)S(1)}, bf16[192,192]{1,0:T(8,128)(2,1)}, u32[]{:S(2)}) copy-start(bf16[192,192]{1,0:T(8,128)(2,1)} %w_proj.3) | copy-start | bytes 221188
  8.2 3.4 %collective-permute-start.2 = (bf16[8,4,192]{2,1,0:T(4,128)(2,1)S(1)}, bf16[8,4,192]{2,1,0:T(4,128)(2,1)S(1)}, u32[]{:S(2)}, u32[]{:S(2)}) collective-permute-start(bf16[8,4,192]{2,1,0:T(4,128)(2,1)S(1)} %get-tuple-element.50), channel_id=1, source_target_pairs={{0,15},{1,12},{2,13},{3,14},{4,3},{5,0},{6,1},{7,2},{8,7},{9,4},{1... | collective-permute-start | bytes 36872 | tf_op jit(solution)/shard_map/ppermute | solution.py:697
  14.1 1.9 %collective-permute-start.5 = (bf16[592,128]{1,0:T(8,128)(2,1)S(1)}, bf16[592,128]{1,0:T(8,128)(2,1)S(1)}, u32[]{:S(2)}, u32[]{:S(2)}) collective-permute-start(bf16[592,128]{1,0:T(8,128)(2,1)S(1)} %get-tuple-element.65), channel_id=1, source_target_pairs={{0,4},{4,0},{8,12},{12,8},{1,5},{5,1},{9,13},{13,9},{2,6},{6,2},{1... | collective-permute-start | bytes 454664 | tf_op jit(solution)/shard_map/ppermute | solution.py:707
  16.0 5.3 %collective-permute-start.6 = (bf16[592,128]{1,0:T(8,128)(2,1)S(1)}, bf16[592,128]{1,0:T(8,128)(2,1)S(1)}, u32[]{:S(2)}, u32[]{:S(2)}) collective-permute-start(bf16[592,128]{1,0:T(8,128)(2,1)S(1)} %add.6.a), channel_id=1, source_target_pairs={{0,1},{1,0},{2,3},{3,2},{4,12},{5,13},{6,14},{7,15},{8,9},{9,8},{1... | collective-permute-start | bytes 454664 | tf_op jit(solution)/shard_map/ppermute | solution.py:713
  19.3 5.1 %collective-permute-start.3 = (bf16[4,192,128]{2,1,0:T(8,128)(2,1)S(1)}, bf16[4,192,128]{2,1,0:T(8,128)(2,1)S(1)}, u32[]{:S(2)}, u32[]{:S(2)}) collective-permute-start(bf16[4,192,128]{2,1,0:T(8,128)(2,1)S(1)} %get-tuple-element.60), channel_id=1, source_target_pairs={{12,0},{0,4},{4,8},{8,12},{13,1},{1,5},{5,9},{9,13},{14,2},{2,6},{... | collective-permute-start | bytes 589832 | tf_op jit(solution)/shard_map/ppermute | solution.py:705
  21.3 5.3 %collective-permute-start.7 = (bf16[592,128]{1,0:T(8,128)(2,1)S(1)}, bf16[592,128]{1,0:T(8,128)(2,1)S(1)}, u32[]{:S(2)}, u32[]{:S(2)}) collective-permute-start(bf16[592,128]{1,0:T(8,128)(2,1)S(1)} %add.7.a), channel_id=1, source_target_pairs={{0,8},{1,9},{2,10},{3,11},{4,6},{5,7},{6,4},{7,5},{8,0},{9,1},{10,... | collective-permute-start | bytes 454664 | tf_op jit(solution)/shard_map/ppermute | solution.py:713
  24.5 5.6 %collective-permute-start.4 = (bf16[8,4,192]{2,1,0:T(4,128)(2,1)S(1)}, bf16[8,4,192]{2,1,0:T(4,128)(2,1)S(1)}, u32[]{:S(2)}, u32[]{:S(2)}) collective-permute-start(bf16[8,4,192]{2,1,0:T(4,128)(2,1)S(1)} %collect.1.refs_0_), channel_id=1, source_target_pairs={{3,0},{0,1},{1,2},{2,3},{7,4},{4,5},{5,6},{6,7},{11,8},{8,9},{9,10... | collective-permute-start | bytes 36872 | tf_op jit(solution)/shard_map/ppermute | solution.py:719
  26.6 6.7 %collective-permute-start.8 = (bf16[592,128]{1,0:T(8,128)(2,1)S(1)}, bf16[592,128]{1,0:T(8,128)(2,1)S(1)}, u32[]{:S(2)}, u32[]{:S(2)}) collective-permute-start(bf16[592,128]{1,0:T(8,128)(2,1)S(1)} %add.8.a), channel_id=1, source_target_pairs={{0,2},{1,3},{2,0},{3,1},{4,5},{5,4},{6,7},{7,6},{8,10},{9,11},{10,... | collective-permute-start | bytes 454664 | tf_op jit(solution)/shard_map/ppermute | solution.py:713
  33.3 1.4 %collective-permute-start.9 = (bf16[592,128]{1,0:T(8,128)(2,1)S(1)}, bf16[592,128]{1,0:T(8,128)(2,1)S(1)}, u32[]{:S(2)}, u32[]{:S(2)}) collective-permute-start(bf16[592,128]{1,0:T(8,128)(2,1)S(1)} %add.9.mine), channel_id=1, source_target_pairs={{0,4},{4,0},{8,12},{12,8},{1,5},{5,1},{9,13},{13,9},{2,6},{6,2},{1... | collective-permute-start | bytes 454664 | tf_op jit(solution)/shard_map/ppermute | solution.py:727

commit v8 on v7

--- a/solution.py
+++ b/solution.py
@@ -160,7 +160,7 @@
 
 
 def attention(
-    last, read, gain, w_qkv, w_qkv_t, w_proj, mask,
+    last, earlier, read, gain, w_qkv, w_qkv_t, w_proj, mask,
     n_t, upstream, dq_t, dk_n, dv_n, att_t,
     normed, q_t, k_t, v_t, do_t, k_n, v_n, q_n, do_n,
 ):
@@ -292,6 +292,8 @@
     state = front(0)
     done = None
     for p in range(pairs):
+        if earlier is not None and p == pairs - 1:
+            earlier()
         later = front(p + 1) if p + 1 < pairs else None
         if done is not None:
             rear(*done)
@@ -333,7 +335,7 @@
         dy_high[i] = pltpu.roll(dy, cols - SHIFT, 0)
     write_masks(mask)
     read = lambda w: (window(hat_low, hat_high, w), window(dy_low, dy_high, w))
-    attention(False, read, gain, w_qkv, w_qkv_t, w_proj, mask, *outs, *scratch)
+    attention(False, None, read, gain, w_qkv, w_qkv_t, w_proj, mask, *outs, *scratch)
 
 
 def first(hat_low, dy_low, inv_low, row_halo, gain, w_qkv, w_qkv_t, w_proj):
@@ -376,17 +378,19 @@
         )
 
     write_masks(mask)
-    for n, piece in enumerate(
-        (
-            dot_nt(n_t_a[...], dq_t_a[...]),
-            dot_nn(n_t_a[...], dk_n_a[...]),
-            dot_nn(n_t_a[...], dv_n_a[...]),
-            dot_nn(att_t_a[...], upstream_a[...]),
-        )
-    ):
-        partial[n] = piece
+    def earlier():
+        for n, piece in enumerate(
+            (
+                dot_nt(n_t_a[...], dq_t_a[...]),
+                dot_nn(n_t_a[...], dk_n_a[...]),
+                dot_nn(n_t_a[...], dv_n_a[...]),
+                dot_nn(att_t_a[...], upstream_a[...]),
+            )
+        ):
+            partial[n] = piece
+
     attention(
-        True, read, gain, w_qkv, w_qkv_t, w_proj, mask,
+        True, earlier, read, gain, w_qkv, w_qkv_t, w_proj, mask,
         n_t, upstream, dq_t, dk_n, dv_n, att_t, *scratch,
     )
     wide = jnp.concatenate(
@@ -414,9 +418,8 @@
     even = core() == 0
 
     def store(rows, one, two):
-        one, two = one.astype(BF16), two.astype(BF16)
         keep[rows, :] = jnp.where(even, one, two)
-        send[rows, :] = jnp.where(even, two, one)
+        send[rows, :] = jnp.where(even, two, one).astype(BF16)
 
     for j in range(6):
         lanes = slice(j * 128, (j + 1) * 128)
@@ -432,7 +435,7 @@
     return pl.pallas_call(
         second_body,
         out_shape=(
-            half, half,
+            shape(F32, *half.shape), half,
             shape(F32, 2, half_rows, SHIFT, channels), shape(F32, 2, half_rows, SHIFT, 128),
             dq_t, dk_n, dv_n,
         ),
@@ -704,7 +707,8 @@
     low, high, strip = back(out_a[2:5], out_b, tokens, gain, w_qkv_t)
     rows_back = lax.ppermute(high, "row", turn(up))
     orders = bit_orders(row_extent, col_extent)
-    total = keep + lax.ppermute(send, "row", flip(row_extent, 1))
+    total = lax.ppermute(send, "row", flip(row_extent, 1)).astype(F32)
+    total = (keep + total).astype(BF16)
     steps = len(orders[0])
     for step in range(steps):
         route = [

time: 35.7 us -> 35.8 us (level)
  no operation moved by 1% of the time
where the time goes in v8:
time: 35.8 us; the launch traced here: 35.6 us
  starting transfers between devices  14.2 us (40%)
  Pallas kernels  10.4 us (29%)
  waiting for transfers between devices  10.1 us (28%)
  between operations  0.78 us (2%)
    ppermute x3, waiting for transfers between devices, on_device(): arrived = lax.ppermute(total, ('row', 'col'), route)  6.27 us
    ppermute x3, starting transfers between devices, on_device(): arrived = lax.ppermute(total, ('row', 'col'), route)  6.18 us
    ppermute x1, starting transfers between devices, on_device(): strip = lax.ppermute(strip, 'col', left)  3.65 us
    pallas_call x1, Pallas kernels, second(): pl.pallas_call(second_body, out_shape=(shape(F32, *half.shape), half, sha...  2.54 us
    ppermute x1, starting transfers between devices, on_device(): row_halo = lax.ppermute(message, 'row', up)  2.43 us
    pallas_call x1, Pallas kernels, first(): pl.pallas_call(first_body, out_shape=(block, block, shape(F32, 2 * half_r...  2.1 us
    ppermute x1, waiting for transfers between devices, on_device(): rows_back = lax.ppermute(high, 'row', turn(up))  1.48 us
    pallas_call x1, Pallas kernels, back(): pl.pallas_call(back_body, out_shape=(shape(BF16, half_rows, channels, col...  1.33 us
  transfers between devices with their start and end apart: 10, of which 8 were waited for; matrix products, arithmetic and copies ran while one was open for 0% of the time, Pallas kernels for 17%

profile of v8, /device:TPU:0, one launch (start us, length us, event | category | flops | bytes accessed | tf_op | source)
XLA Modules:
  0.0 35.6 jit_solution(13601716736059815350)
XLA Ops:
  0.6 0.0 copy-start.2
  0.6 1.1 %gather.1 = (bf16[8,192,128]{2,1,0:T(8,128)(2,1)S(1)}, f32[1,192]{1,0:T(1,128)S(1)}) custom-call(bf16[8,192,128]{2,1,0:T(8,128)(2,1)} %bitcast.5, bf16[8,192,128]{2,1,0:T(8,128)(2,1)} %bitcast.7, f32[1,192]{1,0:T(1,128)} %bitcast.9), custom_call_target="tpu_custom_call" | custom-call | tf_op jit(solution)/shard_map/gather/pallas_call | solution.py:64
  1.7 0.0 copy-start.3
  1.8 2.4 %collective-permute-start = (bf16[8,192,128]{2,1,0:T(8,128)(2,1)S(1)}, bf16[8,192,128]{2,1,0:T(8,128)(2,1)S(1)}, u32[]{:S(2)}, u32[]{:S(2)}) collective-permute-start(bf16[8,192,128]{2,1,0:T(8,128)(2,1)S(1)} %get-tuple-element.41.message), channel_id=1, source_target_pairs={{0,12},{4,0},{8,4},{12,8},{1,13},{5,1},{9,5},{13,9},{2,14},{6,2},{... | collective-permute-start | bytes 1179656 | tf_op jit(solution)/shard_map/ppermute | solution.py:696
  4.2 0.0 copy-done.2
  4.2 0.0 copy-done.3
  4.3 0.0 copy-start
  4.3 0.2 strips.1
  4.5 3.6 %collective-permute-start.1 = (bf16[8,4,192]{2,1,0:T(4,128)(2,1)S(1)}, bf16[8,4,192]{2,1,0:T(4,128)(2,1)S(1)}, u32[]{:S(2)}, u32[]{:S(2)}) collective-permute-start(bf16[8,4,192]{2,1,0:T(4,128)(2,1)S(1)} %get-tuple-element.49), channel_id=1, source_target_pairs={{0,3},{1,0},{2,1},{3,2},{4,7},{5,4},{6,5},{7,6},{8,11},{9,8},{10,9... | collective-permute-start | bytes 36872 | tf_op jit(solution)/shard_map/ppermute | solution.py:699
  8.2 0.0 copy-start.1
  8.2 0.5 %collective-permute-start.2 = (bf16[8,4,192]{2,1,0:T(4,128)(2,1)S(1)}, bf16[8,4,192]{2,1,0:T(4,128)(2,1)S(1)}, u32[]{:S(2)}, u32[]{:S(2)}) collective-permute-start(bf16[8,4,192]{2,1,0:T(4,128)(2,1)S(1)} %get-tuple-element.50), channel_id=1, source_target_pairs={{0,15},{1,12},{2,13},{3,14},{4,3},{5,0},{6,1},{7,2},{8,7},{9,4},{1... | collective-permute-start | bytes 36872 | tf_op jit(solution)/shard_map/ppermute | solution.py:700
  8.7 0.0 copy-done
  8.7 0.5 %prep.1 = (f32[4,128,192]{2,1,0:T(8,128)S(1)}, f32[4,128,192]{2,1,0:T(8,128)S(1)}, f32[4,128]{1,0:T(4,128)S(1)}, bf16[576,192]{1,0:T(8,128)(2,1)S(1)}) custom-call(bf16[8,192,128]{2,1,0:T(8,128)(2,1)S(1)} %pad_maximum_fusion.rest, bf16[192,576]{1,0:T(8,128)(2,1)S(1)} %copy-done), custom_call_target="tpu_custom_call" | custom-call | tf_op jit(solution)/shard_map/prep/pallas_call | solution.py:114
  9.2 0.3 collective-permute-done.row_halo
  9.5 0.0 copy-done.1
  9.5 2.1 %first.1 = (f32[4,128,192]{2,1,0:T(8,128)S(1)}, f32[4,128,192]{2,1,0:T(8,128)S(1)}, f32[8,128]{1,0:T(8,128)S(1)}, bf16[192,512]{1,0:T(8,128)(2,1)S(1)}, bf16[512...) custom-call(f32[4,128,192]{2,1,0:T(8,128)S(1)} %get-tuple-element.38, ...), custom_call_target="tpu_custom_call" | custom-call | tf_op jit(solution)/shard_map/first/pallas_call | solution.py:345
  11.6 0.0 collective-permute-done.1.strip.refs_13_
  11.6 0.0 collective-permute-done.2.corner.refs_14_
  11.6 2.5 %second.1 = (f32[592,128]{1,0:T(8,128)S(1)}, bf16[592,128]{1,0:T(8,128)(2,1)S(1)}, f32[2,4,4,192]{3,2,1,0:T(4,128)S(1)}, f32[2,4,4,128]{3,2,1,0:T(4,128)S(1)}, b...) custom-call(f32[4,128,192]{2,1,0:T(8,128)S(1)} %get-tuple-element.38.hat_low.refs_6_, ...), custom_call_target="tpu_custom_call" | custom-call | tf_op jit(solution)/shard_map/second/pallas_call | solution.py:435
  14.2 0.9 %collective-permute-start.5 = (bf16[592,128]{1,0:T(8,128)(2,1)S(1)}, bf16[592,128]{1,0:T(8,128)(2,1)S(1)}, u32[]{:S(2)}, u32[]{:S(2)}) collective-permute-start(bf16[592,128]{1,0:T(8,128)(2,1)S(1)} %get-tuple-element.65), channel_id=1, source_target_pairs={{0,4},{4,0},{8,12},{12,8},{1,5},{5,1},{9,13},{13,9},{2,6},{6,2},{1... | collective-permute-start | bytes 454664 | tf_op jit(solution)/shard_map/ppermute | solution.py:710
  15.1 1.0 %collective-permute-done.5 = bf16[592,128]{1,0:T(8,128)(2,1)S(1)} collective-permute-done((bf16[592,128]{1,0:T(8,128)(2,1)S(1)}, bf16[592,128]{1,0:T(8,128)(2,1)S(1)}, u32[]{:S(2)}, u32[]{:S(2)}) %collective-permute-start.5) | collective-permute-done | bytes 151584 | tf_op jit(solution)/shard_map/ppermute | solution.py:710
  16.1 1.8 %collective-permute-start.6 = (bf16[592,128]{1,0:T(8,128)(2,1)S(1)}, bf16[592,128]{1,0:T(8,128)(2,1)S(1)}, u32[]{:S(2)}, u32[]{:S(2)}) collective-permute-start(bf16[592,128]{1,0:T(8,128)(2,1)S(1)} %add_convert_fusion.a), channel_id=1, source_target_pairs={{0,1},{1,0},{2,3},{3,2},{4,12},{5,13},{6,14},{7,15},{8,9},{9,8},{1... | collective-permute-start | bytes 454664 | tf_op jit(solution)/shard_map/ppermute | solution.py:717
  17.9 1.3 %back.1 = (bf16[4,192,128]{2,1,0:T(8,128)(2,1)S(1)}, bf16[4,192,128]{2,1,0:T(8,128)(2,1)S(1)}, bf16[4,4,192]{2,1,0:T(4,128)(2,1)S(1)}) custom-call(bf16[192,512]{1,0:T(8,128)(2,1)S(1)} %get-tuple-element.44.dq_t_a.refs_0_, bf16[512,192]{1,0:T(8,128)(2,1)S(1)} %get-tuple-element.45.dk_n_a.refs_1_, bf16[512,192]{1,0:T(8,128)(2,1)S(1)} %get-tuple-element.46.dv_n_a.refs_2_, ...), custom_call_target="tpu_custom_call" | custom-call | flops 226492416 | bytes 8388608 | tf_op jit(solution)/shard_map/back/pallas_call | solution.py:509
  19.3 0.1 collective-permute-start.3
  19.3 2.0 %collective-permute-done.6.b = bf16[592,128]{1,0:T(8,128)(2,1)S(1)} collective-permute-done((bf16[592,128]{1,0:T(8,128)(2,1)S(1)}, bf16[592,128]{1,0:T(8,128)(2,1)S(1)}, u32[]{:S(2)}, u32[]{:S(2)}) %collective-permute-start.6) | collective-permute-done | bytes 151584 | tf_op jit(solution)/shard_map/ppermute | solution.py:717
  21.4 1.5 %collective-permute-start.7 = (bf16[592,128]{1,0:T(8,128)(2,1)S(1)}, bf16[592,128]{1,0:T(8,128)(2,1)S(1)}, u32[]{:S(2)}, u32[]{:S(2)}) collective-permute-start(bf16[592,128]{1,0:T(8,128)(2,1)S(1)} %add.8.a), channel_id=1, source_target_pairs={{0,8},{1,9},{2,10},{3,11},{4,6},{5,7},{6,4},{7,5},{8,0},{9,1},{10,... | collective-permute-start | bytes 454664 | tf_op jit(solution)/shard_map/ppermute | solution.py:717
  22.9 1.5 %collective-permute-done.3.rows_back.high = bf16[4,192,128]{2,1,0:T(8,128)(2,1)S(1)} collective-permute-done((bf16[4,192,128]{2,1,0:T(8,128)(2,1)S(1)}, bf16[4,192,128]{2,1,0:T(8,128)(2,1)S(1)}, u32[]{:S(2)}, u32[]{:S(2)}) %collective-permute-start.3) | collective-permute-done | bytes 196640 | tf_op jit(solution)/shard_map/ppermute | solution.py:708
  24.4 0.1 collect.1.refs_0_
  24.5 0.3 collective-permute-start.4
  24.8 1.8 %collective-permute-done.7.b = bf16[592,128]{1,0:T(8,128)(2,1)S(1)} collective-permute-done((bf16[592,128]{1,0:T(8,128)(2,1)S(1)}, bf16[592,128]{1,0:T(8,128)(2,1)S(1)}, u32[]{:S(2)}, u32[]{:S(2)}) %collective-permute-start.7) | collective-permute-done | bytes 151584 | tf_op jit(solution)/shard_map/ppermute | solution.py:717
  26.7 2.8 %collective-permute-start.8 = (bf16[592,128]{1,0:T(8,128)(2,1)S(1)}, bf16[592,128]{1,0:T(8,128)(2,1)S(1)}, u32[]{:S(2)}, u32[]{:S(2)}) collective-permute-start(bf16[592,128]{1,0:T(8,128)(2,1)S(1)} %add.9.a), channel_id=1, source_target_pairs={{0,2},{1,3},{2,0},{3,1},{4,5},{5,4},{6,7},{7,6},{8,10},{9,11},{10,... | collective-permute-start | bytes 454664 | tf_op jit(solution)/shard_map/ppermute | solution.py:717
  29.5 0.5 %collective-permute-done.4.strip = bf16[8,4,192]{2,1,0:T(4,128)(2,1)S(1)} collective-permute-done((bf16[8,4,192]{2,1,0:T(4,128)(2,1)S(1)}, bf16[8,4,192]{2,1,0:T(4,128)(2,1)S(1)}, u32[]{:S(2)}, u32[]{:S(2)}) %collective-permute-start.4) | collective-permute-done | bytes 12320 | tf_op jit(solution)/shard_map/ppermute | solution.py:723
  30.1 0.9 %join.1 = (bf16[8,192,128]{2,1,0:T(8,128)(2,1)}, f32[8,128]{1,0:T(8,128)S(1)}) custom-call(bf16[4,192,128]{2,1,0:T(8,128)(2,1)S(1)} %collective-permute-done.3.rows_back.high, bf16[4,192,128]{2,1,0:T(8,128)(2,1)S(1)} %get-tuple-element.61.low.refs_0_, bf16[8,4,192]{2,1,0:T(4,128)(2,1)S(1)} %collective-permute-done.4.strip), custom_call_target="tpu_custom_call" | custom-call | flops 4000000000 | tf_op jit(solution)/shard_map/join/pallas_call | solution.py:583
  31.0 2.4 %collective-permute-done.8.b = bf16[592,128]{1,0:T(8,128)(2,1)S(1)} collective-permute-done((bf16[592,128]{1,0:T(8,128)(2,1)S(1)}, bf16[592,128]{1,0:T(8,128)(2,1)S(1)}, u32[]{:S(2)}, u32[]{:S(2)}) %collective-permute-start.8) | collective-permute-done | bytes 151584 | tf_op jit(solution)/shard_map/ppermute | solution.py:717
  33.4 0.2 collective-permute-start.9
  33.6 0.8 %scale_own.1 = (f32[192,576]{1,0:T(8,128)}, f32[192,192]{1,0:T(8,128)}) custom-call(bf16[592,128]{1,0:T(8,128)(2,1)S(1)} %add.10.mine), custom_call_target="tpu_custom_call" | custom-call | flops 1000000000 | tf_op jit(solution)/shard_map/scale_own/pallas_call | solution.py:642
  34.4 0.5 %collective-permute-done.9.other = bf16[592,128]{1,0:T(8,128)(2,1)S(1)} collective-permute-done((bf16[592,128]{1,0:T(8,128)(2,1)S(1)}, bf16[592,128]{1,0:T(8,128)(2,1)S(1)}, u32[]{:S(2)}, u32[]{:S(2)}) %collective-permute-start.9) | collective-permute-done | bytes 151584 | tf_op jit(solution)/shard_map/ppermute | solution.py:731
  34.9 0.8 %scale_other.1 = (f32[192,576]{1,0:T(8,128)}, f32[192,192]{1,0:T(8,128)}, f32[1,192]{1,0:T(1,128)}) custom-call(bf16[592,128]{1,0:T(8,128)(2,1)S(1)} %add.10.mine, bf16[592,128]{1,0:T(8,128)(2,1)S(1)} %collective-permute-done.9.other, f32[192,576]{1,0:T(8,128)} %get-tuple-element.67.wqkv_in, ...), custom_call_target="tpu_custom_call", output_to_operand_aliasing={{0}: (2, {}), {1}: (3, {})} | custom-call | tf_op jit(solution)/shard_map/scale_other/pallas_call | solution.py:655
  (7 shorter events, 0.2 us)
Async XLA Ops:
  0.6 3.6 %copy-start.2 = (bf16[8,128,192]{1,2,0:T(8,128)(2,1)S(1)}, bf16[8,128,192]{1,2,0:T(8,128)(2,1)}, u32[]{:S(2)}) copy-start(bf16[8,128,192]{1,2,0:T(8,128)(2,1)} %param.5) | copy-start | bytes 1179652
  1.7 2.5 %copy-start.3 = (bf16[8,128,192]{1,2,0:T(8,128)(2,1)S(1)}, bf16[8,128,192]{1,2,0:T(8,128)(2,1)}, u32[]{:S(2)}) copy-start(bf16[8,128,192]{1,2,0:T(8,128)(2,1)} %param.6) | copy-start | bytes 1179652
  1.8 7.7 %collective-permute-start = (bf16[8,192,128]{2,1,0:T(8,128)(2,1)S(1)}, bf16[8,192,128]{2,1,0:T(8,128)(2,1)S(1)}, u32[]{:S(2)}, u32[]{:S(2)}) collective-permute-start(bf16[8,192,128]{2,1,0:T(8,128)(2,1)S(1)} %get-tuple-element.41.message), channel_id=1, source_target_pairs={{0,12},{4,0},{8,4},{12,8},{1,13},{5,1},{9,5},{13,9},{2,14},{6,2},{... | collective-permute-start | bytes 1179656 | tf_op jit(solution)/shard_map/ppermute | solution.py:696
  4.3 4.4 %copy-start = (bf16[192,576]{1,0:T(8,128)(2,1)S(1)}, bf16[192,576]{1,0:T(8,128)(2,1)}, u32[]{:S(2)}) copy-start(bf16[192,576]{1,0:T(8,128)(2,1)} %w_qkv.5) | copy-start | bytes 663556
  4.5 7.1 %collective-permute-start.1 = (bf16[8,4,192]{2,1,0:T(4,128)(2,1)S(1)}, bf16[8,4,192]{2,1,0:T(4,128)(2,1)S(1)}, u32[]{:S(2)}, u32[]{:S(2)}) collective-permute-start(bf16[8,4,192]{2,1,0:T(4,128)(2,1)S(1)} %get-tuple-element.49), channel_id=1, source_target_pairs={{0,3},{1,0},{2,1},{3,2},{4,7},{5,4},{6,5},{7,6},{8,11},{9,8},{10,9... | collective-permute-start | bytes 36872 | tf_op jit(solution)/shard_map/ppermute | solution.py:699
  8.2 1.3 %copy-start.1 = (bf16[192,192]{1,0:T(8,128)(2,1)S(1)}, bf16[192,192]{1,0:T(8,128)(2,1)}, u32[]{:S(2)}) copy-start(bf16[192,192]{1,0:T(8,128)(2,1)} %w_proj.3) | copy-start | bytes 221188
  8.2 3.4 %collective-permute-start.2 = (bf16[8,4,192]{2,1,0:T(4,128)(2,1)S(1)}, bf16[8,4,192]{2,1,0:T(4,128)(2,1)S(1)}, u32[]{:S(2)}, u32[]{:S(2)}) collective-permute-start(bf16[8,4,192]{2,1,0:T(4,128)(2,1)S(1)} %get-tuple-element.50), channel_id=1, source_target_pairs={{0,15},{1,12},{2,13},{3,14},{4,3},{5,0},{6,1},{7,2},{8,7},{9,4},{1... | collective-permute-start | bytes 36872 | tf_op jit(solution)/shard_map/ppermute | solution.py:700
  14.2 1.9 %collective-permute-start.5 = (bf16[592,128]{1,0:T(8,128)(2,1)S(1)}, bf16[592,128]{1,0:T(8,128)(2,1)S(1)}, u32[]{:S(2)}, u32[]{:S(2)}) collective-permute-start(bf16[592,128]{1,0:T(8,128)(2,1)S(1)} %get-tuple-element.65), channel_id=1, source_target_pairs={{0,4},{4,0},{8,12},{12,8},{1,5},{5,1},{9,13},{13,9},{2,6},{6,2},{1... | collective-permute-start | bytes 454664 | tf_op jit(solution)/shard_map/ppermute | solution.py:710
  16.1 5.3 %collective-permute-start.6 = (bf16[592,128]{1,0:T(8,128)(2,1)S(1)}, bf16[592,128]{1,0:T(8,128)(2,1)S(1)}, u32[]{:S(2)}, u32[]{:S(2)}) collective-permute-start(bf16[592,128]{1,0:T(8,128)(2,1)S(1)} %add_convert_fusion.a), channel_id=1, source_target_pairs={{0,1},{1,0},{2,3},{3,2},{4,12},{5,13},{6,14},{7,15},{8,9},{9,8},{1... | collective-permute-start | bytes 454664 | tf_op jit(solution)/shard_map/ppermute | solution.py:717
  19.3 5.1 %collective-permute-start.3 = (bf16[4,192,128]{2,1,0:T(8,128)(2,1)S(1)}, bf16[4,192,128]{2,1,0:T(8,128)(2,1)S(1)}, u32[]{:S(2)}, u32[]{:S(2)}) collective-permute-start(bf16[4,192,128]{2,1,0:T(8,128)(2,1)S(1)} %get-tuple-element.60), channel_id=1, source_target_pairs={{12,0},{0,4},{4,8},{8,12},{13,1},{1,5},{5,9},{9,13},{14,2},{2,6},{... | collective-permute-start | bytes 589832 | tf_op jit(solution)/shard_map/ppermute | solution.py:708
  21.4 5.3 %collective-permute-start.7 = (bf16[592,128]{1,0:T(8,128)(2,1)S(1)}, bf16[592,128]{1,0:T(8,128)(2,1)S(1)}, u32[]{:S(2)}, u32[]{:S(2)}) collective-permute-start(bf16[592,128]{1,0:T(8,128)(2,1)S(1)} %add.8.a), channel_id=1, source_target_pairs={{0,8},{1,9},{2,10},{3,11},{4,6},{5,7},{6,4},{7,5},{8,0},{9,1},{10,... | collective-permute-start | bytes 454664 | tf_op jit(solution)/shard_map/ppermute | solution.py:717
  24.5 5.6 %collective-permute-start.4 = (bf16[8,4,192]{2,1,0:T(4,128)(2,1)S(1)}, bf16[8,4,192]{2,1,0:T(4,128)(2,1)S(1)}, u32[]{:S(2)}, u32[]{:S(2)}) collective-permute-start(bf16[8,4,192]{2,1,0:T(4,128)(2,1)S(1)} %collect.1.refs_0_), channel_id=1, source_target_pairs={{3,0},{0,1},{1,2},{2,3},{7,4},{4,5},{5,6},{6,7},{11,8},{8,9},{9,10... | collective-permute-start | bytes 36872 | tf_op jit(solution)/shard_map/ppermute | solution.py:723
  26.7 6.7 %collective-permute-start.8 = (bf16[592,128]{1,0:T(8,128)(2,1)S(1)}, bf16[592,128]{1,0:T(8,128)(2,1)S(1)}, u32[]{:S(2)}, u32[]{:S(2)}) collective-permute-start(bf16[592,128]{1,0:T(8,128)(2,1)S(1)} %add.9.a), channel_id=1, source_target_pairs={{0,2},{1,3},{2,0},{3,1},{4,5},{5,4},{6,7},{7,6},{8,10},{9,11},{10,... | collective-permute-start | bytes 454664 | tf_op jit(solution)/shard_map/ppermute | solution.py:717
  33.4 1.4 %collective-permute-start.9 = (bf16[592,128]{1,0:T(8,128)(2,1)S(1)}, bf16[592,128]{1,0:T(8,128)(2,1)S(1)}, u32[]{:S(2)}, u32[]{:S(2)}) collective-permute-start(bf16[592,128]{1,0:T(8,128)(2,1)S(1)} %add.10.mine), channel_id=1, source_target_pairs={{0,4},{4,0},{8,12},{12,8},{1,5},{5,1},{9,13},{13,9},{2,6},{6,2},{1... | collective-permute-start | bytes 454664 | tf_op jit(solution)/shard_map/ppermute | solution.py:731

commit v9 on v8

--- a/solution.py
+++ b/solution.py
@@ -16,6 +16,7 @@
 EPSILON = 1e-05
 MASKED = -100.0
 SCALE = HEAD_DIM ** (-0.5)
+LOG2E = math.log2(math.e)
 F32 = jnp.float32
 BF16 = jnp.bfloat16
 
@@ -45,31 +46,30 @@
     return [pltpu.with_memory_space_constraint(v, pltpu.HBM) for v in arrays]
 
 
-def gather_body(x, dy, gain, out, gain_out, sems):
+def gather_body(x, dy, out, sems):
     copies = [
         pltpu.make_async_copy(
             source.at[pl.ds(0, SHIFT)], out.at[pl.ds(n * SHIFT, SHIFT)], sems.at[n]
         )
         for n, source in enumerate((x, dy))
     ]
-    copies.append(pltpu.make_async_copy(gain, gain_out, sems.at[2]))
     for copy in copies:
         copy.start()
     for copy in copies:
         copy.wait()
 
 
-def gather(x, dy, gain):
+def gather(x, dy):
     _, channels, cols = x.shape
     return pl.pallas_call(
         gather_body,
-        out_shape=(shape(BF16, 2 * SHIFT, channels, cols), shape(F32, *gain.shape)),
-        in_specs=[HBM] * 3,
-        out_specs=(VMEM, VMEM),
-        scratch_shapes=[pltpu.SemaphoreType.DMA((3,))],
+        out_shape=shape(BF16, 2 * SHIFT, channels, cols),
+        in_specs=[HBM] * 2,
+        out_specs=VMEM,
+        scratch_shapes=[pltpu.SemaphoreType.DMA((2,))],
         compiler_params=params(8),
         name="gather",
-    )(*in_hbm(x, dy, gain))
+    )(*in_hbm(x, dy))
 
 
 def strips_body(message, rest, strip, corner):
@@ -98,7 +98,9 @@
     return centred * inv, inv
 
 
-def prep_body(rest, w_qkv, hats, dys, inv, w_qkv_t):
+def prep_body(rest, w_qkv, gain, hats, dys, inv, w_qkv_t, gain_out, sem):
+    copy = pltpu.make_async_copy(gain, gain_out, sem)
+    copy.start()
     cols = rest.shape[2]
     for i in range(SHIFT):
         hat, inv_row = standard(rest[i], 0)
@@ -107,9 +109,10 @@
         line = jnp.transpose(rest[SHIFT + i])
         dys[i] = pltpu.roll(line.astype(F32), cols - SHIFT, 0)
     w_qkv_t[...] = jnp.transpose(w_qkv[...])
-
-
-def prep(rest, w_qkv):
+    copy.wait()
+
+
+def prep(rest, w_qkv, gain):
     _, channels, cols = rest.shape
     return pl.pallas_call(
         prep_body,
@@ -118,12 +121,14 @@
             shape(F32, SHIFT, cols, channels),
             shape(F32, SHIFT, cols),
             shape(BF16, w_qkv.shape[1], channels),
+            shape(F32, *gain.shape),
         ),
-        in_specs=[VMEM] * 2,
-        out_specs=(VMEM,) * 4,
+        in_specs=[VMEM] * 2 + [HBM],
+        out_specs=(VMEM,) * 5,
+        scratch_shapes=[pltpu.SemaphoreType.DMA],
         compiler_params=params(8),
         name="prep",
-    )(rest, w_qkv)
+    )(rest, w_qkv, *in_hbm(gain))
 
 
 def is_last(axis):
@@ -155,8 +160,8 @@
     col_cut = (k_pos % WINDOW >= SHIFT) != (q_pos % WINDOW >= SHIFT)
     row_mask = jnp.where(row_cut, 1.0, 0.0) * is_last("row")
     col_mask = jnp.where(col_cut, 1.0, 0.0) * is_last("col")
-    mask[0] = row_mask * MASKED
-    mask[1] = jnp.maximum(row_mask, col_mask) * MASKED
+    mask[0] = row_mask * (MASKED * LOG2E)
+    mask[1] = jnp.maximum(row_mask, col_mask) * (MASKED * LOG2E)
 
 
 def attention(
@@ -268,8 +273,8 @@
             masking = mask[1 if last and p == pairs - 1 and w == 1 else 0]
             p_units, s_units = [], []
             for j in range(HEADS // 2):
-                s = scores[w][j] * SCALE + masking
-                grown = jnp.exp(s - jnp.max(s, axis=0, keepdims=True))
+                s = scores[w][j] * (SCALE * LOG2E) + masking
+                grown = jnp.exp2(s - jnp.max(s, axis=0, keepdims=True))
                 probs = grown * (1.0 / jnp.sum(grown, axis=0, keepdims=True))
                 inner = jnp.sum(grad_probs[w][j] * probs, axis=0, keepdims=True)
                 grad_scores = probs * (grad_probs[w][j] - inner) * SCALE
@@ -692,13 +697,15 @@
     turn = lambda route: [(b, a) for a, b in route]
     swap = lambda v: jnp.transpose(v, (0, 2, 1))
     x_t, dy_t = swap(activations), swap(cotangent)
-    message, gain = gather(x_t, dy_t, norm_gain.reshape(1, channels))
+    message = gather(x_t, dy_t)
     row_halo = lax.ppermute(message, "row", up)
     rest = jnp.concatenate((x_t[SHIFT:], dy_t[SHIFT:]), axis=0)
     strip, corner = strips(message, rest)
     strip = lax.ppermute(strip, "col", left)
     corner = lax.ppermute(corner, ("row", "col"), both)
-    hat_low, dy_low, inv_low, w_qkv_t = prep(rest, w_qkv)
+    hat_low, dy_low, inv_low, w_qkv_t, gain = prep(
+        rest, w_qkv, norm_gain.reshape(1, channels)
+    )
     weights = (gain, w_qkv, w_qkv_t, w_proj)
     hat_high, dy_high, inv, *out_a = first(hat_low, dy_low, inv_low, row_halo, *weights)
     tokens = (hat_low, hat_high, dy_low, dy_high)

time: 35.8 us -> 35.7 us (level)
  transfers between devices with their start and end apart: 10 -> 10, of which waited for: 8 -> 7; matrix products, arithmetic and copies ran while one was open for 0% -> 0% of each run, Pallas kernels for 17% -> 17%
where the time goes in v9:
time: 35.7 us; the launch traced here: 35.6 us
  starting transfers between devices  14.1 us (39%)
  Pallas kernels  10.6 us (30%)
  waiting for transfers between devices  9.85 us (28%)
  between operations  0.78 us (2%)
    ppermute x3, waiting for transfers between devices, on_device(): arrived = lax.ppermute(total, ('row', 'col'), route)  6.27 us
    ppermute x3, starting transfers between devices, on_device(): arrived = lax.ppermute(total, ('row', 'col'), route)  6.17 us
    ppermute x1, starting transfers between devices, on_device(): strip = lax.ppermute(strip, 'col', left)  3.65 us
    pallas_call x1, Pallas kernels, second(): pl.pallas_call(second_body, out_shape=(shape(F32, *half.shape), half, sha...  2.52 us
    ppermute x1, starting transfers between devices, on_device(): row_halo = lax.ppermute(message, 'row', up)  2.43 us
    pallas_call x1, Pallas kernels, first(): pl.pallas_call(first_body, out_shape=(block, block, shape(F32, 2 * half_r...  2.04 us
    ppermute x1, waiting for transfers between devices, on_device(): rows_back = lax.ppermute(high, 'row', turn(up))  1.49 us
    pallas_call x1, Pallas kernels, back(): pl.pallas_call(back_body, out_shape=(shape(BF16, half_rows, channels, col...  1.33 us
  transfers between devices with their start and end apart: 10, of which 7 were waited for; matrix products, arithmetic and copies ran while one was open for 0% of the time, Pallas kernels for 17%

profile of v9, /device:TPU:0, one launch (start us, length us, event | category | flops | bytes accessed | tf_op | source)
XLA Modules:
  0.0 35.6 jit_solution(10136260611548942736)
XLA Ops:
  0.6 0.0 copy-start.2
  0.6 1.1 %gather.1.message = bf16[8,192,128]{2,1,0:T(8,128)(2,1)S(1)} custom-call(bf16[8,192,128]{2,1,0:T(8,128)(2,1)} %bitcast.5, bf16[8,192,128]{2,1,0:T(8,128)(2,1)} %bitcast.7), custom_call_target="tpu_custom_call" | custom-call | tf_op jit(solution)/shard_map/gather/pallas_call | solution.py:64
  1.7 0.0 copy-start.3
  1.7 2.4 %collective-permute-start = (bf16[8,192,128]{2,1,0:T(8,128)(2,1)S(1)}, bf16[8,192,128]{2,1,0:T(8,128)(2,1)S(1)}, u32[]{:S(2)}, u32[]{:S(2)}) collective-permute-start(bf16[8,192,128]{2,1,0:T(8,128)(2,1)S(1)} %gather.1.message), channel_id=1, source_target_pairs={{0,12},{4,0},{8,4},{12,8},{1,13},{5,1},{9,5},{13,9},{2,14},{6,2},{... | collective-permute-start | bytes 1179656 | tf_op jit(solution)/shard_map/ppermute | solution.py:701
  4.2 0.0 copy-done.2
  4.2 0.0 copy-done.3
  4.3 0.0 copy-start
  4.3 0.2 strips.1
  4.5 3.6 %collective-permute-start.1 = (bf16[8,4,192]{2,1,0:T(4,128)(2,1)S(1)}, bf16[8,4,192]{2,1,0:T(4,128)(2,1)S(1)}, u32[]{:S(2)}, u32[]{:S(2)}) collective-permute-start(bf16[8,4,192]{2,1,0:T(4,128)(2,1)S(1)} %get-tuple-element.47), channel_id=1, source_target_pairs={{0,3},{1,0},{2,1},{3,2},{4,7},{5,4},{6,5},{7,6},{8,11},{9,8},{10,9... | collective-permute-start | bytes 36872 | tf_op jit(solution)/shard_map/ppermute | solution.py:704
  8.2 0.5 %collective-permute-start.2 = (bf16[8,4,192]{2,1,0:T(4,128)(2,1)S(1)}, bf16[8,4,192]{2,1,0:T(4,128)(2,1)S(1)}, u32[]{:S(2)}, u32[]{:S(2)}) collective-permute-start(bf16[8,4,192]{2,1,0:T(4,128)(2,1)S(1)} %get-tuple-element.48), channel_id=1, source_target_pairs={{0,15},{1,12},{2,13},{3,14},{4,3},{5,0},{6,1},{7,2},{8,7},{9,4},{1... | collective-permute-start | bytes 36872 | tf_op jit(solution)/shard_map/ppermute | solution.py:705
  8.7 0.0 copy-done
  8.7 0.0 copy-start.1
  8.7 0.7 %prep.1 = (f32[4,128,192]{2,1,0:T(8,128)S(1)}, f32[4,128,192]{2,1,0:T(8,128)S(1)}, f32[4,128]{1,0:T(4,128)S(1)}, bf16[576,192]{1,0:T(8,128)(2,1)S(1)}, f32[1,192]{1,0:T(1,128)S(1)}) custom-call(bf16[8,192,128]{2,1,0:T(8,128)(2,1)S(1)} %pad_maximum_fusion.rest, bf16[192,576]{1,0:T(8,128)(2,1)S(1)} %copy-done, f32[1,192]{1,0:T(1,128)} %bitcast.9), custom_call_target="tpu_custom_call" | custom-call | tf_op jit(solution)/shard_map/prep/pallas_call | solution.py:117
  9.4 0.0 collective-permute-done.row_halo
  9.5 0.1 copy-done.1
  9.6 2.0 %first.1 = (f32[4,128,192]{2,1,0:T(8,128)S(1)}, f32[4,128,192]{2,1,0:T(8,128)S(1)}, f32[8,128]{1,0:T(8,128)S(1)}, bf16[192,512]{1,0:T(8,128)(2,1)S(1)}, bf16[512...) custom-call(f32[4,128,192]{2,1,0:T(8,128)S(1)} %get-tuple-element.37, ...), custom_call_target="tpu_custom_call" | custom-call | tf_op jit(solution)/shard_map/first/pallas_call | solution.py:350
  11.7 0.0 collective-permute-done.1.strip.refs_13_
  11.7 0.0 collective-permute-done.2.corner.refs_14_
  11.7 2.5 %second.1 = (f32[592,128]{1,0:T(8,128)S(1)}, bf16[592,128]{1,0:T(8,128)(2,1)S(1)}, f32[2,4,4,192]{3,2,1,0:T(4,128)S(1)}, f32[2,4,4,128]{3,2,1,0:T(4,128)S(1)}, b...) custom-call(f32[4,128,192]{2,1,0:T(8,128)S(1)} %get-tuple-element.37.hat_low.refs_6_, ...), custom_call_target="tpu_custom_call" | custom-call | tf_op jit(solution)/shard_map/second/pallas_call | solution.py:440
  14.2 0.8 %collective-permute-start.5 = (bf16[592,128]{1,0:T(8,128)(2,1)S(1)}, bf16[592,128]{1,0:T(8,128)(2,1)S(1)}, u32[]{:S(2)}, u32[]{:S(2)}) collective-permute-start(bf16[592,128]{1,0:T(8,128)(2,1)S(1)} %get-tuple-element.63), channel_id=1, source_target_pairs={{0,4},{4,0},{8,12},{12,8},{1,5},{5,1},{9,13},{13,9},{2,6},{6,2},{1... | collective-permute-start | bytes 454664 | tf_op jit(solution)/shard_map/ppermute | solution.py:717
  15.0 1.0 %collective-permute-done.5 = bf16[592,128]{1,0:T(8,128)(2,1)S(1)} collective-permute-done((bf16[592,128]{1,0:T(8,128)(2,1)S(1)}, bf16[592,128]{1,0:T(8,128)(2,1)S(1)}, u32[]{:S(2)}, u32[]{:S(2)}) %collective-permute-start.5) | collective-permute-done | bytes 151584 | tf_op jit(solution)/shard_map/ppermute | solution.py:717
  16.0 1.8 %collective-permute-start.6 = (bf16[592,128]{1,0:T(8,128)(2,1)S(1)}, bf16[592,128]{1,0:T(8,128)(2,1)S(1)}, u32[]{:S(2)}, u32[]{:S(2)}) collective-permute-start(bf16[592,128]{1,0:T(8,128)(2,1)S(1)} %add_convert_fusion.a), channel_id=1, source_target_pairs={{0,1},{1,0},{2,3},{3,2},{4,12},{5,13},{6,14},{7,15},{8,9},{9,8},{1... | collective-permute-start | bytes 454664 | tf_op jit(solution)/shard_map/ppermute | solution.py:724
  17.9 1.3 %back.1 = (bf16[4,192,128]{2,1,0:T(8,128)(2,1)S(1)}, bf16[4,192,128]{2,1,0:T(8,128)(2,1)S(1)}, bf16[4,4,192]{2,1,0:T(4,128)(2,1)S(1)}) custom-call(bf16[192,512]{1,0:T(8,128)(2,1)S(1)} %get-tuple-element.42.dq_t_a.refs_0_, bf16[512,192]{1,0:T(8,128)(2,1)S(1)} %get-tuple-element.43.dk_n_a.refs_1_, bf16[512,192]{1,0:T(8,128)(2,1)S(1)} %get-tuple-element.44.dv_n_a.refs_2_, ...), custom_call_target="tpu_custom_call" | custom-call | flops 226492416 | bytes 8388608 | tf_op jit(solution)/shard_map/back/pallas_call | solution.py:514
  19.2 0.1 collective-permute-start.3
  19.3 2.0 %collective-permute-done.6.b = bf16[592,128]{1,0:T(8,128)(2,1)S(1)} collective-permute-done((bf16[592,128]{1,0:T(8,128)(2,1)S(1)}, bf16[592,128]{1,0:T(8,128)(2,1)S(1)}, u32[]{:S(2)}, u32[]{:S(2)}) %collective-permute-start.6) | collective-permute-done | bytes 151584 | tf_op jit(solution)/shard_map/ppermute | solution.py:724
  21.3 1.5 %collective-permute-start.7 = (bf16[592,128]{1,0:T(8,128)(2,1)S(1)}, bf16[592,128]{1,0:T(8,128)(2,1)S(1)}, u32[]{:S(2)}, u32[]{:S(2)}) collective-permute-start(bf16[592,128]{1,0:T(8,128)(2,1)S(1)} %add.8.a), channel_id=1, source_target_pairs={{0,8},{1,9},{2,10},{3,11},{4,6},{5,7},{6,4},{7,5},{8,0},{9,1},{10,... | collective-permute-start | bytes 454664 | tf_op jit(solution)/shard_map/ppermute | solution.py:724
  22.9 1.5 %collective-permute-done.3.rows_back.high = bf16[4,192,128]{2,1,0:T(8,128)(2,1)S(1)} collective-permute-done((bf16[4,192,128]{2,1,0:T(8,128)(2,1)S(1)}, bf16[4,192,128]{2,1,0:T(8,128)(2,1)S(1)}, u32[]{:S(2)}, u32[]{:S(2)}) %collective-permute-start.3) | collective-permute-done | bytes 196640 | tf_op jit(solution)/shard_map/ppermute | solution.py:715
  24.3 0.1 collect.1.refs_0_
  24.4 0.3 collective-permute-start.4
  24.7 1.8 %collective-permute-done.7.b = bf16[592,128]{1,0:T(8,128)(2,1)S(1)} collective-permute-done((bf16[592,128]{1,0:T(8,128)(2,1)S(1)}, bf16[592,128]{1,0:T(8,128)(2,1)S(1)}, u32[]{:S(2)}, u32[]{:S(2)}) %collective-permute-start.7) | collective-permute-done | bytes 151584 | tf_op jit(solution)/shard_map/ppermute | solution.py:724
  26.6 2.8 %collective-permute-start.8 = (bf16[592,128]{1,0:T(8,128)(2,1)S(1)}, bf16[592,128]{1,0:T(8,128)(2,1)S(1)}, u32[]{:S(2)}, u32[]{:S(2)}) collective-permute-start(bf16[592,128]{1,0:T(8,128)(2,1)S(1)} %add.9.a), channel_id=1, source_target_pairs={{0,2},{1,3},{2,0},{3,1},{4,5},{5,4},{6,7},{7,6},{8,10},{9,11},{10,... | collective-permute-start | bytes 454664 | tf_op jit(solution)/shard_map/ppermute | solution.py:724
  29.5 0.5 %collective-permute-done.4.strip = bf16[8,4,192]{2,1,0:T(4,128)(2,1)S(1)} collective-permute-done((bf16[8,4,192]{2,1,0:T(4,128)(2,1)S(1)}, bf16[8,4,192]{2,1,0:T(4,128)(2,1)S(1)}, u32[]{:S(2)}, u32[]{:S(2)}) %collective-permute-start.4) | collective-permute-done | bytes 12320 | tf_op jit(solution)/shard_map/ppermute | solution.py:730
  30.0 0.9 %join.1 = (bf16[8,192,128]{2,1,0:T(8,128)(2,1)}, f32[8,128]{1,0:T(8,128)S(1)}) custom-call(bf16[4,192,128]{2,1,0:T(8,128)(2,1)S(1)} %collective-permute-done.3.rows_back.high, bf16[4,192,128]{2,1,0:T(8,128)(2,1)S(1)} %get-tuple-element.59.low.refs_0_, bf16[8,4,192]{2,1,0:T(4,128)(2,1)S(1)} %collective-permute-done.4.strip), custom_call_target="tpu_custom_call" | custom-call | flops 4000000000 | tf_op jit(solution)/shard_map/join/pallas_call | solution.py:588
  30.9 2.4 %collective-permute-done.8.b = bf16[592,128]{1,0:T(8,128)(2,1)S(1)} collective-permute-done((bf16[592,128]{1,0:T(8,128)(2,1)S(1)}, bf16[592,128]{1,0:T(8,128)(2,1)S(1)}, u32[]{:S(2)}, u32[]{:S(2)}) %collective-permute-start.8) | collective-permute-done | bytes 151584 | tf_op jit(solution)/shard_map/ppermute | solution.py:724
  33.3 0.2 collective-permute-start.9
  33.5 0.8 %scale_own.1 = (f32[192,576]{1,0:T(8,128)}, f32[192,192]{1,0:T(8,128)}) custom-call(bf16[592,128]{1,0:T(8,128)(2,1)S(1)} %add.10.mine), custom_call_target="tpu_custom_call" | custom-call | flops 1000000000 | tf_op jit(solution)/shard_map/scale_own/pallas_call | solution.py:647
  34.3 0.5 %collective-permute-done.9.other = bf16[592,128]{1,0:T(8,128)(2,1)S(1)} collective-permute-done((bf16[592,128]{1,0:T(8,128)(2,1)S(1)}, bf16[592,128]{1,0:T(8,128)(2,1)S(1)}, u32[]{:S(2)}, u32[]{:S(2)}) %collective-permute-start.9) | collective-permute-done | bytes 151584 | tf_op jit(solution)/shard_map/ppermute | solution.py:738
  34.8 0.8 %scale_other.1 = (f32[192,576]{1,0:T(8,128)}, f32[192,192]{1,0:T(8,128)}, f32[1,192]{1,0:T(1,128)}) custom-call(bf16[592,128]{1,0:T(8,128)(2,1)S(1)} %add.10.mine, bf16[592,128]{1,0:T(8,128)(2,1)S(1)} %collective-permute-done.9.other, f32[192,576]{1,0:T(8,128)} %get-tuple-element.65.wqkv_in, ...), custom_call_target="tpu_custom_call", output_to_operand_aliasing={{0}: (2, {}), {1}: (3, {})} | custom-call | tf_op jit(solution)/shard_map/scale_other/pallas_call | solution.py:660
  (7 shorter events, 0.2 us)
Async XLA Ops:
  0.6 3.6 %copy-start.2 = (bf16[8,128,192]{1,2,0:T(8,128)(2,1)S(1)}, bf16[8,128,192]{1,2,0:T(8,128)(2,1)}, u32[]{:S(2)}) copy-start(bf16[8,128,192]{1,2,0:T(8,128)(2,1)} %param.5) | copy-start | bytes 1179652
  1.7 2.5 %copy-start.3 = (bf16[8,128,192]{1,2,0:T(8,128)(2,1)S(1)}, bf16[8,128,192]{1,2,0:T(8,128)(2,1)}, u32[]{:S(2)}) copy-start(bf16[8,128,192]{1,2,0:T(8,128)(2,1)} %param.6) | copy-start | bytes 1179652
  1.7 7.7 %collective-permute-start = (bf16[8,192,128]{2,1,0:T(8,128)(2,1)S(1)}, bf16[8,192,128]{2,1,0:T(8,128)(2,1)S(1)}, u32[]{:S(2)}, u32[]{:S(2)}) collective-permute-start(bf16[8,192,128]{2,1,0:T(8,128)(2,1)S(1)} %gather.1.message), channel_id=1, source_target_pairs={{0,12},{4,0},{8,4},{12,8},{1,13},{5,1},{9,5},{13,9},{2,14},{6,2},{... | collective-permute-start | bytes 1179656 | tf_op jit(solution)/shard_map/ppermute | solution.py:701
  4.3 4.4 %copy-start = (bf16[192,576]{1,0:T(8,128)(2,1)S(1)}, bf16[192,576]{1,0:T(8,128)(2,1)}, u32[]{:S(2)}) copy-start(bf16[192,576]{1,0:T(8,128)(2,1)} %w_qkv.5) | copy-start | bytes 663556
  4.5 7.1 %collective-permute-start.1 = (bf16[8,4,192]{2,1,0:T(4,128)(2,1)S(1)}, bf16[8,4,192]{2,1,0:T(4,128)(2,1)S(1)}, u32[]{:S(2)}, u32[]{:S(2)}) collective-permute-start(bf16[8,4,192]{2,1,0:T(4,128)(2,1)S(1)} %get-tuple-element.47), channel_id=1, source_target_pairs={{0,3},{1,0},{2,1},{3,2},{4,7},{5,4},{6,5},{7,6},{8,11},{9,8},{10,9... | collective-permute-start | bytes 36872 | tf_op jit(solution)/shard_map/ppermute | solution.py:704
  8.2 3.5 %collective-permute-start.2 = (bf16[8,4,192]{2,1,0:T(4,128)(2,1)S(1)}, bf16[8,4,192]{2,1,0:T(4,128)(2,1)S(1)}, u32[]{:S(2)}, u32[]{:S(2)}) collective-permute-start(bf16[8,4,192]{2,1,0:T(4,128)(2,1)S(1)} %get-tuple-element.48), channel_id=1, source_target_pairs={{0,15},{1,12},{2,13},{3,14},{4,3},{5,0},{6,1},{7,2},{8,7},{9,4},{1... | collective-permute-start | bytes 36872 | tf_op jit(solution)/shard_map/ppermute | solution.py:705
  8.7 0.9 %copy-start.1 = (bf16[192,192]{1,0:T(8,128)(2,1)S(1)}, bf16[192,192]{1,0:T(8,128)(2,1)}, u32[]{:S(2)}) copy-start(bf16[192,192]{1,0:T(8,128)(2,1)} %w_proj.3) | copy-start | bytes 221188
  14.2 1.8 %collective-permute-start.5 = (bf16[592,128]{1,0:T(8,128)(2,1)S(1)}, bf16[592,128]{1,0:T(8,128)(2,1)S(1)}, u32[]{:S(2)}, u32[]{:S(2)}) collective-permute-start(bf16[592,128]{1,0:T(8,128)(2,1)S(1)} %get-tuple-element.63), channel_id=1, source_target_pairs={{0,4},{4,0},{8,12},{12,8},{1,5},{5,1},{9,13},{13,9},{2,6},{6,2},{1... | collective-permute-start | bytes 454664 | tf_op jit(solution)/shard_map/ppermute | solution.py:717
  16.0 5.3 %collective-permute-start.6 = (bf16[592,128]{1,0:T(8,128)(2,1)S(1)}, bf16[592,128]{1,0:T(8,128)(2,1)S(1)}, u32[]{:S(2)}, u32[]{:S(2)}) collective-permute-start(bf16[592,128]{1,0:T(8,128)(2,1)S(1)} %add_convert_fusion.a), channel_id=1, source_target_pairs={{0,1},{1,0},{2,3},{3,2},{4,12},{5,13},{6,14},{7,15},{8,9},{9,8},{1... | collective-permute-start | bytes 454664 | tf_op jit(solution)/shard_map/ppermute | solution.py:724
  19.2 5.1 %collective-permute-start.3 = (bf16[4,192,128]{2,1,0:T(8,128)(2,1)S(1)}, bf16[4,192,128]{2,1,0:T(8,128)(2,1)S(1)}, u32[]{:S(2)}, u32[]{:S(2)}) collective-permute-start(bf16[4,192,128]{2,1,0:T(8,128)(2,1)S(1)} %get-tuple-element.58), channel_id=1, source_target_pairs={{12,0},{0,4},{4,8},{8,12},{13,1},{1,5},{5,9},{9,13},{14,2},{2,6},{... | collective-permute-start | bytes 589832 | tf_op jit(solution)/shard_map/ppermute | solution.py:715
  21.3 5.3 %collective-permute-start.7 = (bf16[592,128]{1,0:T(8,128)(2,1)S(1)}, bf16[592,128]{1,0:T(8,128)(2,1)S(1)}, u32[]{:S(2)}, u32[]{:S(2)}) collective-permute-start(bf16[592,128]{1,0:T(8,128)(2,1)S(1)} %add.8.a), channel_id=1, source_target_pairs={{0,8},{1,9},{2,10},{3,11},{4,6},{5,7},{6,4},{7,5},{8,0},{9,1},{10,... | collective-permute-start | bytes 454664 | tf_op jit(solution)/shard_map/ppermute | solution.py:724
  24.4 5.6 %collective-permute-start.4 = (bf16[8,4,192]{2,1,0:T(4,128)(2,1)S(1)}, bf16[8,4,192]{2,1,0:T(4,128)(2,1)S(1)}, u32[]{:S(2)}, u32[]{:S(2)}) collective-permute-start(bf16[8,4,192]{2,1,0:T(4,128)(2,1)S(1)} %collect.1.refs_0_), channel_id=1, source_target_pairs={{3,0},{0,1},{1,2},{2,3},{7,4},{4,5},{5,6},{6,7},{11,8},{8,9},{9,10... | collective-permute-start | bytes 36872 | tf_op jit(solution)/shard_map/ppermute | solution.py:730
  26.6 6.7 %collective-permute-start.8 = (bf16[592,128]{1,0:T(8,128)(2,1)S(1)}, bf16[592,128]{1,0:T(8,128)(2,1)S(1)}, u32[]{:S(2)}, u32[]{:S(2)}) collective-permute-start(bf16[592,128]{1,0:T(8,128)(2,1)S(1)} %add.9.a), channel_id=1, source_target_pairs={{0,2},{1,3},{2,0},{3,1},{4,5},{5,4},{6,7},{7,6},{8,10},{9,11},{10,... | collective-permute-start | bytes 454664 | tf_op jit(solution)/shard_map/ppermute | solution.py:724
  33.3 1.4 %collective-permute-start.9 = (bf16[592,128]{1,0:T(8,128)(2,1)S(1)}, bf16[592,128]{1,0:T(8,128)(2,1)S(1)}, u32[]{:S(2)}, u32[]{:S(2)}) collective-permute-start(bf16[592,128]{1,0:T(8,128)(2,1)S(1)} %add.10.mine), channel_id=1, source_target_pairs={{0,4},{4,0},{8,12},{12,8},{1,5},{5,1},{9,13},{13,9},{2,6},{6,2},{1... | collective-permute-start | bytes 454664 | tf_op jit(solution)/shard_map/ppermute | solution.py:738

commit v10 on v9

--- a/solution.py
+++ b/solution.py
@@ -46,12 +46,10 @@
     return [pltpu.with_memory_space_constraint(v, pltpu.HBM) for v in arrays]
 
 
-def gather_body(x, dy, out, sems):
+def gather_body(x, dy, x_out, dy_out, sems):
     copies = [
-        pltpu.make_async_copy(
-            source.at[pl.ds(0, SHIFT)], out.at[pl.ds(n * SHIFT, SHIFT)], sems.at[n]
-        )
-        for n, source in enumerate((x, dy))
+        pltpu.make_async_copy(source.at[pl.ds(0, SHIFT)], dest, sems.at[n])
+        for n, (source, dest) in enumerate(((x, x_out), (dy, dy_out)))
     ]
     for copy in copies:
         copy.start()
@@ -61,34 +59,35 @@
 
 def gather(x, dy):
     _, channels, cols = x.shape
+    out = shape(BF16, SHIFT, channels, cols)
     return pl.pallas_call(
         gather_body,
-        out_shape=shape(BF16, 2 * SHIFT, channels, cols),
+        out_shape=(out, out),
         in_specs=[HBM] * 2,
-        out_specs=VMEM,
+        out_specs=(VMEM, VMEM),
         scratch_shapes=[pltpu.SemaphoreType.DMA((2,))],
         compiler_params=params(8),
         name="gather",
     )(*in_hbm(x, dy))
 
 
-def strips_body(message, rest, strip, corner):
+def strips_body(x_rows, dy_rows, rest, strip, corner):
     for i in range(2 * SHIFT):
-        corner[i] = jnp.transpose(message[i])[:SHIFT]
+        corner[i] = jnp.transpose((x_rows, dy_rows)[i // SHIFT][i % SHIFT])[:SHIFT]
         strip[i] = jnp.transpose(rest[i])[:SHIFT]
 
 
-def strips(message, rest):
+def strips(x_rows, dy_rows, rest):
     _, channels, cols = rest.shape
     out = shape(BF16, 2 * SHIFT, SHIFT, channels)
     return pl.pallas_call(
         strips_body,
         out_shape=(out, out),
-        in_specs=[VMEM] * 2,
+        in_specs=[VMEM] * 3,
         out_specs=(VMEM,) * 2,
         compiler_params=params(8),
         name="strips",
-    )(message, rest)
+    )(x_rows, dy_rows, rest)
 
 
 def standard(v, axis):
@@ -327,35 +326,35 @@
     return [flat, turned, turned, turned, turned, flat, flat, padded, padded]
 
 
-def first_body(hat_low, dy_low, inv_low, row_halo, gain, w_qkv, w_qkv_t, w_proj, *refs):
+def first_body(hat_low, dy_low, inv_low, x_halo, dy_halo, gain, w_qkv, w_qkv_t, w_proj, *refs):
     hat_high, dy_high, inv, *refs = refs
     outs, mask, scratch = refs[:6], refs[6], refs[7:]
     half_rows, cols, channels = hat_low.shape
     inv[:half_rows, :] = inv_low[...]
     for i in range(half_rows):
-        hat, inv_row = standard(row_halo[i], 0)
+        hat, inv_row = standard(x_halo[i], 0)
         inv[half_rows + i : half_rows + i + 1, :] = inv_row
         hat_high[i] = pltpu.roll(jnp.transpose(hat), cols - SHIFT, 0)
-        dy = jnp.transpose(row_halo[half_rows + i]).astype(F32)
+        dy = jnp.transpose(dy_halo[i]).astype(F32)
         dy_high[i] = pltpu.roll(dy, cols - SHIFT, 0)
     write_masks(mask)
     read = lambda w: (window(hat_low, hat_high, w), window(dy_low, dy_high, w))
     attention(False, None, read, gain, w_qkv, w_qkv_t, w_proj, mask, *outs, *scratch)
 
 
-def first(hat_low, dy_low, inv_low, row_halo, gain, w_qkv, w_qkv_t, w_proj):
+def first(hat_low, dy_low, inv_low, x_halo, dy_halo, gain, w_qkv, w_qkv_t, w_proj):
     half_rows, cols, channels = hat_low.shape
     sizes = (cols // 2, 2 * half_rows, channels)
     block = shape(F32, *hat_low.shape)
     return pl.pallas_call(
         first_body,
         out_shape=(block, block, shape(F32, 2 * half_rows, cols)) + attention_outs(*sizes),
-        in_specs=[VMEM] * 8,
+        in_specs=[VMEM] * 9,
         out_specs=(VMEM,) * 9,
         scratch_shapes=[pltpu.VMEM((2, PAIR // 2, PAIR), F32)] + attention_scratch(*sizes),
         compiler_params=params(24),
         name="first",
-    )(hat_low, dy_low, inv_low, row_halo, gain, w_qkv, w_qkv_t, w_proj)
+    )(hat_low, dy_low, inv_low, x_halo, dy_halo, gain, w_qkv, w_qkv_t, w_proj)
 
 
 def second_body(
@@ -697,17 +696,18 @@
     turn = lambda route: [(b, a) for a, b in route]
     swap = lambda v: jnp.transpose(v, (0, 2, 1))
     x_t, dy_t = swap(activations), swap(cotangent)
-    message = gather(x_t, dy_t)
-    row_halo = lax.ppermute(message, "row", up)
+    x_rows, dy_rows = gather(x_t, dy_t)
+    x_halo = lax.ppermute(x_rows, "row", up)
+    dy_halo = lax.ppermute(dy_rows, "row", up)
     rest = jnp.concatenate((x_t[SHIFT:], dy_t[SHIFT:]), axis=0)
-    strip, corner = strips(message, rest)
+    strip, corner = strips(x_rows, dy_rows, rest)
     strip = lax.ppermute(strip, "col", left)
     corner = lax.ppermute(corner, ("row", "col"), both)
     hat_low, dy_low, inv_low, w_qkv_t, gain = prep(
         rest, w_qkv, norm_gain.reshape(1, channels)
     )
     weights = (gain, w_qkv, w_qkv_t, w_proj)
-    hat_high, dy_high, inv, *out_a = first(hat_low, dy_low, inv_low, row_halo, *weights)
+    hat_high, dy_high, inv, *out_a = first(hat_low, dy_low, inv_low, x_halo, dy_halo, *weights)
     tokens = (hat_low, hat_high, dy_low, dy_high)
     keep, send, hat_tail, inv_tail, *out_b = second(*tokens, strip, corner, *weights, *out_a)
     tokens += (hat_tail, inv_tail, inv, strip, corner)

time: 35.7 us -> 36 us (level)
  waiting for transfers between devices: 9.85 us -> 10.6 us
  starting transfers between devices: 14.1 us -> 13.6 us
    ppermute x1 -> x2, starting transfers between devices: 2.43 us -> 3.1 us  [the longest x1 2.43 us: on_device(): x_halo = lax.ppermute(x_rows, 'row', up)]
    ppermute x1, starting transfers between devices: 0.52 us -> 0.01 us  [on_device(): corner = lax.ppermute(corner, ('row', 'col'), both)]
    ppermute x1, starting transfers between devices: 0.78 us -> 0.37 us  [on_device(): total = lax.ppermute(send, 'row', flip(row_extent, 1)).astype(F32)]
    ppermute x3, starting transfers between devices: 6.17 us -> 5.81 us  [on_device(): arrived = lax.ppermute(total, ('row', 'col'), route)]
    ppermute x3, waiting for transfers between devices: 6.27 us -> 6.64 us  [on_device(): arrived = lax.ppermute(total, ('row', 'col'), route)]
  transfers between devices with their start and end apart: 10 -> 11, of which waited for: 7 -> 8; matrix products, arithmetic and copies ran while one was open for 0% -> 0% of each run, Pallas kernels for 17% -> 17%
where the time goes in v10:
time: 36 us; the launch traced here: 35.8 us
  starting transfers between devices  13.6 us (38%)
  Pallas kernels  10.6 us (29%)
  waiting for transfers between devices  10.6 us (29%)
  between operations  0.79 us (2%)
    ppermute x3, waiting for transfers between devices, on_device(): arrived = lax.ppermute(total, ('row', 'col'), route)  6.64 us
    ppermute x3, starting transfers between devices, on_device(): arrived = lax.ppermute(total, ('row', 'col'), route)  5.81 us
    ppermute x1, starting transfers between devices, on_device(): strip = lax.ppermute(strip, 'col', left)  3.65 us
    pallas_call x1, Pallas kernels, second(): pl.pallas_call(second_body, out_shape=(shape(F32, *half.shape), half, sha...  2.51 us
    ppermute x1, starting transfers between devices, on_device(): x_halo = lax.ppermute(x_rows, 'row', up)  2.43 us
    pallas_call x1, Pallas kernels, first(): pl.pallas_call(first_body, out_shape=(block, block, shape(F32, 2 * half_r...  2.04 us
    ppermute x1, waiting for transfers between devices, on_device(): rows_back = lax.ppermute(high, 'row', turn(up))  1.49 us
    pallas_call x1, Pallas kernels, back(): pl.pallas_call(back_body, out_shape=(shape(BF16, half_rows, channels, col...  1.34 us
  transfers between devices with their start and end apart: 11, of which 8 were waited for; matrix products, arithmetic and copies ran while one was open for 0% of the time, Pallas kernels for 17%

profile of v10, /device:TPU:0, one launch (start us, length us, event | category | flops | bytes accessed | tf_op | source)
XLA Modules:
  0.0 35.8 jit_solution(11925777140016132146)
XLA Ops:
  0.6 0.0 copy-start.2
  0.6 1.1 %gather.1 = (bf16[4,192,128]{2,1,0:T(8,128)(2,1)S(1)}, bf16[4,192,128]{2,1,0:T(8,128)(2,1)S(1)}) custom-call(bf16[8,192,128]{2,1,0:T(8,128)(2,1)} %bitcast.5, bf16[8,192,128]{2,1,0:T(8,128)(2,1)} %bitcast.7), custom_call_target="tpu_custom_call" | custom-call | tf_op jit(solution)/shard_map/gather/pallas_call | solution.py:63
  1.7 0.0 copy-start.3
  1.7 2.4 %collective-permute-start = (bf16[4,192,128]{2,1,0:T(8,128)(2,1)S(1)}, bf16[4,192,128]{2,1,0:T(8,128)(2,1)S(1)}, u32[]{:S(2)}, u32[]{:S(2)}) collective-permute-start(bf16[4,192,128]{2,1,0:T(8,128)(2,1)S(1)} %get-tuple-element.42.x_rows), channel_id=1, source_target_pairs={{0,12},{4,0},{8,4},{12,8},{1,13},{5,1},{9,5},{13,9},{2,14},{6,2},{... | collective-permute-start | bytes 589832 | tf_op jit(solution)/shard_map/ppermute | solution.py:700
  4.2 0.7 %collective-permute-start.1 = (bf16[4,192,128]{2,1,0:T(8,128)(2,1)S(1)}, bf16[4,192,128]{2,1,0:T(8,128)(2,1)S(1)}, u32[]{:S(2)}, u32[]{:S(2)}) collective-permute-start(bf16[4,192,128]{2,1,0:T(8,128)(2,1)S(1)} %get-tuple-element.43.dy_rows), channel_id=1, source_target_pairs={{0,12},{4,0},{8,4},{12,8},{1,13},{5,1},{9,5},{13,9},{2,14},{6,2},{... | collective-permute-start | bytes 589832 | tf_op jit(solution)/shard_map/ppermute | solution.py:701
  4.9 0.0 copy-done.2
  4.9 0.0 copy-done.3
  5.0 0.0 copy-start
  5.0 0.2 strips.1
  5.2 3.6 %collective-permute-start.2 = (bf16[8,4,192]{2,1,0:T(4,128)(2,1)S(1)}, bf16[8,4,192]{2,1,0:T(4,128)(2,1)S(1)}, u32[]{:S(2)}, u32[]{:S(2)}) collective-permute-start(bf16[8,4,192]{2,1,0:T(4,128)(2,1)S(1)} %get-tuple-element.51), channel_id=1, source_target_pairs={{0,3},{1,0},{2,1},{3,2},{4,7},{5,4},{6,5},{7,6},{8,11},{9,8},{10,9... | collective-permute-start | bytes 36872 | tf_op jit(solution)/shard_map/ppermute | solution.py:704
  8.8 0.0 collective-permute-start.3
  8.9 0.0 copy-done
  8.9 0.0 copy-start.1
  8.9 0.7 %prep.1 = (f32[4,128,192]{2,1,0:T(8,128)S(1)}, f32[4,128,192]{2,1,0:T(8,128)S(1)}, f32[4,128]{1,0:T(4,128)S(1)}, bf16[576,192]{1,0:T(8,128)(2,1)S(1)}, f32[1,192]{1,0:T(1,128)S(1)}) custom-call(bf16[8,192,128]{2,1,0:T(8,128)(2,1)S(1)} %pad_maximum_fusion.rest, bf16[192,576]{1,0:T(8,128)(2,1)S(1)} %copy-done, f32[1,192]{1,0:T(1,128)} %bitcast.9), custom_call_target="tpu_custom_call" | custom-call | tf_op jit(solution)/shard_map/prep/pallas_call | solution.py:116
  9.6 0.0 collective-permute-done.x_halo
  9.6 0.0 collective-permute-done.1.dy_halo
  9.6 0.2 copy-done.1
  9.8 2.0 %first.1 = (f32[4,128,192]{2,1,0:T(8,128)S(1)}, f32[4,128,192]{2,1,0:T(8,128)S(1)}, f32[8,128]{1,0:T(8,128)S(1)}, bf16[192,512]{1,0:T(8,128)(2,1)S(1)}, bf16[512...) custom-call(f32[4,128,192]{2,1,0:T(8,128)S(1)} %get-tuple-element.39, ...), custom_call_target="tpu_custom_call" | custom-call | tf_op jit(solution)/shard_map/first/pallas_call | solution.py:349
  11.8 0.0 collective-permute-done.2.strip.refs_13_
  11.8 0.3 collective-permute-done.3.corner.refs_14_
  12.2 2.5 %second.1 = (f32[592,128]{1,0:T(8,128)S(1)}, bf16[592,128]{1,0:T(8,128)(2,1)S(1)}, f32[2,4,4,192]{3,2,1,0:T(4,128)S(1)}, f32[2,4,4,128]{3,2,1,0:T(4,128)S(1)}, b...) custom-call(f32[4,128,192]{2,1,0:T(8,128)S(1)} %get-tuple-element.39.hat_low.refs_6_, ...), custom_call_target="tpu_custom_call" | custom-call | tf_op jit(solution)/shard_map/second/pallas_call | solution.py:439
  14.7 0.4 %collective-permute-start.6 = (bf16[592,128]{1,0:T(8,128)(2,1)S(1)}, bf16[592,128]{1,0:T(8,128)(2,1)S(1)}, u32[]{:S(2)}, u32[]{:S(2)}) collective-permute-start(bf16[592,128]{1,0:T(8,128)(2,1)S(1)} %get-tuple-element.67), channel_id=1, source_target_pairs={{0,4},{4,0},{8,12},{12,8},{1,5},{5,1},{9,13},{13,9},{2,6},{6,2},{1... | collective-permute-start | bytes 454664 | tf_op jit(solution)/shard_map/ppermute | solution.py:717
  15.0 1.1 %collective-permute-done.6 = bf16[592,128]{1,0:T(8,128)(2,1)S(1)} collective-permute-done((bf16[592,128]{1,0:T(8,128)(2,1)S(1)}, bf16[592,128]{1,0:T(8,128)(2,1)S(1)}, u32[]{:S(2)}, u32[]{:S(2)}) %collective-permute-start.6) | collective-permute-done | bytes 151584 | tf_op jit(solution)/shard_map/ppermute | solution.py:717
  16.2 1.7 %collective-permute-start.7 = (bf16[592,128]{1,0:T(8,128)(2,1)S(1)}, bf16[592,128]{1,0:T(8,128)(2,1)S(1)}, u32[]{:S(2)}, u32[]{:S(2)}) collective-permute-start(bf16[592,128]{1,0:T(8,128)(2,1)S(1)} %add_convert_fusion.a), channel_id=1, source_target_pairs={{0,1},{1,0},{2,3},{3,2},{4,12},{5,13},{6,14},{7,15},{8,9},{9,8},{1... | collective-permute-start | bytes 454664 | tf_op jit(solution)/shard_map/ppermute | solution.py:724
  17.9 1.3 %back.1 = (bf16[4,192,128]{2,1,0:T(8,128)(2,1)S(1)}, bf16[4,192,128]{2,1,0:T(8,128)(2,1)S(1)}, bf16[4,4,192]{2,1,0:T(4,128)(2,1)S(1)}) custom-call(bf16[192,512]{1,0:T(8,128)(2,1)S(1)} %get-tuple-element.46.dq_t_a.refs_0_, bf16[512,192]{1,0:T(8,128)(2,1)S(1)} %get-tuple-element.47.dk_n_a.refs_1_, bf16[512,192]{1,0:T(8,128)(2,1)S(1)} %get-tuple-element.48.dv_n_a.refs_2_, ...), custom_call_target="tpu_custom_call" | custom-call | flops 226492416 | bytes 8388608 | tf_op jit(solution)/shard_map/back/pallas_call | solution.py:513
  19.2 0.1 collective-permute-start.4
  19.3 2.2 %collective-permute-done.7.b = bf16[592,128]{1,0:T(8,128)(2,1)S(1)} collective-permute-done((bf16[592,128]{1,0:T(8,128)(2,1)S(1)}, bf16[592,128]{1,0:T(8,128)(2,1)S(1)}, u32[]{:S(2)}, u32[]{:S(2)}) %collective-permute-start.7) | collective-permute-done | bytes 151584 | tf_op jit(solution)/shard_map/ppermute | solution.py:724
  21.5 1.4 %collective-permute-start.8 = (bf16[592,128]{1,0:T(8,128)(2,1)S(1)}, bf16[592,128]{1,0:T(8,128)(2,1)S(1)}, u32[]{:S(2)}, u32[]{:S(2)}) collective-permute-start(bf16[592,128]{1,0:T(8,128)(2,1)S(1)} %add.8.a), channel_id=1, source_target_pairs={{0,8},{1,9},{2,10},{3,11},{4,6},{5,7},{6,4},{7,5},{8,0},{9,1},{10,... | collective-permute-start | bytes 454664 | tf_op jit(solution)/shard_map/ppermute | solution.py:724
  22.9 1.5 %collective-permute-done.4.rows_back.high = bf16[4,192,128]{2,1,0:T(8,128)(2,1)S(1)} collective-permute-done((bf16[4,192,128]{2,1,0:T(8,128)(2,1)S(1)}, bf16[4,192,128]{2,1,0:T(8,128)(2,1)S(1)}, u32[]{:S(2)}, u32[]{:S(2)}) %collective-permute-start.4) | collective-permute-done | bytes 196640 | tf_op jit(solution)/shard_map/ppermute | solution.py:715
  24.3 0.1 collect.1.refs_0_
  24.4 0.4 %collective-permute-start.5 = (bf16[8,4,192]{2,1,0:T(4,128)(2,1)S(1)}, bf16[8,4,192]{2,1,0:T(4,128)(2,1)S(1)}, u32[]{:S(2)}, u32[]{:S(2)}) collective-permute-start(bf16[8,4,192]{2,1,0:T(4,128)(2,1)S(1)} %collect.1.refs_0_), channel_id=1, source_target_pairs={{3,0},{0,1},{1,2},{2,3},{7,4},{4,5},{5,6},{6,7},{11,8},{8,9},{9,10... | collective-permute-start | bytes 36872 | tf_op jit(solution)/shard_map/ppermute | solution.py:730
  24.9 1.8 %collective-permute-done.8.b = bf16[592,128]{1,0:T(8,128)(2,1)S(1)} collective-permute-done((bf16[592,128]{1,0:T(8,128)(2,1)S(1)}, bf16[592,128]{1,0:T(8,128)(2,1)S(1)}, u32[]{:S(2)}, u32[]{:S(2)}) %collective-permute-start.8) | collective-permute-done | bytes 151584 | tf_op jit(solution)/shard_map/ppermute | solution.py:724
  26.8 2.7 %collective-permute-start.9 = (bf16[592,128]{1,0:T(8,128)(2,1)S(1)}, bf16[592,128]{1,0:T(8,128)(2,1)S(1)}, u32[]{:S(2)}, u32[]{:S(2)}) collective-permute-start(bf16[592,128]{1,0:T(8,128)(2,1)S(1)} %add.9.a), channel_id=1, source_target_pairs={{0,2},{1,3},{2,0},{3,1},{4,5},{5,4},{6,7},{7,6},{8,10},{9,11},{10,... | collective-permute-start | bytes 454664 | tf_op jit(solution)/shard_map/ppermute | solution.py:724
  29.5 0.5 %collective-permute-done.5.strip = bf16[8,4,192]{2,1,0:T(4,128)(2,1)S(1)} collective-permute-done((bf16[8,4,192]{2,1,0:T(4,128)(2,1)S(1)}, bf16[8,4,192]{2,1,0:T(4,128)(2,1)S(1)}, u32[]{:S(2)}, u32[]{:S(2)}) %collective-permute-start.5) | collective-permute-done | bytes 12320 | tf_op jit(solution)/shard_map/ppermute | solution.py:730
  30.0 0.9 %join.1 = (bf16[8,192,128]{2,1,0:T(8,128)(2,1)}, f32[8,128]{1,0:T(8,128)S(1)}) custom-call(bf16[4,192,128]{2,1,0:T(8,128)(2,1)S(1)} %collective-permute-done.4.rows_back.high, bf16[4,192,128]{2,1,0:T(8,128)(2,1)S(1)} %get-tuple-element.63.low.refs_0_, bf16[8,4,192]{2,1,0:T(4,128)(2,1)S(1)} %collective-permute-done.5.strip), custom_call_target="tpu_custom_call" | custom-call | flops 4000000000 | tf_op jit(solution)/shard_map/join/pallas_call | solution.py:587
  30.9 2.6 %collective-permute-done.9.b = bf16[592,128]{1,0:T(8,128)(2,1)S(1)} collective-permute-done((bf16[592,128]{1,0:T(8,128)(2,1)S(1)}, bf16[592,128]{1,0:T(8,128)(2,1)S(1)}, u32[]{:S(2)}, u32[]{:S(2)}) %collective-permute-start.9) | collective-permute-done | bytes 151584 | tf_op jit(solution)/shard_map/ppermute | solution.py:724
  33.6 0.2 collective-permute-start.10
  33.8 0.8 %scale_own.1 = (f32[192,576]{1,0:T(8,128)}, f32[192,192]{1,0:T(8,128)}) custom-call(bf16[592,128]{1,0:T(8,128)(2,1)S(1)} %add.10.mine), custom_call_target="tpu_custom_call" | custom-call | flops 1000000000 | tf_op jit(solution)/shard_map/scale_own/pallas_call | solution.py:646
  34.5 0.5 %collective-permute-done.10.other = bf16[592,128]{1,0:T(8,128)(2,1)S(1)} collective-permute-done((bf16[592,128]{1,0:T(8,128)(2,1)S(1)}, bf16[592,128]{1,0:T(8,128)(2,1)S(1)}, u32[]{:S(2)}, u32[]{:S(2)}) %collective-permute-start.10) | collective-permute-done | bytes 151584 | tf_op jit(solution)/shard_map/ppermute | solution.py:738
  35.0 0.8 %scale_other.1 = (f32[192,576]{1,0:T(8,128)}, f32[192,192]{1,0:T(8,128)}, f32[1,192]{1,0:T(1,128)}) custom-call(bf16[592,128]{1,0:T(8,128)(2,1)S(1)} %add.10.mine, bf16[592,128]{1,0:T(8,128)(2,1)S(1)} %collective-permute-done.10.other, f32[192,576]{1,0:T(8,128)} %get-tuple-element.69.wqkv_in, ...), custom_call_target="tpu_custom_call", output_to_operand_aliasing={{0}: (2, {}), {1}: (3, {})} | custom-call | tf_op jit(solution)/shard_map/scale_other/pallas_call | solution.py:659
  (7 shorter events, 0.2 us)
Async XLA Ops:
  0.6 4.2 %copy-start.2 = (bf16[8,128,192]{1,2,0:T(8,128)(2,1)S(1)}, bf16[8,128,192]{1,2,0:T(8,128)(2,1)}, u32[]{:S(2)}) copy-start(bf16[8,128,192]{1,2,0:T(8,128)(2,1)} %param.5) | copy-start | bytes 1179652
  1.7 3.1 %copy-start.3 = (bf16[8,128,192]{1,2,0:T(8,128)(2,1)S(1)}, bf16[8,128,192]{1,2,0:T(8,128)(2,1)}, u32[]{:S(2)}) copy-start(bf16[8,128,192]{1,2,0:T(8,128)(2,1)} %param.6) | copy-start | bytes 1179652
  1.7 7.8 %collective-permute-start = (bf16[4,192,128]{2,1,0:T(8,128)(2,1)S(1)}, bf16[4,192,128]{2,1,0:T(8,128)(2,1)S(1)}, u32[]{:S(2)}, u32[]{:S(2)}) collective-permute-start(bf16[4,192,128]{2,1,0:T(8,128)(2,1)S(1)} %get-tuple-element.42.x_rows), channel_id=1, source_target_pairs={{0,12},{4,0},{8,4},{12,8},{1,13},{5,1},{9,5},{13,9},{2,14},{6,2},{... | collective-permute-start | bytes 589832 | tf_op jit(solution)/shard_map/ppermute | solution.py:700
  4.2 5.4 %collective-permute-start.1 = (bf16[4,192,128]{2,1,0:T(8,128)(2,1)S(1)}, bf16[4,192,128]{2,1,0:T(8,128)(2,1)S(1)}, u32[]{:S(2)}, u32[]{:S(2)}) collective-permute-start(bf16[4,192,128]{2,1,0:T(8,128)(2,1)S(1)} %get-tuple-element.43.dy_rows), channel_id=1, source_target_pairs={{0,12},{4,0},{8,4},{12,8},{1,13},{5,1},{9,5},{13,9},{2,14},{6,2},{... | collective-permute-start | bytes 589832 | tf_op jit(solution)/shard_map/ppermute | solution.py:701
  5.0 3.9 %copy-start = (bf16[192,576]{1,0:T(8,128)(2,1)S(1)}, bf16[192,576]{1,0:T(8,128)(2,1)}, u32[]{:S(2)}) copy-start(bf16[192,576]{1,0:T(8,128)(2,1)} %w_qkv.5) | copy-start | bytes 663556
  5.2 6.6 %collective-permute-start.2 = (bf16[8,4,192]{2,1,0:T(4,128)(2,1)S(1)}, bf16[8,4,192]{2,1,0:T(4,128)(2,1)S(1)}, u32[]{:S(2)}, u32[]{:S(2)}) collective-permute-start(bf16[8,4,192]{2,1,0:T(4,128)(2,1)S(1)} %get-tuple-element.51), channel_id=1, source_target_pairs={{0,3},{1,0},{2,1},{3,2},{4,7},{5,4},{6,5},{7,6},{8,11},{9,8},{10,9... | collective-permute-start | bytes 36872 | tf_op jit(solution)/shard_map/ppermute | solution.py:704
  8.8 3.3 %collective-permute-start.3 = (bf16[8,4,192]{2,1,0:T(4,128)(2,1)S(1)}, bf16[8,4,192]{2,1,0:T(4,128)(2,1)S(1)}, u32[]{:S(2)}, u32[]{:S(2)}) collective-permute-start(bf16[8,4,192]{2,1,0:T(4,128)(2,1)S(1)} %get-tuple-element.52), channel_id=1, source_target_pairs={{0,15},{1,12},{2,13},{3,14},{4,3},{5,0},{6,1},{7,2},{8,7},{9,4},{1... | collective-permute-start | bytes 36872 | tf_op jit(solution)/shard_map/ppermute | solution.py:705
  8.9 0.9 %copy-start.1 = (bf16[192,192]{1,0:T(8,128)(2,1)S(1)}, bf16[192,192]{1,0:T(8,128)(2,1)}, u32[]{:S(2)}) copy-start(bf16[192,192]{1,0:T(8,128)(2,1)} %w_proj.3) | copy-start | bytes 221188
  14.7 1.4 %collective-permute-start.6 = (bf16[592,128]{1,0:T(8,128)(2,1)S(1)}, bf16[592,128]{1,0:T(8,128)(2,1)S(1)}, u32[]{:S(2)}, u32[]{:S(2)}) collective-permute-start(bf16[592,128]{1,0:T(8,128)(2,1)S(1)} %get-tuple-element.67), channel_id=1, source_target_pairs={{0,4},{4,0},{8,12},{12,8},{1,5},{5,1},{9,13},{13,9},{2,6},{6,2},{1... | collective-permute-start | bytes 454664 | tf_op jit(solution)/shard_map/ppermute | solution.py:717
  16.2 5.3 %collective-permute-start.7 = (bf16[592,128]{1,0:T(8,128)(2,1)S(1)}, bf16[592,128]{1,0:T(8,128)(2,1)S(1)}, u32[]{:S(2)}, u32[]{:S(2)}) collective-permute-start(bf16[592,128]{1,0:T(8,128)(2,1)S(1)} %add_convert_fusion.a), channel_id=1, source_target_pairs={{0,1},{1,0},{2,3},{3,2},{4,12},{5,13},{6,14},{7,15},{8,9},{9,8},{1... | collective-permute-start | bytes 454664 | tf_op jit(solution)/shard_map/ppermute | solution.py:724
  19.2 5.1 %collective-permute-start.4 = (bf16[4,192,128]{2,1,0:T(8,128)(2,1)S(1)}, bf16[4,192,128]{2,1,0:T(8,128)(2,1)S(1)}, u32[]{:S(2)}, u32[]{:S(2)}) collective-permute-start(bf16[4,192,128]{2,1,0:T(8,128)(2,1)S(1)} %get-tuple-element.62), channel_id=1, source_target_pairs={{12,0},{0,4},{4,8},{8,12},{13,1},{1,5},{5,9},{9,13},{14,2},{2,6},{... | collective-permute-start | bytes 589832 | tf_op jit(solution)/shard_map/ppermute | solution.py:715
  21.5 5.3 %collective-permute-start.8 = (bf16[592,128]{1,0:T(8,128)(2,1)S(1)}, bf16[592,128]{1,0:T(8,128)(2,1)S(1)}, u32[]{:S(2)}, u32[]{:S(2)}) collective-permute-start(bf16[592,128]{1,0:T(8,128)(2,1)S(1)} %add.8.a), channel_id=1, source_target_pairs={{0,8},{1,9},{2,10},{3,11},{4,6},{5,7},{6,4},{7,5},{8,0},{9,1},{10,... | collective-permute-start | bytes 454664 | tf_op jit(solution)/shard_map/ppermute | solution.py:724
  24.4 5.6 %collective-permute-start.5 = (bf16[8,4,192]{2,1,0:T(4,128)(2,1)S(1)}, bf16[8,4,192]{2,1,0:T(4,128)(2,1)S(1)}, u32[]{:S(2)}, u32[]{:S(2)}) collective-permute-start(bf16[8,4,192]{2,1,0:T(4,128)(2,1)S(1)} %collect.1.refs_0_), channel_id=1, source_target_pairs={{3,0},{0,1},{1,2},{2,3},{7,4},{4,5},{5,6},{6,7},{11,8},{8,9},{9,10... | collective-permute-start | bytes 36872 | tf_op jit(solution)/shard_map/ppermute | solution.py:730
  26.8 6.8 %collective-permute-start.9 = (bf16[592,128]{1,0:T(8,128)(2,1)S(1)}, bf16[592,128]{1,0:T(8,128)(2,1)S(1)}, u32[]{:S(2)}, u32[]{:S(2)}) collective-permute-start(bf16[592,128]{1,0:T(8,128)(2,1)S(1)} %add.9.a), channel_id=1, source_target_pairs={{0,2},{1,3},{2,0},{3,1},{4,5},{5,4},{6,7},{7,6},{8,10},{9,11},{10,... | collective-permute-start | bytes 454664 | tf_op jit(solution)/shard_map/ppermute | solution.py:724
  33.6 1.4 %collective-permute-start.10 = (bf16[592,128]{1,0:T(8,128)(2,1)S(1)}, bf16[592,128]{1,0:T(8,128)(2,1)S(1)}, u32[]{:S(2)}, u32[]{:S(2)}) collective-permute-start(bf16[592,128]{1,0:T(8,128)(2,1)S(1)} %add.10.mine), channel_id=1, source_target_pairs={{0,4},{4,0},{8,12},{12,8},{1,5},{5,1},{9,13},{13,9},{2,6},{6,2},{1... | collective-permute-start | bytes 454664 | tf_op jit(solution)/shard_map/ppermute | solution.py:738

commit v11 on v9

--- a/solution.py
+++ b/solution.py
@@ -599,17 +599,20 @@
 
 def write_half(half, row, factor, wqkv, wproj, wide, tall, sems):
     part = wide.shape[0]
-    whole = jnp.concatenate([half[j * part : (j + 1) * part, :] for j in range(6)], axis=1)
-    whole = whole.astype(F32) * factor
-    wide[...] = whole[:, : wide.shape[1]]
-    tall[...] = whole[:, wide.shape[1] :]
-    rows = pl.ds(pl.multiple_of(row, 8), part)
-    copies = [
-        pltpu.make_async_copy(wide, wqkv.at[rows], sems.at[0]),
-        pltpu.make_async_copy(tall, wproj.at[rows], sems.at[1]),
-    ]
-    for copy in copies:
-        copy.start()
+    piece = part // 2
+    copies = []
+    for n in range(2):
+        whole = jnp.concatenate(
+            [half[j * part + n * piece : j * part + (n + 1) * piece, :] for j in range(6)], axis=1
+        )
+        whole = whole.astype(F32) * factor
+        here = pl.ds(n * piece, piece)
+        wide[here, :] = whole[:, : wide.shape[1]]
+        tall[here, :] = whole[:, wide.shape[1] :]
+        rows = pl.ds(pl.multiple_of(row + n * piece, 8), piece)
+        for k, (source, dest) in enumerate(((wide, wqkv), (tall, wproj))):
+            copies.append(pltpu.make_async_copy(source.at[here], dest.at[rows], sems.at[2 * n + k]))
+            copies[-1].start()
     return copies
 
 
@@ -628,8 +631,8 @@
     row = jnp.concatenate((a, b), axis=1).astype(F32)
     row = jnp.where(core() == 0, row, swapped)
     line[...] = row[0:1, :channels] * factor
-    copies.append(pltpu.make_async_copy(line, gain, sems.at[2]))
-    copies[2].start()
+    copies.append(pltpu.make_async_copy(line, gain, sems.at[4]))
+    copies[4].start()
     for copy in copies:
         copy.wait()
 
@@ -639,7 +642,7 @@
         pltpu.VMEM((channels // 2, 3 * channels), F32),
         pltpu.VMEM((channels // 2, channels), F32),
         pltpu.VMEM((1, channels), F32),
-        pltpu.SemaphoreType.DMA((3,)),
+        pltpu.SemaphoreType.DMA((5,)),
     ]
 
 

time: 35.7 us -> 35.8 us (level)
  no operation moved by 1% of the time
where the time goes in v11:
time: 35.8 us; the launch traced here: 35.6 us
  starting transfers between devices  14.1 us (39%)
  Pallas kernels  10.6 us (30%)
  waiting for transfers between devices  9.82 us (27%)
  between operations  0.78 us (2%)
    ppermute x3, waiting for transfers between devices, on_device(): arrived = lax.ppermute(total, ('row', 'col'), route)  6.27 us
    ppermute x3, starting transfers between devices, on_device(): arrived = lax.ppermute(total, ('row', 'col'), route)  6.17 us
    ppermute x1, starting transfers between devices, on_device(): strip = lax.ppermute(strip, 'col', left)  3.65 us
    pallas_call x1, Pallas kernels, second(): pl.pallas_call(second_body, out_shape=(shape(F32, *half.shape), half, sha...  2.52 us
    ppermute x1, starting transfers between devices, on_device(): row_halo = lax.ppermute(message, 'row', up)  2.43 us
    pallas_call x1, Pallas kernels, first(): pl.pallas_call(first_body, out_shape=(block, block, shape(F32, 2 * half_r...  2.04 us
    ppermute x1, waiting for transfers between devices, on_device(): rows_back = lax.ppermute(high, 'row', turn(up))  1.49 us
    pallas_call x1, Pallas kernels, back(): pl.pallas_call(back_body, out_shape=(shape(BF16, half_rows, channels, col...  1.33 us
  transfers between devices with their start and end apart: 10, of which 7 were waited for; matrix products, arithmetic and copies ran while one was open for 0% of the time, Pallas kernels for 17%

profile of v11, /device:TPU:0, one launch (start us, length us, event | category | flops | bytes accessed | tf_op | source)
XLA Modules:
  0.0 35.6 jit_solution(15963847746935066299)
XLA Ops:
  0.6 0.0 copy-start.2
  0.6 1.1 %gather.1.message = bf16[8,192,128]{2,1,0:T(8,128)(2,1)S(1)} custom-call(bf16[8,192,128]{2,1,0:T(8,128)(2,1)} %bitcast.5, bf16[8,192,128]{2,1,0:T(8,128)(2,1)} %bitcast.7), custom_call_target="tpu_custom_call" | custom-call | tf_op jit(solution)/shard_map/gather/pallas_call | solution.py:64
  1.7 0.0 copy-start.3
  1.7 2.4 %collective-permute-start = (bf16[8,192,128]{2,1,0:T(8,128)(2,1)S(1)}, bf16[8,192,128]{2,1,0:T(8,128)(2,1)S(1)}, u32[]{:S(2)}, u32[]{:S(2)}) collective-permute-start(bf16[8,192,128]{2,1,0:T(8,128)(2,1)S(1)} %gather.1.message), channel_id=1, source_target_pairs={{0,12},{4,0},{8,4},{12,8},{1,13},{5,1},{9,5},{13,9},{2,14},{6,2},{... | collective-permute-start | bytes 1179656 | tf_op jit(solution)/shard_map/ppermute | solution.py:704
  4.2 0.0 copy-done.2
  4.2 0.0 copy-done.3
  4.3 0.0 copy-start
  4.3 0.2 strips.1
  4.5 3.6 %collective-permute-start.1 = (bf16[8,4,192]{2,1,0:T(4,128)(2,1)S(1)}, bf16[8,4,192]{2,1,0:T(4,128)(2,1)S(1)}, u32[]{:S(2)}, u32[]{:S(2)}) collective-permute-start(bf16[8,4,192]{2,1,0:T(4,128)(2,1)S(1)} %get-tuple-element.47), channel_id=1, source_target_pairs={{0,3},{1,0},{2,1},{3,2},{4,7},{5,4},{6,5},{7,6},{8,11},{9,8},{10,9... | collective-permute-start | bytes 36872 | tf_op jit(solution)/shard_map/ppermute | solution.py:707
  8.2 0.5 %collective-permute-start.2 = (bf16[8,4,192]{2,1,0:T(4,128)(2,1)S(1)}, bf16[8,4,192]{2,1,0:T(4,128)(2,1)S(1)}, u32[]{:S(2)}, u32[]{:S(2)}) collective-permute-start(bf16[8,4,192]{2,1,0:T(4,128)(2,1)S(1)} %get-tuple-element.48), channel_id=1, source_target_pairs={{0,15},{1,12},{2,13},{3,14},{4,3},{5,0},{6,1},{7,2},{8,7},{9,4},{1... | collective-permute-start | bytes 36872 | tf_op jit(solution)/shard_map/ppermute | solution.py:708
  8.7 0.0 copy-done
  8.7 0.0 copy-start.1
  8.7 0.7 %prep.1 = (f32[4,128,192]{2,1,0:T(8,128)S(1)}, f32[4,128,192]{2,1,0:T(8,128)S(1)}, f32[4,128]{1,0:T(4,128)S(1)}, bf16[576,192]{1,0:T(8,128)(2,1)S(1)}, f32[1,192]{1,0:T(1,128)S(1)}) custom-call(bf16[8,192,128]{2,1,0:T(8,128)(2,1)S(1)} %pad_maximum_fusion.rest, bf16[192,576]{1,0:T(8,128)(2,1)S(1)} %copy-done, f32[1,192]{1,0:T(1,128)} %bitcast.9), custom_call_target="tpu_custom_call" | custom-call | tf_op jit(solution)/shard_map/prep/pallas_call | solution.py:117
  9.4 0.0 collective-permute-done.row_halo
  9.5 0.1 copy-done.1
  9.6 2.0 %first.1 = (f32[4,128,192]{2,1,0:T(8,128)S(1)}, f32[4,128,192]{2,1,0:T(8,128)S(1)}, f32[8,128]{1,0:T(8,128)S(1)}, bf16[192,512]{1,0:T(8,128)(2,1)S(1)}, bf16[512...) custom-call(f32[4,128,192]{2,1,0:T(8,128)S(1)} %get-tuple-element.37, ...), custom_call_target="tpu_custom_call" | custom-call | tf_op jit(solution)/shard_map/first/pallas_call | solution.py:350
  11.7 0.0 collective-permute-done.1.strip.refs_13_
  11.7 0.0 collective-permute-done.2.corner.refs_14_
  11.7 2.5 %second.1 = (f32[592,128]{1,0:T(8,128)S(1)}, bf16[592,128]{1,0:T(8,128)(2,1)S(1)}, f32[2,4,4,192]{3,2,1,0:T(4,128)S(1)}, f32[2,4,4,128]{3,2,1,0:T(4,128)S(1)}, b...) custom-call(f32[4,128,192]{2,1,0:T(8,128)S(1)} %get-tuple-element.37.hat_low.refs_6_, ...), custom_call_target="tpu_custom_call" | custom-call | tf_op jit(solution)/shard_map/second/pallas_call | solution.py:440
  14.2 0.8 %collective-permute-start.5 = (bf16[592,128]{1,0:T(8,128)(2,1)S(1)}, bf16[592,128]{1,0:T(8,128)(2,1)S(1)}, u32[]{:S(2)}, u32[]{:S(2)}) collective-permute-start(bf16[592,128]{1,0:T(8,128)(2,1)S(1)} %get-tuple-element.63), channel_id=1, source_target_pairs={{0,4},{4,0},{8,12},{12,8},{1,5},{5,1},{9,13},{13,9},{2,6},{6,2},{1... | collective-permute-start | bytes 454664 | tf_op jit(solution)/shard_map/ppermute | solution.py:720
  15.0 1.0 %collective-permute-done.5 = bf16[592,128]{1,0:T(8,128)(2,1)S(1)} collective-permute-done((bf16[592,128]{1,0:T(8,128)(2,1)S(1)}, bf16[592,128]{1,0:T(8,128)(2,1)S(1)}, u32[]{:S(2)}, u32[]{:S(2)}) %collective-permute-start.5) | collective-permute-done | bytes 151584 | tf_op jit(solution)/shard_map/ppermute | solution.py:720
  16.0 1.8 %collective-permute-start.6 = (bf16[592,128]{1,0:T(8,128)(2,1)S(1)}, bf16[592,128]{1,0:T(8,128)(2,1)S(1)}, u32[]{:S(2)}, u32[]{:S(2)}) collective-permute-start(bf16[592,128]{1,0:T(8,128)(2,1)S(1)} %add_convert_fusion.a), channel_id=1, source_target_pairs={{0,1},{1,0},{2,3},{3,2},{4,12},{5,13},{6,14},{7,15},{8,9},{9,8},{1... | collective-permute-start | bytes 454664 | tf_op jit(solution)/shard_map/ppermute | solution.py:727
  17.9 1.3 %back.1 = (bf16[4,192,128]{2,1,0:T(8,128)(2,1)S(1)}, bf16[4,192,128]{2,1,0:T(8,128)(2,1)S(1)}, bf16[4,4,192]{2,1,0:T(4,128)(2,1)S(1)}) custom-call(bf16[192,512]{1,0:T(8,128)(2,1)S(1)} %get-tuple-element.42.dq_t_a.refs_0_, bf16[512,192]{1,0:T(8,128)(2,1)S(1)} %get-tuple-element.43.dk_n_a.refs_1_, bf16[512,192]{1,0:T(8,128)(2,1)S(1)} %get-tuple-element.44.dv_n_a.refs_2_, ...), custom_call_target="tpu_custom_call" | custom-call | flops 226492416 | bytes 8388608 | tf_op jit(solution)/shard_map/back/pallas_call | solution.py:514
  19.2 0.1 collective-permute-start.3
  19.3 2.0 %collective-permute-done.6.b = bf16[592,128]{1,0:T(8,128)(2,1)S(1)} collective-permute-done((bf16[592,128]{1,0:T(8,128)(2,1)S(1)}, bf16[592,128]{1,0:T(8,128)(2,1)S(1)}, u32[]{:S(2)}, u32[]{:S(2)}) %collective-permute-start.6) | collective-permute-done | bytes 151584 | tf_op jit(solution)/shard_map/ppermute | solution.py:727
  21.3 1.5 %collective-permute-start.7 = (bf16[592,128]{1,0:T(8,128)(2,1)S(1)}, bf16[592,128]{1,0:T(8,128)(2,1)S(1)}, u32[]{:S(2)}, u32[]{:S(2)}) collective-permute-start(bf16[592,128]{1,0:T(8,128)(2,1)S(1)} %add.8.a), channel_id=1, source_target_pairs={{0,8},{1,9},{2,10},{3,11},{4,6},{5,7},{6,4},{7,5},{8,0},{9,1},{10,... | collective-permute-start | bytes 454664 | tf_op jit(solution)/shard_map/ppermute | solution.py:727
  22.9 1.5 %collective-permute-done.3.rows_back.high = bf16[4,192,128]{2,1,0:T(8,128)(2,1)S(1)} collective-permute-done((bf16[4,192,128]{2,1,0:T(8,128)(2,1)S(1)}, bf16[4,192,128]{2,1,0:T(8,128)(2,1)S(1)}, u32[]{:S(2)}, u32[]{:S(2)}) %collective-permute-start.3) | collective-permute-done | bytes 196640 | tf_op jit(solution)/shard_map/ppermute | solution.py:718
  24.3 0.1 collect.1.refs_0_
  24.4 0.3 collective-permute-start.4
  24.7 1.8 %collective-permute-done.7.b = bf16[592,128]{1,0:T(8,128)(2,1)S(1)} collective-permute-done((bf16[592,128]{1,0:T(8,128)(2,1)S(1)}, bf16[592,128]{1,0:T(8,128)(2,1)S(1)}, u32[]{:S(2)}, u32[]{:S(2)}) %collective-permute-start.7) | collective-permute-done | bytes 151584 | tf_op jit(solution)/shard_map/ppermute | solution.py:727
  26.6 2.8 %collective-permute-start.8 = (bf16[592,128]{1,0:T(8,128)(2,1)S(1)}, bf16[592,128]{1,0:T(8,128)(2,1)S(1)}, u32[]{:S(2)}, u32[]{:S(2)}) collective-permute-start(bf16[592,128]{1,0:T(8,128)(2,1)S(1)} %add.9.a), channel_id=1, source_target_pairs={{0,2},{1,3},{2,0},{3,1},{4,5},{5,4},{6,7},{7,6},{8,10},{9,11},{10,... | collective-permute-start | bytes 454664 | tf_op jit(solution)/shard_map/ppermute | solution.py:727
  29.5 0.5 %collective-permute-done.4.strip = bf16[8,4,192]{2,1,0:T(4,128)(2,1)S(1)} collective-permute-done((bf16[8,4,192]{2,1,0:T(4,128)(2,1)S(1)}, bf16[8,4,192]{2,1,0:T(4,128)(2,1)S(1)}, u32[]{:S(2)}, u32[]{:S(2)}) %collective-permute-start.4) | collective-permute-done | bytes 12320 | tf_op jit(solution)/shard_map/ppermute | solution.py:733
  30.0 0.9 %join.1 = (bf16[8,192,128]{2,1,0:T(8,128)(2,1)}, f32[8,128]{1,0:T(8,128)S(1)}) custom-call(bf16[4,192,128]{2,1,0:T(8,128)(2,1)S(1)} %collective-permute-done.3.rows_back.high, bf16[4,192,128]{2,1,0:T(8,128)(2,1)S(1)} %get-tuple-element.59.low.refs_0_, bf16[8,4,192]{2,1,0:T(4,128)(2,1)S(1)} %collective-permute-done.4.strip), custom_call_target="tpu_custom_call" | custom-call | flops 4000000000 | tf_op jit(solution)/shard_map/join/pallas_call | solution.py:588
  30.9 2.4 %collective-permute-done.8.b = bf16[592,128]{1,0:T(8,128)(2,1)S(1)} collective-permute-done((bf16[592,128]{1,0:T(8,128)(2,1)S(1)}, bf16[592,128]{1,0:T(8,128)(2,1)S(1)}, u32[]{:S(2)}, u32[]{:S(2)}) %collective-permute-start.8) | collective-permute-done | bytes 151584 | tf_op jit(solution)/shard_map/ppermute | solution.py:727
  33.3 0.2 collective-permute-start.9
  33.5 0.8 %scale_own.1 = (f32[192,576]{1,0:T(8,128)}, f32[192,192]{1,0:T(8,128)}) custom-call(bf16[592,128]{1,0:T(8,128)(2,1)S(1)} %add.10.mine), custom_call_target="tpu_custom_call" | custom-call | flops 1000000000 | tf_op jit(solution)/shard_map/scale_own/pallas_call | solution.py:650
  34.3 0.5 %collective-permute-done.9.other = bf16[592,128]{1,0:T(8,128)(2,1)S(1)} collective-permute-done((bf16[592,128]{1,0:T(8,128)(2,1)S(1)}, bf16[592,128]{1,0:T(8,128)(2,1)S(1)}, u32[]{:S(2)}, u32[]{:S(2)}) %collective-permute-start.9) | collective-permute-done | bytes 151584 | tf_op jit(solution)/shard_map/ppermute | solution.py:741
  34.8 0.8 %scale_other.1 = (f32[192,576]{1,0:T(8,128)}, f32[192,192]{1,0:T(8,128)}, f32[1,192]{1,0:T(1,128)}) custom-call(bf16[592,128]{1,0:T(8,128)(2,1)S(1)} %add.10.mine, bf16[592,128]{1,0:T(8,128)(2,1)S(1)} %collective-permute-done.9.other, f32[192,576]{1,0:T(8,128)} %get-tuple-element.65.wqkv_in, ...), custom_call_target="tpu_custom_call", output_to_operand_aliasing={{0}: (2, {}), {1}: (3, {})} | custom-call | tf_op jit(solution)/shard_map/scale_other/pallas_call | solution.py:663
  (7 shorter events, 0.2 us)
Async XLA Ops:
  0.6 3.6 %copy-start.2 = (bf16[8,128,192]{1,2,0:T(8,128)(2,1)S(1)}, bf16[8,128,192]{1,2,0:T(8,128)(2,1)}, u32[]{:S(2)}) copy-start(bf16[8,128,192]{1,2,0:T(8,128)(2,1)} %param.5) | copy-start | bytes 1179652
  1.7 2.5 %copy-start.3 = (bf16[8,128,192]{1,2,0:T(8,128)(2,1)S(1)}, bf16[8,128,192]{1,2,0:T(8,128)(2,1)}, u32[]{:S(2)}) copy-start(bf16[8,128,192]{1,2,0:T(8,128)(2,1)} %param.6) | copy-start | bytes 1179652
  1.7 7.7 %collective-permute-start = (bf16[8,192,128]{2,1,0:T(8,128)(2,1)S(1)}, bf16[8,192,128]{2,1,0:T(8,128)(2,1)S(1)}, u32[]{:S(2)}, u32[]{:S(2)}) collective-permute-start(bf16[8,192,128]{2,1,0:T(8,128)(2,1)S(1)} %gather.1.message), channel_id=1, source_target_pairs={{0,12},{4,0},{8,4},{12,8},{1,13},{5,1},{9,5},{13,9},{2,14},{6,2},{... | collective-permute-start | bytes 1179656 | tf_op jit(solution)/shard_map/ppermute | solution.py:704
  4.3 4.4 %copy-start = (bf16[192,576]{1,0:T(8,128)(2,1)S(1)}, bf16[192,576]{1,0:T(8,128)(2,1)}, u32[]{:S(2)}) copy-start(bf16[192,576]{1,0:T(8,128)(2,1)} %w_qkv.5) | copy-start | bytes 663556
  4.5 7.1 %collective-permute-start.1 = (bf16[8,4,192]{2,1,0:T(4,128)(2,1)S(1)}, bf16[8,4,192]{2,1,0:T(4,128)(2,1)S(1)}, u32[]{:S(2)}, u32[]{:S(2)}) collective-permute-start(bf16[8,4,192]{2,1,0:T(4,128)(2,1)S(1)} %get-tuple-element.47), channel_id=1, source_target_pairs={{0,3},{1,0},{2,1},{3,2},{4,7},{5,4},{6,5},{7,6},{8,11},{9,8},{10,9... | collective-permute-start | bytes 36872 | tf_op jit(solution)/shard_map/ppermute | solution.py:707
  8.2 3.5 %collective-permute-start.2 = (bf16[8,4,192]{2,1,0:T(4,128)(2,1)S(1)}, bf16[8,4,192]{2,1,0:T(4,128)(2,1)S(1)}, u32[]{:S(2)}, u32[]{:S(2)}) collective-permute-start(bf16[8,4,192]{2,1,0:T(4,128)(2,1)S(1)} %get-tuple-element.48), channel_id=1, source_target_pairs={{0,15},{1,12},{2,13},{3,14},{4,3},{5,0},{6,1},{7,2},{8,7},{9,4},{1... | collective-permute-start | bytes 36872 | tf_op jit(solution)/shard_map/ppermute | solution.py:708
  8.7 0.9 %copy-start.1 = (bf16[192,192]{1,0:T(8,128)(2,1)S(1)}, bf16[192,192]{1,0:T(8,128)(2,1)}, u32[]{:S(2)}) copy-start(bf16[192,192]{1,0:T(8,128)(2,1)} %w_proj.3) | copy-start | bytes 221188
  14.2 1.8 %collective-permute-start.5 = (bf16[592,128]{1,0:T(8,128)(2,1)S(1)}, bf16[592,128]{1,0:T(8,128)(2,1)S(1)}, u32[]{:S(2)}, u32[]{:S(2)}) collective-permute-start(bf16[592,128]{1,0:T(8,128)(2,1)S(1)} %get-tuple-element.63), channel_id=1, source_target_pairs={{0,4},{4,0},{8,12},{12,8},{1,5},{5,1},{9,13},{13,9},{2,6},{6,2},{1... | collective-permute-start | bytes 454664 | tf_op jit(solution)/shard_map/ppermute | solution.py:720
  16.0 5.3 %collective-permute-start.6 = (bf16[592,128]{1,0:T(8,128)(2,1)S(1)}, bf16[592,128]{1,0:T(8,128)(2,1)S(1)}, u32[]{:S(2)}, u32[]{:S(2)}) collective-permute-start(bf16[592,128]{1,0:T(8,128)(2,1)S(1)} %add_convert_fusion.a), channel_id=1, source_target_pairs={{0,1},{1,0},{2,3},{3,2},{4,12},{5,13},{6,14},{7,15},{8,9},{9,8},{1... | collective-permute-start | bytes 454664 | tf_op jit(solution)/shard_map/ppermute | solution.py:727
  19.2 5.1 %collective-permute-start.3 = (bf16[4,192,128]{2,1,0:T(8,128)(2,1)S(1)}, bf16[4,192,128]{2,1,0:T(8,128)(2,1)S(1)}, u32[]{:S(2)}, u32[]{:S(2)}) collective-permute-start(bf16[4,192,128]{2,1,0:T(8,128)(2,1)S(1)} %get-tuple-element.58), channel_id=1, source_target_pairs={{12,0},{0,4},{4,8},{8,12},{13,1},{1,5},{5,9},{9,13},{14,2},{2,6},{... | collective-permute-start | bytes 589832 | tf_op jit(solution)/shard_map/ppermute | solution.py:718
  21.3 5.3 %collective-permute-start.7 = (bf16[592,128]{1,0:T(8,128)(2,1)S(1)}, bf16[592,128]{1,0:T(8,128)(2,1)S(1)}, u32[]{:S(2)}, u32[]{:S(2)}) collective-permute-start(bf16[592,128]{1,0:T(8,128)(2,1)S(1)} %add.8.a), channel_id=1, source_target_pairs={{0,8},{1,9},{2,10},{3,11},{4,6},{5,7},{6,4},{7,5},{8,0},{9,1},{10,... | collective-permute-start | bytes 454664 | tf_op jit(solution)/shard_map/ppermute | solution.py:727
  24.4 5.6 %collective-permute-start.4 = (bf16[8,4,192]{2,1,0:T(4,128)(2,1)S(1)}, bf16[8,4,192]{2,1,0:T(4,128)(2,1)S(1)}, u32[]{:S(2)}, u32[]{:S(2)}) collective-permute-start(bf16[8,4,192]{2,1,0:T(4,128)(2,1)S(1)} %collect.1.refs_0_), channel_id=1, source_target_pairs={{3,0},{0,1},{1,2},{2,3},{7,4},{4,5},{5,6},{6,7},{11,8},{8,9},{9,10... | collective-permute-start | bytes 36872 | tf_op jit(solution)/shard_map/ppermute | solution.py:733
  26.6 6.7 %collective-permute-start.8 = (bf16[592,128]{1,0:T(8,128)(2,1)S(1)}, bf16[592,128]{1,0:T(8,128)(2,1)S(1)}, u32[]{:S(2)}, u32[]{:S(2)}) collective-permute-start(bf16[592,128]{1,0:T(8,128)(2,1)S(1)} %add.9.a), channel_id=1, source_target_pairs={{0,2},{1,3},{2,0},{3,1},{4,5},{5,4},{6,7},{7,6},{8,10},{9,11},{10,... | collective-permute-start | bytes 454664 | tf_op jit(solution)/shard_map/ppermute | solution.py:727
  33.3 1.4 %collective-permute-start.9 = (bf16[592,128]{1,0:T(8,128)(2,1)S(1)}, bf16[592,128]{1,0:T(8,128)(2,1)S(1)}, u32[]{:S(2)}, u32[]{:S(2)}) collective-permute-start(bf16[592,128]{1,0:T(8,128)(2,1)S(1)} %add.10.mine), channel_id=1, source_target_pairs={{0,4},{4,0},{8,12},{12,8},{1,5},{5,1},{9,13},{13,9},{2,6},{6,2},{1... | collective-permute-start | bytes 454664 | tf_op jit(solution)/shard_map/ppermute | solution.py:741
